TPU v7x, 32 devices: a whole 2x2x4 slice. The times are simulated.
32 devices in a mesh: lon: 2 (over x), lat: 4 (over z), lev: 4 (over y, core).
Axes of the slice: x: 2, y: 2, z: 4, core: 2. Of those that a mesh axis runs over, the one named last changes fastest.
Arguments:
- tokens_in: bfloat16 [4, 64, 32, 512], P('lev', 'lat', 'lon'), may hold values from -6 to 6
- cotangent: bfloat16 [4, 64, 32, 512], P('lev', 'lat', 'lon'), may hold values from -6 to 6
- qkv_weight: bfloat16 [512, 1536], replicated, may hold values from -5 to 5
- out_weight: bfloat16 [512, 512], replicated, may hold values from -0.25 to 0.25
- norm_gain: float32 [512], replicated, may hold values from 0.5 to 1.5
- ocean_mask: int32 [4, 64, 32], P('lev', 'lat', 'lon'), may hold values from 0 to 1, as said below
Outputs:
- layer_out: bfloat16 [4, 64, 32, 512], P('lev', 'lat', 'lon')
- input_grad: bfloat16 [4, 64, 32, 512], P('lev', 'lat', 'lon')
- qkv_grad: float32 [512, 1536], P('lev')
- out_grad: float32 [512, 512], P('lev')
- gain_grad: float32 [512], P('lev')
Inputs may be any that keep to these rules, and one draw needn't show every extreme that they name: `ocean_mask`: at each level group, at most 3 of the windows of one device hold an ocean patch, and some device holds exactly 3 such windows.
All inputs are finite; a program needn't handle non-finite values.
Results may differ from a plain program's by a relative error of at most 0.017.
The roundings to bfloat16 on the way count: a program that leaves them out, or rounds other values in their place, can miss the bound.
Values may be sent and summed in bfloat16 or wider, within the bound.
No kernel may reach another device: no remote copies, remote signals or barrier semaphores. Data moves between devices by JAX's collectives and lax.ppermute only.
A program may use at most 128 MiB of HBM per device.

v0:
```python
import jax
import jax.numpy as jnp
from jax import lax
from jax.sharding import PartitionSpec as P

HEADS = 8
WIN = 8


def with_halo(block, sides, width, periodic):
    for axis, dim in sides:
        count = lax.axis_size(axis)
        forward = [(i, i + 1) for i in range(count - 1)]
        if periodic:
            forward.append((count - 1, 0))
        backward = [(target, source) for source, target in forward]
        low = lax.ppermute(
            lax.slice_in_dim(block, block.shape[dim] - width, None, axis=dim), axis, forward
        )
        high = lax.ppermute(lax.slice_in_dim(block, 0, width, axis=dim), axis, backward)
        block = jnp.concatenate([low, block, high], axis=dim)
    return block


def norm_rows(values_in):
    center = values_in - jnp.mean(values_in, axis=-1, keepdims=True)
    spread = jnp.mean(center * center, axis=-1, keepdims=True)
    scaling = lax.rsqrt(spread + 1e-05)
    return (center * scaling, scaling)


def to_windows(grid_in, lat_windows, lon_windows, window_side):
    channels = grid_in.shape[-1]
    blocks = grid_in.reshape(lat_windows, window_side, lon_windows, window_side, channels)
    return jnp.transpose(blocks, (0, 2, 1, 3, 4)).reshape(
        lat_windows * lon_windows, window_side * window_side, channels
    )


def from_windows(blocks, lat_windows, lon_windows, window_side):
    channels = blocks.shape[-1]
    grid_out = blocks.reshape(lat_windows, lon_windows, window_side, window_side, channels)
    return jnp.transpose(grid_out, (0, 2, 1, 3, 4)).reshape(
        lat_windows * window_side, lon_windows * window_side, channels
    )


def neighbours(padded, lat_windows, lon_windows, window_side):
    pieces = []
    for lat_step in range(3):
        for lon_step in range(3):
            section = padded[
                lat_step * window_side : (lat_step + lat_windows) * window_side,
                lon_step * window_side : (lon_step + lon_windows) * window_side,
            ]
            pieces.append(to_windows(section, lat_windows, lon_windows, window_side))
    return jnp.concatenate(pieces, axis=1)


def spread_back(gathered, lat_windows, lon_windows, window_side):
    channels = gathered.shape[-1]
    window_area = window_side * window_side
    totals = jnp.zeros(
        ((lat_windows + 2) * window_side, (lon_windows + 2) * window_side, channels), jnp.float32
    )
    for lat_step in range(3):
        for lon_step in range(3):
            slot_index = lat_step * 3 + lon_step
            section = from_windows(
                gathered[:, slot_index * window_area : (slot_index + 1) * window_area],
                lat_windows,
                lon_windows,
                window_side,
            )
            totals = totals.at[
                lat_step * window_side : (lat_step + lat_windows) * window_side,
                lon_step * window_side : (lon_step + lon_windows) * window_side,
            ].add(section)
    return totals


def split_heads(array_in, head_count):
    return array_in.reshape(
        array_in.shape[0], array_in.shape[1], head_count, array_in.shape[2] // head_count
    )


def attend_forward(queries, key_rows, value_rows, key_mask, alive_flag, head_count):
    features = queries.shape[-1]
    inv_root = (features // head_count) ** (-0.5)
    scores = (
        jnp.einsum(
            "wqhd,wkhd->whqk",
            split_heads(queries, head_count),
            split_heads(key_rows, head_count),
            preferred_element_type=jnp.float32,
        )
        * inv_root
    )
    scores = scores + (key_mask[:, None, None, :] - 1.0) * 1000000000.0
    row_top = jnp.max(scores, axis=-1, keepdims=True)
    weights = jnp.exp(scores - row_top)
    probabilities = weights / jnp.sum(weights, axis=-1, keepdims=True)
    probabilities_low = probabilities.astype(jnp.bfloat16)
    mixed_out = jnp.einsum(
        "whqk,wkhd->wqhd",
        probabilities_low,
        split_heads(value_rows, head_count),
        preferred_element_type=jnp.float32,
    )
    mixed_out = mixed_out.reshape(queries.shape) * alive_flag[:, None, None]
    return (mixed_out.astype(jnp.bfloat16), probabilities)


def attend_backward(
    queries, key_rows, value_rows, probabilities, mixed_out, grad_mixed, head_count
):
    features = queries.shape[-1]
    inv_root = (features // head_count) ** (-0.5)
    grad_heads = split_heads(grad_mixed, head_count)
    query_heads = split_heads(queries, head_count)
    grad_probs = jnp.einsum(
        "wqhd,wkhd->whqk",
        grad_heads,
        split_heads(value_rows, head_count),
        preferred_element_type=jnp.float32,
    )
    delta_rows = jnp.einsum(
        "wqhd,wqhd->whq",
        grad_heads,
        split_heads(mixed_out, head_count),
        preferred_element_type=jnp.float32,
    )
    grad_scores = (probabilities * (grad_probs - delta_rows[..., None]) * inv_root).astype(
        jnp.bfloat16
    )
    grad_query = jnp.einsum(
        "whqk,wkhd->wqhd",
        grad_scores,
        split_heads(key_rows, head_count),
        preferred_element_type=jnp.float32,
    ).reshape(queries.shape)
    key_shape = (key_rows.shape[0], key_rows.shape[1], features)
    grad_key = jnp.einsum(
        "whqk,wqhd->wkhd", grad_scores, query_heads, preferred_element_type=jnp.float32
    ).reshape(key_shape)
    grad_value = jnp.einsum(
        "whqk,wqhd->wkhd",
        probabilities.astype(jnp.bfloat16),
        grad_heads,
        preferred_element_type=jnp.float32,
    ).reshape(key_shape)
    return (grad_query, jnp.concatenate([grad_key, grad_value], axis=-1))


def fold_lat(grad_pad, window_side):
    inner_rows = grad_pad.shape[0] - 2 * window_side
    filler = jnp.zeros((inner_rows - 2 * window_side,) + grad_pad.shape[1:], jnp.float32)
    folded = jnp.concatenate(
        [grad_pad[:window_side], filler, grad_pad[inner_rows + window_side :]], axis=0
    )
    arrived = with_halo(folded, (("lat", 0),), window_side, False)
    middle = grad_pad[window_side : inner_rows + window_side]
    middle = middle.at[:window_side].add(arrived[:window_side])
    return middle.at[inner_rows - window_side :].add(arrived[inner_rows + window_side :])


def fold_lon(grad_pad, window_side):
    inner_cols = grad_pad.shape[1] - 2 * window_side
    filler = jnp.zeros(
        (grad_pad.shape[0], inner_cols - 2 * window_side, grad_pad.shape[2]), jnp.float32
    )
    folded = jnp.concatenate(
        [grad_pad[:, :window_side], filler, grad_pad[:, inner_cols + window_side :]], axis=1
    )
    arrived = with_halo(folded, (("lon", 1),), window_side, True)
    middle = grad_pad[:, window_side : inner_cols + window_side]
    middle = middle.at[:, :window_side].add(arrived[:, :window_side])
    return middle.at[:, inner_cols - window_side :].add(arrived[:, inner_cols + window_side :])


def plane_sum(gradients):
    return lax.psum((gradients[0], gradients[1], gradients[2]), ("lon", "lat"))


def level_share(gradients):
    return (
        lax.psum_scatter(gradients[0], "lev", scatter_dimension=0, tiled=True),
        lax.psum_scatter(gradients[1], "lev", scatter_dimension=0, tiled=True),
        lax.psum_scatter(gradients[2], "lev", scatter_dimension=0, tiled=True),
    )


def on_device(tokens_in, cotangent, qkv_weight, out_weight, norm_gain, ocean_mask):
    lat_rows = tokens_in.shape[1]
    lon_cols = tokens_in.shape[2]
    features = tokens_in.shape[3]
    window_side = WIN
    lat_windows = lat_rows // window_side
    lon_windows = lon_cols // window_side
    flat_in = tokens_in.reshape(-1, features).astype(jnp.float32)
    normed, scaling = norm_rows(flat_in)
    hidden = (normed * norm_gain).astype(jnp.bfloat16)
    ocean = ocean_mask[0].astype(jnp.float32)
    ocean_low = ocean.astype(jnp.bfloat16)
    queries = jnp.dot(hidden, qkv_weight[:, :features], preferred_element_type=jnp.float32).astype(
        jnp.bfloat16
    )
    payload = hidden.reshape(lat_rows, lon_cols, features)
    padded, padded_mask = (
        with_halo(payload, (("lat", 0), ("lon", 1)), window_side, True),
        with_halo(ocean_low, (("lat", 0), ("lon", 1)), window_side, True),
    )
    lat_place = lax.axis_index("lat")
    lat_count = lax.axis_size("lat")
    row_ids = jnp.arange(lat_rows + 2 * window_side)
    keep_rows = jnp.where(
        row_ids < window_side,
        lat_place > 0,
        jnp.where(row_ids >= lat_rows + window_side, lat_place < lat_count - 1, True),
    )
    keep_low = keep_rows.astype(jnp.bfloat16)
    padded = padded * keep_low[:, None, None]
    padded_mask = padded_mask * keep_low[:, None]
    key_vals = jnp.dot(
        padded.reshape(-1, features), qkv_weight[:, features:], preferred_element_type=jnp.float32
    ).astype(jnp.bfloat16)
    key_vals = key_vals.reshape(
        lat_rows + 2 * window_side, lon_cols + 2 * window_side, 2 * features
    )
    near = neighbours(key_vals, lat_windows, lon_windows, window_side)
    near_mask = neighbours(padded_mask[..., None], lat_windows, lon_windows, window_side)[
        ..., 0
    ].astype(jnp.float32)
    query_windows = to_windows(
        queries.reshape(lat_rows, lon_cols, features), lat_windows, lon_windows, window_side
    )
    ocean_windows = to_windows(ocean[..., None], lat_windows, lon_windows, window_side)[..., 0]
    alive_flag = jnp.max(ocean_windows, axis=1)
    grad_branch = (cotangent[0] * ocean_low[..., None]).reshape(-1, features)
    grad_mixed = jnp.einsum(
        "te,de->td", grad_branch, out_weight, preferred_element_type=jnp.float32
    ).astype(jnp.bfloat16)
    grad_windows = to_windows(
        grad_mixed.reshape(lat_rows, lon_cols, features), lat_windows, lon_windows, window_side
    )
    key_rows = near[..., :features]
    value_rows = near[..., features:]
    mixed_windows, probabilities = attend_forward(
        query_windows, key_rows, value_rows, near_mask, alive_flag, HEADS
    )
    grad_query, grad_near = attend_backward(
        query_windows, key_rows, value_rows, probabilities, mixed_windows, grad_windows, HEADS
    )
    mixed_flat = from_windows(mixed_windows, lat_windows, lon_windows, window_side).reshape(
        -1, features
    )
    branch = jnp.dot(mixed_flat, out_weight, preferred_element_type=jnp.float32)
    layer_out = (
        (flat_in + ocean.reshape(-1, 1) * branch).astype(jnp.bfloat16).reshape(tokens_in.shape)
    )
    out_grad_local = jnp.einsum(
        "td,te->de", mixed_flat, grad_branch, preferred_element_type=jnp.float32
    )
    grad_pad = spread_back(grad_near, lat_windows, lon_windows, window_side)
    grad_kv = fold_lon(fold_lat(grad_pad, window_side), window_side)
    grad_query_flat = from_windows(grad_query, lat_windows, lon_windows, window_side).reshape(
        -1, features
    )
    grad_qkv = jnp.concatenate(
        [
            grad_query_flat.astype(jnp.bfloat16),
            grad_kv.reshape(-1, 2 * features).astype(jnp.bfloat16),
        ],
        axis=1,
    )
    grad_hidden = jnp.einsum("tc,dc->td", grad_qkv, qkv_weight, preferred_element_type=jnp.float32)
    qkv_grad_local = jnp.einsum("td,tc->dc", hidden, grad_qkv, preferred_element_type=jnp.float32)
    gain_grad_local = jnp.sum(grad_hidden * normed, axis=0)
    scaled = grad_hidden * norm_gain
    correction = (
        scaled
        - jnp.mean(scaled, axis=-1, keepdims=True)
        - normed * jnp.mean(scaled * normed, axis=-1, keepdims=True)
    )
    input_grad = (
        (cotangent.reshape(-1, features).astype(jnp.float32) + scaling * correction)
        .astype(jnp.bfloat16)
        .reshape(tokens_in.shape)
    )
    local_grads = (qkv_grad_local, out_grad_local, gain_grad_local)
    qkv_grad, out_grad, gain_grad = level_share(plane_sum(local_grads))
    return (layer_out, input_grad, qkv_grad, out_grad, gain_grad)


def solution(mesh):
    placed = (
        P("lev", "lat", "lon", None),
        P("lev", "lat", "lon", None),
        P(),
        P(),
        P(),
        P("lev", "lat", "lon"),
    )
    return jax.shard_map(
        on_device,
        mesh=mesh,
        in_specs=placed,
        out_specs=(
            P("lev", "lat", "lon", None),
            P("lev", "lat", "lon", None),
            P("lev", None),
            P("lev", None),
            P("lev"),
        ),
        check_vma=False,
    )
```

profile of v0, /device:TPU:0, one launch (start us, length us, event | category | flops | bytes accessed | tf_op | source)
XLA Modules:
  0.0 331.2 jit_solution(11692474018854287951)
XLA Ops:
  8.0 3.0 collective-permute-start.4
  11.0 2.0 collective-permute-start.5
  14.2 1.2 fusion.44
  16.6 2.1 collective-permute-start.1
  22.9 1.3 convolution_convert_fusion.3
  26.6 1.7 collective-permute-start.6
  30.2 1.3 copy.152
  32.1 1.4 collective-permute-start.2
  36.1 5.2 %collective-permute-done.2 = bf16[32,8,512]{2,1,0:T(8,128)(2,1)S(1)} collective-permute-done((bf16[32,8,512]{2,1,0:T(8,128)(2,1)S(1)}, bf16[32,8,512]{2,1,0:T(8,128)(2,1)S(1)}, u32[]{:S(2)}, u32[]{:S(2)}) %collective-permute-start.2) | collective-permute-done | bytes 262176 | tf_op jit(solution)/shard_map/ppermute | solution.py:17
  41.3 2.8 collective-permute-done.3
  44.4 1.2 convolution_convert_fusion
  47.2 2.6 fusion.55
  49.8 3.1 copy.117
  52.9 4.4 %copy.115 = bf16[4,576,512]{1,2,0:T(8,128)(2,1)} copy(bf16[4,576,512]{2,1,0:T(8,128)(2,1)} %get-tuple-element.178) | data formatting | bytes 4718592 | tf_op jit(solution)/shard_map/slice | solution.py:248
  57.2 5.2 %fusion.66 = (f32[4,8,64]{2,1,0:T(8,128)S(1)}, f32[4,8,64,576]{3,2,1,0:T(8,128)}) fusion(f32[4,576]{1,0:T(4,128)S(1)} %multiply_bitcast_fusion, bf16[4,64,8,64]{1,3,2,0:T(8,128)(2,1)} %copy.134, bf16[4,576,8,64]{1,3,2,0:T(8,128)(2,1)S(1)} %bitcast.263), kind=kOutput, calls=%fused_computation.148 | convolution fusion | flops 155714112 | bytes 7357440 | tf_op jit(solution)/shard_map/sub | solution.py:102
  62.5 3.0 fusion.4
  65.5 3.2 fusion.68
  68.8 1.9 multiply_reduce_fusion
  70.7 1.5 multiply_convert_fusion
  72.3 3.2 fusion.67
  75.4 5.7 %copy.136 = f32[4,576,512]{2,1,0:T(8,128)} copy(f32[4,576,512]{1,2,0:T(8,128)} %bitcast.262) | data formatting | bytes 9437184 | tf_op jit(solution)/shard_map/reshape | solution.py:146
  81.1 5.7 %copy.137 = f32[4,576,512]{2,1,0:T(8,128)} copy(f32[4,576,512]{1,2,0:T(8,128)} %bitcast.261) | data formatting | bytes 9437184 | tf_op jit(solution)/shard_map/reshape | solution.py:152
  86.9 4.1 %pad_maximum_fusion = (f32[4,64,1024]{2,1,0:T(8,128)S(1)}, f32[4,64,1024]{2,1,0:T(8,128)S(1)}, f32[4,64,1024]{2,1,0:T(8,128)S(1)}, f32[4,64,1024]{2,1,0:T(8,128)...) fusion(f32[4,576,512]{2,1,0:T(8,128)} %copy.137, ...), kind=kLoop, calls=%fused_computation.49 | loop fusion | flops 2359296 | bytes 18874368 | tf_op jit(solution)/shard_map/concatenate | solution.py:153
  94.3 1.1 copy.142
  98.7 2.5 scatter-add.44
  101.2 3.2 add_select_fusion.1
  104.4 7.3 %scatter-add.45 = f32[32,32,1024]{2,1,0:T(8,128)} dynamic-update-slice(f32[32,32,1024]{2,1,0:T(8,128)} %scatter-add.44, f32[16,16,1024]{2,1,0:T(8,128)} %add_select_fusion.1, s32[]{:T(128)} %bitcast.72, s32[]{:T(128)} %bitcast.73, s32[]{:T(128)} %constant.387.clone.1) | dynamic-update-slice | bytes 2097156 | tf_op jit(solution)/shard_map/scatter-add | solution.py:78
  111.7 4.8 %add_select_fusion = f32[16,16,1024]{2,1,0:T(8,128)} fusion(f32[16,16,1024]{2,1,0:T(8,128)} %bitcast.288, f32[32,32,1024]{2,1,0:T(8,128)} %scatter-add.45, s32[]{:T(128)} %bitcast.77, s32[]{:T(128)} %bitcast.78, pred[]{:T(512)} %get-tuple-element.164), kind=kLoop, calls=%fused_computation.26 | loop fusion | flops 524288 | bytes 3145737 | tf_op jit(solution)/shard_map/select.15
  116.6 6.8 %scatter-add.46 = f32[32,32,1024]{2,1,0:T(8,128)} dynamic-update-slice(f32[32,32,1024]{2,1,0:T(8,128)} %scatter-add.45, f32[16,16,1024]{2,1,0:T(8,128)} %add_select_fusion, s32[]{:T(128)} %bitcast.77, s32[]{:T(128)} %bitcast.78, s32[]{:T(128)} %constant.387.clone.1) | dynamic-update-slice | bytes 2097156 | tf_op jit(solution)/shard_map/scatter-add | solution.py:78
  123.3 2.9 fusion.23
  126.2 2.8 fusion.22
  129.1 2.4 fusion.21
  131.5 2.4 fusion.20
  133.9 2.4 fusion.19
  136.3 2.4 fusion.18
  138.6 3.3 fusion.56
  141.9 3.2 collective-permute-start.8
  145.1 1.3 collective-permute-start.9
  147.2 1.5 slice.621
  148.7 2.5 copy.128
  151.2 2.3 reshape.894
  153.5 1.1 fusion.50
  155.4 2.3 fusion.69
  158.0 6.4 %collective-permute-done.8 = f32[8,32,1024]{2,1,0:T(8,128)} collective-permute-done((f32[8,32,1024]{2,1,0:T(8,128)}, f32[8,32,1024]{2,1,0:T(8,128)}, u32[]{:S(2)}, u32[]{:S(2)}) %collective-permute-start.8) | collective-permute-done | bytes 1048608 | tf_op jit(solution)/shard_map/ppermute | solution.py:17
  164.4 2.7 fusion.17
  167.1 2.4 collective-permute-done.9
  169.5 2.8 fusion.16
  172.3 2.3 fusion.57
  174.6 1.6 collective-permute-start.10
  176.6 1.8 fusion.5
  178.4 1.4 copy.132
  180.1 1.3 slice.626
  181.5 8.3 %collective-permute-done.10 = f32[16,8,1024]{2,1,0:T(8,128)} collective-permute-done((f32[16,8,1024]{2,1,0:T(8,128)}, f32[16,8,1024]{2,1,0:T(8,128)}, u32[]{:S(2)}, u32[]{:S(2)}) %collective-permute-start.10) | collective-permute-done | bytes 524320 | tf_op jit(solution)/shard_map/ppermute | solution.py:17
  189.7 1.3 fusion.27
  191.0 5.4 %collective-permute-done.11 = f32[16,8,1024]{2,1,0:T(8,128)} collective-permute-done((f32[16,8,1024]{2,1,0:T(8,128)}, f32[16,8,1024]{2,1,0:T(8,128)}, u32[]{:S(2)}, u32[]{:S(2)}) %collective-permute-start.11) | collective-permute-done | bytes 524320 | tf_op jit(solution)/shard_map/ppermute | solution.py:20
  196.4 1.2 fusion.26
  197.7 2.3 fusion.46
  201.3 37.5 %reduce-scatter.3.cloned.1.call-done = f32[128,1536]{1,0:T(8,128)} async-done(((f32[512,1536]{1,0:T(8,128)}), f32[128,1536]{1,0:T(8,128)}) %reduce-scatter.3.cloned.1.call-update) | async-done | bytes 786448 | tf_op jit(solution)/shard_map/reduce_scatter | solution.py:188
  239.8 2.2 fusion.42
  242.0 5.8 %all-reduce.1 = f32[512]{0:T(512)S(1)} all-reduce(f32[512]{0:T(512)S(1)} %get-tuple-element.161), channel_id=4, replica_groups=mesh['lon'=2,'lat'=4,'lev'=4] {'lev'}, use_global_device_ids=true, to_apply=%region_15.16.clone | all-reduce | flops 512 | bytes 4096
  247.8 22.4 %psum.26 = f32[128]{0:T(128)} all-reduce(f32[128]{0:T(128)S(1)} %dynamic-slice.107), channel_id=1, replica_groups=mesh['lon'=2,'lat'=4,'lev'=4] {'lon','lat'}, use_global_device_ids=true, to_apply=%region_14.15 | all-reduce | flops 128 | bytes 1024 | tf_op jit(solution)/shard_map/psum | solution.py:183
  271.3 49.7 %all-reduce.5.cloned.1.call-done = (f32[128,1536]{1,0:T(8,128)}, f32[128,512]{1,0:T(8,128)}) async-done(((f32[128,1536]{1,0:T(8,128)}, f32[128,512]{1,0:T(8,128)}), (f32[128,1536]{1,0:T(8,128)}, f32[128,512]{1,0:T(8,128)})) %all-reduce.5.cloned.1.call-update) | async-done | bytes 1048592 | tf_op jit(solution)/shard_map/psum | solution.py:183
  320.9 2.1 copy.179
  323.0 1.7 copy.180
  (172 shorter events, 28.2 us)
Async XLA Ops:
  7.2 15.1 %copy-start = (bf16[512,512]{1,0:T(8,128)(2,1)S(1)}, bf16[512,512]{1,0:T(8,128)(2,1)}, u32[]{:S(2)}) copy-start(bf16[512,512]{1,0:T(8,128)(2,1)} %param.35) | copy-start | bytes 1572868
  7.2 17.1 %copy-start.19 = (s32[3]{0:T(128)S(1)}, s32[3]{0:T(128)}, u32[]{:S(2)}) copy-start(s32[3]{0:T(128)} %constant.396.clone.1) | copy-start | bytes 40
  7.2 194.1 %reduce-scatter.5.cloned.1.call-start = ((), (), s32[]{:S(2)}) async-start(), calls=%async_computation.3 | async-start | bytes 1310720 | tf_op jit(solution)/shard_map/reduce_scatter | solution.py:189
  8.0 18.5 %collective-permute-start.4 = (bf16[8,16]{1,0:T(8,128)(2,1)S(1)}, bf16[8,16]{1,0:T(8,128)(2,1)S(1)}, u32[]{:S(2)}, u32[]{:S(2)}) collective-permute-start(bf16[8,16]{1,0:T(8,128)(2,1)S(1)} %get-tuple-element.211), channel_id=1, source_target_pairs={{0,4},{4,8},{8,12},{12,0},{1,5},{5,9},{9,13},{13,1},{2,6},{6,10},{... | collective-permute-start | bytes 776 | tf_op jit(solution)/shard_map/ppermute | solution.py:17
  11.0 15.4 %collective-permute-start.5 = (bf16[8,16]{1,0:T(8,128)(2,1)S(1)}, bf16[8,16]{1,0:T(8,128)(2,1)S(1)}, u32[]{:S(2)}, u32[]{:S(2)}) collective-permute-start(bf16[8,16]{1,0:T(8,128)(2,1)S(1)} %get-tuple-element.212), channel_id=1, source_target_pairs={{4,0},{8,4},{12,8},{0,12},{5,1},{9,5},{13,9},{1,13},{6,2},{10,6},{... | collective-permute-start | bytes 776 | tf_op jit(solution)/shard_map/ppermute | solution.py:20
  16.6 6.3 %copy-start.14 = (bf16[256,512]{1,0:T(8,128)(2,1)}, bf16[256,512]{1,0:T(8,128)(2,1)S(1)}, u32[]{:S(2)}) copy-start(bf16[256,512]{1,0:T(8,128)(2,1)S(1)} %fusion.36) | copy-start | bytes 786436
  16.6 15.4 %collective-permute-start.1 = (bf16[8,16,512]{2,1,0:T(8,128)(2,1)S(1)}, bf16[8,16,512]{2,1,0:T(8,128)(2,1)S(1)}, u32[]{:S(2)}, u32[]{:S(2)}) collective-permute-start(bf16[8,16,512]{2,1,0:T(8,128)(2,1)S(1)} %bitcast.323), channel_id=1, source_target_pairs={{4,0},{8,4},{12,8},{0,12},{5,1},{9,5},{13,9},{1,13},{6,2},{10,6},{... | collective-permute-start | bytes 393224 | tf_op jit(solution)/shard_map/ppermute | solution.py:20
  18.7 13.3 %collective-permute-start = (bf16[8,16,512]{2,1,0:T(8,128)(2,1)S(1)}, bf16[8,16,512]{2,1,0:T(8,128)(2,1)S(1)}, u32[]{:S(2)}, u32[]{:S(2)}) collective-permute-start(bf16[8,16,512]{2,1,0:T(8,128)(2,1)S(1)} %bitcast.322), channel_id=1, source_target_pairs={{0,4},{4,8},{8,12},{12,0},{1,5},{5,9},{9,13},{13,1},{2,6},{6,10},{... | collective-permute-start | bytes 393224 | tf_op jit(solution)/shard_map/ppermute | solution.py:17
  26.6 5.0 %collective-permute-start.6 = (bf16[32,8]{1,0:T(8,128)(2,1)S(1)}, bf16[32,8]{1,0:T(8,128)(2,1)S(1)}, u32[]{:S(2)}, u32[]{:S(2)}) collective-permute-start(bf16[32,8]{1,0:T(8,128)(2,1)S(1)} %get-tuple-element.207), channel_id=1, source_target_pairs={{0,16},{16,0},{1,17},{17,1},{2,18},{18,2},{3,19},{19,3},{4,20},{20... | collective-permute-start | bytes 1544 | tf_op jit(solution)/shard_map/ppermute | solution.py:17
  28.3 3.7 %collective-permute-start.7 = (bf16[32,8]{1,0:T(8,128)(2,1)S(1)}, bf16[32,8]{1,0:T(8,128)(2,1)S(1)}, u32[]{:S(2)}, u32[]{:S(2)}) collective-permute-start(bf16[32,8]{1,0:T(8,128)(2,1)S(1)} %get-tuple-element.208), channel_id=1, source_target_pairs={{16,0},{0,16},{17,1},{1,17},{18,2},{2,18},{19,3},{3,19},{20,4},{4,... | collective-permute-start | bytes 1544 | tf_op jit(solution)/shard_map/ppermute | solution.py:20
  32.1 9.1 %collective-permute-start.2 = (bf16[32,8,512]{2,1,0:T(8,128)(2,1)S(1)}, bf16[32,8,512]{2,1,0:T(8,128)(2,1)S(1)}, u32[]{:S(2)}, u32[]{:S(2)}) collective-permute-start(bf16[32,8,512]{2,1,0:T(8,128)(2,1)S(1)} %get-tuple-element.192), channel_id=1, source_target_pairs={{0,16},{16,0},{1,17},{17,1},{2,18},{18,2},{3,19},{19,3},{4,20},{20... | collective-permute-start | bytes 786440 | tf_op jit(solution)/shard_map/ppermute | solution.py:17
  33.5 10.6 %collective-permute-start.3 = (bf16[32,8,512]{2,1,0:T(8,128)(2,1)S(1)}, bf16[32,8,512]{2,1,0:T(8,128)(2,1)S(1)}, u32[]{:S(2)}, u32[]{:S(2)}) collective-permute-start(bf16[32,8,512]{2,1,0:T(8,128)(2,1)S(1)} %get-tuple-element.193), channel_id=1, source_target_pairs={{16,0},{0,16},{17,1},{1,17},{18,2},{2,18},{19,3},{3,19},{20,4},{4,... | collective-permute-start | bytes 786440 | tf_op jit(solution)/shard_map/ppermute | solution.py:20
  36.0 8.4 %copy-start.20 = (bf16[512,1536]{1,0:T(8,128)(2,1)S(1)}, bf16[512,1536]{1,0:T(8,128)(2,1)}, u32[]{:S(2)}) copy-start(bf16[512,1536]{1,0:T(8,128)(2,1)} %param.34) | copy-start | bytes 4718596
  62.4 3.1 copy-start.12
  62.4 8.3 %slice-start = ((s8[5242880]{0:T(1024)(128)(4,1)}), s8[4194304]{0:T(1024)(128)(4,1)S(1)}, s32[]{:S(2)}) async-start(s8[5242880]{0:T(1024)(128)(4,1)} %bitcast.265), calls=%async_computation.5 | async-start | bytes 8388608
  65.5 3.3 copy-start.4
  65.5 3.3 copy-start.11
  65.5 5.2 %slice-start.1 = ((s8[5242880]{0:T(1024)(128)(4,1)}), s8[1048576]{0:T(1024)(128)(4,1)S(1)}, s32[]{:S(2)}) async-start(s8[5242880]{0:T(1024)(128)(4,1)} %bitcast.265), calls=%async_computation.6 | async-start | bytes 2097152
  70.7 1.5 copy-start.6
  72.2 3.2 copy-start.2
  123.3 5.7 %copy-start.10 = (f32[2,8,2,8,1024]{4,3,2,1,0:T(8,128)S(1)}, f32[2,8,2,8,1024]{4,3,2,1,0:T(8,128)}, u32[]{:S(2)}) copy-start(f32[2,8,2,8,1024]{4,3,2,1,0:T(8,128)} %copy.143) | copy-start | bytes 3145732
  123.3 8.2 %copy-start.8 = (f32[2,8,2,8,1024]{4,3,2,1,0:T(8,128)S(1)}, f32[2,8,2,8,1024]{4,3,2,1,0:T(8,128)}, u32[]{:S(2)}) copy-start(f32[2,8,2,8,1024]{4,3,2,1,0:T(8,128)} %copy.144) | copy-start | bytes 3145732
  126.2 7.6 %copy-start.9 = (f32[2,8,2,8,1024]{4,3,2,1,0:T(8,128)S(1)}, f32[2,8,2,8,1024]{4,3,2,1,0:T(8,128)}, u32[]{:S(2)}) copy-start(f32[2,8,2,8,1024]{4,3,2,1,0:T(8,128)} %copy.145) | copy-start | bytes 3145732
  129.1 7.2 %copy-start.7 = (f32[2,8,2,8,1024]{4,3,2,1,0:T(8,128)S(1)}, f32[2,8,2,8,1024]{4,3,2,1,0:T(8,128)}, u32[]{:S(2)}) copy-start(f32[2,8,2,8,1024]{4,3,2,1,0:T(8,128)} %copy.146) | copy-start | bytes 3145732
  136.2 10.1 %copy-start.13 = (bf16[1,16,16,512]{3,2,1,0:T(8,128)(2,1)S(1)}, bf16[1,16,16,512]{3,2,1,0:T(8,128)(2,1)}, u32[]{:S(2)}) copy-start(bf16[1,16,16,512]{3,2,1,0:T(8,128)(2,1)} %param.33) | copy-start | bytes 786436
  138.6 8.6 %copy-start.1 = (f32[32,32,1024]{2,1,0:T(8,128)S(1)}, f32[32,32,1024]{2,1,0:T(8,128)}, u32[]{:S(2)}) copy-start(f32[32,32,1024]{2,1,0:T(8,128)} %fusion.18) | copy-start | bytes 12582916
  141.9 22.5 %collective-permute-start.8 = (f32[8,32,1024]{2,1,0:T(8,128)}, f32[8,32,1024]{2,1,0:T(8,128)}, u32[]{:S(2)}, u32[]{:S(2)}) collective-permute-start(f32[8,32,1024]{2,1,0:T(8,128)} %get-tuple-element.180), channel_id=1, source_target_pairs={{0,4},{4,8},{8,12},{1,5},{5,9},{9,13},{2,6},{6,10},{10,14},{3,7},{... | collective-permute-start | bytes 3145736 | tf_op jit(solution)/shard_map/ppermute | solution.py:17
  145.1 24.4 %collective-permute-start.9 = (f32[8,32,1024]{2,1,0:T(8,128)}, f32[8,32,1024]{2,1,0:T(8,128)}, u32[]{:S(2)}, u32[]{:S(2)}) collective-permute-start(f32[8,32,1024]{2,1,0:T(8,128)} %get-tuple-element.179), channel_id=1, source_target_pairs={{4,0},{8,4},{12,8},{5,1},{9,5},{13,9},{6,2},{10,6},{14,10},{7,3},{... | collective-permute-start | bytes 3145736 | tf_op jit(solution)/shard_map/ppermute | solution.py:20
  154.7 0.7 copy-start.16
  157.7 81.1 %reduce-scatter.3.cloned.1.call-start = ((), (), s32[]{:S(2)}) async-start(), calls=%async_computation.2 | async-start | bytes 3932160 | tf_op jit(solution)/shard_map/reduce_scatter | solution.py:188
  157.9 18.7 %copy-start.3 = (bf16[4,8,64,576]{3,2,1,0:T(8,128)(2,1)S(1)}, bf16[4,8,64,576]{3,2,1,0:T(8,128)(2,1)}, u32[]{:S(2)}) copy-start(bf16[4,8,64,576]{3,2,1,0:T(8,128)(2,1)} %copy-done.2) | copy-start | bytes 7077892
  174.6 15.2 %collective-permute-start.10 = (f32[16,8,1024]{2,1,0:T(8,128)}, f32[16,8,1024]{2,1,0:T(8,128)}, u32[]{:S(2)}, u32[]{:S(2)}) collective-permute-start(f32[16,8,1024]{2,1,0:T(8,128)} %get-tuple-element.182), channel_id=1, source_target_pairs={{0,16},{16,0},{1,17},{17,1},{2,18},{18,2},{3,19},{19,3},{4,20},{20... | collective-permute-start | bytes 1572872 | tf_op jit(solution)/shard_map/ppermute | solution.py:17
  176.2 20.2 %collective-permute-start.11 = (f32[16,8,1024]{2,1,0:T(8,128)}, f32[16,8,1024]{2,1,0:T(8,128)}, u32[]{:S(2)}, u32[]{:S(2)}) collective-permute-start(f32[16,8,1024]{2,1,0:T(8,128)} %get-tuple-element.181), channel_id=1, source_target_pairs={{16,0},{0,16},{17,1},{1,17},{18,2},{2,18},{19,3},{3,19},{20,4},{4,... | collective-permute-start | bytes 1572872 | tf_op jit(solution)/shard_map/ppermute | solution.py:20
  179.8 17.9 %copy-start.15 = (bf16[256,512]{1,0:T(8,128)(2,1)S(1)}, bf16[256,512]{1,0:T(8,128)(2,1)}, u32[]{:S(2)}) copy-start(bf16[256,512]{1,0:T(8,128)(2,1)} %copy-done.14) | copy-start | bytes 786436
  197.6 2.5 copy-start.21
  197.7 41.1 %copy-start.5 = (bf16[1,16,16,512]{3,2,1,0:T(8,128)(2,1)S(1)}, bf16[1,16,16,512]{3,2,1,0:T(8,128)(2,1)}, u32[]{:S(2)}) copy-start(bf16[1,16,16,512]{3,2,1,0:T(8,128)(2,1)} %param.32) | copy-start | bytes 786436
  197.7 41.1 %copy-start.17 = (bf16[2,8,2,8,512]{4,3,2,1,0:T(8,128)(2,1)S(1)}, bf16[2,8,2,8,512]{4,3,2,1,0:T(8,128)(2,1)}, u32[]{:S(2)}) copy-start(bf16[2,8,2,8,512]{4,3,2,1,0:T(8,128)(2,1)} %copy-done.16) | copy-start | bytes 786436
  197.7 42.2 %copy-start.18 = (f32[512]{0:T(512)S(1)}, f32[512]{0:T(512)}, u32[]{:S(2)}) copy-start(f32[512]{0:T(512)} %param.36) | copy-start | bytes 6148
  200.0 121.0 %all-reduce.5.cloned.1.call-start = ((), (), s32[]{:S(2)}) async-start(), calls=%async_computation.4 | async-start | bytes 2097152 | tf_op jit(solution)/shard_map/psum | solution.py:183
Sparse Core Ops, SparseCore 0:
  157.8 28.5 reduce-scatter.4
  200.1 38.6 reduce-scatter.2
  242.3 78.5 all-reduce.4
where the time goes:
time: 333 us; the launch traced here: 331 us
  waiting for transfers between devices  118 us (35%)
  local copies, waits for them, and re-layouts  75.2 us (23%)
  other arithmetic  49 us (15%)
  blocking collectives  28.2 us (8%)
  matrix products  27.5 us (8%)
  starting transfers between devices  18.1 us (5%)
  between operations  15.1 us (5%)
    psum x1, waiting for transfers between devices, plane_sum(): return lax.psum((gradients[0], gradients[1], gradients[2]), ('lon', 'lat'))  49.7 us
    reduce_scatter x1, waiting for transfers between devices, level_share(): lax.psum_scatter(gradients[0], 'lev', scatter_dimension=0, tiled=True)  37.5 us
    psum x1, blocking collectives, plane_sum(): return lax.psum((gradients[0], gradients[1], gradients[2]), ('lon', 'lat'))  22.4 us
    ppermute x6, waiting for transfers between devices, with_halo(): lax.ppermute(lax.slice_in_dim(block, block.shape[dim] - width, None, axis...  19.9 us
    scatter-add x3, local copies, waits for them, and re-layouts, spread_back(): totals = totals.at[lat_step * window_side:(lat_step + lat_windows) * wind...  16.6 us
    scatter-add x6, other arithmetic, spread_back(): totals = totals.at[lat_step * window_side:(lat_step + lat_windows) * wind...  15.3 us
    ppermute x6, starting transfers between devices, with_halo(): lax.ppermute(lax.slice_in_dim(block, block.shape[dim] - width, None, axis...  11 us
    ppermute x6, waiting for transfers between devices, with_halo(): lax.ppermute(lax.slice_in_dim(block, 0, width, axis=dim), axis, backward)  10.9 us
  transfers between devices with their start and end apart: 15, of which 9 were waited for; matrix products, arithmetic and copies ran while one was open for 15% of the time, Pallas kernels for 0%

commit v1 on v0

v1 whole, which is shorter than its diff:
```python
import functools

import jax
import jax.numpy as jnp
from jax import lax
from jax.experimental import pallas as pl
from jax.experimental.pallas import tpu as pltpu
from jax.sharding import PartitionSpec as P

HEADS = 8
WIN = 8
AREA = WIN * WIN
D = 512
HEAD_DIM = D // HEADS
GROUP = 256
GROUP_HEADS = GROUP // HEAD_DIM
GROUPS = D // GROUP
KEYS = 8 * AREA
LAND = 1000.0
NEVER = -1e9
FAR = 1e30
F32 = jnp.float32
BF16 = jnp.bfloat16
EXACT = lax.Precision.HIGHEST


def dot(a, b, ca, cb, precision=None):
    return lax.dot_general(
        a, b, (((ca,), (cb,)), ((), ())), preferred_element_type=F32, precision=precision
    )


def iota(shape, dim):
    return lax.broadcasted_iota(jnp.int32, shape, dim)


def window_of(grid, w):
    r, c = divmod(w, 2)
    part = grid[r * WIN : (r + 1) * WIN, c * WIN : (c + 1) * WIN, :]
    return part.reshape(AREA, grid.shape[-1])


def grid_of(windows):
    rows = []
    for r in range(2):
        parts = [windows[2 * r + c].reshape(WIN, WIN, -1) for c in range(2)]
        rows.append(jnp.concatenate(parts, axis=1))
    return jnp.concatenate(rows, axis=0)


def token_mask(mask):
    t = iota((4 * AREA, 2 * WIN), 0)
    lane = iota((4 * AREA, 2 * WIN), 1)
    w, i, j = t // AREA, (t % AREA) // WIN, t % WIN
    pick_row = (lane == WIN * (w // 2) + i).astype(F32)
    pick_col = (lane == WIN * (w % 2) + j).astype(F32)
    rows = dot(pick_row, mask, 1, 0)
    return jnp.sum(rows * pick_col, axis=1, keepdims=True)


def norm_rows(x):
    center = x - jnp.mean(x, axis=-1, keepdims=True)
    spread = jnp.mean(center * center, axis=-1, keepdims=True)
    scaling = lax.rsqrt(spread + 1e-05)
    return center * scaling, scaling


def head_blocks():
    row = iota((GROUP, GROUP), 0) // HEAD_DIM
    col = iota((GROUP, GROUP), 1) // HEAD_DIM
    return (row == col).astype(F32)


def stack_heads(part, blocks):
    return jnp.concatenate([part] * GROUP_HEADS, axis=0) * blocks.astype(part.dtype)


def unstack_heads(full, blocks):
    kept = full * blocks
    return sum(kept[h * AREA : (h + 1) * AREA] for h in range(GROUP_HEADS))


def lanes(g):
    return slice(g * GROUP, (g + 1) * GROUP)


def prep_kernel(x_ref, mask_ref, all_ref, top_ref, bottom_ref):
    ocean = token_mask(mask_ref[0].astype(F32))
    x = x_ref[0].astype(F32)
    for w in range(4):
        part = jnp.where(ocean[w * AREA : (w + 1) * AREA] > 0.5, window_of(x, w), LAND)
        part = part.astype(BF16)
        all_ref[w] = part
        (top_ref if w < 2 else bottom_ref)[w % 2] = part


def own_kernel(
    tok_ref, cot_ref, mask_ref, wqkv_ref, wout_ref, gain_ref,
    q_ref, kv_ref, gm_ref, gm_top_ref, gm_bottom_ref, gb_ref, hid_ref, bias_ref, info_ref,
):
    mask = mask_ref[0].astype(F32)
    ocean = token_mask(mask)
    tokens = tok_ref[...].reshape(4 * AREA, D).astype(F32)
    normed, _ = norm_rows(tokens)
    hidden = (normed * gain_ref[...]).astype(BF16)
    hid_ref[...] = hidden
    projected = dot(hidden, wqkv_ref[...], 1, 0).astype(BF16)
    q_ref[...] = (projected[:, :D] * BF16(HEAD_DIM ** -0.5)).reshape(4, AREA, D)
    kv_ref[...] = projected[:, D:].reshape(4, AREA, 2 * D)
    bias_ref[...] = jnp.where(tokens[:, :128] > 0.5 * LAND, NEVER, 0.0).reshape(4, AREA, 128)
    cot = cot_ref[0].astype(F32)
    for w in range(4):
        branch = window_of(cot, w) * ocean[w * AREA : (w + 1) * AREA]
        gb_ref[w * AREA : (w + 1) * AREA, :] = branch.astype(BF16)
    gm = dot(gb_ref[...], wout_ref[...], 1, 1).astype(BF16).reshape(4, AREA, D)
    gm_ref[...] = gm
    gm_top_ref[...] = gm[:2]
    gm_bottom_ref[...] = gm[2:]
    alive = []
    for w in range(4):
        alive.append((jnp.max(ocean[w * AREA : (w + 1) * AREA]) > 0.5).astype(jnp.int32))
        info_ref[1 + w] = alive[w]
    left_out = jnp.where(
        alive[3] == 0, 3, jnp.where(alive[2] == 0, 2, jnp.where(alive[1] == 0, 1, 0))
    )
    info_ref[0] = left_out


def slot_window(info_ref, slot):
    left_out = info_ref[0]
    return slot + (slot >= left_out).astype(jnp.int32)


def fill_slots(info_ref, own_ref, cat_ref):
    for slot in range(3):
        cat_ref[slot * AREA : (slot + 1) * AREA] = own_ref[slot_window(info_ref, slot)]


def fill_near(w, halo_ref, cat_ref):
    r, c = w // 2, w % 2
    base = 3 * AREA
    lon_at, lat_at, corner_at = 2 * (1 - c), 4 + 2 * r, 8 + 2 * r + 1 - c
    for k, at in enumerate((lon_at, lon_at + 1, lat_at, lat_at + 1, corner_at)):
        cat_ref[base + k * AREA : base + (k + 1) * AREA] = halo_ref[at]


def forward_kernel(
    info_ref, place_ref, q_ref, kv_ref, bias_ref, lon_ref, up_ref, down_ref, upc_ref, downc_ref,
    wqkv_ref, gain_ref,
    mixed_ref, stats_ref, srow_ref, qh_ref, kvh_ref, biash_ref,
    gm_ref, kcat, bcat,
):
    up_ok, down_ok = place_ref[0] > 0, place_ref[0] < place_ref[1] - 1
    groups = (
        ((lon_ref, 0, None), (lon_ref, 2, None), (lon_ref, 1, None), (lon_ref, 3, None)),
        ((up_ref, 0, up_ok), (up_ref, 1, up_ok), (down_ref, 0, down_ok), (down_ref, 1, down_ok)),
        ((upc_ref, 0, up_ok), (upc_ref, 1, up_ok), (downc_ref, 0, down_ok), (downc_ref, 1, down_ok)),
    )
    for n, group in enumerate(groups):
        tokens = jnp.concatenate([ref[at] for ref, at, _ in group], axis=0).astype(F32)
        normed, _ = norm_rows(tokens)
        hidden = (normed * gain_ref[...]).astype(BF16)
        projected = dot(hidden, wqkv_ref[...], 1, 0).astype(BF16)
        span = slice(4 * n, 4 * n + 4)
        qh_ref[span] = (projected[:, :D] * BF16(HEAD_DIM ** -0.5)).reshape(4, AREA, D)
        kvh_ref[span] = projected[:, D:].reshape(4, AREA, 2 * D)
        for k, (_, _, ok) in enumerate(group):
            out = tokens[k * AREA : (k + 1) * AREA, :128] > 0.5 * LAND
            bias = jnp.where(out, NEVER, 0.0)
            if ok is not None:
                bias = jnp.where(ok, bias, NEVER)
            biash_ref[4 * n + k] = bias
    mixed_ref[...] = jnp.zeros_like(mixed_ref)
    stats_ref[:, :HEADS, :] = jnp.full((4, HEADS, AREA), FAR, F32)
    stats_ref[:, HEADS:, :] = jnp.zeros((4, HEADS, AREA), F32)
    srow_ref[...] = jnp.zeros_like(srow_ref)
    blocks = head_blocks()
    head_row = (iota((8, GROUP), 0) == iota((8, GROUP), 1) // HEAD_DIM).astype(F32)
    spot = (iota((GROUP, AREA), 0) % AREA == iota((GROUP, AREA), 1)).astype(F32)
    ones = jnp.ones((8, GROUP), F32)
    fill_slots(info_ref, kv_ref, kcat)
    fill_slots(info_ref, bias_ref, bcat)

    def slot_step(slot, carry):
        w = slot_window(info_ref, slot)

        @pl.when(info_ref[1 + w] > 0)
        def _():
            fill_near(w, kvh_ref, kcat)
            fill_near(w, biash_ref, bcat)
            bias = bcat[...]
            bias = jnp.concatenate([bias, bias], axis=1)
            for g in range(GROUPS):
                q_stack = stack_heads(q_ref[w, :, lanes(g)], blocks)
                scores = dot(kcat[:, lanes(g)], q_stack, 1, 1) + bias
                top = jnp.max(scores, axis=0, keepdims=True)
                weights = jnp.exp(scores - top)
                total = jnp.sum(weights, axis=0, keepdims=True)
                low = (weights * (1.0 / total)).astype(BF16)
                values = kcat[:, D + g * GROUP : D + (g + 1) * GROUP]
                out = unstack_heads(dot(low, values, 0, 0), blocks).astype(BF16)
                mixed_ref[w, :, lanes(g)] = out
                log_sum = top + jnp.log(total)
                product = out.astype(F32) * gm_ref[w, :, lanes(g)].astype(F32)
                product = jnp.concatenate([product] * GROUP_HEADS, axis=0) * blocks
                delta = dot(ones, product, 1, 1, EXACT)[:1]
                srow_ref[w, g : g + 1] = log_sum
                srow_ref[w, 2 + g : 3 + g] = delta
                low_rows = dot(head_row * log_sum, spot, 1, 0, EXACT)
                delta_rows = dot(head_row * delta, spot, 1, 0, EXACT)
                at = g * GROUP_HEADS
                stats_ref[w, at : at + GROUP_HEADS] = low_rows[:GROUP_HEADS]
                stats_ref[w, HEADS + at : HEADS + at + GROUP_HEADS] = delta_rows[:GROUP_HEADS]

        return carry

    lax.fori_loop(0, 3, slot_step, 0)


def query_kernel(
    info_ref, place_ref, q_ref, kv_ref, bias_ref, kvh_ref, biash_ref, gm_ref, mixed_ref, srow_ref,
    hid_ref, gb_ref, x_ref, mask_ref, wout_ref,
    gq_ref, out_ref, keep_ref, send_ref,
    kcat, bcat,
):
    blocks = head_blocks()
    gq_ref[...] = jnp.zeros_like(gq_ref)
    fill_slots(info_ref, kv_ref, kcat)
    fill_slots(info_ref, bias_ref, bcat)

    def slot_step(slot, carry):
        w = slot_window(info_ref, slot)

        @pl.when(info_ref[1 + w] > 0)
        def _():
            fill_near(w, kvh_ref, kcat)
            fill_near(w, biash_ref, bcat)
            bias = bcat[...]
            bias = jnp.concatenate([bias, bias], axis=1)
            for g in range(GROUPS):
                q_stack = stack_heads(q_ref[w, :, lanes(g)], blocks)
                gm_stack = stack_heads(gm_ref[w, :, lanes(g)], blocks)
                keys = kcat[:, lanes(g)]
                values = kcat[:, D + g * GROUP : D + (g + 1) * GROUP]
                scores = dot(keys, q_stack, 1, 1) + bias
                probs = jnp.exp(scores - srow_ref[w, g : g + 1])
                grad_probs = dot(values, gm_stack, 1, 1)
                grad_scores = (probs * (grad_probs - srow_ref[w, 2 + g : 3 + g])).astype(BF16)
                grad = unstack_heads(dot(grad_scores, keys, 0, 0), blocks)
                gq_ref[w, :, lanes(g)] = (grad * HEAD_DIM ** -0.5).astype(BF16)

        return carry

    lax.fori_loop(0, 3, slot_step, 0)
    mixed = mixed_ref[...].reshape(4 * AREA, D)
    branch = dot(mixed, wout_ref[...], 1, 0)
    ocean = token_mask(mask_ref[0].astype(F32))
    added = (branch * ocean).reshape(4, AREA, D)
    out_ref[0] = (x_ref[0].astype(F32) + grid_of([added[w] for w in range(4)])).astype(BF16)
    gq = gq_ref[...].reshape(4 * AREA, D)
    gb = gb_ref[...]
    lev = place_ref[2]
    for rel in range(4):
        at = pl.ds(pl.multiple_of((lev ^ rel) * 128, 128), 128)
        to = keep_ref if rel % 2 == 0 else send_ref
        to[rel // 2, :, :D] = dot(hid_ref[:, at], gq, 0, 0).astype(BF16)
        mixed_cols = mixed_ref[:, :, at].reshape(4 * AREA, 128)
        to[rel // 2, :, D:] = dot(mixed_cols, gb, 0, 0).astype(BF16)


def key_kernel(
    info_ref, place_ref, q_ref, kv_ref, gm_ref, stats_ref, qh_ref,
    gm_lon_ref, gm_up_ref, gm_down_ref, gm_upc_ref, gm_downc_ref,
    st_lon_ref, st_up_ref, st_down_ref, st_upc_ref, st_downc_ref,
    hid_ref, gq_ref, tok_ref, cot_ref, wqkv_ref, gain_ref,
    ing_ref, keep_ref, send_ref,
    qcat, gmcat, gmh, scat, gkv,
):
    blocks = head_blocks()
    gkv[...] = jnp.zeros_like(gkv)
    halo = (
        (gm_lon_ref, 0), (gm_lon_ref, 2), (gm_lon_ref, 1), (gm_lon_ref, 3),
        (gm_up_ref, 0), (gm_up_ref, 1), (gm_down_ref, 0), (gm_down_ref, 1),
        (gm_upc_ref, 0), (gm_upc_ref, 1), (gm_downc_ref, 0), (gm_downc_ref, 1),
    )
    for k, (ref, at) in enumerate(halo):
        gmh[k] = ref[at]
    stats = (
        (st_lon_ref, 0), (st_lon_ref, 2), (st_lon_ref, 1), (st_lon_ref, 3),
        (st_up_ref, 0), (st_up_ref, 1), (st_down_ref, 0), (st_down_ref, 1),
        (st_upc_ref, 0), (st_upc_ref, 1), (st_downc_ref, 0), (st_downc_ref, 1),
    )
    spread = [
        (iota((HEADS, GROUP), 0) == g * GROUP_HEADS + iota((HEADS, GROUP), 1) // HEAD_DIM).astype(F32)
        for g in range(GROUPS)
    ]
    for k, (ref, at) in enumerate(stats):
        scat[3 + k] = ref[at]
    for slot in range(3):
        scat[slot] = stats_ref[slot_window(info_ref, slot)]
    fill_slots(info_ref, q_ref, qcat)
    fill_slots(info_ref, gm_ref, gmcat)

    def slot_step(slot, carry):
        w = slot_window(info_ref, slot)

        @pl.when(info_ref[1 + w] > 0)
        def _():
            fill_near(w, qh_ref, qcat)
            fill_near(w, gmh, gmcat)
            r, c = w // 2, w % 2
            lon_at, lat_at, corner_at = 3 + 2 * (1 - c), 7 + 2 * r, 11 + 2 * r + 1 - c
            picked = [scat[k] for k in (0, 1, 2, lon_at, lon_at + 1, lat_at, lat_at + 1, corner_at)]
            for g in range(GROUPS):
                k_stack = stack_heads(kv_ref[w, :, lanes(g)], blocks)
                v_stack = stack_heads(kv_ref[w, :, D + g * GROUP : D + (g + 1) * GROUP], blocks)
                queries = qcat[:, lanes(g)]
                grads = gmcat[:, lanes(g)]
                scores = dot(queries, k_stack, 1, 1)
                log_sum = jnp.concatenate([dot(p[:HEADS], spread[g], 0, 0, EXACT) for p in picked], axis=0)
                probs = jnp.exp(jnp.minimum(scores - log_sum, 0.0))
                grad_probs = dot(grads, v_stack, 1, 1)
                delta = jnp.concatenate([dot(p[HEADS:], spread[g], 0, 0, EXACT) for p in picked], axis=0)
                grad_scores = (probs * (grad_probs - delta)).astype(BF16)
                gkv[w, :, lanes(g)] = unstack_heads(dot(grad_scores, queries, 0, 0), blocks)
                gkv[w, :, D + g * GROUP : D + (g + 1) * GROUP] = unstack_heads(
                    dot(probs.astype(BF16), grads, 0, 0), blocks
                )

        return carry

    lax.fori_loop(0, 3, slot_step, 0)
    tokens = tok_ref[...].reshape(4 * AREA, D).astype(F32)
    land = tokens[:, :1] > 0.5 * LAND
    grad_kv = jnp.where(land, 0.0, gkv[...].reshape(4 * AREA, 2 * D)).astype(BF16)
    lev = place_ref[2]
    for rel in range(4):
        at = pl.ds(pl.multiple_of((lev ^ rel) * 128, 128), 128)
        to = keep_ref if rel % 2 == 0 else send_ref
        to[rel // 2] = dot(hid_ref[:, at], grad_kv, 0, 0).astype(BF16)
    gq = gq_ref[...].reshape(4 * AREA, D)
    grad_hidden = dot(gq, wqkv_ref[:, :D], 1, 1) + dot(grad_kv, wqkv_ref[:, D:], 1, 1)
    normed, scaling = norm_rows(tokens)
    scaled = grad_hidden * gain_ref[...]
    correction = (
        scaled
        - jnp.mean(scaled, axis=-1, keepdims=True)
        - normed * jnp.mean(scaled * normed, axis=-1, keepdims=True)
    )
    added = (scaling * correction).reshape(4, AREA, D)
    ing_ref[0] = (cot_ref[0].astype(F32) + grid_of([added[w] for w in range(4)])).astype(BF16)


def finish_kernel(whole_rows, place_ref, own_ref, *refs):
    others, (wqkv_ref, gain_ref, qkv_ref, out_ref, gg_ref) = refs[:-5], refs[-5:]
    lat, lat_count, lev = place_ref[0], place_ref[1], place_ref[2]
    for k, ref in enumerate((own_ref,) + tuple(others)):
        z = lax.rem(lat - k + lat_count, lat_count)
        value = ref[...].astype(F32)
        for x in range(value.shape[0]):
            qkv_ref[x, z, :, :D] = value[x, :, :D]
            qkv_ref[x, z, :, D:] = value[x, :, 2 * D :]
            out_ref[x, z] = value[x, :, D : 2 * D]
    if whole_rows:
        at = pl.ds(pl.multiple_of(lev * 128, 128), 128)
        product = wqkv_ref[at, :].astype(F32) * qkv_ref[...].reshape(128, 3 * D)
        sums = dot(jnp.ones((8, 3 * D), F32), product, 1, 1, EXACT)[:1]
        gg_ref[...] = sums / gain_ref[:, at]
    else:
        gg_ref[...] = jnp.zeros_like(gg_ref)


VMEM = pl.BlockSpec(memory_space=pltpu.VMEM)
SMEM = pl.BlockSpec(memory_space=pltpu.SMEM)


def call(kernel, outs, scalars, arrays, scratch=(), flops=0, name=None, smem_out=False):
    moved = sum(a.size * a.dtype.itemsize for a in arrays)
    moved += sum(o.size * o.dtype.itemsize for o in outs)
    out_specs = [VMEM] * len(outs)
    if smem_out:
        out_specs[-1] = SMEM
    return pl.pallas_call(
        kernel,
        out_shape=outs,
        in_specs=[SMEM] * len(scalars) + [VMEM] * len(arrays),
        out_specs=out_specs,
        scratch_shapes=list(scratch),
        compiler_params=pltpu.CompilerParams(vmem_limit_bytes=40 * 1024 * 1024),
        cost_estimate=pl.CostEstimate(flops=flops, bytes_accessed=moved, transcendentals=0),
        name=name,
    )(*scalars, *arrays)


def shape(dims, dtype=BF16):
    return jax.ShapeDtypeStruct(dims, dtype)


def ring(count, step, periodic):
    return [
        (i, (i + step) % count) for i in range(count) if periodic or 0 <= i + step < count
    ]


def lon_halo(own):
    count = lax.axis_size("lon")
    if count == 2:
        return lax.ppermute(own, "lon", [(0, 1), (1, 0)])
    left = lax.ppermute(own[1::2], "lon", ring(count, 1, True))
    right = lax.ppermute(own[0::2], "lon", ring(count, -1, True))
    return jnp.stack([right, left], axis=1).reshape(own.shape)


def lat_halo(top, bottom):
    count = lax.axis_size("lat")
    up = lax.ppermute(bottom, "lat", ring(count, 1, False))
    down = lax.ppermute(top, "lat", ring(count, -1, False))
    return up, down


def lev_sum(keep, send):
    arrived = lax.ppermute(send, "lev", [(i, i ^ 1) for i in range(4)]).astype(F32)
    onward = (keep[1].astype(F32) + arrived[1]).astype(BF16)
    last = lax.ppermute(onward, "lev", [(i, i ^ 2) for i in range(4)])
    return keep[0].astype(F32) + arrived[0] + last.astype(F32)


def plane_parts(total):
    lon, lon_count = lax.axis_index("lon"), lax.axis_size("lon")
    lat, lat_count = lax.axis_index("lat"), lax.axis_size("lat")
    width = total.shape[1]
    parts = total.reshape(lon_count, -1, width)
    own = lax.dynamic_index_in_dim(parts, lon, 0, False)
    low = parts.astype(BF16)
    for k in range(1, lon_count):
        piece = lax.dynamic_index_in_dim(low, (lon + k) % lon_count, 0, False)
        own = own + lax.ppermute(piece, "lon", ring(lon_count, k, True)).astype(F32)
    parts = own.reshape(lat_count, -1, width)
    own = lax.dynamic_index_in_dim(parts, lat, 0, False)
    low = parts.astype(BF16)
    for k in range(1, lat_count):
        piece = lax.dynamic_index_in_dim(low, (lat + k) % lat_count, 0, False)
        own = own + lax.ppermute(piece, "lat", ring(lat_count, k, True)).astype(F32)
    own = own.astype(BF16)
    across = [own] + [
        lax.ppermute(own, "lon", ring(lon_count, k, True)) for k in range(1, lon_count)
    ]
    if lon_count == 2:
        first = lon == 0
        across = [jnp.where(first, across[0], across[1]), jnp.where(first, across[1], across[0])]
        both = jnp.stack(across)
    else:
        both = jnp.roll(jnp.stack(across[:1] + across[:0:-1]), lon, axis=0)
    return [both] + [lax.ppermute(both, "lat", ring(lat_count, k, True)) for k in range(1, lat_count)]


def on_device(tokens_in, cotangent, qkv_weight, out_weight, norm_gain, ocean_mask):
    lat_count, lon_count = lax.axis_size("lat"), lax.axis_size("lon")
    gain = norm_gain.reshape(1, D)
    place = jnp.stack(
        [lax.axis_index("lat"), jnp.int32(lat_count), lax.axis_index("lev")]
    ).astype(jnp.int32)
    half = shape((2, AREA, D))
    four = shape((4, AREA, D))
    flat = shape((4 * AREA, D))
    tok, tok_top, tok_bottom = call(
        prep_kernel, [four, half, half], [], [tokens_in, ocean_mask], name="prep"
    )
    tok_lon = lon_halo(tok)
    tok_up, tok_down = lat_halo(tok_top, tok_bottom)
    q, kv, gm, gm_top, gm_bottom, gb, hid, bias, info = call(
        own_kernel,
        [four, shape((4, AREA, 2 * D)), four, half, half, flat, flat,
         shape((4, AREA, 128), F32), shape((8,), jnp.int32)],
        [],
        [tok, cotangent, ocean_mask, qkv_weight, out_weight, gain],
        flops=2 * 256 * 512 * 2048,
        name="own",
        smem_out=True,
    )
    tok_upc, tok_downc = lat_halo(tok_lon[:2], tok_lon[2:])
    gm_lon = lon_halo(gm)
    gm_up, gm_down = lat_halo(gm_top, gm_bottom)
    cat_scratch = [pltpu.VMEM((KEYS, 2 * D), BF16), pltpu.VMEM((KEYS, 128), F32)]
    mixed, stats, srow, qh, kvh, biash = call(
        lambda *refs: forward_kernel(*refs[:10], *refs[11:13], *refs[13:19], refs[10], *refs[19:]),
        [four, shape((4, 2 * HEADS, AREA), F32), shape((4, 8, GROUP), F32), shape((12, AREA, D)),
         shape((12, AREA, 2 * D)), shape((12, AREA, 128), F32)],
        [info, place],
        [q, kv, bias, tok_lon, tok_up, tok_down, tok_upc, tok_downc, gm, qkv_weight, gain],
        cat_scratch,
        flops=2 * 768 * 512 * 1536 + 3 * 4 * 2 * 512 * 256 * 256,
        name="forward",
    )
    gm_upc, gm_downc = lat_halo(gm_lon[:2], gm_lon[2:])
    st_lon = lon_halo(stats)
    st_up, st_down = lat_halo(stats[:2], stats[2:])
    st_upc, st_downc = lat_halo(st_lon[:2], st_lon[2:])
    share = shape((2, 128, 2 * D))
    gq, layer_out, keep_a, send_a = call(
        query_kernel,
        [four, shape(tokens_in.shape), share, share],
        [info, place],
        [q, kv, bias, kvh, biash, gm, mixed, srow, hid, gb, tokens_in, ocean_mask, out_weight],
        cat_scratch,
        flops=3 * 6 * 2 * 512 * 256 * 256 + 3 * 2 * 256 * 512 * 512,
        name="query",
    )
    total_a = lev_sum(keep_a, send_a)
    input_grad, keep_b, send_b = call(
        key_kernel,
        [shape(tokens_in.shape), share, share],
        [info, place],
        [q, kv, gm, stats, qh, gm_lon, gm_up, gm_down, gm_upc, gm_downc,
         st_lon, st_up, st_down, st_upc, st_downc, hid, gq, tok, cotangent, qkv_weight, gain],
        [pltpu.VMEM((KEYS, D), BF16), pltpu.VMEM((KEYS, D), BF16), pltpu.VMEM((12, AREA, D), BF16),
         pltpu.VMEM((15, 2 * HEADS, AREA), F32), pltpu.VMEM((4, AREA, 2 * D), F32)],
        flops=3 * 8 * 2 * 512 * 256 * 256 + 2 * 2 * 256 * 512 * 1536,
        name="key",
    )
    total_b = lev_sum(keep_b, send_b)
    parts = plane_parts(jnp.concatenate([total_a, total_b], axis=1))
    rows = parts[0].shape[1]
    whole_rows = rows % 8 == 0
    qkv_grad, out_grad, gain_grad = call(
        functools.partial(finish_kernel, whole_rows),
        [shape((lon_count, lat_count, rows, 3 * D), F32), shape((lon_count, lat_count, rows, D), F32),
         shape((1, 128), F32)],
        [place],
        parts + [qkv_weight, gain],
        name="finish",
    )
    qkv_grad = qkv_grad.reshape(128, 3 * D)
    out_grad = out_grad.reshape(128, D)
    if whole_rows:
        gain_grad = gain_grad.reshape(128)
    else:
        at = lax.axis_index("lev") * 128
        rows_in = lax.dynamic_slice_in_dim(qkv_weight, at, 128, 0).astype(F32)
        gain_grad = jnp.sum(rows_in * qkv_grad, axis=1)
        gain_grad = gain_grad / lax.dynamic_slice_in_dim(norm_gain, at, 128, 0)
    return layer_out, input_grad, qkv_grad, out_grad, gain_grad


def solution(mesh):
    placed = (
        P("lev", "lat", "lon", None),
        P("lev", "lat", "lon", None),
        P(),
        P(),
        P(),
        P("lev", "lat", "lon"),
    )
    return jax.shard_map(
        on_device,
        mesh=mesh,
        in_specs=placed,
        out_specs=(
            P("lev", "lat", "lon", None),
            P("lev", "lat", "lon", None),
            P("lev", None),
            P("lev", None),
            P("lev"),
        ),
        check_vma=False,
    )
```

time: 333 us -> 136 us (0.41)
  waiting for transfers between devices: 118 us -> 38.1 us
  local copies, waits for them, and re-layouts: 75.2 us -> 12.5 us
  other arithmetic: 49 us -> 1.53 us
  starting transfers between devices: 18.1 us -> 51.6 us
  Pallas kernels: 0 us -> 30.8 us
  blocking collectives: 28.2 us -> 0 us
  matrix products: 27.5 us -> 0 us
  between operations: 15.1 us -> 1.09 us
    psum x1 -> x0, waiting for transfers between devices: 49.7 us -> none  [plane_sum(): return lax.psum((gradients[0], gradients[1], gradients[2]), ('lon', 'lat'))]
    reduce_scatter x2 -> x0, waiting for transfers between devices: 37.5 us -> none  [the longest x1 37.5 us: level_share(): lax.psum_scatter(gradients[0], 'lev', scatter_dimension=0, tiled=True)]
    ppermute x12 -> x27, starting transfers between devices: 17.7 us -> 51.6 us  [the longest x6 24.5 us: lat_halo(): up = lax.ppermute(bottom, 'lat', ring(count, 1, False))]
    pallas_call x0 -> x6, Pallas kernels: none -> 30.8 us  [call(): pl.pallas_call(kernel, out_shape=outs, in_specs=[SMEM] * len(scalars) + [...]
    scatter-add x10 -> x0, other arithmetic: 23.2 us -> none  [the longest x6 15.3 us: spread_back(): totals = totals.at[lat_step * window_side:(lat_step + lat_windows) * wind...]
    psum x1 -> x0, blocking collectives: 22.4 us -> none  [plane_sum(): return lax.psum((gradients[0], gradients[1], gradients[2]), ('lon', 'lat'))]
    dot_general x12 -> x0, matrix products: 22.3 us -> none  [the longest x1 3.23 us: attend_backward(): jnp.einsum('whqk,wqhd->wkhd', probabilities.astype(jnp.bfloat16), grad_he...]
    slice x13 -> x4, local copies, waits for them, and re-layouts: 19.4 us -> 0.04 us  [the longest x1 0.02 us: on_device(): gm_upc, gm_downc = lat_halo(gm_lon[:2], gm_lon[2:])]
  transfers between devices with their start and end apart: 15 -> 27, of which waited for: 9 -> 12; matrix products, arithmetic and copies ran while one was open for 15% -> 1% of each run, Pallas kernels for 0% -> 21%
where the time goes in v1:
time: 136 us
  starting transfers between devices  51.6 us (38%)
  waiting for transfers between devices  38.1 us (28%)
  Pallas kernels  30.8 us (23%)
  local copies, waits for them, and re-layouts  12.5 us (9%)
  other arithmetic  1.53 us (1%)
    pallas_call x6, Pallas kernels, call(): pl.pallas_call(kernel, out_shape=outs, in_specs=[SMEM] * len(scalars) + [...  30.8 us
    ppermute x6, starting transfers between devices, lat_halo(): up = lax.ppermute(bottom, 'lat', ring(count, 1, False))  24.5 us
    unnamed x52, local copies, waits for them, and re-layouts  12.4 us
    ppermute x2, waiting for transfers between devices, lev_sum(): last = lax.ppermute(onward, 'lev', [(i, i ^ 2) for i in range(4)])  12.2 us
    ppermute x6, starting transfers between devices, lat_halo(): down = lax.ppermute(top, 'lat', ring(count, -1, False))  7.74 us
    ppermute x1, waiting for transfers between devices, plane_parts(): own = own + lax.ppermute(piece, 'lon', ring(lon_count, k, True)).astype(F32)  7.41 us
    ppermute x3, waiting for transfers between devices, plane_parts(): lax.ppermute(both, 'lat', ring(lat_count, k, True))  6.79 us
    ppermute x3, starting transfers between devices, plane_parts(): own = own + lax.ppermute(piece, 'lat', ring(lat_count, k, True)).astype(F32)  6.44 us
  transfers between devices with their start and end apart: 27, of which 12 were waited for; matrix products, arithmetic and copies ran while one was open for 1% of the time, Pallas kernels for 21%

profile of v1, /device:TPU:0, one launch (start us, length us, event | category | flops | bytes accessed | tf_op | source)
XLA Modules:
  0.0 135.5 jit_solution(1724520727134175901)
XLA Ops:
  0.6 0.0 copy-start.6
  0.6 0.9 copy-done.6
  1.6 0.7 copy-done.8
  2.3 1.0 prep.1
  3.3 2.9 %collective-permute-start = (bf16[4,64,512]{2,1,0:T(8,128)(2,1)S(1)}, bf16[4,64,512]{2,1,0:T(8,128)(2,1)S(1)}, u32[]{:S(2)}, u32[]{:S(2)}) collective-permute-start(bf16[4,64,512]{2,1,0:T(8,128)(2,1)S(1)} %get-tuple-element.33.tok_ref), channel_id=1, source_target_pairs={{0,16},{16,0},{1,17},{17,1},{2,18},{18,2},{3,19},{19,3},{4,20},{20... | collective-permute-start | bytes 786440 | tf_op jit(solution)/shard_map/ppermute | solution.py:408
  6.2 4.1 %collective-permute-start.1 = (bf16[2,64,512]{2,1,0:T(8,128)(2,1)}, bf16[2,64,512]{2,1,0:T(8,128)(2,1)}, u32[]{:S(2)}, u32[]{:S(2)}) collective-permute-start(bf16[2,64,512]{2,1,0:T(8,128)(2,1)} %get-tuple-element.38), channel_id=1, source_target_pairs={{0,4},{4,8},{8,12},{1,5},{5,9},{9,13},{2,6},{6,10},{10,14},{3,7},{... | collective-permute-start | bytes 393224 | tf_op jit(solution)/shard_map/ppermute | solution.py:416
  10.3 1.3 collective-permute-start.2
  11.6 1.4 %copy-done = bf16[512,1536]{1,0:T(8,128)(2,1)S(1)} copy-done((bf16[512,1536]{1,0:T(8,128)(2,1)S(1)}, bf16[512,1536]{1,0:T(8,128)(2,1)}, u32[]{:S(2)}) %copy-start) | copy-done | bytes 1572888
  13.0 1.0 copy-done.2
  14.1 0.9 copy-done.4
  15.0 0.7 copy-done.10
  15.7 1.6 %own.1 = (bf16[4,64,512]{2,1,0:T(8,128)(2,1)S(1)}, bf16[4,64,1024]{2,1,0:T(8,128)(2,1)S(1)}, bf16[4,64,512]{2,1,0:T(8,128)(2,1)S(1)}, bf16[2,64,512]{2,1,0:T(8,1...) custom-call(bf16[4,64,512]{2,1,0:T(8,128)(2,1)S(1)} %get-tuple-eleme, ...), custom_call_target="tpu_custom_call" | custom-call | flops 536870912 | bytes 4590624 | tf_op jit(solution)/shard_map/own/pallas_call | solution.py:383
  17.3 0.7 copy-done.16
  18.0 0.7 copy-done.18
  18.7 0.7 copy-done.20
  19.4 0.6 copy-done.21
  20.0 0.5 collective-permute-start.5
  20.6 4.5 %collective-permute-start.6 = (bf16[2,64,512]{2,1,0:T(8,128)(2,1)}, bf16[2,64,512]{2,1,0:T(8,128)(2,1)S(1)}, u32[]{:S(2)}, u32[]{:S(2)}) collective-permute-start(bf16[2,64,512]{2,1,0:T(8,128)(2,1)} %get-tuple-element.50), channel_id=1, source_target_pairs={{0,4},{4,8},{8,12},{1,5},{5,9},{9,13},{2,6},{6,10},{10,14},{3,7},{... | collective-permute-start | bytes 393224 | tf_op jit(solution)/shard_map/ppermute | solution.py:416
  25.1 0.1 pad_add_fusion.refs_1_.place_ref
  25.2 2.9 %collective-permute-start.3 = (bf16[2,64,512]{2,1,0:T(8,128)(2,1)S(1)}, bf16[2,64,512]{2,1,0:T(8,128)(2,1)S(1)}, u32[]{:S(2)}, u32[]{:S(2)}) collective-permute-start(bf16[2,64,512]{2,1,0:T(8,128)(2,1)S(1)} %get-tuple-element.67), channel_id=1, source_target_pairs={{0,4},{4,8},{8,12},{1,5},{5,9},{9,13},{2,6},{6,10},{10,14},{3,7},{... | collective-permute-start | bytes 393224 | tf_op jit(solution)/shard_map/ppermute | solution.py:416
  28.1 1.3 collective-permute-start.4
  29.4 1.3 collective-permute-start.7
  30.7 5.4 %collective-permute-start.8 = (bf16[2,64,512]{2,1,0:T(8,128)(2,1)S(1)}, bf16[2,64,512]{2,1,0:T(8,128)(2,1)S(1)}, u32[]{:S(2)}, u32[]{:S(2)}) collective-permute-start(bf16[2,64,512]{2,1,0:T(8,128)(2,1)S(1)} %get-tuple-element.65), channel_id=1, source_target_pairs={{0,4},{4,8},{8,12},{1,5},{5,9},{9,13},{2,6},{6,10},{10,14},{3,7},{... | collective-permute-start | bytes 393224 | tf_op jit(solution)/shard_map/ppermute | solution.py:416
  36.2 1.3 collective-permute-start.9
  37.5 0.9 copy-done.22
  38.4 10.9 %forward.1 = (bf16[4,64,512]{2,1,0:T(8,128)(2,1)S(1)}, f32[4,16,64]{2,1,0:T(8,128)S(1)}, f32[4,8,256]{2,1,0:T(8,128)S(1)}, bf16[12,64,512]{2,1,0:T(8,128)(2,1)S(...) custom-call(s32[8]{0:T(128)S(1)} %get-tuple-element.34.refs_0_.info_ref, ...), custom_call_target="tpu_custom_call" | custom-call | flops 2013265920 | bytes 6604800 | tf_op jit(solution)/shard_map/forward/pallas_call | solution.py:383
  49.3 1.6 %collective-permute-start.10 = (f32[4,16,64]{2,1,0:T(8,128)S(1)}, f32[4,16,64]{2,1,0:T(8,128)S(1)}, u32[]{:S(2)}, u32[]{:S(2)}) collective-permute-start(f32[4,16,64]{2,1,0:T(8,128)S(1)} %get-tuple-element.48.stats_ref), channel_id=1, source_target_pairs={{0,16},{16,0},{1,17},{17,1},{2,18},{18,2},{3,19},{19,3},{4,20},{20... | collective-permute-start | bytes 49160 | tf_op jit(solution)/shard_map/ppermute | solution.py:408
  51.0 0.9 copy-done.15
  51.9 4.7 %query.1 = (bf16[4,64,512]{2,1,0:T(8,128)(2,1)S(1)}, bf16[1,16,16,512]{3,2,1,0:T(8,128)(2,1)}, bf16[2,128,1024]{2,1,0:T(8,128)(2,1)S(1)}, bf16[2,128,1024]{2,1,0:T(8,128)(2,1)S(1)}) custom-call(s32[8]{0:T(128)S(1)} %get-tuple-element.34.refs_0_.info_ref, s32[3]{0:T(128)S(1)} %pad_add_fusion.refs_1_.place_ref, ...), custom_call_target="tpu_custom_call" | custom-call | flops 1610612736 | bytes 6325248 | tf_op jit(solution)/shard_map/query/pallas_call | solution.py:383
  56.6 2.7 %collective-permute-start.11 = (f32[2,16,64]{2,1,0:T(8,128)S(1)}, f32[2,16,64]{2,1,0:T(8,128)S(1)}, u32[]{:S(2)}, u32[]{:S(2)}) collective-permute-start(f32[2,16,64]{2,1,0:T(8,128)S(1)} %get-tuple-element.73), channel_id=1, source_target_pairs={{0,4},{4,8},{8,12},{1,5},{5,9},{9,13},{2,6},{6,10},{10,14},{3,7},{... | collective-permute-start | bytes 24584 | tf_op jit(solution)/shard_map/ppermute | solution.py:416
  59.3 1.3 collective-permute-start.12
  60.6 4.9 %collective-permute-start.13 = (f32[2,16,64]{2,1,0:T(8,128)S(1)}, f32[2,16,64]{2,1,0:T(8,128)S(1)}, u32[]{:S(2)}, u32[]{:S(2)}) collective-permute-start(f32[2,16,64]{2,1,0:T(8,128)S(1)} %get-tuple-element.71), channel_id=1, source_target_pairs={{0,4},{4,8},{8,12},{1,5},{5,9},{9,13},{2,6},{6,10},{10,14},{3,7},{... | collective-permute-start | bytes 24584 | tf_op jit(solution)/shard_map/ppermute | solution.py:416
  65.6 1.3 collective-permute-start.14
  66.9 0.1 collective-permute-done.13.st_upc_ref
  67.0 5.7 %collective-permute-done.14.st_downc_ref = f32[2,16,64]{2,1,0:T(8,128)S(1)} collective-permute-done((f32[2,16,64]{2,1,0:T(8,128)S(1)}, f32[2,16,64]{2,1,0:T(8,128)S(1)}, u32[]{:S(2)}, u32[]{:S(2)}) %collective-permute-start.14) | collective-permute-done | bytes 8224 | tf_op jit(solution)/shard_map/ppermute | solution.py:417
  72.7 1.0 copy-done.13
  73.7 10.8 %key.1 = (bf16[1,16,16,512]{3,2,1,0:T(8,128)(2,1)}, bf16[2,128,1024]{2,1,0:T(8,128)(2,1)S(1)}, bf16[2,128,1024]{2,1,0:T(8,128)(2,1)}) custom-call(s32[8]{0:T(128)S(1)} %get-tuple-element.34.refs_0_.info_ref, s32[3]{0:T(128)S(1)} %pad_add_fusion.refs_1_.place_ref, bf16[4,64,512]{2,1,0:T(8,128)(2,1)S(1)} %get-tuple-element.35.refs_2_.q_ref, ...), custom_call_target="tpu_custom_call" | custom-call | flops 2415919104 | bytes 6621184 | tf_op jit(solution)/shard_map/key/pallas_call | solution.py:383
  84.5 0.1 convert_element_type.62
  84.6 1.0 copy-done.24
  85.6 0.8 fusion.6
  86.4 0.2 collective-permute-done.17
  86.6 0.1 convert_element_type.68
  86.7 0.1 fusion.7
  86.8 1.9 %collective-permute-start.18 = (bf16[128,1024]{1,0:T(8,128)(2,1)S(1)}, bf16[128,1024]{1,0:T(8,128)(2,1)S(1)}, u32[]{:S(2)}, u32[]{:S(2)}) collective-permute-start(bf16[128,1024]{1,0:T(8,128)(2,1)S(1)} %fusion.7), channel_id=1, source_target_pairs={{0,2},{1,3},{2,0},{3,1},{4,6},{5,7},{6,4},{7,5},{8,10},{9,11},{10,... | collective-permute-start | bytes 786440 | tf_op jit(solution)/shard_map/ppermute | solution.py:424
  88.7 7.0 %collective-permute-done.16 = bf16[128,1024]{1,0:T(8,128)(2,1)S(1)} collective-permute-done((bf16[128,1024]{1,0:T(8,128)(2,1)}, bf16[128,1024]{1,0:T(8,128)(2,1)S(1)}, u32[]{:S(2)}, u32[]{:S(2)}) %collective-permute-start.16) | collective-permute-done | bytes 262176 | tf_op jit(solution)/shard_map/ppermute | solution.py:424
  95.7 0.1 fusion.5
  95.8 5.1 %collective-permute-done.18 = bf16[128,1024]{1,0:T(8,128)(2,1)S(1)} collective-permute-done((bf16[128,1024]{1,0:T(8,128)(2,1)S(1)}, bf16[128,1024]{1,0:T(8,128)(2,1)S(1)}, u32[]{:S(2)}, u32[]{:S(2)}) %collective-permute-start.18) | collective-permute-done | bytes 262176 | tf_op jit(solution)/shard_map/ppermute | solution.py:424
  100.9 0.1 fusion.2
  101.0 0.1 pad_maximum_fusion
  101.2 0.6 collective-permute-start.19
  101.8 7.4 %collective-permute-done.19 = bf16[64,2048]{1,0:T(8,128)(2,1)S(1)} collective-permute-done((bf16[64,2048]{1,0:T(8,128)(2,1)S(1)}, bf16[64,2048]{1,0:T(8,128)(2,1)S(1)}, u32[]{:S(2)}, u32[]{:S(2)}) %collective-permute-start.19) | collective-permute-done | bytes 262176 | tf_op jit(solution)/shard_map/ppermute | solution.py:437
  109.3 0.8 collective-permute-start.20
  110.2 2.7 %collective-permute-start.21 = (bf16[16,2048]{1,0:T(8,128)(2,1)S(1)}, bf16[16,2048]{1,0:T(8,128)(2,1)S(1)}, u32[]{:S(2)}, u32[]{:S(2)}) collective-permute-start(bf16[16,2048]{1,0:T(8,128)(2,1)S(1)} %get-tuple-element.63), channel_id=1, source_target_pairs={{0,8},{4,12},{8,0},{12,4},{1,9},{5,13},{9,1},{13,5},{2,10},{6,14},... | collective-permute-start | bytes 196616 | tf_op jit(solution)/shard_map/ppermute | solution.py:443
  112.9 2.8 %collective-permute-start.22 = (bf16[16,2048]{1,0:T(8,128)(2,1)S(1)}, bf16[16,2048]{1,0:T(8,128)(2,1)S(1)}, u32[]{:S(2)}, u32[]{:S(2)}) collective-permute-start(bf16[16,2048]{1,0:T(8,128)(2,1)S(1)} %get-tuple-element.62), channel_id=1, source_target_pairs={{0,12},{4,0},{8,4},{12,8},{1,13},{5,1},{9,5},{13,9},{2,14},{6,2},{... | collective-permute-start | bytes 196616 | tf_op jit(solution)/shard_map/ppermute | solution.py:443
  115.7 0.3 collective-permute-done.20
  116.1 0.8 collective-permute-done.21
  116.9 0.7 collective-permute-done.22
  117.7 0.6 collective-permute-start.23
  118.2 3.8 %collective-permute-done.23 = bf16[16,2048]{1,0:T(8,128)(2,1)S(1)} collective-permute-done((bf16[16,2048]{1,0:T(8,128)(2,1)S(1)}, bf16[16,2048]{1,0:T(8,128)(2,1)S(1)}, u32[]{:S(2)}, u32[]{:S(2)}) %collective-permute-start.23) | collective-permute-done | bytes 65568 | tf_op jit(solution)/shard_map/ppermute | solution.py:446
  122.1 1.2 collective-permute-start.24
  123.3 3.5 %collective-permute-start.25 = (bf16[2,16,2048]{2,1,0:T(8,128)(2,1)S(1)}, bf16[2,16,2048]{2,1,0:T(8,128)(2,1)S(1)}, u32[]{:S(2)}, u32[]{:S(2)}) collective-permute-start(bf16[2,16,2048]{2,1,0:T(8,128)(2,1)S(1)} %pad_maximum_fusion.1.own_ref), channel_id=1, source_target_pairs={{0,8},{4,12},{8,0},{12,4},{1,9},{5,13},{9,1},{13,5},{2,10},{6,14},... | collective-permute-start | bytes 393224 | tf_op jit(solution)/shard_map/ppermute | solution.py:454
  126.8 2.7 %collective-permute-done.24.refs_0_ = bf16[2,16,2048]{2,1,0:T(8,128)(2,1)S(1)} collective-permute-done((bf16[2,16,2048]{2,1,0:T(8,128)(2,1)S(1)}, bf16[2,16,2048]{2,1,0:T(8,128)(2,1)S(1)}, u32[]{:S(2)}, u32[]{:S(2)}) %collective-permute-start.24) | collective-permute-done | bytes 131104 | tf_op jit(solution)/shard_map/ppermute | solution.py:454
  129.6 4.1 %collective-permute-done.25.refs_1_ = bf16[2,16,2048]{2,1,0:T(8,128)(2,1)S(1)} collective-permute-done((bf16[2,16,2048]{2,1,0:T(8,128)(2,1)S(1)}, bf16[2,16,2048]{2,1,0:T(8,128)(2,1)S(1)}, u32[]{:S(2)}, u32[]{:S(2)}) %collective-permute-start.25) | collective-permute-done | bytes 131104 | tf_op jit(solution)/shard_map/ppermute | solution.py:454
  133.6 1.9 %finish.1 = (f32[2,4,16,1536]{3,2,1,0:T(8,128)}, f32[2,4,16,512]{3,2,1,0:T(8,128)}, f32[1,128]{1,0:T(1,128)}) custom-call(s32[3]{0:T(128)S(1)} %pad_add_fusion.refs_1_.place_ref, bf16[2,16,2048]{2,1,0:T(8,128)(2,1)S(1)} %pad_maximum_fusion.1.own_ref, bf16[2,16,2048]{2,1,0:T(8,128)(2,1)S(1)} %collective-permute-done.24.refs_0_, ...), custom_call_target="tpu_custom_call" | custom-call | bytes 3148288 | tf_op jit(solution)/shard_map/finish/pallas_call | solution.py:383
  (67 shorter events, 0.4 us)
Async XLA Ops:
  0.6 1.0 copy-start.6
  1.6 0.7 copy-start.8
  3.3 22.0 %collective-permute-start = (bf16[4,64,512]{2,1,0:T(8,128)(2,1)S(1)}, bf16[4,64,512]{2,1,0:T(8,128)(2,1)S(1)}, u32[]{:S(2)}, u32[]{:S(2)}) collective-permute-start(bf16[4,64,512]{2,1,0:T(8,128)(2,1)S(1)} %get-tuple-element.33.tok_ref), channel_id=1, source_target_pairs={{0,16},{16,0},{1,17},{17,1},{2,18},{18,2},{3,19},{19,3},{4,20},{20... | collective-permute-start | bytes 786440 | tf_op jit(solution)/shard_map/ppermute | solution.py:408
  6.2 23.2 %collective-permute-start.1 = (bf16[2,64,512]{2,1,0:T(8,128)(2,1)}, bf16[2,64,512]{2,1,0:T(8,128)(2,1)}, u32[]{:S(2)}, u32[]{:S(2)}) collective-permute-start(bf16[2,64,512]{2,1,0:T(8,128)(2,1)} %get-tuple-element.38), channel_id=1, source_target_pairs={{0,4},{4,8},{8,12},{1,5},{5,9},{9,13},{2,6},{6,10},{10,14},{3,7},{... | collective-permute-start | bytes 393224 | tf_op jit(solution)/shard_map/ppermute | solution.py:416
  10.3 20.4 %collective-permute-start.2 = (bf16[2,64,512]{2,1,0:T(8,128)(2,1)}, bf16[2,64,512]{2,1,0:T(8,128)(2,1)}, u32[]{:S(2)}, u32[]{:S(2)}) collective-permute-start(bf16[2,64,512]{2,1,0:T(8,128)(2,1)} %get-tuple-element.39), channel_id=1, source_target_pairs={{4,0},{8,4},{12,8},{5,1},{9,5},{13,9},{6,2},{10,6},{14,10},{7,3},{... | collective-permute-start | bytes 393224 | tf_op jit(solution)/shard_map/ppermute | solution.py:417
  11.6 1.4 %copy-start = (bf16[512,1536]{1,0:T(8,128)(2,1)S(1)}, bf16[512,1536]{1,0:T(8,128)(2,1)}, u32[]{:S(2)}) copy-start(bf16[512,1536]{1,0:T(8,128)(2,1)} %refs_3_.1) | copy-start | bytes 4718596
  13.0 1.0 copy-start.2
  14.1 0.9 copy-start.4
  15.0 0.7 copy-start.10
  15.7 21.8 %copy-start.1 = (bf16[512,1536]{1,0:T(8,128)(2,1)S(1)}, bf16[512,1536]{1,0:T(8,128)(2,1)}, u32[]{:S(2)}) copy-start(bf16[512,1536]{1,0:T(8,128)(2,1)} %refs_3_.1) | copy-start | bytes 4718596
  15.7 21.8 %copy-start.11 = (f32[512]{0:T(512)S(1)}, f32[512]{0:T(512)}, u32[]{:S(2)}) copy-start(f32[512]{0:T(512)} %param.10) | copy-start | bytes 6148
  17.3 0.7 copy-start.16
  18.0 0.7 copy-start.18
  18.7 0.7 copy-start.20
  19.4 0.6 copy-start.21
  20.0 29.3 %copy-start.14 = (bf16[4,64,512]{2,1,0:T(8,128)(2,1)}, bf16[4,64,512]{2,1,0:T(8,128)(2,1)S(1)}, u32[]{:S(2)}) copy-start(bf16[4,64,512]{2,1,0:T(8,128)(2,1)S(1)} %get-tuple-element.40.refs_10_.gm_ref) | copy-start | bytes 786436
  20.0 30.9 %copy-start.12 = (bf16[4,64,1024]{2,1,0:T(8,128)(2,1)}, bf16[4,64,1024]{2,1,0:T(8,128)(2,1)S(1)}, u32[]{:S(2)}) copy-start(bf16[4,64,1024]{2,1,0:T(8,128)(2,1)S(1)} %get-tuple-element.36.refs_3_.kv_ref) | copy-start | bytes 1572868
  20.0 8.1 %collective-permute-start.5 = (bf16[4,64,512]{2,1,0:T(8,128)(2,1)S(1)}, bf16[4,64,512]{2,1,0:T(8,128)(2,1)S(1)}, u32[]{:S(2)}, u32[]{:S(2)}) collective-permute-start(bf16[4,64,512]{2,1,0:T(8,128)(2,1)S(1)} %get-tuple-element.40.refs_10_.gm_ref), channel_id=1, source_target_pairs={{0,16},{16,0},{1,17},{17,1},{2,18},{18,2},{3,19},{19,3},{4,20},{20... | collective-permute-start | bytes 786440 | tf_op jit(solution)/shard_map/ppermute | solution.py:408
  20.6 36.0 %collective-permute-start.6 = (bf16[2,64,512]{2,1,0:T(8,128)(2,1)}, bf16[2,64,512]{2,1,0:T(8,128)(2,1)S(1)}, u32[]{:S(2)}, u32[]{:S(2)}) collective-permute-start(bf16[2,64,512]{2,1,0:T(8,128)(2,1)} %get-tuple-element.50), channel_id=1, source_target_pairs={{0,4},{4,8},{8,12},{1,5},{5,9},{9,13},{2,6},{6,10},{10,14},{3,7},{... | collective-permute-start | bytes 393224 | tf_op jit(solution)/shard_map/ppermute | solution.py:416
  25.2 10.9 %collective-permute-start.3 = (bf16[2,64,512]{2,1,0:T(8,128)(2,1)S(1)}, bf16[2,64,512]{2,1,0:T(8,128)(2,1)S(1)}, u32[]{:S(2)}, u32[]{:S(2)}) collective-permute-start(bf16[2,64,512]{2,1,0:T(8,128)(2,1)S(1)} %get-tuple-element.67), channel_id=1, source_target_pairs={{0,4},{4,8},{8,12},{1,5},{5,9},{9,13},{2,6},{6,10},{10,14},{3,7},{... | collective-permute-start | bytes 393224 | tf_op jit(solution)/shard_map/ppermute | solution.py:416
  28.1 9.4 %collective-permute-start.4 = (bf16[2,64,512]{2,1,0:T(8,128)(2,1)S(1)}, bf16[2,64,512]{2,1,0:T(8,128)(2,1)S(1)}, u32[]{:S(2)}, u32[]{:S(2)}) collective-permute-start(bf16[2,64,512]{2,1,0:T(8,128)(2,1)S(1)} %get-tuple-element.66), channel_id=1, source_target_pairs={{4,0},{8,4},{12,8},{5,1},{9,5},{13,9},{6,2},{10,6},{14,10},{7,3},{... | collective-permute-start | bytes 393224 | tf_op jit(solution)/shard_map/ppermute | solution.py:417
  29.4 29.9 %collective-permute-start.7 = (bf16[2,64,512]{2,1,0:T(8,128)(2,1)}, bf16[2,64,512]{2,1,0:T(8,128)(2,1)S(1)}, u32[]{:S(2)}, u32[]{:S(2)}) collective-permute-start(bf16[2,64,512]{2,1,0:T(8,128)(2,1)} %copy-done.20), channel_id=1, source_target_pairs={{4,0},{8,4},{12,8},{5,1},{9,5},{13,9},{6,2},{10,6},{14,10},{7,3},{... | collective-permute-start | bytes 393224 | tf_op jit(solution)/shard_map/ppermute | solution.py:417
  30.7 29.9 %collective-permute-start.8 = (bf16[2,64,512]{2,1,0:T(8,128)(2,1)S(1)}, bf16[2,64,512]{2,1,0:T(8,128)(2,1)S(1)}, u32[]{:S(2)}, u32[]{:S(2)}) collective-permute-start(bf16[2,64,512]{2,1,0:T(8,128)(2,1)S(1)} %get-tuple-element.65), channel_id=1, source_target_pairs={{0,4},{4,8},{8,12},{1,5},{5,9},{9,13},{2,6},{6,10},{10,14},{3,7},{... | collective-permute-start | bytes 393224 | tf_op jit(solution)/shard_map/ppermute | solution.py:416
  36.2 29.4 %collective-permute-start.9 = (bf16[2,64,512]{2,1,0:T(8,128)(2,1)S(1)}, bf16[2,64,512]{2,1,0:T(8,128)(2,1)S(1)}, u32[]{:S(2)}, u32[]{:S(2)}) collective-permute-start(bf16[2,64,512]{2,1,0:T(8,128)(2,1)S(1)} %get-tuple-element.64), channel_id=1, source_target_pairs={{4,0},{8,4},{12,8},{5,1},{9,5},{13,9},{6,2},{10,6},{14,10},{7,3},{... | collective-permute-start | bytes 393224 | tf_op jit(solution)/shard_map/ppermute | solution.py:417
  37.5 0.9 copy-start.22
  38.4 12.5 %copy-start.3 = (bf16[512,512]{1,0:T(8,128)(2,1)S(1)}, bf16[512,512]{1,0:T(8,128)(2,1)}, u32[]{:S(2)}) copy-start(bf16[512,512]{1,0:T(8,128)(2,1)} %wout_ref.3) | copy-start | bytes 1572868
  38.4 12.5 %copy-start.7 = (bf16[1,16,16,512]{3,2,1,0:T(8,128)(2,1)S(1)}, bf16[1,16,16,512]{3,2,1,0:T(8,128)(2,1)}, u32[]{:S(2)}) copy-start(bf16[1,16,16,512]{3,2,1,0:T(8,128)(2,1)} %x_ref.3) | copy-start | bytes 786436
  38.4 12.5 %copy-start.9 = (s32[1,16,16]{2,1,0:T(8,128)S(1)}, s32[1,16,16]{2,1,0:T(8,128)}, u32[]{:S(2)}) copy-start(s32[1,16,16]{2,1,0:T(8,128)} %mask_ref.5) | copy-start | bytes 3076
  38.4 12.5 %copy-start.17 = (bf16[256,512]{1,0:T(8,128)(2,1)S(1)}, bf16[256,512]{1,0:T(8,128)(2,1)}, u32[]{:S(2)}) copy-start(bf16[256,512]{1,0:T(8,128)(2,1)} %copy-done.16) | copy-start | bytes 786436
  38.4 12.5 %copy-start.19 = (bf16[256,512]{1,0:T(8,128)(2,1)S(1)}, bf16[256,512]{1,0:T(8,128)(2,1)}, u32[]{:S(2)}) copy-start(bf16[256,512]{1,0:T(8,128)(2,1)} %copy-done.18) | copy-start | bytes 786436
  38.4 12.5 %copy-start.23 = (f32[4,64,128]{2,1,0:T(8,128)S(1)}, f32[4,64,128]{2,1,0:T(8,128)}, u32[]{:S(2)}) copy-start(f32[4,64,128]{2,1,0:T(8,128)} %copy-done.21) | copy-start | bytes 393220
  49.3 7.2 %collective-permute-start.10 = (f32[4,16,64]{2,1,0:T(8,128)S(1)}, f32[4,16,64]{2,1,0:T(8,128)S(1)}, u32[]{:S(2)}, u32[]{:S(2)}) collective-permute-start(f32[4,16,64]{2,1,0:T(8,128)S(1)} %get-tuple-element.48.stats_ref), channel_id=1, source_target_pairs={{0,16},{16,0},{1,17},{17,1},{2,18},{18,2},{3,19},{19,3},{4,20},{20... | collective-permute-start | bytes 49160 | tf_op jit(solution)/shard_map/ppermute | solution.py:408
  51.0 1.0 copy-start.15
  51.9 20.8 %copy-start.5 = (bf16[1,16,16,512]{3,2,1,0:T(8,128)(2,1)S(1)}, bf16[1,16,16,512]{3,2,1,0:T(8,128)(2,1)}, u32[]{:S(2)}) copy-start(bf16[1,16,16,512]{3,2,1,0:T(8,128)(2,1)} %cot_ref.3) | copy-start | bytes 786436
  56.6 27.9 %collective-permute-start.15 = (bf16[2,128,1024]{2,1,0:T(8,128)(2,1)S(1)}, bf16[2,128,1024]{2,1,0:T(8,128)(2,1)S(1)}, u32[]{:S(2)}, u32[]{:S(2)}) collective-permute-start(bf16[2,128,1024]{2,1,0:T(8,128)(2,1)S(1)} %get-tuple-element.55), channel_id=1, source_target_pairs={{0,1},{1,0},{2,3},{3,2},{4,5},{5,4},{6,7},{7,6},{8,9},{9,8},{10,11... | collective-permute-start | bytes 1572872 | tf_op jit(solution)/shard_map/ppermute | solution.py:422
  56.6 10.3 %collective-permute-start.11 = (f32[2,16,64]{2,1,0:T(8,128)S(1)}, f32[2,16,64]{2,1,0:T(8,128)S(1)}, u32[]{:S(2)}, u32[]{:S(2)}) collective-permute-start(f32[2,16,64]{2,1,0:T(8,128)S(1)} %get-tuple-element.73), channel_id=1, source_target_pairs={{0,4},{4,8},{8,12},{1,5},{5,9},{9,13},{2,6},{6,10},{10,14},{3,7},{... | collective-permute-start | bytes 24584 | tf_op jit(solution)/shard_map/ppermute | solution.py:416
  59.3 7.6 %collective-permute-start.12 = (f32[2,16,64]{2,1,0:T(8,128)S(1)}, f32[2,16,64]{2,1,0:T(8,128)S(1)}, u32[]{:S(2)}, u32[]{:S(2)}) collective-permute-start(f32[2,16,64]{2,1,0:T(8,128)S(1)} %get-tuple-element.72), channel_id=1, source_target_pairs={{4,0},{8,4},{12,8},{5,1},{9,5},{13,9},{6,2},{10,6},{14,10},{7,3},{... | collective-permute-start | bytes 24584 | tf_op jit(solution)/shard_map/ppermute | solution.py:417
  60.6 6.4 %collective-permute-start.13 = (f32[2,16,64]{2,1,0:T(8,128)S(1)}, f32[2,16,64]{2,1,0:T(8,128)S(1)}, u32[]{:S(2)}, u32[]{:S(2)}) collective-permute-start(f32[2,16,64]{2,1,0:T(8,128)S(1)} %get-tuple-element.71), channel_id=1, source_target_pairs={{0,4},{4,8},{8,12},{1,5},{5,9},{9,13},{2,6},{6,10},{10,14},{3,7},{... | collective-permute-start | bytes 24584 | tf_op jit(solution)/shard_map/ppermute | solution.py:416
  65.6 7.1 %collective-permute-start.14 = (f32[2,16,64]{2,1,0:T(8,128)S(1)}, f32[2,16,64]{2,1,0:T(8,128)S(1)}, u32[]{:S(2)}, u32[]{:S(2)}) collective-permute-start(f32[2,16,64]{2,1,0:T(8,128)S(1)} %get-tuple-element.70), channel_id=1, source_target_pairs={{4,0},{8,4},{12,8},{5,1},{9,5},{13,9},{6,2},{10,6},{14,10},{7,3},{... | collective-permute-start | bytes 24584 | tf_op jit(solution)/shard_map/ppermute | solution.py:417
  72.7 1.0 copy-start.13
  84.5 2.1 %collective-permute-start.17 = (bf16[2,128,1024]{2,1,0:T(8,128)(2,1)}, bf16[2,128,1024]{2,1,0:T(8,128)(2,1)S(1)}, u32[]{:S(2)}, u32[]{:S(2)}) collective-permute-start(bf16[2,128,1024]{2,1,0:T(8,128)(2,1)} %get-tuple-element.57), channel_id=1, source_target_pairs={{0,1},{1,0},{2,3},{3,2},{4,5},{5,4},{6,7},{7,6},{8,9},{9,8},{10,11... | collective-permute-start | bytes 1572872 | tf_op jit(solution)/shard_map/ppermute | solution.py:422
  84.6 1.0 copy-start.24
  86.4 9.3 %collective-permute-start.16 = (bf16[128,1024]{1,0:T(8,128)(2,1)}, bf16[128,1024]{1,0:T(8,128)(2,1)S(1)}, u32[]{:S(2)}, u32[]{:S(2)}) collective-permute-start(bf16[128,1024]{1,0:T(8,128)(2,1)} %fusion.6), channel_id=1, source_target_pairs={{0,2},{1,3},{2,0},{3,1},{4,6},{5,7},{6,4},{7,5},{8,10},{9,11},{10,... | collective-permute-start | bytes 786440 | tf_op jit(solution)/shard_map/ppermute | solution.py:424
  86.4 9.3 %copy-start.25 = (f32[2,128,1024]{2,1,0:T(8,128)S(1)}, f32[2,128,1024]{2,1,0:T(8,128)}, u32[]{:S(2)}) copy-start(f32[2,128,1024]{2,1,0:T(8,128)} %copy-done.24) | copy-start | bytes 3145732
  86.8 14.2 %collective-permute-start.18 = (bf16[128,1024]{1,0:T(8,128)(2,1)S(1)}, bf16[128,1024]{1,0:T(8,128)(2,1)S(1)}, u32[]{:S(2)}, u32[]{:S(2)}) collective-permute-start(bf16[128,1024]{1,0:T(8,128)(2,1)S(1)} %fusion.7), channel_id=1, source_target_pairs={{0,2},{1,3},{2,0},{3,1},{4,6},{5,7},{6,4},{7,5},{8,10},{9,11},{10,... | collective-permute-start | bytes 786440 | tf_op jit(solution)/shard_map/ppermute | solution.py:424
  101.2 8.0 %collective-permute-start.19 = (bf16[64,2048]{1,0:T(8,128)(2,1)S(1)}, bf16[64,2048]{1,0:T(8,128)(2,1)S(1)}, u32[]{:S(2)}, u32[]{:S(2)}) collective-permute-start(bf16[64,2048]{1,0:T(8,128)(2,1)S(1)} %fusion.8), channel_id=1, source_target_pairs={{0,16},{16,0},{1,17},{17,1},{2,18},{18,2},{3,19},{19,3},{4,20},{20... | collective-permute-start | bytes 786440 | tf_op jit(solution)/shard_map/ppermute | solution.py:437
  109.3 6.8 %collective-permute-start.20 = (bf16[16,2048]{1,0:T(8,128)(2,1)S(1)}, bf16[16,2048]{1,0:T(8,128)(2,1)S(1)}, u32[]{:S(2)}, u32[]{:S(2)}) collective-permute-start(bf16[16,2048]{1,0:T(8,128)(2,1)S(1)} %get-tuple-element.61), channel_id=1, source_target_pairs={{0,4},{4,8},{8,12},{12,0},{1,5},{5,9},{9,13},{13,1},{2,6},{6,10},{... | collective-permute-start | bytes 196616 | tf_op jit(solution)/shard_map/ppermute | solution.py:443
  110.2 6.8 %collective-permute-start.21 = (bf16[16,2048]{1,0:T(8,128)(2,1)S(1)}, bf16[16,2048]{1,0:T(8,128)(2,1)S(1)}, u32[]{:S(2)}, u32[]{:S(2)}) collective-permute-start(bf16[16,2048]{1,0:T(8,128)(2,1)S(1)} %get-tuple-element.63), channel_id=1, source_target_pairs={{0,8},{4,12},{8,0},{12,4},{1,9},{5,13},{9,1},{13,5},{2,10},{6,14},... | collective-permute-start | bytes 196616 | tf_op jit(solution)/shard_map/ppermute | solution.py:443
  112.9 4.8 %collective-permute-start.22 = (bf16[16,2048]{1,0:T(8,128)(2,1)S(1)}, bf16[16,2048]{1,0:T(8,128)(2,1)S(1)}, u32[]{:S(2)}, u32[]{:S(2)}) collective-permute-start(bf16[16,2048]{1,0:T(8,128)(2,1)S(1)} %get-tuple-element.62), channel_id=1, source_target_pairs={{0,12},{4,0},{8,4},{12,8},{1,13},{5,1},{9,5},{13,9},{2,14},{6,2},{... | collective-permute-start | bytes 196616 | tf_op jit(solution)/shard_map/ppermute | solution.py:443
  117.7 4.3 %collective-permute-start.23 = (bf16[16,2048]{1,0:T(8,128)(2,1)S(1)}, bf16[16,2048]{1,0:T(8,128)(2,1)S(1)}, u32[]{:S(2)}, u32[]{:S(2)}) collective-permute-start(bf16[16,2048]{1,0:T(8,128)(2,1)S(1)} %fusion.11), channel_id=1, source_target_pairs={{0,16},{16,0},{1,17},{17,1},{2,18},{18,2},{3,19},{19,3},{4,20},{20... | collective-permute-start | bytes 196616 | tf_op jit(solution)/shard_map/ppermute | solution.py:446
  122.1 7.5 %collective-permute-start.24 = (bf16[2,16,2048]{2,1,0:T(8,128)(2,1)S(1)}, bf16[2,16,2048]{2,1,0:T(8,128)(2,1)S(1)}, u32[]{:S(2)}, u32[]{:S(2)}) collective-permute-start(bf16[2,16,2048]{2,1,0:T(8,128)(2,1)S(1)} %pad_maximum_fusion.1.own_ref), channel_id=1, source_target_pairs={{0,4},{4,8},{8,12},{12,0},{1,5},{5,9},{9,13},{13,1},{2,6},{6,10},{... | collective-permute-start | bytes 393224 | tf_op jit(solution)/shard_map/ppermute | solution.py:454
  123.3 10.3 %collective-permute-start.25 = (bf16[2,16,2048]{2,1,0:T(8,128)(2,1)S(1)}, bf16[2,16,2048]{2,1,0:T(8,128)(2,1)S(1)}, u32[]{:S(2)}, u32[]{:S(2)}) collective-permute-start(bf16[2,16,2048]{2,1,0:T(8,128)(2,1)S(1)} %pad_maximum_fusion.1.own_ref), channel_id=1, source_target_pairs={{0,8},{4,12},{8,0},{12,4},{1,9},{5,13},{9,1},{13,5},{2,10},{6,14},... | collective-permute-start | bytes 393224 | tf_op jit(solution)/shard_map/ppermute | solution.py:454
  126.8 6.8 %collective-permute-start.26 = (bf16[2,16,2048]{2,1,0:T(8,128)(2,1)S(1)}, bf16[2,16,2048]{2,1,0:T(8,128)(2,1)S(1)}, u32[]{:S(2)}, u32[]{:S(2)}) collective-permute-start(bf16[2,16,2048]{2,1,0:T(8,128)(2,1)S(1)} %pad_maximum_fusion.1.own_ref), channel_id=1, source_target_pairs={{0,12},{4,0},{8,4},{12,8},{1,13},{5,1},{9,5},{13,9},{2,14},{6,2},{... | collective-permute-start | bytes 393224 | tf_op jit(solution)/shard_map/ppermute | solution.py:454

commit v2 on v1

v2 whole, which is shorter than its diff:
```python
import functools

import jax
import jax.numpy as jnp
from jax import lax
from jax.experimental import pallas as pl
from jax.experimental.pallas import tpu as pltpu
from jax.sharding import PartitionSpec as P

HEADS = 8
WIN = 8
AREA = WIN * WIN
D = 512
HEAD_DIM = D // HEADS
GROUP = 256
GROUP_HEADS = GROUP // HEAD_DIM
GROUPS = D // GROUP
KEYS = 8 * AREA
LAND = 1000.0
NEVER = -1e9
FAR = 1e30
F32 = jnp.float32
BF16 = jnp.bfloat16
EXACT = lax.Precision.HIGHEST


def dot(a, b, ca, cb, precision=None):
    return lax.dot_general(
        a, b, (((ca,), (cb,)), ((), ())), preferred_element_type=F32, precision=precision
    )


def iota(shape, dim):
    return lax.broadcasted_iota(jnp.int32, shape, dim)


def window_of(grid, w):
    r, c = divmod(w, 2)
    part = grid[r * WIN : (r + 1) * WIN, c * WIN : (c + 1) * WIN, :]
    return part.reshape(AREA, grid.shape[-1])


def grid_of(windows):
    rows = []
    for r in range(2):
        parts = [windows[2 * r + c].reshape(WIN, WIN, -1) for c in range(2)]
        rows.append(jnp.concatenate(parts, axis=1))
    return jnp.concatenate(rows, axis=0)


def token_mask(mask):
    t = iota((4 * AREA, 2 * WIN), 0)
    lane = iota((4 * AREA, 2 * WIN), 1)
    w, i, j = t // AREA, (t % AREA) // WIN, t % WIN
    pick_row = (lane == WIN * (w // 2) + i).astype(F32)
    pick_col = (lane == WIN * (w % 2) + j).astype(F32)
    rows = dot(pick_row, mask, 1, 0)
    return jnp.sum(rows * pick_col, axis=1, keepdims=True)


def norm_rows(x):
    center = x - jnp.mean(x, axis=-1, keepdims=True)
    spread = jnp.mean(center * center, axis=-1, keepdims=True)
    scaling = lax.rsqrt(spread + 1e-05)
    return center * scaling, scaling


def head_blocks():
    row = iota((GROUP, GROUP), 0) // HEAD_DIM
    col = iota((GROUP, GROUP), 1) // HEAD_DIM
    return (row == col).astype(F32)


def stack_heads(part, blocks):
    return jnp.concatenate([part] * GROUP_HEADS, axis=0) * blocks.astype(part.dtype)


def unstack_heads(full, blocks):
    kept = full * blocks
    return sum(kept[h * AREA : (h + 1) * AREA] for h in range(GROUP_HEADS))


def lanes(g):
    return slice(g * GROUP, (g + 1) * GROUP)


def prep_kernel(x_ref, mask_ref, all_ref, top_ref, bottom_ref):
    ocean = token_mask(mask_ref[0].astype(F32))
    x = x_ref[0].astype(F32)
    for w in range(4):
        part = jnp.where(ocean[w * AREA : (w + 1) * AREA] > 0.5, window_of(x, w), LAND)
        part = part.astype(BF16)
        all_ref[w] = part
        (top_ref if w < 2 else bottom_ref)[w % 2] = part


def own_kernel(
    tok_ref, cot_ref, mask_ref, wqkv_ref, wout_ref, gain_ref,
    q_ref, kv_ref, gm_ref, gb_ref, hid_ref, info_ref,
):
    ocean = token_mask(mask_ref[0].astype(F32))
    tokens = tok_ref[...].reshape(4 * AREA, D).astype(F32)
    normed, _ = norm_rows(tokens)
    hidden = (normed * gain_ref[...]).astype(BF16)
    hid_ref[...] = hidden
    projected = dot(hidden, wqkv_ref[...], 1, 0).astype(BF16)
    q_ref[...] = (projected[:, :D] * BF16(HEAD_DIM ** -0.5)).reshape(4, AREA, D)
    kv_ref[...] = projected[:, D:].reshape(4, AREA, 2 * D)
    cot = cot_ref[0].astype(F32)
    for w in range(4):
        branch = window_of(cot, w) * ocean[w * AREA : (w + 1) * AREA]
        gb_ref[w * AREA : (w + 1) * AREA, :] = branch.astype(BF16)
    gm = dot(gb_ref[...], wout_ref[...], 1, 1).astype(BF16)
    gm_ref[...] = gm.reshape(4, AREA, D)
    alive = []
    for w in range(4):
        alive.append((jnp.max(ocean[w * AREA : (w + 1) * AREA]) > 0.5).astype(jnp.int32))
        info_ref[1 + w] = alive[w]
    info_ref[0] = jnp.where(
        alive[3] == 0, 3, jnp.where(alive[2] == 0, 2, jnp.where(alive[1] == 0, 1, 0))
    )


def slot_window(info_ref, slot):
    return slot + (slot >= info_ref[0]).astype(jnp.int32)


def near_places(w):
    r, c = w // 2, w % 2
    lon_at, lat_at = 2 * (1 - c), 4 + 2 * r
    return lon_at, lon_at + 1, lat_at, lat_at + 1, 8 + 2 * r + 1 - c


def land_bias(tokens):
    first = (iota((8, D), 1) == 0).astype(BF16)
    picked = dot(first, tokens, 1, 1)[:1]
    return jnp.where(picked > 0.5 * LAND, NEVER, 0.0)


def main_kernel(
    info_ref, place_ref, q_ref, kv_ref, gm_ref, gb_ref, hid_ref, tok_ref, lon_ref, up_ref,
    down_ref, upc_ref, downc_ref, x_ref, mask_ref, wqkv_ref, wout_ref, gain_ref,
    out_ref, gq_ref, own_ref, side_ref, top_ref, bottom_ref,
    keep_a_ref, send_a_ref, keep_b_ref, send_b_ref,
    kvh, hidh, bias, kcat, acc, mixed,
):
    up_ok, down_ok = place_ref[0] > 0, place_ref[0] < place_ref[1] - 1
    groups = (
        ((lon_ref, 0), (lon_ref, 2), (lon_ref, 1), (lon_ref, 3)),
        ((up_ref, 0), (up_ref, 1), (down_ref, 0), (down_ref, 1)),
        ((upc_ref, 0), (upc_ref, 1), (downc_ref, 0), (downc_ref, 1)),
    )
    for n, group in enumerate(groups):
        low = jnp.concatenate([ref[at] for ref, at in group], axis=0)
        normed, _ = norm_rows(low.astype(F32))
        hidden = (normed * gain_ref[...]).astype(BF16)
        hidh[n * 4 * AREA : (n + 1) * 4 * AREA] = hidden
        kvh[4 * n : 4 * n + 4] = dot(hidden, wqkv_ref[:, D:], 1, 0).astype(BF16).reshape(4, AREA, 2 * D)
        row = land_bias(low)
        for k in range(4):
            part = row[:, k * AREA : (k + 1) * AREA]
            if n > 0:
                part = jnp.where(up_ok if k < 2 else down_ok, part, NEVER)
            bias[4 + 4 * n + k] = jnp.broadcast_to(part, (8, AREA))
    own_row = land_bias(tok_ref[...].reshape(4 * AREA, D))
    for w in range(4):
        bias[w] = jnp.broadcast_to(own_row[:, w * AREA : (w + 1) * AREA], (8, AREA))
    acc[...] = jnp.zeros_like(acc)
    mixed[...] = jnp.zeros_like(mixed)
    gq_ref[...] = jnp.zeros_like(gq_ref)
    blocks = head_blocks()
    for slot in range(3):
        kcat[slot * AREA : (slot + 1) * AREA] = kv_ref[slot_window(info_ref, slot)]

    def slot_step(slot, carry):
        w = slot_window(info_ref, slot)

        @pl.when(info_ref[1 + w] > 0)
        def _():
            places = [slot_window(info_ref, k) for k in range(3)] + [4 + at for at in near_places(w)]
            for k in range(3, 8):
                kcat[k * AREA : (k + 1) * AREA] = kvh[places[k] - 4]
            bias_row = jnp.concatenate([bias[at][:1] for at in places], axis=1)
            for g in range(GROUPS):
                at_v = slice(D + g * GROUP, D + (g + 1) * GROUP)
                q_stack = stack_heads(q_ref[w, :, lanes(g)], blocks)
                gm_stack = stack_heads(gm_ref[w, :, lanes(g)], blocks)
                keys = kcat[:, lanes(g)]
                values = kcat[:, at_v]
                scores = dot(q_stack, keys, 1, 1) + bias_row
                weights = jnp.exp(scores - jnp.max(scores, axis=1, keepdims=True))
                probs = weights * (1.0 / jnp.sum(weights, axis=1, keepdims=True))
                low = probs.astype(BF16)
                out = unstack_heads(dot(low, values, 1, 0), blocks).astype(BF16)
                mixed[w, :, lanes(g)] = out
                out_stack = jnp.concatenate([out] * GROUP_HEADS, axis=0).astype(F32)
                delta = jnp.sum(out_stack * gm_stack.astype(F32), axis=1, keepdims=True)
                grad_probs = dot(gm_stack, values, 1, 1)
                grad_scores = (probs * (grad_probs - delta)).astype(BF16)
                grad = unstack_heads(dot(grad_scores, keys, 1, 0), blocks)
                gq_ref[w, :, lanes(g)] = (grad * HEAD_DIM ** -0.5).astype(BF16)
                grad_keys = dot(grad_scores, q_stack, 0, 0)
                grad_values = dot(low, gm_stack, 0, 0)
                for k in range(8):
                    rows = slice(k * AREA, (k + 1) * AREA)
                    acc[places[k], :, lanes(g)] += grad_keys[rows]
                    acc[places[k], :, at_v] += grad_values[rows]

        return carry

    lax.fori_loop(0, 3, slot_step, 0)
    flat = mixed[...].reshape(4 * AREA, D)
    ocean = token_mask(mask_ref[0].astype(F32))
    added = (dot(flat, wout_ref[...], 1, 0) * ocean).reshape(4, AREA, D)
    out_ref[0] = (x_ref[0].astype(F32) + grid_of([added[w] for w in range(4)])).astype(BF16)
    own_ref[...] = acc[:4]
    side_ref[...] = acc[4:8]
    low = acc[4:].astype(BF16)
    for k in range(2):
        top_ref[k], top_ref[2 + k] = low[4 + k], low[8 + k]
        bottom_ref[k], bottom_ref[2 + k] = low[6 + k], low[10 + k]
    grad_own = acc[:4].astype(BF16).reshape(4 * AREA, 2 * D)
    grad_halo = low.reshape(12 * AREA, 2 * D)
    gq = gq_ref[...].reshape(4 * AREA, D)
    lev = place_ref[2]
    for rel in range(4):
        at = pl.ds(pl.multiple_of((lev ^ rel) * 128, 128), 128)
        to_a, to_b = (keep_a_ref, keep_b_ref) if rel % 2 == 0 else (send_a_ref, send_b_ref)
        hid = hid_ref[:, at]
        to_a[rel // 2, :, :D] = dot(hid, gq, 0, 0).astype(BF16)
        to_a[rel // 2, :, D:] = dot(mixed[:, :, at].reshape(4 * AREA, 128), gb_ref[...], 0, 0).astype(BF16)
        to_b[rel // 2] = (dot(hid, grad_own, 0, 0) + dot(hidh[:, at], grad_halo, 0, 0)).astype(BF16)


def input_kernel(
    own_ref, up_ref, down_ref, lon_ref, gq_ref, tok_ref, cot_ref, wqkv_ref, gain_ref, ing_ref, gkv
):
    for w in range(4):
        lat_ref = up_ref if w < 2 else down_ref
        total = own_ref[w] + lat_ref[w % 2].astype(F32) + lon_ref[w].astype(F32)
        gkv[w * AREA : (w + 1) * AREA] = total.astype(BF16)
    grad_hidden = dot(gq_ref[...].reshape(4 * AREA, D), wqkv_ref[:, :D], 1, 1)
    grad_hidden = grad_hidden + dot(gkv[...], wqkv_ref[:, D:], 1, 1)
    normed, scaling = norm_rows(tok_ref[...].reshape(4 * AREA, D).astype(F32))
    scaled = grad_hidden * gain_ref[...]
    correction = (
        scaled
        - jnp.mean(scaled, axis=-1, keepdims=True)
        - normed * jnp.mean(scaled * normed, axis=-1, keepdims=True)
    )
    added = (scaling * correction).reshape(4, AREA, D)
    ing_ref[0] = (cot_ref[0].astype(F32) + grid_of([added[w] for w in range(4)])).astype(BF16)


def finish_kernel(whole_rows, place_ref, own_ref, *refs):
    others, (wqkv_ref, gain_ref, qkv_ref, out_ref, gg_ref) = refs[:-5], refs[-5:]
    lat, lat_count, lev = place_ref[0], place_ref[1], place_ref[2]
    for k, ref in enumerate((own_ref,) + tuple(others)):
        z = lax.rem(lat - k + lat_count, lat_count)
        value = ref[...].astype(F32)
        for x in range(value.shape[0]):
            qkv_ref[x, z, :, :D] = value[x, :, :D]
            qkv_ref[x, z, :, D:] = value[x, :, 2 * D :]
            out_ref[x, z] = value[x, :, D : 2 * D]
    if whole_rows:
        at = pl.ds(pl.multiple_of(lev * 128, 128), 128)
        product = wqkv_ref[at, :].astype(F32) * qkv_ref[...].reshape(128, 3 * D)
        sums = dot(jnp.ones((8, 3 * D), F32), product, 1, 1, EXACT)[:1]
        gg_ref[...] = sums / gain_ref[:, at]
    else:
        gg_ref[...] = jnp.zeros_like(gg_ref)


SMEM = pl.BlockSpec(memory_space=pltpu.SMEM)


def whole_block(dims):
    return pl.BlockSpec(dims, lambda i: (0,) * len(dims), pipeline_mode=pl.Buffered(1))


def call(kernel, outs, scalars, arrays, scratch=(), flops=0, name=None, smem_out=False):
    moved = sum(a.size * a.dtype.itemsize for a in arrays)
    moved += sum(o.size * o.dtype.itemsize for o in outs)
    out_specs = [whole_block(o.shape) for o in outs]
    if smem_out:
        out_specs[-1] = SMEM
    return pl.pallas_call(
        kernel,
        grid=(1,),
        out_shape=outs,
        in_specs=[SMEM] * len(scalars) + [whole_block(a.shape) for a in arrays],
        out_specs=out_specs,
        scratch_shapes=list(scratch),
        compiler_params=pltpu.CompilerParams(vmem_limit_bytes=62 * 1024 * 1024),
        cost_estimate=pl.CostEstimate(flops=flops, bytes_accessed=moved, transcendentals=0),
        name=name,
    )(*scalars, *arrays)


def shape(dims, dtype=BF16):
    return jax.ShapeDtypeStruct(dims, dtype)


def ring(count, step, periodic):
    return [
        (i, (i + step) % count) for i in range(count) if periodic or 0 <= i + step < count
    ]


def lon_halo(own):
    count = lax.axis_size("lon")
    if count == 2:
        return lax.ppermute(own, "lon", [(0, 1), (1, 0)])
    left = lax.ppermute(own[1::2], "lon", ring(count, 1, True))
    right = lax.ppermute(own[0::2], "lon", ring(count, -1, True))
    return jnp.stack([right, left], axis=1).reshape(own.shape)


def lon_return(side):
    count = lax.axis_size("lon")
    if count == 2:
        return lax.ppermute(side, "lon", [(0, 1), (1, 0)])
    from_left = lax.ppermute(side[0::2], "lon", ring(count, 1, True))
    from_right = lax.ppermute(side[1::2], "lon", ring(count, -1, True))
    return jnp.stack([from_left, from_right], axis=1).reshape(side.shape)


def lat_halo(top, bottom):
    count = lax.axis_size("lat")
    up = lax.ppermute(bottom, "lat", ring(count, 1, False))
    down = lax.ppermute(top, "lat", ring(count, -1, False))
    return up, down


def core_sum(keep, send):
    arrived = lax.ppermute(send, "lev", [(i, i ^ 1) for i in range(4)])
    return keep.astype(F32) + arrived.astype(F32)


def level_sum(parts):
    arrived = lax.ppermute(parts[1].astype(BF16), "lev", [(i, i ^ 2) for i in range(4)])
    return parts[0] + arrived.astype(F32)


def lon_sum(parts):
    lon, count = lax.axis_index("lon"), lax.axis_size("lon")
    own = lax.dynamic_index_in_dim(parts, lon, 0, False)
    for k in range(1, count):
        piece = lax.dynamic_index_in_dim(parts, (lon + k) % count, 0, False).astype(BF16)
        own = own + lax.ppermute(piece, "lon", ring(count, k, True)).astype(F32)
    return own


def plane_parts(own):
    lon, lon_count = lax.axis_index("lon"), lax.axis_size("lon")
    lat, lat_count = lax.axis_index("lat"), lax.axis_size("lat")
    parts = own.reshape(lat_count, -1, own.shape[1])
    own = lax.dynamic_index_in_dim(parts, lat, 0, False)
    low = parts.astype(BF16)
    for k in range(1, lat_count):
        piece = lax.dynamic_index_in_dim(low, (lat + k) % lat_count, 0, False)
        own = own + lax.ppermute(piece, "lat", ring(lat_count, k, True)).astype(F32)
    own = own.astype(BF16)
    across = [own] + [
        lax.ppermute(own, "lon", ring(lon_count, k, True)) for k in range(1, lon_count)
    ]
    if lon_count == 2:
        first = lon == 0
        across = [jnp.where(first, across[0], across[1]), jnp.where(first, across[1], across[0])]
        both = jnp.stack(across)
    else:
        both = jnp.roll(jnp.stack(across[:1] + across[:0:-1]), lon, axis=0)
    return [both] + [lax.ppermute(both, "lat", ring(lat_count, k, True)) for k in range(1, lat_count)]


def on_device(tokens_in, cotangent, qkv_weight, out_weight, norm_gain, ocean_mask):
    lat_count, lon_count = lax.axis_size("lat"), lax.axis_size("lon")
    gain = norm_gain.reshape(1, D)
    place = jnp.stack(
        [lax.axis_index("lat"), jnp.int32(lat_count), lax.axis_index("lev")]
    ).astype(jnp.int32)
    half = shape((2, AREA, D))
    four = shape((4, AREA, D))
    flat = shape((4 * AREA, D))
    wide = shape((4, AREA, 2 * D))
    tok, tok_top, tok_bottom = call(
        prep_kernel, [four, half, half], [], [tokens_in, ocean_mask], name="prep"
    )
    tok_lon = lon_halo(tok)
    tok_up, tok_down = lat_halo(tok_top, tok_bottom)
    q, kv, gm, gb, hid, info = call(
        own_kernel,
        [four, wide, four, flat, flat, shape((8,), jnp.int32)],
        [],
        [tok, cotangent, ocean_mask, qkv_weight, out_weight, gain],
        flops=2 * 256 * 512 * 2048,
        name="own",
        smem_out=True,
    )
    tok_upc, tok_downc = lat_halo(tok_lon[:2], tok_lon[2:])
    share = shape((2, 128, 2 * D))
    wide32 = shape((4, AREA, 2 * D), F32)
    layer_out, gq, own_kv, side_kv, top_kv, bottom_kv, keep_a, send_a, keep_b, send_b = call(
        main_kernel,
        [shape(tokens_in.shape), four, wide32, wide32, wide, wide, share, share, share, share],
        [info, place],
        [q, kv, gm, gb, hid, tok, tok_lon, tok_up, tok_down, tok_upc, tok_downc,
         tokens_in, ocean_mask, qkv_weight, out_weight, gain],
        [pltpu.VMEM((12, AREA, 2 * D), BF16), pltpu.VMEM((12 * AREA, D), BF16),
         pltpu.VMEM((16, 8, AREA), F32), pltpu.VMEM((KEYS, 2 * D), BF16),
         pltpu.VMEM((16, AREA, 2 * D), F32), pltpu.VMEM((4, AREA, D), BF16)],
        flops=2 * 768 * 512 * 1024 + 3 * 12 * 2 * 512 * 256 * 256 + 2 * 1024 * 512 * 2048,
        name="main",
    )
    part_a = level_sum(core_sum(keep_a, send_a))
    part_a = lon_sum(part_a.reshape(lon_count, -1, 2 * D))
    part_b = core_sum(keep_b, send_b)
    part_b = jnp.swapaxes(part_b.reshape(2, lon_count, -1, 2 * D), 0, 1)
    part_b = level_sum(lon_sum(part_b))
    up_kv, down_kv = lat_halo(top_kv, bottom_kv)
    side_kv = side_kv.reshape(2, 2, AREA, 2 * D)
    arrived = jnp.stack([up_kv[2:], down_kv[2:]], axis=1).astype(F32)
    side_kv = jnp.swapaxes(side_kv + arrived, 0, 1).astype(BF16).reshape(4, AREA, 2 * D)
    lon_kv = lon_return(side_kv)
    input_grad = call(
        input_kernel,
        [shape(tokens_in.shape)],
        [],
        [own_kv, up_kv, down_kv, lon_kv, gq, tok, cotangent, qkv_weight, gain],
        [pltpu.VMEM((4 * AREA, 2 * D), BF16)],
        flops=2 * 256 * 512 * 1536,
        name="input",
    )[0]
    parts = plane_parts(jnp.concatenate([part_a, part_b], axis=1))
    rows = parts[0].shape[1]
    whole_rows = rows % 8 == 0
    qkv_grad, out_grad, gain_grad = call(
        functools.partial(finish_kernel, whole_rows),
        [shape((lon_count, lat_count, rows, 3 * D), F32), shape((lon_count, lat_count, rows, D), F32),
         shape((1, 128), F32)],
        [place],
        parts + [qkv_weight, gain],
        name="finish",
    )
    qkv_grad = qkv_grad.reshape(128, 3 * D)
    out_grad = out_grad.reshape(128, D)
    if whole_rows:
        gain_grad = gain_grad.reshape(128)
    else:
        at = lax.axis_index("lev") * 128
        rows_in = lax.dynamic_slice_in_dim(qkv_weight, at, 128, 0).astype(F32)
        gain_grad = jnp.sum(rows_in * qkv_grad, axis=1)
        gain_grad = gain_grad / lax.dynamic_slice_in_dim(norm_gain, at, 128, 0)
    return layer_out, input_grad, qkv_grad, out_grad, gain_grad


def solution(mesh):
    placed = (
        P("lev", "lat", "lon", None),
        P("lev", "lat", "lon", None),
        P(),
        P(),
        P(),
        P("lev", "lat", "lon"),
    )
    return jax.shard_map(
        on_device,
        mesh=mesh,
        in_specs=placed,
        out_specs=(
            P("lev", "lat", "lon", None),
            P("lev", "lat", "lon", None),
            P("lev", None),
            P("lev", None),
            P("lev"),
        ),
        check_vma=False,
    )
```

time: 136 us -> 91.4 us (0.67)
  waiting for transfers between devices: 38.1 us -> 19.9 us
  starting transfers between devices: 51.6 us -> 40 us
  local copies, waits for them, and re-layouts: 12.5 us -> 2.97 us
  Pallas kernels: 30.8 us -> 24.5 us
    ppermute x6 -> x3, starting transfers between devices: 24.5 us -> 11.8 us  [lat_halo(): up = lax.ppermute(bottom, 'lat', ring(count, 1, False))]
    ppermute x5 -> x7, waiting for transfers between devices: 19.8 us -> 7.08 us  [the longest x1 3.45 us: lon_return(): return lax.ppermute(side, 'lon', [(0, 1), (1, 0)])]
    unnamed x52 -> x28, local copies, waits for them, and re-layouts: 12.4 us -> 2.79 us
    ppermute x5 -> x7, starting transfers between devices: 2.49 us -> 11.3 us  [the longest x2 7.02 us: level_sum(): lax.ppermute(parts[1].astype(BF16), 'lev', [(i, i ^ 2) for i in range(4)])]
    ppermute x3, waiting for transfers between devices: 6.79 us -> 0.01 us  [plane_parts(): lax.ppermute(both, 'lat', ring(lat_count, k, True))]
    pallas_call x6 -> x5, Pallas kernels: 30.8 us -> 24.5 us  [call(): pl.pallas_call(kernel, grid=(1,), out_shape=outs, in_specs=[SMEM] * len(s...]
    ppermute x6 -> x3, starting transfers between devices: 7.74 us -> 3.86 us  [lat_halo(): down = lax.ppermute(top, 'lat', ring(count, -1, False))]
    ppermute x3 -> x1, starting transfers between devices: 5.04 us -> 2.94 us  [lon_halo(): return lax.ppermute(own, 'lon', [(0, 1), (1, 0)])]
  transfers between devices with their start and end apart: 27 -> 21, of which waited for: 12 -> 9; matrix products, arithmetic and copies ran while one was open for 1% -> 3% of each run, Pallas kernels for 21% -> 8%
where the time goes in v2:
time: 91.4 us; the launch traced here: 90.9 us
  starting transfers between devices  40 us (44%)
  Pallas kernels  24.5 us (27%)
  waiting for transfers between devices  19.9 us (22%)
  local copies, waits for them, and re-layouts  2.97 us (3%)
  other arithmetic  2.45 us (3%)
  between operations  0.98 us (1%)
    pallas_call x5, Pallas kernels, call(): pl.pallas_call(kernel, grid=(1,), out_shape=outs, in_specs=[SMEM] * len(s...  24.5 us
    ppermute x3, starting transfers between devices, lat_halo(): up = lax.ppermute(bottom, 'lat', ring(count, 1, False))  11.8 us
    ppermute x2, starting transfers between devices, level_sum(): lax.ppermute(parts[1].astype(BF16), 'lev', [(i, i ^ 2) for i in range(4)])  7.02 us
    ppermute x3, waiting for transfers between devices, lat_halo(): down = lax.ppermute(top, 'lat', ring(count, -1, False))  5.29 us
    ppermute x3, starting transfers between devices, plane_parts(): own = own + lax.ppermute(piece, 'lat', ring(lat_count, k, True)).astype(F32)  4.46 us
    ppermute x3, starting transfers between devices, plane_parts(): lax.ppermute(both, 'lat', ring(lat_count, k, True))  4.27 us
    ppermute x3, starting transfers between devices, lat_halo(): down = lax.ppermute(top, 'lat', ring(count, -1, False))  3.86 us
    ppermute x1, waiting for transfers between devices, lon_return(): return lax.ppermute(side, 'lon', [(0, 1), (1, 0)])  3.45 us
  transfers between devices with their start and end apart: 21, of which 9 were waited for; matrix products, arithmetic and copies ran while one was open for 3% of the time, Pallas kernels for 8%

profile of v2, /device:TPU:0, one launch (start us, length us, event | category | flops | bytes accessed | tf_op | source)
XLA Modules:
  0.0 90.9 jit_solution(18083455647523818201)
XLA Ops:
  0.6 2.0 %prep.1 = (bf16[4,64,512]{2,1,0:T(8,128)(2,1)}, bf16[2,64,512]{2,1,0:T(8,128)(2,1)}, bf16[2,64,512]{2,1,0:T(8,128)(2,1)}) custom-call(bf16[1,16,16,512]{3,2,1,0:T(8,128)(2,1)} %x_ref.3, s32[1,16,16]{2,1,0:T(8,128)} %mask_ref.5), custom_call_target="tpu_custom_call" | custom-call | bytes 787456 | tf_op jit(solution)/shard_map/prep/pallas_call | solution.py:287
  2.6 2.9 %collective-permute-start = (bf16[4,64,512]{2,1,0:T(8,128)(2,1)}, bf16[4,64,512]{2,1,0:T(8,128)(2,1)S(1)}, u32[]{:S(2)}, u32[]{:S(2)}) collective-permute-start(bf16[4,64,512]{2,1,0:T(8,128)(2,1)} %get-tuple-element.27.tok_ref), channel_id=1, source_target_pairs={{0,16},{16,0},{1,17},{17,1},{2,18},{18,2},{3,19},{19,3},{4,20},{20... | collective-permute-start | bytes 786440 | tf_op jit(solution)/shard_map/ppermute | solution.py:313
  5.5 3.5 %collective-permute-start.1 = (bf16[2,64,512]{2,1,0:T(8,128)(2,1)}, bf16[2,64,512]{2,1,0:T(8,128)(2,1)S(1)}, u32[]{:S(2)}, u32[]{:S(2)}) collective-permute-start(bf16[2,64,512]{2,1,0:T(8,128)(2,1)} %get-tuple-element.34), channel_id=1, source_target_pairs={{0,4},{4,8},{8,12},{1,5},{5,9},{9,13},{2,6},{6,10},{10,14},{3,7},{... | collective-permute-start | bytes 393224 | tf_op jit(solution)/shard_map/ppermute | solution.py:330
  9.0 1.3 %collective-permute-start.2 = (bf16[2,64,512]{2,1,0:T(8,128)(2,1)}, bf16[2,64,512]{2,1,0:T(8,128)(2,1)S(1)}, u32[]{:S(2)}, u32[]{:S(2)}) collective-permute-start(bf16[2,64,512]{2,1,0:T(8,128)(2,1)} %get-tuple-element.35), channel_id=1, source_target_pairs={{4,0},{8,4},{12,8},{5,1},{9,5},{13,9},{6,2},{10,6},{14,10},{7,3},{... | collective-permute-start | bytes 393224 | tf_op jit(solution)/shard_map/ppermute | solution.py:331
  10.3 1.7 %collective-permute-done.lon_ref = bf16[4,64,512]{2,1,0:T(8,128)(2,1)S(1)} collective-permute-done((bf16[4,64,512]{2,1,0:T(8,128)(2,1)}, bf16[4,64,512]{2,1,0:T(8,128)(2,1)S(1)}, u32[]{:S(2)}, u32[]{:S(2)}) %collective-permute-start) | collective-permute-done | bytes 262176 | tf_op jit(solution)/shard_map/ppermute | solution.py:313
  12.1 3.7 %collective-permute-start.3 = (bf16[2,64,512]{2,1,0:T(8,128)(2,1)S(1)}, bf16[2,64,512]{2,1,0:T(8,128)(2,1)S(1)}, u32[]{:S(2)}, u32[]{:S(2)}) collective-permute-start(bf16[2,64,512]{2,1,0:T(8,128)(2,1)S(1)} %get-tuple-element.53), channel_id=1, source_target_pairs={{0,4},{4,8},{8,12},{1,5},{5,9},{9,13},{2,6},{6,10},{10,14},{3,7},{... | collective-permute-start | bytes 393224 | tf_op jit(solution)/shard_map/ppermute | solution.py:330
  15.8 1.3 %collective-permute-start.4 = (bf16[2,64,512]{2,1,0:T(8,128)(2,1)S(1)}, bf16[2,64,512]{2,1,0:T(8,128)(2,1)S(1)}, u32[]{:S(2)}, u32[]{:S(2)}) collective-permute-start(bf16[2,64,512]{2,1,0:T(8,128)(2,1)S(1)} %get-tuple-element.52), channel_id=1, source_target_pairs={{4,0},{8,4},{12,8},{5,1},{9,5},{13,9},{6,2},{10,6},{14,10},{7,3},{... | collective-permute-start | bytes 393224 | tf_op jit(solution)/shard_map/ppermute | solution.py:331
  17.1 3.4 %own.1 = (bf16[4,64,512]{2,1,0:T(8,128)(2,1)}, bf16[4,64,1024]{2,1,0:T(8,128)(2,1)}, bf16[4,64,512]{2,1,0:T(8,128)(2,1)}, bf16[256,512]{1,0:T(8,128)(2,1)}, bf16[256,512]{1,0:T(8,128)(2,1)}, /*index=5*/s32[8]{0:T(128)}) custom-call(bf16[4,64,512]{2,1,0:T(8,128)(2,1)} %get-tuple-element.27.tok_ref, bf16[1,16,16,512]{3,2,1,0:T(8,128)(2,1)} %cot_ref.3, ...), custom_call_target="tpu_custom_call" | custom-call | flops 536870912 | bytes 4197408 | tf_op jit(solution)/shard_map/own/pallas_call | solution.py:287
  20.5 0.0 copy-done.6
  20.6 0.6 pad_add_fusion.place_ref
  21.2 0.0 collective-permute-done.1.up_ref
  21.2 0.0 collective-permute-done.2.down_ref
  21.2 0.0 copy-start.11
  21.2 0.0 collective-permute-done.3.upc_ref
  21.2 1.5 %collective-permute-done.4.downc_ref = bf16[2,64,512]{2,1,0:T(8,128)(2,1)S(1)} collective-permute-done((bf16[2,64,512]{2,1,0:T(8,128)(2,1)S(1)}, bf16[2,64,512]{2,1,0:T(8,128)(2,1)S(1)}, u32[]{:S(2)}, u32[]{:S(2)}) %collective-permute-start.4) | collective-permute-done | bytes 131104 | tf_op jit(solution)/shard_map/ppermute | solution.py:331
  22.7 0.6 copy-done.13
  23.3 12.2 %main.1 = (bf16[1,16,16,512]{3,2,1,0:T(8,128)(2,1)}, bf16[4,64,512]{2,1,0:T(8,128)(2,1)}, f32[4,64,1024]{2,1,0:T(8,128)}, f32[4,64,1024]{2,1,0:T(8,128)}, bf16[4...) custom-call(s32[8]{0:T(128)} %get-tuple-element.28.info_ref, ...), custom_call_target="tpu_custom_call" | custom-call | flops 5368709120 | bytes 10750976 | tf_op jit(solution)/shard_map/main/pallas_call | solution.py:287
  35.6 0.0 copy-start.4
  35.6 0.1 collective-permute-start.11
  35.7 0.5 collective-permute-start.8
  36.2 1.3 %collective-permute-start.6 = (bf16[4,64,1024]{2,1,0:T(8,128)(2,1)}, bf16[4,64,1024]{2,1,0:T(8,128)(2,1)S(1)}, u32[]{:S(2)}, u32[]{:S(2)}) collective-permute-start(bf16[4,64,1024]{2,1,0:T(8,128)(2,1)} %get-tuple-element.39), channel_id=1, source_target_pairs={{4,0},{8,4},{12,8},{5,1},{9,5},{13,9},{6,2},{10,6},{14,10},{7,3},{... | collective-permute-start | bytes 1572872 | tf_op jit(solution)/shard_map/ppermute | solution.py:331
  37.5 4.6 %collective-permute-start.5 = (bf16[4,64,1024]{2,1,0:T(8,128)(2,1)}, bf16[4,64,1024]{2,1,0:T(8,128)(2,1)S(1)}, u32[]{:S(2)}, u32[]{:S(2)}) collective-permute-start(bf16[4,64,1024]{2,1,0:T(8,128)(2,1)} %get-tuple-element.38), channel_id=1, source_target_pairs={{0,4},{4,8},{8,12},{1,5},{5,9},{9,13},{2,6},{6,10},{10,14},{3,7},{... | collective-permute-start | bytes 1572872 | tf_op jit(solution)/shard_map/ppermute | solution.py:330
  42.1 0.0 collective-permute-done.11
  42.1 1.2 %convert_add_fusion = f32[2,128,1024]{2,1,0:T(8,128)S(1)} fusion(bf16[2,128,1024]{2,1,0:T(8,128)(2,1)S(1)} %collective-permute-done.11, bf16[2,128,1024]{2,1,0:T(8,128)(2,1)} %get-tuple-element.44), kind=kLoop, calls=%fused_computation.2 | loop fusion | flops 786432 | bytes 2097152 | tf_op jit(solution)/shard_map/add | solution.py:337
  43.3 1.6 %collective-permute-start.12 = (bf16[2,64,1024]{2,1,0:T(8,128)(2,1)S(1)}, bf16[2,64,1024]{2,1,0:T(8,128)(2,1)S(1)}, u32[]{:S(2)}, u32[]{:S(2)}) collective-permute-start(bf16[2,64,1024]{2,1,0:T(8,128)(2,1)S(1)} %fusion.2), channel_id=1, source_target_pairs={{0,16},{16,0},{1,17},{17,1},{2,18},{18,2},{3,19},{19,3},{4,20},{20... | collective-permute-start | bytes 786440 | tf_op jit(solution)/shard_map/ppermute | solution.py:350
  44.9 0.0 collective-permute-done.8
  44.9 0.2 convert_add_fusion.1
  45.1 3.3 %collective-permute-start.9 = (bf16[128,1024]{1,0:T(8,128)(2,1)S(1)}, bf16[128,1024]{1,0:T(8,128)(2,1)S(1)}, u32[]{:S(2)}, u32[]{:S(2)}) collective-permute-start(bf16[128,1024]{1,0:T(8,128)(2,1)S(1)} %fusion.3), channel_id=1, source_target_pairs={{0,2},{1,3},{2,0},{3,1},{4,6},{5,7},{6,4},{7,5},{8,10},{9,11},{10,... | collective-permute-start | bytes 786440 | tf_op jit(solution)/shard_map/ppermute | solution.py:341
  48.4 3.8 %collective-permute-done.6.down_ref = bf16[4,64,1024]{2,1,0:T(8,128)(2,1)S(1)} collective-permute-done((bf16[4,64,1024]{2,1,0:T(8,128)(2,1)}, bf16[4,64,1024]{2,1,0:T(8,128)(2,1)S(1)}, u32[]{:S(2)}, u32[]{:S(2)}) %collective-permute-start.6) | collective-permute-done | bytes 524320 | tf_op jit(solution)/shard_map/ppermute | solution.py:331
  52.3 0.0 collective-permute-done.12
  52.3 0.1 bitcast_add_fusion
  52.4 3.7 %collective-permute-start.13 = (bf16[64,1024]{1,0:T(8,128)(2,1)S(1)}, bf16[64,1024]{1,0:T(8,128)(2,1)S(1)}, u32[]{:S(2)}, u32[]{:S(2)}) collective-permute-start(bf16[64,1024]{1,0:T(8,128)(2,1)S(1)} %fusion.6), channel_id=1, source_target_pairs={{0,2},{1,3},{2,0},{3,1},{4,6},{5,7},{6,4},{7,5},{8,10},{9,11},{10,... | collective-permute-start | bytes 393224 | tf_op jit(solution)/shard_map/ppermute | solution.py:341
  56.1 0.0 collective-permute-done.9
  56.1 0.1 fusion.1
  56.2 1.4 %collective-permute-start.10 = (bf16[64,1024]{1,0:T(8,128)(2,1)S(1)}, bf16[64,1024]{1,0:T(8,128)(2,1)S(1)}, u32[]{:S(2)}, u32[]{:S(2)}) collective-permute-start(bf16[64,1024]{1,0:T(8,128)(2,1)S(1)} %fusion.5), channel_id=1, source_target_pairs={{0,16},{16,0},{1,17},{17,1},{2,18},{18,2},{3,19},{19,3},{4,20},{20... | collective-permute-start | bytes 393224 | tf_op jit(solution)/shard_map/ppermute | solution.py:350
  57.6 1.4 %collective-permute-done.13 = bf16[64,1024]{1,0:T(8,128)(2,1)S(1)} collective-permute-done((bf16[64,1024]{1,0:T(8,128)(2,1)S(1)}, bf16[64,1024]{1,0:T(8,128)(2,1)S(1)}, u32[]{:S(2)}, u32[]{:S(2)}) %collective-permute-start.13) | collective-permute-done | bytes 131104 | tf_op jit(solution)/shard_map/ppermute | solution.py:341
  59.0 2.2 %collective-permute-done.10 = bf16[64,1024]{1,0:T(8,128)(2,1)S(1)} collective-permute-done((bf16[64,1024]{1,0:T(8,128)(2,1)S(1)}, bf16[64,1024]{1,0:T(8,128)(2,1)S(1)}, u32[]{:S(2)}, u32[]{:S(2)}) %collective-permute-start.10) | collective-permute-done | bytes 131104 | tf_op jit(solution)/shard_map/ppermute | solution.py:350
  61.4 1.6 %collective-permute-start.14 = (bf16[16,2048]{1,0:T(8,128)(2,1)S(1)}, bf16[16,2048]{1,0:T(8,128)(2,1)S(1)}, u32[]{:S(2)}, u32[]{:S(2)}) collective-permute-start(bf16[16,2048]{1,0:T(8,128)(2,1)S(1)} %get-tuple-element.49), channel_id=1, source_target_pairs={{0,4},{4,8},{8,12},{12,0},{1,5},{5,9},{9,13},{13,1},{2,6},{6,10},{... | collective-permute-start | bytes 196616 | tf_op jit(solution)/shard_map/ppermute | solution.py:362
  63.0 0.0 collective-permute-start.15
  63.0 2.8 %collective-permute-start.16 = (bf16[16,2048]{1,0:T(8,128)(2,1)S(1)}, bf16[16,2048]{1,0:T(8,128)(2,1)S(1)}, u32[]{:S(2)}, u32[]{:S(2)}) collective-permute-start(bf16[16,2048]{1,0:T(8,128)(2,1)S(1)} %get-tuple-element.50), channel_id=1, source_target_pairs={{0,12},{4,0},{8,4},{12,8},{1,13},{5,1},{9,5},{13,9},{2,14},{6,2},{... | collective-permute-start | bytes 196616 | tf_op jit(solution)/shard_map/ppermute | solution.py:362
  65.8 0.0 collective-permute-done.5.up_ref
  65.9 1.6 %collective-permute-done.14 = bf16[16,2048]{1,0:T(8,128)(2,1)S(1)} collective-permute-done((bf16[16,2048]{1,0:T(8,128)(2,1)S(1)}, bf16[16,2048]{1,0:T(8,128)(2,1)S(1)}, u32[]{:S(2)}, u32[]{:S(2)}) %collective-permute-start.14) | collective-permute-done | bytes 65568 | tf_op jit(solution)/shard_map/ppermute | solution.py:362
  67.5 1.4 %collective-permute-done.15 = bf16[16,2048]{1,0:T(8,128)(2,1)S(1)} collective-permute-done((bf16[16,2048]{1,0:T(8,128)(2,1)S(1)}, bf16[16,2048]{1,0:T(8,128)(2,1)S(1)}, u32[]{:S(2)}, u32[]{:S(2)}) %collective-permute-start.15) | collective-permute-done | bytes 65568 | tf_op jit(solution)/shard_map/ppermute | solution.py:362
  68.9 0.0 collective-permute-done.16
  68.9 1.4 %collective-permute-start.17 = (bf16[16,2048]{1,0:T(8,128)(2,1)S(1)}, bf16[16,2048]{1,0:T(8,128)(2,1)S(1)}, u32[]{:S(2)}, u32[]{:S(2)}) collective-permute-start(bf16[16,2048]{1,0:T(8,128)(2,1)S(1)} %fusion.9), channel_id=1, source_target_pairs={{0,16},{16,0},{1,17},{17,1},{2,18},{18,2},{3,19},{19,3},{4,20},{20... | collective-permute-start | bytes 196616 | tf_op jit(solution)/shard_map/ppermute | solution.py:365
  70.3 0.0 copy-done.2
  70.4 0.1 fusion
  70.5 0.8 collective-permute-start.7
  71.3 2.8 %collective-permute-done.17 = bf16[16,2048]{1,0:T(8,128)(2,1)S(1)} collective-permute-done((bf16[16,2048]{1,0:T(8,128)(2,1)S(1)}, bf16[16,2048]{1,0:T(8,128)(2,1)S(1)}, u32[]{:S(2)}, u32[]{:S(2)}) %collective-permute-start.17) | collective-permute-done | bytes 65568 | tf_op jit(solution)/shard_map/ppermute | solution.py:365
  74.1 0.0 copy-done.1
  74.1 1.3 %collective-permute-start.18 = (bf16[2,16,2048]{2,1,0:T(8,128)(2,1)S(1)}, bf16[2,16,2048]{2,1,0:T(8,128)(2,1)S(1)}, u32[]{:S(2)}, u32[]{:S(2)}) collective-permute-start(bf16[2,16,2048]{2,1,0:T(8,128)(2,1)S(1)} %pad_maximum_fusion.1.own_ref), channel_id=1, source_target_pairs={{0,4},{4,8},{8,12},{12,0},{1,5},{5,9},{9,13},{13,1},{2,6},{6,10},{... | collective-permute-start | bytes 393224 | tf_op jit(solution)/shard_map/ppermute | solution.py:373
  75.4 2.3 %collective-permute-start.19 = (bf16[2,16,2048]{2,1,0:T(8,128)(2,1)S(1)}, bf16[2,16,2048]{2,1,0:T(8,128)(2,1)S(1)}, u32[]{:S(2)}, u32[]{:S(2)}) collective-permute-start(bf16[2,16,2048]{2,1,0:T(8,128)(2,1)S(1)} %pad_maximum_fusion.1.own_ref), channel_id=1, source_target_pairs={{0,8},{4,12},{8,0},{12,4},{1,9},{5,13},{9,1},{13,5},{2,10},{6,14},... | collective-permute-start | bytes 393224 | tf_op jit(solution)/shard_map/ppermute | solution.py:373
  77.7 0.7 collective-permute-start.20
  78.4 3.5 %collective-permute-done.7.lon_ref = bf16[4,64,1024]{2,1,0:T(8,128)(2,1)S(1)} collective-permute-done((bf16[4,64,1024]{2,1,0:T(8,128)(2,1)S(1)}, bf16[4,64,1024]{2,1,0:T(8,128)(2,1)S(1)}, u32[]{:S(2)}, u32[]{:S(2)}) %collective-permute-start.7) | collective-permute-done | bytes 524320 | tf_op jit(solution)/shard_map/ppermute | solution.py:322
  81.8 0.8 copy-done.3
  82.6 3.8 %input.1 = bf16[1,16,16,512]{3,2,1,0:T(8,128)(2,1)} custom-call(f32[4,64,1024]{2,1,0:T(8,128)} %get-tuple-element.37.own_ref, bf16[4,64,1024]{2,1,0:T(8,128)(2,1)} %copy-done.1, bf16[4,64,1024]{2,1,0:T(8,128)(2,1)} %copy-done, bf16[4,64,1024]{2,1,0:T(8,128)(2,1)} %copy-done.3, bf16[4,64,512]{2,1,0:T(8,128)(2,1)} %get-tuple-element.41.gq_ref, ...), custom_call_target="tpu_custom_call" | custom-call | flops 402653184 | bytes 5244928 | tf_op jit(solution)/shard_map/input/pallas_call | solution.py:287
  86.4 0.0 collective-permute-done.18.refs_0_
  86.5 0.0 collective-permute-done.19.refs_1_
  86.5 0.0 copy-start.8
  86.5 0.0 collective-permute-done.20.refs_2_
  86.5 0.6 copy-done.7
  87.1 0.1 copy-done.8
  87.2 0.6 copy-done.9
  87.8 3.0 %finish.1 = (f32[2,4,16,1536]{3,2,1,0:T(8,128)}, f32[2,4,16,512]{3,2,1,0:T(8,128)}, f32[1,128]{1,0:T(1,128)}) custom-call(s32[3]{0:T(128)} %pad_add_fusion.place_ref, bf16[2,16,2048]{2,1,0:T(8,128)(2,1)} %copy-done.5, bf16[2,16,2048]{2,1,0:T(8,128)(2,1)} %copy-done.7, bf16[2,16,2048]{2,1,0:T(8,128)(2,1)} %copy-done.8, bf16[2,16,2048]{2,1,0:T(8,128)(2,1)} %copy-done.9, ...), custom_call_target="tpu_custom_call" | custom-call | bytes 3148288 | tf_op jit(solution)/shard_map/finish/pallas_call | solution.py:287
  (32 shorter events, 0.4 us)
Async XLA Ops:
  2.6 9.5 %collective-permute-start = (bf16[4,64,512]{2,1,0:T(8,128)(2,1)}, bf16[4,64,512]{2,1,0:T(8,128)(2,1)S(1)}, u32[]{:S(2)}, u32[]{:S(2)}) collective-permute-start(bf16[4,64,512]{2,1,0:T(8,128)(2,1)} %get-tuple-element.27.tok_ref), channel_id=1, source_target_pairs={{0,16},{16,0},{1,17},{17,1},{2,18},{18,2},{3,19},{19,3},{4,20},{20... | collective-permute-start | bytes 786440 | tf_op jit(solution)/shard_map/ppermute | solution.py:313
  5.5 15.6 %collective-permute-start.1 = (bf16[2,64,512]{2,1,0:T(8,128)(2,1)}, bf16[2,64,512]{2,1,0:T(8,128)(2,1)S(1)}, u32[]{:S(2)}, u32[]{:S(2)}) collective-permute-start(bf16[2,64,512]{2,1,0:T(8,128)(2,1)} %get-tuple-element.34), channel_id=1, source_target_pairs={{0,4},{4,8},{8,12},{1,5},{5,9},{9,13},{2,6},{6,10},{10,14},{3,7},{... | collective-permute-start | bytes 393224 | tf_op jit(solution)/shard_map/ppermute | solution.py:330
  9.0 12.2 %collective-permute-start.2 = (bf16[2,64,512]{2,1,0:T(8,128)(2,1)}, bf16[2,64,512]{2,1,0:T(8,128)(2,1)S(1)}, u32[]{:S(2)}, u32[]{:S(2)}) collective-permute-start(bf16[2,64,512]{2,1,0:T(8,128)(2,1)} %get-tuple-element.35), channel_id=1, source_target_pairs={{4,0},{8,4},{12,8},{5,1},{9,5},{13,9},{6,2},{10,6},{14,10},{7,3},{... | collective-permute-start | bytes 393224 | tf_op jit(solution)/shard_map/ppermute | solution.py:331
  12.1 8.5 %copy-start.6 = (bf16[4,64,512]{2,1,0:T(8,128)(2,1)}, bf16[4,64,512]{2,1,0:T(8,128)(2,1)S(1)}, u32[]{:S(2)}) copy-start(bf16[4,64,512]{2,1,0:T(8,128)(2,1)S(1)} %collective-permute-done.lon_ref) | copy-start | bytes 786436
  12.1 9.1 %collective-permute-start.3 = (bf16[2,64,512]{2,1,0:T(8,128)(2,1)S(1)}, bf16[2,64,512]{2,1,0:T(8,128)(2,1)S(1)}, u32[]{:S(2)}, u32[]{:S(2)}) collective-permute-start(bf16[2,64,512]{2,1,0:T(8,128)(2,1)S(1)} %get-tuple-element.53), channel_id=1, source_target_pairs={{0,4},{4,8},{8,12},{1,5},{5,9},{9,13},{2,6},{6,10},{10,14},{3,7},{... | collective-permute-start | bytes 393224 | tf_op jit(solution)/shard_map/ppermute | solution.py:330
  15.8 6.9 %collective-permute-start.4 = (bf16[2,64,512]{2,1,0:T(8,128)(2,1)S(1)}, bf16[2,64,512]{2,1,0:T(8,128)(2,1)S(1)}, u32[]{:S(2)}, u32[]{:S(2)}) collective-permute-start(bf16[2,64,512]{2,1,0:T(8,128)(2,1)S(1)} %get-tuple-element.52), channel_id=1, source_target_pairs={{4,0},{8,4},{12,8},{5,1},{9,5},{13,9},{6,2},{10,6},{14,10},{7,3},{... | collective-permute-start | bytes 393224 | tf_op jit(solution)/shard_map/ppermute | solution.py:331
  21.2 1.5 %copy-start.10 = (bf16[2,64,512]{2,1,0:T(8,128)(2,1)}, bf16[2,64,512]{2,1,0:T(8,128)(2,1)S(1)}, u32[]{:S(2)}) copy-start(bf16[2,64,512]{2,1,0:T(8,128)(2,1)S(1)} %collective-permute-done.1.up_ref) | copy-start | bytes 393220
  21.2 1.5 %copy-start.11 = (bf16[2,64,512]{2,1,0:T(8,128)(2,1)}, bf16[2,64,512]{2,1,0:T(8,128)(2,1)S(1)}, u32[]{:S(2)}) copy-start(bf16[2,64,512]{2,1,0:T(8,128)(2,1)S(1)} %collective-permute-done.2.down_ref) | copy-start | bytes 393220
  21.2 1.5 %copy-start.12 = (bf16[2,64,512]{2,1,0:T(8,128)(2,1)}, bf16[2,64,512]{2,1,0:T(8,128)(2,1)S(1)}, u32[]{:S(2)}) copy-start(bf16[2,64,512]{2,1,0:T(8,128)(2,1)S(1)} %collective-permute-done.3.upc_ref) | copy-start | bytes 393220
  22.7 0.7 copy-start.13
  35.6 9.3 %copy-start.4 = (bf16[2,128,1024]{2,1,0:T(8,128)(2,1)S(1)}, bf16[2,128,1024]{2,1,0:T(8,128)(2,1)}, u32[]{:S(2)}) copy-start(bf16[2,128,1024]{2,1,0:T(8,128)(2,1)} %get-tuple-element.42) | copy-start | bytes 1572868
  35.6 6.5 %collective-permute-start.11 = (bf16[2,128,1024]{2,1,0:T(8,128)(2,1)}, bf16[2,128,1024]{2,1,0:T(8,128)(2,1)S(1)}, u32[]{:S(2)}, u32[]{:S(2)}) collective-permute-start(bf16[2,128,1024]{2,1,0:T(8,128)(2,1)} %get-tuple-element.45), channel_id=1, source_target_pairs={{0,1},{1,0},{2,3},{3,2},{4,5},{5,4},{6,7},{7,6},{8,9},{9,8},{10,11... | collective-permute-start | bytes 1572872 | tf_op jit(solution)/shard_map/ppermute | solution.py:336
  35.7 9.2 %collective-permute-start.8 = (bf16[2,128,1024]{2,1,0:T(8,128)(2,1)}, bf16[2,128,1024]{2,1,0:T(8,128)(2,1)S(1)}, u32[]{:S(2)}, u32[]{:S(2)}) collective-permute-start(bf16[2,128,1024]{2,1,0:T(8,128)(2,1)} %get-tuple-element.43), channel_id=1, source_target_pairs={{0,1},{1,0},{2,3},{3,2},{4,5},{5,4},{6,7},{7,6},{8,9},{9,8},{10,11... | collective-permute-start | bytes 1572872 | tf_op jit(solution)/shard_map/ppermute | solution.py:336
  36.2 16.1 %collective-permute-start.6 = (bf16[4,64,1024]{2,1,0:T(8,128)(2,1)}, bf16[4,64,1024]{2,1,0:T(8,128)(2,1)S(1)}, u32[]{:S(2)}, u32[]{:S(2)}) collective-permute-start(bf16[4,64,1024]{2,1,0:T(8,128)(2,1)} %get-tuple-element.39), channel_id=1, source_target_pairs={{4,0},{8,4},{12,8},{5,1},{9,5},{13,9},{6,2},{10,6},{14,10},{7,3},{... | collective-permute-start | bytes 1572872 | tf_op jit(solution)/shard_map/ppermute | solution.py:331
  37.5 28.4 %collective-permute-start.5 = (bf16[4,64,1024]{2,1,0:T(8,128)(2,1)}, bf16[4,64,1024]{2,1,0:T(8,128)(2,1)S(1)}, u32[]{:S(2)}, u32[]{:S(2)}) collective-permute-start(bf16[4,64,1024]{2,1,0:T(8,128)(2,1)} %get-tuple-element.38), channel_id=1, source_target_pairs={{0,4},{4,8},{8,12},{1,5},{5,9},{9,13},{2,6},{6,10},{10,14},{3,7},{... | collective-permute-start | bytes 1572872 | tf_op jit(solution)/shard_map/ppermute | solution.py:330
  43.3 8.9 %collective-permute-start.12 = (bf16[2,64,1024]{2,1,0:T(8,128)(2,1)S(1)}, bf16[2,64,1024]{2,1,0:T(8,128)(2,1)S(1)}, u32[]{:S(2)}, u32[]{:S(2)}) collective-permute-start(bf16[2,64,1024]{2,1,0:T(8,128)(2,1)S(1)} %fusion.2), channel_id=1, source_target_pairs={{0,16},{16,0},{1,17},{17,1},{2,18},{18,2},{3,19},{19,3},{4,20},{20... | collective-permute-start | bytes 786440 | tf_op jit(solution)/shard_map/ppermute | solution.py:350
  45.1 11.0 %collective-permute-start.9 = (bf16[128,1024]{1,0:T(8,128)(2,1)S(1)}, bf16[128,1024]{1,0:T(8,128)(2,1)S(1)}, u32[]{:S(2)}, u32[]{:S(2)}) collective-permute-start(bf16[128,1024]{1,0:T(8,128)(2,1)S(1)} %fusion.3), channel_id=1, source_target_pairs={{0,2},{1,3},{2,0},{3,1},{4,6},{5,7},{6,4},{7,5},{8,10},{9,11},{10,... | collective-permute-start | bytes 786440 | tf_op jit(solution)/shard_map/ppermute | solution.py:341
  52.2 3.9 %copy-start = (bf16[4,64,1024]{2,1,0:T(8,128)(2,1)}, bf16[4,64,1024]{2,1,0:T(8,128)(2,1)S(1)}, u32[]{:S(2)}) copy-start(bf16[4,64,1024]{2,1,0:T(8,128)(2,1)S(1)} %collective-permute-done.6.down_ref) | copy-start | bytes 1572868
  52.4 6.6 %collective-permute-start.13 = (bf16[64,1024]{1,0:T(8,128)(2,1)S(1)}, bf16[64,1024]{1,0:T(8,128)(2,1)S(1)}, u32[]{:S(2)}, u32[]{:S(2)}) collective-permute-start(bf16[64,1024]{1,0:T(8,128)(2,1)S(1)} %fusion.6), channel_id=1, source_target_pairs={{0,2},{1,3},{2,0},{3,1},{4,6},{5,7},{6,4},{7,5},{8,10},{9,11},{10,... | collective-permute-start | bytes 393224 | tf_op jit(solution)/shard_map/ppermute | solution.py:341
  56.2 5.0 %collective-permute-start.10 = (bf16[64,1024]{1,0:T(8,128)(2,1)S(1)}, bf16[64,1024]{1,0:T(8,128)(2,1)S(1)}, u32[]{:S(2)}, u32[]{:S(2)}) collective-permute-start(bf16[64,1024]{1,0:T(8,128)(2,1)S(1)} %fusion.5), channel_id=1, source_target_pairs={{0,16},{16,0},{1,17},{17,1},{2,18},{18,2},{3,19},{19,3},{4,20},{20... | collective-permute-start | bytes 393224 | tf_op jit(solution)/shard_map/ppermute | solution.py:350
  61.3 9.1 %copy-start.2 = (f32[4,64,1024]{2,1,0:T(8,128)S(1)}, f32[4,64,1024]{2,1,0:T(8,128)}, u32[]{:S(2)}) copy-start(f32[4,64,1024]{2,1,0:T(8,128)} %get-tuple-element.40) | copy-start | bytes 3145732
  61.4 6.1 %collective-permute-start.14 = (bf16[16,2048]{1,0:T(8,128)(2,1)S(1)}, bf16[16,2048]{1,0:T(8,128)(2,1)S(1)}, u32[]{:S(2)}, u32[]{:S(2)}) collective-permute-start(bf16[16,2048]{1,0:T(8,128)(2,1)S(1)} %get-tuple-element.49), channel_id=1, source_target_pairs={{0,4},{4,8},{8,12},{12,0},{1,5},{5,9},{9,13},{13,1},{2,6},{6,10},{... | collective-permute-start | bytes 196616 | tf_op jit(solution)/shard_map/ppermute | solution.py:362
  63.0 5.9 %collective-permute-start.15 = (bf16[16,2048]{1,0:T(8,128)(2,1)S(1)}, bf16[16,2048]{1,0:T(8,128)(2,1)S(1)}, u32[]{:S(2)}, u32[]{:S(2)}) collective-permute-start(bf16[16,2048]{1,0:T(8,128)(2,1)S(1)} %get-tuple-element.51), channel_id=1, source_target_pairs={{0,8},{4,12},{8,0},{12,4},{1,9},{5,13},{9,1},{13,5},{2,10},{6,14},... | collective-permute-start | bytes 196616 | tf_op jit(solution)/shard_map/ppermute | solution.py:362
  63.0 5.9 %collective-permute-start.16 = (bf16[16,2048]{1,0:T(8,128)(2,1)S(1)}, bf16[16,2048]{1,0:T(8,128)(2,1)S(1)}, u32[]{:S(2)}, u32[]{:S(2)}) collective-permute-start(bf16[16,2048]{1,0:T(8,128)(2,1)S(1)} %get-tuple-element.50), channel_id=1, source_target_pairs={{0,12},{4,0},{8,4},{12,8},{1,13},{5,1},{9,5},{13,9},{2,14},{6,2},{... | collective-permute-start | bytes 196616 | tf_op jit(solution)/shard_map/ppermute | solution.py:362
  65.8 8.2 %copy-start.1 = (bf16[4,64,1024]{2,1,0:T(8,128)(2,1)}, bf16[4,64,1024]{2,1,0:T(8,128)(2,1)S(1)}, u32[]{:S(2)}) copy-start(bf16[4,64,1024]{2,1,0:T(8,128)(2,1)S(1)} %collective-permute-done.5.up_ref) | copy-start | bytes 1572868
  68.9 5.1 %collective-permute-start.17 = (bf16[16,2048]{1,0:T(8,128)(2,1)S(1)}, bf16[16,2048]{1,0:T(8,128)(2,1)S(1)}, u32[]{:S(2)}, u32[]{:S(2)}) collective-permute-start(bf16[16,2048]{1,0:T(8,128)(2,1)S(1)} %fusion.9), channel_id=1, source_target_pairs={{0,16},{16,0},{1,17},{17,1},{2,18},{18,2},{3,19},{19,3},{4,20},{20... | collective-permute-start | bytes 196616 | tf_op jit(solution)/shard_map/ppermute | solution.py:365
  70.5 11.3 %collective-permute-start.7 = (bf16[4,64,1024]{2,1,0:T(8,128)(2,1)S(1)}, bf16[4,64,1024]{2,1,0:T(8,128)(2,1)S(1)}, u32[]{:S(2)}, u32[]{:S(2)}) collective-permute-start(bf16[4,64,1024]{2,1,0:T(8,128)(2,1)S(1)} %bitcast.62), channel_id=1, source_target_pairs={{0,16},{16,0},{1,17},{17,1},{2,18},{18,2},{3,19},{19,3},{4,20},{20... | collective-permute-start | bytes 1572872 | tf_op jit(solution)/shard_map/ppermute | solution.py:322
  74.1 12.4 %copy-start.5 = (bf16[2,16,2048]{2,1,0:T(8,128)(2,1)}, bf16[2,16,2048]{2,1,0:T(8,128)(2,1)S(1)}, u32[]{:S(2)}) copy-start(bf16[2,16,2048]{2,1,0:T(8,128)(2,1)S(1)} %pad_maximum_fusion.1.own_ref) | copy-start | bytes 393220
  74.1 12.3 %collective-permute-start.18 = (bf16[2,16,2048]{2,1,0:T(8,128)(2,1)S(1)}, bf16[2,16,2048]{2,1,0:T(8,128)(2,1)S(1)}, u32[]{:S(2)}, u32[]{:S(2)}) collective-permute-start(bf16[2,16,2048]{2,1,0:T(8,128)(2,1)S(1)} %pad_maximum_fusion.1.own_ref), channel_id=1, source_target_pairs={{0,4},{4,8},{8,12},{12,0},{1,5},{5,9},{9,13},{13,1},{2,6},{6,10},{... | collective-permute-start | bytes 393224 | tf_op jit(solution)/shard_map/ppermute | solution.py:373
  75.4 11.0 %collective-permute-start.19 = (bf16[2,16,2048]{2,1,0:T(8,128)(2,1)S(1)}, bf16[2,16,2048]{2,1,0:T(8,128)(2,1)S(1)}, u32[]{:S(2)}, u32[]{:S(2)}) collective-permute-start(bf16[2,16,2048]{2,1,0:T(8,128)(2,1)S(1)} %pad_maximum_fusion.1.own_ref), channel_id=1, source_target_pairs={{0,8},{4,12},{8,0},{12,4},{1,9},{5,13},{9,1},{13,5},{2,10},{6,14},... | collective-permute-start | bytes 393224 | tf_op jit(solution)/shard_map/ppermute | solution.py:373
  77.7 8.8 %collective-permute-start.20 = (bf16[2,16,2048]{2,1,0:T(8,128)(2,1)S(1)}, bf16[2,16,2048]{2,1,0:T(8,128)(2,1)S(1)}, u32[]{:S(2)}, u32[]{:S(2)}) collective-permute-start(bf16[2,16,2048]{2,1,0:T(8,128)(2,1)S(1)} %pad_maximum_fusion.1.own_ref), channel_id=1, source_target_pairs={{0,12},{4,0},{8,4},{12,8},{1,13},{5,1},{9,5},{13,9},{2,14},{6,2},{... | collective-permute-start | bytes 393224 | tf_op jit(solution)/shard_map/ppermute | solution.py:373
  81.8 0.8 copy-start.3
  86.5 0.6 copy-start.7
  86.5 0.7 copy-start.8
  87.2 0.7 copy-start.9

commit v3 on v2

v3 whole, which is shorter than its diff:
```python
import jax
import jax.numpy as jnp
from jax import lax
from jax.experimental import pallas as pl
from jax.experimental.pallas import tpu as pltpu
from jax.sharding import PartitionSpec as P

HEADS = 8
WIN = 8
AREA = WIN * WIN
D = 512
HEAD_DIM = D // HEADS
GROUP = 256
GROUP_HEADS = GROUP // HEAD_DIM
GROUPS = D // GROUP
KEYS = 8 * AREA
LAND = 1000.0
NEVER = -1e9
FAR = 1e30
F32 = jnp.float32
BF16 = jnp.bfloat16
EXACT = lax.Precision.HIGHEST


def dot(a, b, ca, cb, precision=None):
    return lax.dot_general(
        a, b, (((ca,), (cb,)), ((), ())), preferred_element_type=F32, precision=precision
    )


def iota(shape, dim):
    return lax.broadcasted_iota(jnp.int32, shape, dim)


def window_of(grid, w):
    r, c = divmod(w, 2)
    part = grid[r * WIN : (r + 1) * WIN, c * WIN : (c + 1) * WIN, :]
    return part.reshape(AREA, grid.shape[-1])


def grid_of(windows):
    rows = []
    for r in range(2):
        parts = [windows[2 * r + c].reshape(WIN, WIN, -1) for c in range(2)]
        rows.append(jnp.concatenate(parts, axis=1))
    return jnp.concatenate(rows, axis=0)


def token_mask(mask):
    t = iota((4 * AREA, 2 * WIN), 0)
    lane = iota((4 * AREA, 2 * WIN), 1)
    w, i, j = t // AREA, (t % AREA) // WIN, t % WIN
    pick_row = (lane == WIN * (w // 2) + i).astype(F32)
    pick_col = (lane == WIN * (w % 2) + j).astype(F32)
    rows = dot(pick_row, mask, 1, 0)
    return jnp.sum(rows * pick_col, axis=1, keepdims=True)


def norm_rows(x):
    center = x - jnp.mean(x, axis=-1, keepdims=True)
    spread = jnp.mean(center * center, axis=-1, keepdims=True)
    scaling = lax.rsqrt(spread + 1e-05)
    return center * scaling, scaling


def head_blocks():
    row = iota((GROUP, GROUP), 0) // HEAD_DIM
    col = iota((GROUP, GROUP), 1) // HEAD_DIM
    return (row == col).astype(F32)


def stack_heads(part, blocks):
    return jnp.concatenate([part] * GROUP_HEADS, axis=0) * blocks.astype(part.dtype)


def unstack_heads(full, blocks):
    kept = full * blocks
    return sum(kept[h * AREA : (h + 1) * AREA] for h in range(GROUP_HEADS))


def lanes(g):
    return slice(g * GROUP, (g + 1) * GROUP)


def lat_side(row):
    return (row + lax.axis_index("lat") + 1) % 2


def load(pairs, sems):
    copies = [pltpu.make_async_copy(a, b, sems.at[k]) for k, (a, b) in enumerate(pairs)]
    for copy in copies:
        copy.start()
    return copies


def wait(copies):
    for copy in copies:
        copy.wait()


def prep_kernel(
    x_hbm, cot_hbm, mask_hbm, all_ref, first_ref, second_ref, gb_ref, x_ref, cot_ref, mask_ref, sems
):
    copies = load(((mask_hbm, mask_ref), (x_hbm, x_ref), (cot_hbm, cot_ref)), sems)
    copies[0].wait()
    ocean = token_mask(mask_ref[0].astype(F32))
    copies[1].wait()
    x = x_ref[0].astype(F32)
    parts = []
    for w in range(4):
        part = jnp.where(ocean[w * AREA : (w + 1) * AREA] > 0.5, window_of(x, w), LAND)
        parts.append(part.astype(BF16))
        all_ref[w] = parts[w]
    odd = lax.axis_index("lat") % 2 == 1
    for c in range(2):
        first_ref[c] = jnp.where(odd, parts[c], parts[2 + c])
        second_ref[c] = jnp.where(odd, parts[2 + c], parts[c])
    copies[2].wait()
    cot = cot_ref[0].astype(F32)
    for w in range(4):
        rows = slice(w * AREA, (w + 1) * AREA)
        gb_ref[w] = (window_of(cot, w) * ocean[rows]).astype(BF16)


def land_bias(tokens):
    first = (iota((8, D), 1) == 0).astype(BF16)
    picked = dot(first, tokens, 1, 1)[:1]
    return jnp.where(picked > 0.5 * LAND, NEVER, 0.0)


def hidden_of(tokens, gain_ref):
    normed, _ = norm_rows(tokens.astype(F32))
    return (normed * gain_ref[...]).astype(BF16)


def write_block(tokens, wqkv_ref, gain_ref, q_ref, kv_ref, hid_ref, bias_ref, info_ref):
    hidden = hidden_of(tokens, gain_ref)
    hid_ref[: 4 * AREA] = hidden
    projected = dot(hidden, wqkv_ref[...], 1, 0).astype(BF16)
    q_ref[...] = (projected[:, :D] * BF16(HEAD_DIM ** -0.5)).reshape(4, AREA, D)
    kv_ref[:4] = projected[:, D:].reshape(4, AREA, 2 * D)
    row = land_bias(tokens)
    alive = []
    for w in range(4):
        part = row[:, w * AREA : (w + 1) * AREA]
        bias_ref[w] = jnp.broadcast_to(part, (8, AREA))
        alive.append((jnp.max(part) > 0.5 * NEVER).astype(jnp.int32))
        info_ref[1 + w] = alive[w]
    info_ref[0] = jnp.where(
        alive[3] == 0, 3, jnp.where(alive[2] == 0, 2, jnp.where(alive[1] == 0, 1, 0))
    )


def own_kernel(
    tok_ref, wqkv_hbm, gain_hbm, q_ref, kv_ref, hid_ref, bias_ref, info_ref, wqkv_ref, gain_ref, sems
):
    copies = load(((gain_hbm, gain_ref), (wqkv_hbm, wqkv_ref)), sems)
    wait(copies)
    tokens = tok_ref[...].reshape(4 * AREA, D)
    write_block(tokens, wqkv_ref, gain_ref, q_ref, kv_ref, hid_ref, bias_ref, info_ref)


def lat_block(first_ref, second_ref, wkv_ref, gain_ref, kv_ref, hid_ref, bias_ref, at):
    lat, lat_count = lax.axis_index("lat"), lax.axis_size("lat")
    odd = lat % 2 == 1
    first_ok = jnp.logical_or(odd, lat < lat_count - 1)
    second_ok = jnp.where(odd, lat_count - 1 - lat, lat) > 0
    parts = [first_ref[0], first_ref[1], second_ref[0], second_ref[1]]
    tokens = jnp.concatenate(parts, axis=0)
    hidden = hidden_of(tokens, gain_ref)
    hid_ref[at * AREA : (at + 4) * AREA] = hidden
    kv_ref[at : at + 4] = dot(hidden, wkv_ref[...], 1, 0).astype(BF16).reshape(4, AREA, 2 * D)
    row = land_bias(tokens)
    for k in range(4):
        part = row[:, k * AREA : (k + 1) * AREA]
        part = jnp.where(first_ok if k < 2 else second_ok, part, NEVER)
        bias_ref[at + k] = jnp.broadcast_to(part, (8, AREA))


def near_kernel(
    lon_ref, first_ref, second_ref, wqkv_hbm, gain_hbm,
    q_ref, kv_ref, hid_ref, bias_ref, info_ref, wqkv_ref, gain_ref, sems,
):
    wait(load(((gain_hbm, gain_ref), (wqkv_hbm, wqkv_ref)), sems))
    tokens = lon_ref[...].reshape(4 * AREA, D)
    write_block(tokens, wqkv_ref, gain_ref, q_ref, kv_ref, hid_ref, bias_ref, info_ref)
    lat_block(first_ref, second_ref, wqkv_ref.at[:, D:], gain_ref, kv_ref, hid_ref, bias_ref, 4)


def main_kernel(
    pair, info_ref, infon_ref, q_own, q_near, kv_own, kv_near, hid_own, hid_near, bias_own,
    bias_near, gb_own, gb_near, first_ref, second_ref, wqkv_hbm, wout_hbm, gain_hbm,
    mixed_ref, gq_ref, own_ref, back1_ref, back2_ref, *rest,
):
    sums = rest[:-15]
    q, kv, hid, gb, bias, gm, kcat, acc, dkv, mixed, gq, wkv_ref, wout_ref, gain_ref, sems = rest[-15:]
    pairs = [
        (gain_hbm, gain_ref), (wqkv_hbm.at[:, D:], wkv_ref), (wout_hbm, wout_ref),
        (gb_own, gb.at[:4]), (q_own, q.at[:4]), (kv_own, kv.at[:4]), (kv_near, kv.at[4:12]),
        (hid_own, hid.at[: 4 * AREA]), (hid_near, hid.at[4 * AREA : 12 * AREA]),
        (bias_own, bias.at[:4]), (bias_near, bias.at[4:12]),
    ]
    if pair:
        pairs += [(q_near, q.at[4:]), (gb_near, gb.at[4:])]
    copies = load(pairs, sems)
    acc[...] = jnp.zeros_like(acc)
    mixed[...] = jnp.zeros_like(mixed)
    gq[...] = jnp.zeros_like(gq)
    blocks = head_blocks()
    wait(copies[:2])
    lat_block(first_ref, second_ref, wkv_ref, gain_ref, kv, hid, bias, 12)
    wait(copies[2:])
    blocks_held = 2 if pair else 1
    held = 4 * blocks_held
    gb_flat = gb[...].reshape(held * AREA, D)
    gm[...] = dot(gb_flat, wout_ref[...], 1, 1).astype(BF16).reshape(gm.shape)

    def window_at(b, slot):
        left_out = jnp.where(b == 0, info_ref[0], infon_ref[0])
        return slot + (slot >= left_out).astype(jnp.int32)

    def step(n, carry):
        b = n // 3
        w = window_at(b, n % 3)

        @pl.when(jnp.where(b == 0, info_ref[1 + w], infon_ref[1 + w]) > 0)
        def _():
            r, c = w // 2, w % 2
            mine, other, side = 4 * b, 4 * (1 - b), 2 * lat_side(r)
            places = [mine + window_at(b, k) for k in range(3)]
            places += [other + 1 - c, other + 3 - c]
            places += [8 + mine + side, 9 + mine + side, 8 + other + side + 1 - c]
            at = mine + w
            for k in range(8):
                kcat[k * AREA : (k + 1) * AREA] = kv[places[k]]
            bias_row = jnp.concatenate([bias[place][:1] for place in places], axis=1)
            spans = [slice(D + g * GROUP, D + (g + 1) * GROUP) for g in range(GROUPS)]
            both = range(GROUPS)
            q_stack = [stack_heads(q[at, :, lanes(g)], blocks) for g in both]
            gm_stack = [stack_heads(gm[at, :, lanes(g)], blocks) for g in both]
            scores = [dot(q_stack[g], kcat[:, lanes(g)], 1, 1) + bias_row for g in both]
            grad_probs = [dot(gm_stack[g], kcat[:, spans[g]], 1, 1) for g in both]
            weights = [jnp.exp(x - jnp.max(x, axis=1, keepdims=True)) for x in scores]
            probs = [x * (1.0 / jnp.sum(x, axis=1, keepdims=True)) for x in weights]
            low = [x.astype(BF16) for x in probs]
            out = [unstack_heads(dot(low[g], kcat[:, spans[g]], 1, 0), blocks).astype(BF16) for g in both]
            delta = [jnp.sum(probs[g] * grad_probs[g], axis=1, keepdims=True) for g in both]
            grad_scores = [(probs[g] * (grad_probs[g] - delta[g])).astype(BF16) for g in both]
            grad = [unstack_heads(dot(grad_scores[g], kcat[:, lanes(g)], 1, 0), blocks) for g in both]
            grad_keys = [dot(grad_scores[g], q_stack[g], 0, 0) for g in both]
            grad_values = [dot(low[g], gm_stack[g], 0, 0) for g in both]
            for g in both:
                mixed[at, :, lanes(g)] = out[g]
                gq[at, :, lanes(g)] = (grad[g] * HEAD_DIM ** -0.5).astype(BF16)
                for k in range(8):
                    rows = slice(k * AREA, (k + 1) * AREA)
                    acc[places[k], :, lanes(g)] += grad_keys[g][rows]
                    acc[places[k], :, spans[g]] += grad_values[g][rows]

        return carry

    lax.fori_loop(0, 3 * blocks_held, step, 0)
    dkv[...] = acc[...].astype(BF16)
    own_ref[...] = dkv[:4]
    gq_ref[...] = gq[:4]
    mixed_ref[...] = mixed[:4]
    back1_ref[:2] = dkv[8:10]
    back2_ref[:2] = dkv[10:12]
    lev = lax.axis_index("lev")

    def columns(rel):
        return pl.ds(pl.multiple_of((lev ^ rel) * 128, 128), 128)

    def hid_part(rel, windows):
        return hid[: windows * AREA, columns(rel)]

    def mix_part(rel):
        return mixed[:, :, columns(rel)].reshape(held * AREA, 128)

    def grad_part(at, width):
        return dkv[:, :, at : at + width].reshape(16 * AREA, width)

    gq_flat = gq[...].reshape(held * AREA, D)
    if pair:
        keep, send = sums
        odd, lon = lax.axis_index("lat") % 2, lax.axis_index("lon")

        def put(rel, at, value):
            to = keep if rel % 2 == 0 else send
            value = value.astype(BF16)
            for k in range(2):
                to[rel // 2, k ^ odd, :, at : at + D] = value[k * 64 : (k + 1) * 64]

        @pl.when(lon == 0)
        def _():
            for rel in range(4):
                put(rel, 0, dot(hid_part(rel, 8), gq_flat, 0, 0))
                put(rel, D, dot(mix_part(rel), gb_flat, 0, 0))

        @pl.when(lon == 1)
        def _():
            for rel in range(4):
                part = hid_part(rel, 16)
                put(rel, 0, dot(part, grad_part(0, D), 0, 0))
                put(rel, D, dot(part, grad_part(D, D), 0, 0))
    else:
        keep, send, side_ref = sums
        side_ref[...] = dkv[4:8]
        back1_ref[2:] = dkv[12:14]
        back2_ref[2:] = dkv[14:]
        for rel in range(4):
            to = keep if rel % 2 == 0 else send
            to[rel // 2, :, :D] = dot(hid_part(rel, 4), gq_flat, 0, 0).astype(BF16)
            to[rel // 2, :, D : 2 * D] = dot(mix_part(rel), gb_flat, 0, 0).astype(BF16)
            to[rel // 2, :, 2 * D :] = dot(hid_part(rel, 16), grad_part(0, 2 * D), 0, 0).astype(BF16)


def split_kernel(keep_ref, come_ref, own_ref, lev_ref, lat_ref, far_ref):
    for k, ref in enumerate((own_ref, lat_ref, lev_ref, far_ref)):
        total = keep_ref[k // 2, k % 2].astype(F32) + come_ref[k // 2, k % 2].astype(F32)
        ref[...] = total.astype(ref.dtype)


def input_kernel(
    pair, own_ref, back1_ref, back2_ref, gq_ref, tok_ref, mixed_ref, *rest,
):
    refs = rest if pair else rest[1:]
    cot_hbm, x_hbm, mask_hbm, wqkv_hbm, wout_hbm, gain_hbm, out_ref, ing_ref = refs[:8]
    gkv, cot_ref, x_ref, mask_ref, wqkv_ref, wout_ref, gain_ref, sems = refs[8:]
    pairs = (
        (x_hbm, x_ref), (mask_hbm, mask_ref), (wout_hbm, wout_ref), (gain_hbm, gain_ref),
        (wqkv_hbm, wqkv_ref), (cot_hbm, cot_ref),
    )
    copies = load(pairs, sems)
    odd = lax.axis_index("lat") % 2 == 1
    for w in range(4):
        one, two = back1_ref[w % 2].astype(F32), back2_ref[w % 2].astype(F32)
        lat_part = jnp.where(odd, one, two) if w < 2 else jnp.where(odd, two, one)
        total = own_ref[w].astype(F32) + lat_part
        if not pair:
            total = total + rest[0][w].astype(F32)
        gkv[w * AREA : (w + 1) * AREA] = total.astype(BF16)
    normed, scaling = norm_rows(tok_ref[...].reshape(4 * AREA, D).astype(F32))
    wait(copies)
    ocean = token_mask(mask_ref[0].astype(F32))
    added = (dot(mixed_ref[...].reshape(4 * AREA, D), wout_ref[...], 1, 0) * ocean).reshape(4, AREA, D)
    out_ref[0] = (x_ref[0].astype(F32) + grid_of([added[w] for w in range(4)])).astype(BF16)
    grad_hidden = dot(gq_ref[...].reshape(4 * AREA, D), wqkv_ref[:, :D], 1, 1)
    grad_hidden = grad_hidden + dot(gkv[...], wqkv_ref[:, D:], 1, 1)
    scaled = grad_hidden * gain_ref[...]
    correction = (
        scaled
        - jnp.mean(scaled, axis=-1, keepdims=True)
        - normed * jnp.mean(scaled * normed, axis=-1, keepdims=True)
    )
    added = (scaling * correction).reshape(4, AREA, D)
    ing_ref[0] = (cot_ref[0].astype(F32) + grid_of([added[w] for w in range(4)])).astype(BF16)


def gain_row(rows_ref, gain_ref, qkv_ref):
    at = pl.ds(pl.multiple_of(lax.axis_index("lev") * 128, 128), 128)
    product = rows_ref[...].astype(F32) * qkv_ref[...]
    return dot(jnp.ones((8, 3 * D), F32), product, 1, 1, EXACT)[:1] / gain_ref[:, at]


def load_rows(wqkv_hbm, rows_ref, gain_hbm, gain_ref, sems):
    at = pl.ds(pl.multiple_of(lax.axis_index("lev") * 128, 128), 128)
    return load(((wqkv_hbm.at[at, :], rows_ref), (gain_hbm, gain_ref)), sems)


def finish_rows_kernel(
    own_ref, far_ref, wqkv_hbm, gain_hbm, qkv_ref, out_ref, gg_ref, rows_ref, gain_ref, sems
):
    copies = load_rows(wqkv_hbm, rows_ref, gain_hbm, gain_ref, sems)
    half = own_ref.shape[0]
    first = lax.axis_index("lon") % 2 == 0
    own, far = own_ref[...], far_ref[...]
    for k in range(2):
        value = (jnp.where(first, own, far) if k == 0 else jnp.where(first, far, own)).astype(F32)
        rows = slice(k * half, (k + 1) * half)
        qkv_ref[rows, :D] = value[:, :D]
        qkv_ref[rows, D:] = value[:, 2 * D :]
        out_ref[rows] = value[:, D : 2 * D]
    wait(copies)
    gg_ref[...] = gain_row(rows_ref, gain_ref, qkv_ref)


def finish_pair_kernel(
    own_ref, lat_ref, lon_ref, far_ref, wqkv_hbm, gain_hbm, qkv_ref, out_ref, gg_ref,
    rows_ref, gain_ref, sems,
):
    copies = load_rows(wqkv_hbm, rows_ref, gain_hbm, gain_ref, sems)
    odd = lax.axis_index("lat") % 2 == 1
    first = lax.axis_index("lon") == 0
    for k in range(2):
        rows = slice(64 * k, 64 * k + 64)
        mine = odd if k == 1 else jnp.logical_not(odd)
        near = jnp.where(mine, own_ref[...], lat_ref[...]).astype(F32)
        away = jnp.where(mine, lon_ref[...], far_ref[...]).astype(F32)
        low, high = jnp.where(first, near, away), jnp.where(first, away, near)
        qkv_ref[rows, :D] = low[:, :D]
        out_ref[rows] = low[:, D:]
        qkv_ref[rows, D:] = high
    wait(copies)
    gg_ref[...] = gain_row(rows_ref, gain_ref, qkv_ref)


SMEM = pl.BlockSpec(memory_space=pltpu.SMEM)
VMEM = pl.BlockSpec(memory_space=pltpu.VMEM)
ANY = pl.BlockSpec(memory_space=pl.ANY)
DMAS = pltpu.SemaphoreType.DMA


def call(name, kernel, outs, scalars, arrays, far, scratch, mebibytes, flops=0, out_specs=None):
    moved = sum(a.size * a.dtype.itemsize for a in (*arrays, *far, *outs))
    return pl.pallas_call(
        kernel,
        out_shape=outs,
        in_specs=[SMEM] * len(scalars) + [VMEM] * len(arrays) + [ANY] * len(far),
        out_specs=out_specs or [VMEM] * len(outs),
        scratch_shapes=list(scratch),
        compiler_params=pltpu.CompilerParams(vmem_limit_bytes=mebibytes * 1024 * 1024),
        cost_estimate=pl.CostEstimate(flops=flops, bytes_accessed=moved, transcendentals=0),
        name=name,
    )(*scalars, *arrays, *far)


def shape(dims, dtype=BF16):
    return jax.ShapeDtypeStruct(dims, dtype)


def ring(count, step, periodic):
    return [
        (i, (i + step) % count) for i in range(count) if periodic or 0 <= i + step < count
    ]


def lon_halo(own):
    count = lax.axis_size("lon")
    if count == 2:
        return lax.ppermute(own, "lon", [(0, 1), (1, 0)])
    left = lax.ppermute(own[1::2], "lon", ring(count, 1, True))
    right = lax.ppermute(own[0::2], "lon", ring(count, -1, True))
    return jnp.stack([right, left], axis=1).reshape(own.shape)


def lon_return(side):
    count = lax.axis_size("lon")
    if count == 2:
        return lax.ppermute(side, "lon", [(0, 1), (1, 0)])
    from_left = lax.ppermute(side[0::2], "lon", ring(count, 1, True))
    from_right = lax.ppermute(side[1::2], "lon", ring(count, -1, True))
    return jnp.stack([from_left, from_right], axis=1).reshape(side.shape)


def lat_swaps(first, second):
    count = lax.axis_size("lat")
    swaps = []
    for start, value in ((0, first), (1, second)):
        pairs = [(i, i + 1) for i in range(start, count - 1, 2)]
        swaps.append(lax.ppermute(value, "lat", pairs + [(b, a) for a, b in pairs]))
    return swaps


def swap(value, axis, bit):
    return lax.ppermute(value, axis, [(i, i ^ bit) for i in range(lax.axis_size(axis))])


def halve(parts, axis, bit):
    at = (lax.axis_index(axis) // bit) % 2
    sent = lax.dynamic_index_in_dim(parts, 1 - at, 0, False).astype(BF16)
    kept = lax.dynamic_index_in_dim(parts, at, 0, False)
    return kept + swap(sent, axis, bit).astype(F32)


def rejoin(half, axis, bit):
    first = (lax.axis_index(axis) // bit) % 2 == 0
    far = swap(half, axis, bit)
    return jnp.concatenate([jnp.where(first, half, far), jnp.where(first, far, half)], axis=0)


def bits(axis):
    count = lax.axis_size(axis)
    return [1 << k for k in range(count.bit_length() - 1)]


def gradient_sum(keep, send):
    width = keep.shape[2] // 2
    total = keep.astype(F32) + swap(send, "lev", 1).astype(F32)
    part_a = total[0, :, :width] + swap(total[1, :, :width].astype(BF16), "lev", 2).astype(F32)
    part_b = total[:, :, width:]
    for bit in bits("lon"):
        rows = part_a.shape[0] // 2
        part_a = halve(part_a.reshape(2, rows, width), "lon", bit)
        part_b = halve(jnp.swapaxes(part_b.reshape(2, 2, rows, width), 0, 1), "lon", bit)
    part_b = part_b[0] + swap(part_b[1].astype(BF16), "lev", 2).astype(F32)
    return jnp.concatenate([part_a, part_b], axis=1)


def plane_sum(part):
    for bit in bits("lat"):
        part = halve(part.reshape(2, part.shape[0] // 2, -1), "lat", bit)
    part = part.astype(BF16)
    for bit in reversed(bits("lat")):
        part = rejoin(part, "lat", bit)
    for bit in reversed(bits("lon")[1:]):
        part = rejoin(part, "lon", bit)
    return part, swap(part, "lon", 1)


def pair_sum(keep, send):
    count = lax.axis_size("lat")
    width = keep.shape[-1]
    come = swap(send, "lev", 1)
    piece = shape(keep.shape[2:])
    own, to_lev, to_lat, to_far = call(
        "split", split_kernel, [shape(piece.shape, F32), piece, piece, piece], [], [keep, come], [], [], 8
    )
    from_far = lax.ppermute(to_far, ("lat", "lev"), [(i, i ^ 6) for i in range(4 * count)])
    from_lat = swap(to_lat, "lat", 1)
    from_lev = swap(to_lev, "lev", 2)
    own = own + from_lev.astype(F32) + from_lat.astype(F32) + from_far.astype(F32)
    own = own.astype(BF16)
    for bit in bits("lat")[1:]:
        own = (own.astype(F32) + swap(own, "lat", bit).astype(F32)).astype(BF16)
    return own


def pair_spread(own):
    count = lax.axis_size("lat")
    by_far = lax.ppermute(own, ("lon", "lat"), [(i, i ^ (count + 1)) for i in range(2 * count)])
    return own, swap(own, "lat", 1), swap(own, "lon", 1), by_far


def on_device(tokens_in, cotangent, qkv_weight, out_weight, norm_gain, ocean_mask):
    pair = lax.axis_size("lon") == 2
    gain = norm_gain.reshape(1, D)
    half = shape((2, AREA, D))
    four = shape((4, AREA, D))
    wide = shape((4, AREA, 2 * D))
    info_shape = shape((8,), jnp.int32)
    vmem = lambda *dims: pltpu.VMEM(dims, BF16)
    vmem32 = lambda *dims: pltpu.VMEM(dims, F32)
    grid = vmem(*tokens_in.shape)
    mask = pltpu.VMEM(ocean_mask.shape, jnp.int32)
    weight, gains = vmem(*qkv_weight.shape), vmem32(1, D)
    tok, tok_first, tok_second, gb = call(
        "prep", prep_kernel, [four, half, half, four], [], [], [tokens_in, cotangent, ocean_mask],
        [grid, grid, mask, DMAS((3,))], 8,
    )
    tok_lon = lon_halo(tok)
    tok_first, tok_second = lat_swaps(tok_first, tok_second)
    tok, tok_first, tok_second, gb = lax.optimization_barrier((tok, tok_first, tok_second, gb))
    gb_near = lon_halo(gb) if pair else gb
    q, kv, hid, bias, info = call(
        "own", own_kernel,
        [four, wide, shape((4 * AREA, D)), shape((4, 8, AREA), F32), info_shape],
        [], [tok], [qkv_weight, gain], [weight, gains, DMAS((2,))], 16,
        flops=2 * 256 * 512 * 1536, out_specs=[VMEM] * 4 + [SMEM],
    )
    tok_lon, hid = lax.optimization_barrier((tok_lon, hid))
    rows = tok_lon.reshape(2, 2, AREA, D)
    odd = lax.axis_index("lat") % 2
    corner_first, corner_second = lat_swaps(
        lax.dynamic_index_in_dim(rows, 1 - odd, 0, False),
        lax.dynamic_index_in_dim(rows, odd, 0, False),
    )
    q_near, kv_near, hid_near, bias_near, info_near = call(
        "near", near_kernel,
        [four, shape((8, AREA, 2 * D)), shape((8 * AREA, D)), shape((8, 8, AREA), F32), info_shape],
        [], [tok_lon, tok_first, tok_second], [qkv_weight, gain], [weight, gains, DMAS((2,))], 20,
        flops=2 * 512 * 512 * 1280, out_specs=[VMEM] * 4 + [SMEM],
    )
    held = 8 if pair else 4
    back = shape((2 if pair else 4, AREA, 2 * D))
    share = shape((2, 2, 64, 2 * D) if pair else (2, 128, 4 * D))
    mixed, gq, own_kv, back_first, back_second, keep, send, *side = call(
        "main", lambda *refs: main_kernel(pair, *refs),
        [four, four, wide, back, back, share, share] + ([] if pair else [wide]),
        [info, info_near],
        [q, q_near, kv, kv_near, hid, hid_near, bias, bias_near, gb, gb_near, corner_first, corner_second],
        [qkv_weight, out_weight, gain],
        [vmem(held, AREA, D), vmem(16, AREA, 2 * D), vmem(16 * AREA, D), vmem(held, AREA, D),
         vmem32(16, 8, AREA), vmem(held, AREA, D), vmem(KEYS, 2 * D), vmem32(16, AREA, 2 * D),
         vmem(16, AREA, 2 * D), vmem(held, AREA, D), vmem(held, AREA, D), vmem(D, 2 * D),
         vmem(D, D), gains, DMAS((13,))],
        40, flops=3 * 16 * 2 * 512 * 256 * 256 + 2 * 1024 * 512 * 1024,
    )
    if pair:
        total = pair_sum(keep, send)
        back_first, back_second = lat_swaps(back_first, back_second)
        total, back_first, back_second = lax.optimization_barrier((total, back_first, back_second))
        sums = pair_spread(total)
        lon_kv = []
        finish = finish_pair_kernel
    else:
        part = gradient_sum(keep, send)
        back_first, back_second = lat_swaps(back_first, back_second)
        one, two = back_first[2:].astype(F32), back_second[2:].astype(F32)
        rows = jnp.stack([jnp.where(odd == 1, one, two), jnp.where(odd == 1, two, one)])
        side_kv = (side[0].reshape(rows.shape).astype(F32) + rows).astype(BF16)
        lon_kv = [lon_return(side_kv.reshape(wide.shape))]
        sums = plane_sum(part)
        finish = finish_rows_kernel
    layer_out, input_grad = call(
        "input", lambda *refs: input_kernel(pair, *refs),
        [shape(tokens_in.shape), shape(tokens_in.shape)], [],
        [own_kv, back_first, back_second, gq, tok, mixed] + lon_kv,
        [cotangent, tokens_in, ocean_mask, qkv_weight, out_weight, gain],
        [vmem(4 * AREA, 2 * D), grid, grid, mask, weight, vmem(D, D), gains, DMAS((6,))],
        24, flops=2 * 256 * 512 * 1536,
    )
    qkv_grad, out_grad, gain_grad = call(
        "finish", finish,
        [shape((128, 3 * D), F32), shape((128, D), F32), shape((1, 128), F32)], [],
        list(sums), [qkv_weight, gain], [vmem(128, 3 * D), gains, DMAS((2,))], 16,
    )
    return layer_out, input_grad, qkv_grad, out_grad, gain_grad.reshape(128)


def solution(mesh):
    placed = (
        P("lev", "lat", "lon", None),
        P("lev", "lat", "lon", None),
        P(),
        P(),
        P(),
        P("lev", "lat", "lon"),
    )
    return jax.shard_map(
        on_device,
        mesh=mesh,
        in_specs=placed,
        out_specs=(
            P("lev", "lat", "lon", None),
            P("lev", "lat", "lon", None),
            P("lev", None),
            P("lev", None),
            P("lev"),
        ),
        check_vma=False,
    )
```

time: 91.4 us -> 75.4 us (0.82)
  starting transfers between devices: 40 us -> 29.5 us
  Pallas kernels: 24.5 us -> 17.1 us
  waiting for transfers between devices: 19.9 us -> 22.8 us
  other arithmetic: 2.45 us -> 0.1 us
  local copies, waits for them, and re-layouts: 2.97 us -> 4.74 us
    ppermute x20 -> x14, starting transfers between devices: 37.1 us -> 26.1 us  [the longest x6 13.6 us: lat_swaps(): swaps.append(lax.ppermute(value, 'lat', pairs + [(b, a) for a, b in pairs]))]
    pallas_call x5 -> x7, Pallas kernels: 24.5 us -> 17.1 us  [call(): pl.pallas_call(kernel, out_shape=outs, in_specs=[SMEM] * len(scalars) + [...]
    ppermute x20 -> x14, waiting for transfers between devices: 18.2 us -> 22.8 us  [the longest x6 14.8 us: swap(): lax.ppermute(value, axis, [(i, i ^ bit) for i in range(lax.axis_size(axis...]
    unnamed x28 -> x22, local copies, waits for them, and re-layouts: 2.79 us -> 4.71 us
    ppermute x1 -> x2, waiting for transfers between devices: 1.73 us -> 0.01 us  [lon_halo(): return lax.ppermute(own, 'lon', [(0, 1), (1, 0)])]
    add x6 -> x0, other arithmetic: 1.57 us -> none  [the longest x2 1.38 us: core_sum(): return keep.astype(F32) + arrived.astype(F32)]
    ppermute x1 -> x2, starting transfers between devices: 2.94 us -> 3.36 us  [lon_halo(): return lax.ppermute(own, 'lon', [(0, 1), (1, 0)])]
  transfers between devices with their start and end apart: 21 -> 16, of which waited for: 9 -> 9; matrix products, arithmetic and copies ran while one was open for 3% -> 0% of each run, Pallas kernels for 8% -> 7%
where the time goes in v3:
time: 75.4 us; the launch traced here: 75.1 us
  starting transfers between devices  29.5 us (39%)
  waiting for transfers between devices  22.8 us (30%)
  Pallas kernels  17.1 us (23%)
  local copies, waits for them, and re-layouts  4.74 us (6%)
  between operations  0.83 us (1%)
    pallas_call x7, Pallas kernels, call(): pl.pallas_call(kernel, out_shape=outs, in_specs=[SMEM] * len(scalars) + [...  17.1 us
    ppermute x6, waiting for transfers between devices, swap(): lax.ppermute(value, axis, [(i, i ^ bit) for i in range(lax.axis_size(axis...  14.8 us
    ppermute x6, starting transfers between devices, lat_swaps(): swaps.append(lax.ppermute(value, 'lat', pairs + [(b, a) for a, b in pairs]))  13.6 us
    ppermute x6, starting transfers between devices, swap(): lax.ppermute(value, axis, [(i, i ^ bit) for i in range(lax.axis_size(axis...  7.08 us
    ppermute x1, starting transfers between devices, pair_spread(): lax.ppermute(own, ('lon', 'lat'), [(i, i ^ count + 1) for i in range(2 *...  5.45 us
    ppermute x6, waiting for transfers between devices, lat_swaps(): swaps.append(lax.ppermute(value, 'lat', pairs + [(b, a) for a, b in pairs]))  5.28 us
    unnamed x22, local copies, waits for them, and re-layouts  4.71 us
    ppermute x2, starting transfers between devices, lon_halo(): return lax.ppermute(own, 'lon', [(0, 1), (1, 0)])  3.36 us
  transfers between devices with their start and end apart: 16, of which 9 were waited for; matrix products, arithmetic and copies ran while one was open for 0% of the time, Pallas kernels for 7%

profile of v3, /device:TPU:0, one launch (start us, length us, event | category | flops | bytes accessed | tf_op | source)
XLA Modules:
  0.0 75.1 jit_solution(15675734673582174993)
XLA Ops:
  0.6 0.0 copy-start.2
  0.6 0.9 %copy-done.2 = bf16[1,16,16,512]{3,2,1,0:T(8,128)(2,1)S(1)} copy-done((bf16[1,16,16,512]{3,2,1,0:T(8,128)(2,1)S(1)}, bf16[1,16,16,512]{3,2,1,0:T(8,128)(2,1)}, u32[]{:S(2)}) %copy-start.2) | copy-done | bytes 262168
  1.6 0.0 copy-start.4
  1.6 0.9 %copy-done.4 = bf16[1,16,16,512]{3,2,1,0:T(8,128)(2,1)S(1)} copy-done((bf16[1,16,16,512]{3,2,1,0:T(8,128)(2,1)S(1)}, bf16[1,16,16,512]{3,2,1,0:T(8,128)(2,1)}, u32[]{:S(2)}) %copy-start.4) | copy-done | bytes 262168
  2.5 0.0 copy-start.7
  2.5 0.7 copy-done.7
  3.2 0.0 copy-start.10
  3.2 0.4 prep.1
  3.7 3.0 %collective-permute-start.2 = (bf16[4,64,512]{2,1,0:T(8,128)(2,1)S(1)}, bf16[4,64,512]{2,1,0:T(8,128)(2,1)S(1)}, u32[]{:S(2)}, u32[]{:S(2)}) collective-permute-start(bf16[4,64,512]{2,1,0:T(8,128)(2,1)S(1)} %get-tuple-element.48.tok_ref.refs_4_), channel_id=1, source_target_pairs={{0,16},{16,0},{1,17},{17,1},{2,18},{18,2},{3,19},{19,3},{4,20},{20... | collective-permute-start | bytes 786440 | tf_op jit(solution)/shard_map/ppermute | solution.py:441
  6.7 1.6 %collective-permute-start = (bf16[2,64,512]{2,1,0:T(8,128)(2,1)S(1)}, bf16[2,64,512]{2,1,0:T(8,128)(2,1)S(1)}, u32[]{:S(2)}, u32[]{:S(2)}) collective-permute-start(bf16[2,64,512]{2,1,0:T(8,128)(2,1)S(1)} %get-tuple-element.45), channel_id=1, source_target_pairs={{0,4},{8,12},{4,0},{12,8},{1,5},{9,13},{5,1},{13,9},{2,6},{10,14},... | collective-permute-start | bytes 393224 | tf_op jit(solution)/shard_map/ppermute | solution.py:461
  8.3 0.7 collective-permute-start.1
  8.9 2.7 %collective-permute-done.first_ref = bf16[2,64,512]{2,1,0:T(8,128)(2,1)S(1)} collective-permute-done((bf16[2,64,512]{2,1,0:T(8,128)(2,1)S(1)}, bf16[2,64,512]{2,1,0:T(8,128)(2,1)S(1)}, u32[]{:S(2)}, u32[]{:S(2)}) %collective-permute-start) | collective-permute-done | bytes 131104 | tf_op jit(solution)/shard_map/ppermute | solution.py:461
  11.6 0.0 collective-permute-done.1.second_ref
  11.6 0.4 collective-permute-start.3
  12.0 0.0 copy-start
  12.0 1.4 %copy-done = bf16[512,1536]{1,0:T(8,128)(2,1)S(1)} copy-done((bf16[512,1536]{1,0:T(8,128)(2,1)S(1)}, bf16[512,1536]{1,0:T(8,128)(2,1)}, u32[]{:S(2)}) %copy-start) | copy-done | bytes 1572888
  13.4 0.0 copy-start.9
  13.4 0.7 copy-done.9
  14.1 0.0 copy-start.1
  14.1 1.6 %own.1 = (bf16[4,64,512]{2,1,0:T(8,128)(2,1)S(1)}, bf16[4,64,1024]{2,1,0:T(8,128)(2,1)S(1)}, bf16[256,512]{1,0:T(8,128)(2,1)S(1)}, f32[4,8,64]{2,1,0:T(8,128)S(1)}, s32[8]{0:T(128)S(1)}) custom-call(bf16[4,64,512]{2,1,0:T(8,128)(2,1)S(1)} %get-tuple-element.48.tok_ref.refs_4_, bf16[512,1536]{1,0:T(8,128)(2,1)S(1)} %copy-done, f32[1,512]{1,0:T(1,128)S(1)} %bitcast.8), custom_call_target="tpu_custom_call" | custom-call | flops 402653184 | bytes 2893856 | tf_op jit(solution)/shard_map/own/pallas_call | solution.py:416
  15.7 0.0 copy-start.6
  15.7 0.0 collective-permute-done.2.lon_ref
  15.8 0.8 %collective-permute-start.5 = (bf16[2,64,512]{2,1,0:T(8,128)(2,1)S(1)}, bf16[2,64,512]{2,1,0:T(8,128)(2,1)S(1)}, u32[]{:S(2)}, u32[]{:S(2)}) collective-permute-start(bf16[2,64,512]{2,1,0:T(8,128)(2,1)S(1)} %get-tuple-element.83), channel_id=1, source_target_pairs={{4,8},{8,4},{5,9},{9,5},{6,10},{10,6},{7,11},{11,7},{20,24},{24,20... | collective-permute-start | bytes 393224 | tf_op jit(solution)/shard_map/ppermute | solution.py:461
  16.6 8.1 %collective-permute-start.4 = (bf16[2,64,512]{2,1,0:T(8,128)(2,1)S(1)}, bf16[2,64,512]{2,1,0:T(8,128)(2,1)S(1)}, u32[]{:S(2)}, u32[]{:S(2)}) collective-permute-start(bf16[2,64,512]{2,1,0:T(8,128)(2,1)S(1)} %get-tuple-element.84), channel_id=1, source_target_pairs={{0,4},{8,12},{4,0},{12,8},{1,5},{9,13},{5,1},{13,9},{2,6},{10,14},... | collective-permute-start | bytes 393224 | tf_op jit(solution)/shard_map/ppermute | solution.py:461
  24.7 0.0 copy-done.10
  24.7 0.0 copy-done.1
  24.7 1.7 %near.1 = (bf16[4,64,512]{2,1,0:T(8,128)(2,1)S(1)}, bf16[8,64,1024]{2,1,0:T(8,128)(2,1)S(1)}, bf16[512,512]{1,0:T(8,128)(2,1)S(1)}, f32[8,8,64]{2,1,0:T(8,128)S(1)}, s32[8]{0:T(128)S(1)}) custom-call(bf16[4,64,512]{2,1,0:T(8,128)(2,1)S(1)} %collective-permute-done.2.lon_ref, bf16[2,64,512]{2,1,0:T(8,128)(2,1)S(1)} %collective-permute-done.first_ref, ...), custom_call_target="tpu_custom_call" | custom-call | flops 671088640 | bytes 3950624 | tf_op jit(solution)/shard_map/near/pallas_call | solution.py:416
  26.4 0.0 collective-permute-done.3.refs_11_
  26.4 0.0 collective-permute-done.5.refs_13_
  26.5 1.2 %collective-permute-done.4.refs_12_ = bf16[2,64,512]{2,1,0:T(8,128)(2,1)S(1)} collective-permute-done((bf16[2,64,512]{2,1,0:T(8,128)(2,1)S(1)}, bf16[2,64,512]{2,1,0:T(8,128)(2,1)S(1)}, u32[]{:S(2)}, u32[]{:S(2)}) %collective-permute-start.4) | collective-permute-done | bytes 131104 | tf_op jit(solution)/shard_map/ppermute | solution.py:461
  27.6 0.0 copy-done.6
  27.6 9.4 %main.1 = (bf16[4,64,512]{2,1,0:T(8,128)(2,1)S(1)}, bf16[4,64,512]{2,1,0:T(8,128)(2,1)S(1)}, bf16[4,64,1024]{2,1,0:T(8,128)(2,1)S(1)}, bf16[2,64,1024]{2,1,0:T(8...) custom-call(s32[8]{0:T(128)S(1)} %get-tuple-element.49.refs_0_, ...), custom_call_target="tpu_custom_call" | custom-call | flops 4294967296 | bytes 8415232 | tf_op jit(solution)/shard_map/main/pallas_call | solution.py:416
  37.0 0.0 copy-start.3
  37.0 0.0 copy-start.5
  37.1 0.0 copy-start.8
  37.1 0.1 collective-permute-start.6
  37.1 1.9 %collective-permute-done.6.come_ref = bf16[2,2,64,1024]{3,2,1,0:T(8,128)(2,1)S(1)} collective-permute-done((bf16[2,2,64,1024]{3,2,1,0:T(8,128)(2,1)S(1)}, bf16[2,2,64,1024]{3,2,1,0:T(8,128)(2,1)S(1)}, u32[]{:S(2)}, u32[]{:S(2)}) %collective-permute-start.6) | collective-permute-done | bytes 524320 | tf_op jit(solution)/shard_map/ppermute | solution.py:466
  39.0 0.1 split.1
  39.2 0.2 collective-permute-start.7
  39.4 6.1 %collective-permute-start.8 = (bf16[64,1024]{1,0:T(8,128)(2,1)S(1)}, bf16[64,1024]{1,0:T(8,128)(2,1)S(1)}, u32[]{:S(2)}, u32[]{:S(2)}) collective-permute-start(bf16[64,1024]{1,0:T(8,128)(2,1)S(1)} %get-tuple-element.69), channel_id=1, source_target_pairs={{0,4},{4,0},{8,12},{12,8},{1,5},{5,1},{9,13},{13,9},{2,6},{6,2},{1... | collective-permute-start | bytes 393224 | tf_op jit(solution)/shard_map/ppermute | solution.py:466
  45.6 0.0 collective-permute-start.9
  45.6 0.0 collective-permute-done.7
  45.6 4.3 %collective-permute-done.8 = bf16[64,1024]{1,0:T(8,128)(2,1)S(1)} collective-permute-done((bf16[64,1024]{1,0:T(8,128)(2,1)S(1)}, bf16[64,1024]{1,0:T(8,128)(2,1)S(1)}, u32[]{:S(2)}, u32[]{:S(2)}) %collective-permute-start.8) | collective-permute-done | bytes 131104 | tf_op jit(solution)/shard_map/ppermute | solution.py:466
  49.9 1.8 %collective-permute-done.9 = bf16[64,1024]{1,0:T(8,128)(2,1)S(1)} collective-permute-done((bf16[64,1024]{1,0:T(8,128)(2,1)S(1)}, bf16[64,1024]{1,0:T(8,128)(2,1)S(1)}, u32[]{:S(2)}, u32[]{:S(2)}) %collective-permute-start.9) | collective-permute-done | bytes 131104 | tf_op jit(solution)/shard_map/ppermute | solution.py:519
  51.7 0.1 add_convert_fusion.1
  51.7 0.1 collective-permute-start.10
  51.8 1.8 %collective-permute-start.11 = (bf16[2,64,1024]{2,1,0:T(8,128)(2,1)S(1)}, bf16[2,64,1024]{2,1,0:T(8,128)(2,1)S(1)}, u32[]{:S(2)}, u32[]{:S(2)}) collective-permute-start(bf16[2,64,1024]{2,1,0:T(8,128)(2,1)S(1)} %get-tuple-element.71), channel_id=1, source_target_pairs={{0,4},{8,12},{4,0},{12,8},{1,5},{9,13},{5,1},{13,9},{2,6},{10,14},... | collective-permute-start | bytes 786440 | tf_op jit(solution)/shard_map/ppermute | solution.py:461
  53.6 0.7 collective-permute-start.12
  54.3 6.5 %collective-permute-done.10 = bf16[64,1024]{1,0:T(8,128)(2,1)S(1)} collective-permute-done((bf16[64,1024]{1,0:T(8,128)(2,1)S(1)}, bf16[64,1024]{1,0:T(8,128)(2,1)S(1)}, u32[]{:S(2)}, u32[]{:S(2)}) %collective-permute-start.10) | collective-permute-done | bytes 131104 | tf_op jit(solution)/shard_map/ppermute | solution.py:466
  60.8 1.4 %collective-permute-done.11.refs_1_ = bf16[2,64,1024]{2,1,0:T(8,128)(2,1)S(1)} collective-permute-done((bf16[2,64,1024]{2,1,0:T(8,128)(2,1)S(1)}, bf16[2,64,1024]{2,1,0:T(8,128)(2,1)S(1)}, u32[]{:S(2)}, u32[]{:S(2)}) %collective-permute-start.11) | collective-permute-done | bytes 262176 | tf_op jit(solution)/shard_map/ppermute | solution.py:461
  62.2 0.0 collective-permute-done.12.refs_2_
  62.2 5.4 %collective-permute-start.15 = (bf16[64,1024]{1,0:T(8,128)(2,1)S(1)}, bf16[64,1024]{1,0:T(8,128)(2,1)S(1)}, u32[]{:S(2)}, u32[]{:S(2)}) collective-permute-start(bf16[64,1024]{1,0:T(8,128)(2,1)S(1)} %add_convert_fusion.own_ref), channel_id=1, source_target_pairs={{0,20},{4,16},{8,28},{12,24},{16,4},{20,0},{24,12},{28,8},{1,21},{... | collective-permute-start | bytes 393224 | tf_op jit(solution)/shard_map/ppermute | solution.py:531
  67.7 0.0 collective-permute-start.14
  67.7 0.6 collective-permute-start.13
  68.2 0.0 copy-done.3
  68.2 0.0 copy-done.5
  68.2 0.0 copy-done.8
  68.2 2.2 %input.1 = (bf16[1,16,16,512]{3,2,1,0:T(8,128)(2,1)}, bf16[1,16,16,512]{3,2,1,0:T(8,128)(2,1)}) custom-call(bf16[4,64,1024]{2,1,0:T(8,128)(2,1)S(1)} %get-tuple-element.64.refs_0_, bf16[2,64,1024]{2,1,0:T(8,128)(2,1)S(1)} %collective-permute-done.11.refs_1_, bf16[2,64,1024]{2,1,0:T(8,128)(2,1)S(1)} %collective-permute-done.12.refs_2_, ...), custom_call_target="tpu_custom_call" | custom-call | flops 402653184 | bytes 4983808 | tf_op jit(solution)/shard_map/input/pallas_call | solution.py:416
  70.5 0.9 %collective-permute-done.15.far_ref = bf16[64,1024]{1,0:T(8,128)(2,1)S(1)} collective-permute-done((bf16[64,1024]{1,0:T(8,128)(2,1)S(1)}, bf16[64,1024]{1,0:T(8,128)(2,1)S(1)}, u32[]{:S(2)}, u32[]{:S(2)}) %collective-permute-start.15) | collective-permute-done | bytes 131104 | tf_op jit(solution)/shard_map/ppermute | solution.py:531
  71.4 2.1 %collective-permute-done.14.lon_ref = bf16[64,1024]{1,0:T(8,128)(2,1)S(1)} collective-permute-done((bf16[64,1024]{1,0:T(8,128)(2,1)S(1)}, bf16[64,1024]{1,0:T(8,128)(2,1)S(1)}, u32[]{:S(2)}, u32[]{:S(2)}) %collective-permute-start.14) | collective-permute-done | bytes 131104 | tf_op jit(solution)/shard_map/ppermute | solution.py:466
  73.5 0.0 collective-permute-done.13.lat_ref
  73.5 1.6 %finish.1 = (f32[128,1536]{1,0:T(8,128)}, f32[128,512]{1,0:T(8,128)}, f32[1,128]{1,0:T(1,128)}) custom-call(bf16[64,1024]{1,0:T(8,128)(2,1)S(1)} %add_convert_fusion.own_ref, bf16[64,1024]{1,0:T(8,128)(2,1)S(1)} %collective-permute-done.13.lat_ref, bf16[64,1024]{1,0:T(8,128)(2,1)S(1)} %collective-permute-done.14.lon_ref, ...), custom_call_target="tpu_custom_call" | custom-call | bytes 3148288 | tf_op jit(solution)/shard_map/finish/pallas_call | solution.py:416
  (2 shorter events, 0.1 us)
Async XLA Ops:
  0.6 1.0 %copy-start.2 = (bf16[1,16,16,512]{3,2,1,0:T(8,128)(2,1)S(1)}, bf16[1,16,16,512]{3,2,1,0:T(8,128)(2,1)}, u32[]{:S(2)}) copy-start(bf16[1,16,16,512]{3,2,1,0:T(8,128)(2,1)} %refs_7_.1) | copy-start | bytes 786436
  1.6 0.9 %copy-start.4 = (bf16[1,16,16,512]{3,2,1,0:T(8,128)(2,1)S(1)}, bf16[1,16,16,512]{3,2,1,0:T(8,128)(2,1)}, u32[]{:S(2)}) copy-start(bf16[1,16,16,512]{3,2,1,0:T(8,128)(2,1)} %refs_6_.1) | copy-start | bytes 786436
  2.5 0.7 copy-start.7
  3.2 21.5 %copy-start.10 = (f32[512]{0:T(512)S(1)}, f32[512]{0:T(512)}, u32[]{:S(2)}) copy-start(f32[512]{0:T(512)} %param.10) | copy-start | bytes 6148
  3.7 12.1 %collective-permute-start.2 = (bf16[4,64,512]{2,1,0:T(8,128)(2,1)S(1)}, bf16[4,64,512]{2,1,0:T(8,128)(2,1)S(1)}, u32[]{:S(2)}, u32[]{:S(2)}) collective-permute-start(bf16[4,64,512]{2,1,0:T(8,128)(2,1)S(1)} %get-tuple-element.48.tok_ref.refs_4_), channel_id=1, source_target_pairs={{0,16},{16,0},{1,17},{17,1},{2,18},{18,2},{3,19},{19,3},{4,20},{20... | collective-permute-start | bytes 786440 | tf_op jit(solution)/shard_map/ppermute | solution.py:441
  6.7 5.0 %collective-permute-start = (bf16[2,64,512]{2,1,0:T(8,128)(2,1)S(1)}, bf16[2,64,512]{2,1,0:T(8,128)(2,1)S(1)}, u32[]{:S(2)}, u32[]{:S(2)}) collective-permute-start(bf16[2,64,512]{2,1,0:T(8,128)(2,1)S(1)} %get-tuple-element.45), channel_id=1, source_target_pairs={{0,4},{8,12},{4,0},{12,8},{1,5},{9,13},{5,1},{13,9},{2,6},{10,14},... | collective-permute-start | bytes 393224 | tf_op jit(solution)/shard_map/ppermute | solution.py:461
  8.3 3.4 %collective-permute-start.1 = (bf16[2,64,512]{2,1,0:T(8,128)(2,1)S(1)}, bf16[2,64,512]{2,1,0:T(8,128)(2,1)S(1)}, u32[]{:S(2)}, u32[]{:S(2)}) collective-permute-start(bf16[2,64,512]{2,1,0:T(8,128)(2,1)S(1)} %get-tuple-element.46), channel_id=1, source_target_pairs={{4,8},{8,4},{5,9},{9,5},{6,10},{10,6},{7,11},{11,7},{20,24},{24,20... | collective-permute-start | bytes 393224 | tf_op jit(solution)/shard_map/ppermute | solution.py:461
  11.6 14.8 %collective-permute-start.3 = (bf16[4,64,512]{2,1,0:T(8,128)(2,1)S(1)}, bf16[4,64,512]{2,1,0:T(8,128)(2,1)S(1)}, u32[]{:S(2)}, u32[]{:S(2)}) collective-permute-start(bf16[4,64,512]{2,1,0:T(8,128)(2,1)S(1)} %get-tuple-element.63.refs_10_), channel_id=1, source_target_pairs={{0,16},{16,0},{1,17},{17,1},{2,18},{18,2},{3,19},{19,3},{4,20},{20... | collective-permute-start | bytes 786440 | tf_op jit(solution)/shard_map/ppermute | solution.py:441
  12.0 1.4 %copy-start = (bf16[512,1536]{1,0:T(8,128)(2,1)S(1)}, bf16[512,1536]{1,0:T(8,128)(2,1)}, u32[]{:S(2)}) copy-start(bf16[512,1536]{1,0:T(8,128)(2,1)} %wqkv_hbm.5) | copy-start | bytes 4718596
  13.4 0.7 copy-start.9
  14.1 10.6 %copy-start.1 = (bf16[512,1536]{1,0:T(8,128)(2,1)S(1)}, bf16[512,1536]{1,0:T(8,128)(2,1)}, u32[]{:S(2)}) copy-start(bf16[512,1536]{1,0:T(8,128)(2,1)} %wqkv_hbm.5) | copy-start | bytes 4718596
  15.7 11.9 %copy-start.6 = (bf16[512,512]{1,0:T(8,128)(2,1)S(1)}, bf16[512,512]{1,0:T(8,128)(2,1)}, u32[]{:S(2)}) copy-start(bf16[512,512]{1,0:T(8,128)(2,1)} %refs_10_.1) | copy-start | bytes 1572868
  15.8 10.7 %collective-permute-start.5 = (bf16[2,64,512]{2,1,0:T(8,128)(2,1)S(1)}, bf16[2,64,512]{2,1,0:T(8,128)(2,1)S(1)}, u32[]{:S(2)}, u32[]{:S(2)}) collective-permute-start(bf16[2,64,512]{2,1,0:T(8,128)(2,1)S(1)} %get-tuple-element.83), channel_id=1, source_target_pairs={{4,8},{8,4},{5,9},{9,5},{6,10},{10,6},{7,11},{11,7},{20,24},{24,20... | collective-permute-start | bytes 393224 | tf_op jit(solution)/shard_map/ppermute | solution.py:461
  16.6 11.0 %collective-permute-start.4 = (bf16[2,64,512]{2,1,0:T(8,128)(2,1)S(1)}, bf16[2,64,512]{2,1,0:T(8,128)(2,1)S(1)}, u32[]{:S(2)}, u32[]{:S(2)}) collective-permute-start(bf16[2,64,512]{2,1,0:T(8,128)(2,1)S(1)} %get-tuple-element.84), channel_id=1, source_target_pairs={{0,4},{8,12},{4,0},{12,8},{1,5},{9,13},{5,1},{13,9},{2,6},{10,14},... | collective-permute-start | bytes 393224 | tf_op jit(solution)/shard_map/ppermute | solution.py:461
  37.0 31.2 %copy-start.3 = (bf16[1,16,16,512]{3,2,1,0:T(8,128)(2,1)S(1)}, bf16[1,16,16,512]{3,2,1,0:T(8,128)(2,1)}, u32[]{:S(2)}) copy-start(bf16[1,16,16,512]{3,2,1,0:T(8,128)(2,1)} %refs_7_.1) | copy-start | bytes 786436
  37.0 31.2 %copy-start.5 = (bf16[1,16,16,512]{3,2,1,0:T(8,128)(2,1)S(1)}, bf16[1,16,16,512]{3,2,1,0:T(8,128)(2,1)}, u32[]{:S(2)}) copy-start(bf16[1,16,16,512]{3,2,1,0:T(8,128)(2,1)} %refs_6_.1) | copy-start | bytes 786436
  37.1 31.2 %copy-start.8 = (s32[1,16,16]{2,1,0:T(8,128)S(1)}, s32[1,16,16]{2,1,0:T(8,128)}, u32[]{:S(2)}) copy-start(s32[1,16,16]{2,1,0:T(8,128)} %refs_8_.1) | copy-start | bytes 3076
  37.1 2.0 %collective-permute-start.6 = (bf16[2,2,64,1024]{3,2,1,0:T(8,128)(2,1)S(1)}, bf16[2,2,64,1024]{3,2,1,0:T(8,128)(2,1)S(1)}, u32[]{:S(2)}, u32[]{:S(2)}) collective-permute-start(bf16[2,2,64,1024]{3,2,1,0:T(8,128)(2,1)S(1)} %get-tuple-element.66), channel_id=1, source_target_pairs={{0,1},{1,0},{2,3},{3,2},{4,5},{5,4},{6,7},{7,6},{8,9},{9,8},{10,11... | collective-permute-start | bytes 1572872 | tf_op jit(solution)/shard_map/ppermute | solution.py:466
  39.2 6.4 %collective-permute-start.7 = (bf16[64,1024]{1,0:T(8,128)(2,1)S(1)}, bf16[64,1024]{1,0:T(8,128)(2,1)S(1)}, u32[]{:S(2)}, u32[]{:S(2)}) collective-permute-start(bf16[64,1024]{1,0:T(8,128)(2,1)S(1)} %get-tuple-element.68), channel_id=1, source_target_pairs={{0,2},{1,3},{2,0},{3,1},{4,6},{5,7},{6,4},{7,5},{8,10},{9,11},{10,... | collective-permute-start | bytes 393224 | tf_op jit(solution)/shard_map/ppermute | solution.py:466
  39.4 10.4 %collective-permute-start.8 = (bf16[64,1024]{1,0:T(8,128)(2,1)S(1)}, bf16[64,1024]{1,0:T(8,128)(2,1)S(1)}, u32[]{:S(2)}, u32[]{:S(2)}) collective-permute-start(bf16[64,1024]{1,0:T(8,128)(2,1)S(1)} %get-tuple-element.69), channel_id=1, source_target_pairs={{0,4},{4,0},{8,12},{12,8},{1,5},{5,1},{9,13},{13,9},{2,6},{6,2},{1... | collective-permute-start | bytes 393224 | tf_op jit(solution)/shard_map/ppermute | solution.py:466
  45.6 6.1 %collective-permute-start.9 = (bf16[64,1024]{1,0:T(8,128)(2,1)S(1)}, bf16[64,1024]{1,0:T(8,128)(2,1)S(1)}, u32[]{:S(2)}, u32[]{:S(2)}) collective-permute-start(bf16[64,1024]{1,0:T(8,128)(2,1)S(1)} %get-tuple-element.70), channel_id=1, source_target_pairs={{0,6},{1,7},{2,4},{3,5},{4,2},{5,3},{6,0},{7,1},{8,14},{9,15},{10,... | collective-permute-start | bytes 393224 | tf_op jit(solution)/shard_map/ppermute | solution.py:519
  51.7 9.0 %collective-permute-start.10 = (bf16[64,1024]{1,0:T(8,128)(2,1)S(1)}, bf16[64,1024]{1,0:T(8,128)(2,1)S(1)}, u32[]{:S(2)}, u32[]{:S(2)}) collective-permute-start(bf16[64,1024]{1,0:T(8,128)(2,1)S(1)} %add_convert_fusion.1), channel_id=1, source_target_pairs={{0,8},{4,12},{8,0},{12,4},{1,9},{5,13},{9,1},{13,5},{2,10},{6,14},... | collective-permute-start | bytes 393224 | tf_op jit(solution)/shard_map/ppermute | solution.py:466
  51.8 10.4 %collective-permute-start.11 = (bf16[2,64,1024]{2,1,0:T(8,128)(2,1)S(1)}, bf16[2,64,1024]{2,1,0:T(8,128)(2,1)S(1)}, u32[]{:S(2)}, u32[]{:S(2)}) collective-permute-start(bf16[2,64,1024]{2,1,0:T(8,128)(2,1)S(1)} %get-tuple-element.71), channel_id=1, source_target_pairs={{0,4},{8,12},{4,0},{12,8},{1,5},{9,13},{5,1},{13,9},{2,6},{10,14},... | collective-permute-start | bytes 786440 | tf_op jit(solution)/shard_map/ppermute | solution.py:461
  53.6 8.6 %collective-permute-start.12 = (bf16[2,64,1024]{2,1,0:T(8,128)(2,1)S(1)}, bf16[2,64,1024]{2,1,0:T(8,128)(2,1)S(1)}, u32[]{:S(2)}, u32[]{:S(2)}) collective-permute-start(bf16[2,64,1024]{2,1,0:T(8,128)(2,1)S(1)} %get-tuple-element.72), channel_id=1, source_target_pairs={{4,8},{8,4},{5,9},{9,5},{6,10},{10,6},{7,11},{11,7},{20,24},{24,20... | collective-permute-start | bytes 786440 | tf_op jit(solution)/shard_map/ppermute | solution.py:461
  62.2 9.1 %collective-permute-start.15 = (bf16[64,1024]{1,0:T(8,128)(2,1)S(1)}, bf16[64,1024]{1,0:T(8,128)(2,1)S(1)}, u32[]{:S(2)}, u32[]{:S(2)}) collective-permute-start(bf16[64,1024]{1,0:T(8,128)(2,1)S(1)} %add_convert_fusion.own_ref), channel_id=1, source_target_pairs={{0,20},{4,16},{8,28},{12,24},{16,4},{20,0},{24,12},{28,8},{1,21},{... | collective-permute-start | bytes 393224 | tf_op jit(solution)/shard_map/ppermute | solution.py:531
  67.7 5.8 %collective-permute-start.14 = (bf16[64,1024]{1,0:T(8,128)(2,1)S(1)}, bf16[64,1024]{1,0:T(8,128)(2,1)S(1)}, u32[]{:S(2)}, u32[]{:S(2)}) collective-permute-start(bf16[64,1024]{1,0:T(8,128)(2,1)S(1)} %add_convert_fusion.own_ref), channel_id=1, source_target_pairs={{0,16},{16,0},{1,17},{17,1},{2,18},{18,2},{3,19},{19,3},{4,20},{20... | collective-permute-start | bytes 393224 | tf_op jit(solution)/shard_map/ppermute | solution.py:466
  67.7 5.8 %collective-permute-start.13 = (bf16[64,1024]{1,0:T(8,128)(2,1)S(1)}, bf16[64,1024]{1,0:T(8,128)(2,1)S(1)}, u32[]{:S(2)}, u32[]{:S(2)}) collective-permute-start(bf16[64,1024]{1,0:T(8,128)(2,1)S(1)} %add_convert_fusion.own_ref), channel_id=1, source_target_pairs={{0,4},{4,0},{8,12},{12,8},{1,5},{5,1},{9,13},{13,9},{2,6},{6,2},{1... | collective-permute-start | bytes 393224 | tf_op jit(solution)/shard_map/ppermute | solution.py:466

commit v4 on v3

--- a/solution.py
+++ b/solution.py
@@ -99,9 +99,9 @@
 
 
 def prep_kernel(
-    x_hbm, cot_hbm, mask_hbm, all_ref, first_ref, second_ref, gb_ref, x_ref, cot_ref, mask_ref, sems
+    x_hbm, mask_hbm, all_ref, first_ref, second_ref, x_ref, mask_ref, sems
 ):
-    copies = load(((mask_hbm, mask_ref), (x_hbm, x_ref), (cot_hbm, cot_ref)), sems)
+    copies = load(((mask_hbm, mask_ref), (x_hbm, x_ref)), sems)
     copies[0].wait()
     ocean = token_mask(mask_ref[0].astype(F32))
     copies[1].wait()
@@ -115,11 +115,6 @@
     for c in range(2):
         first_ref[c] = jnp.where(odd, parts[c], parts[2 + c])
         second_ref[c] = jnp.where(odd, parts[2 + c], parts[c])
-    copies[2].wait()
-    cot = cot_ref[0].astype(F32)
-    for w in range(4):
-        rows = slice(w * AREA, (w + 1) * AREA)
-        gb_ref[w] = (window_of(cot, w) * ocean[rows]).astype(BF16)
 
 
 def land_bias(tokens):
@@ -152,10 +147,17 @@
 
 
 def own_kernel(
-    tok_ref, wqkv_hbm, gain_hbm, q_ref, kv_ref, hid_ref, bias_ref, info_ref, wqkv_ref, gain_ref, sems
+    tok_ref, cot_hbm, mask_hbm, wqkv_hbm, gain_hbm,
+    q_ref, kv_ref, hid_ref, gb_ref, bias_ref, info_ref, cot_ref, mask_ref, wqkv_ref, gain_ref, sems,
 ):
-    copies = load(((gain_hbm, gain_ref), (wqkv_hbm, wqkv_ref)), sems)
-    wait(copies)
+    pairs = ((mask_hbm, mask_ref), (cot_hbm, cot_ref), (gain_hbm, gain_ref), (wqkv_hbm, wqkv_ref))
+    copies = load(pairs, sems)
+    wait(copies[:2])
+    ocean = token_mask(mask_ref[0].astype(F32))
+    cot = cot_ref[0].astype(F32)
+    for w in range(4):
+        gb_ref[w] = (window_of(cot, w) * ocean[w * AREA : (w + 1) * AREA]).astype(BF16)
+    wait(copies[2:])
     tokens = tok_ref[...].reshape(4 * AREA, D)
     write_block(tokens, wqkv_ref, gain_ref, q_ref, kv_ref, hid_ref, bias_ref, info_ref)
 
@@ -190,10 +192,9 @@
 def main_kernel(
     pair, info_ref, infon_ref, q_own, q_near, kv_own, kv_near, hid_own, hid_near, bias_own,
     bias_near, gb_own, gb_near, first_ref, second_ref, wqkv_hbm, wout_hbm, gain_hbm,
-    mixed_ref, gq_ref, own_ref, back1_ref, back2_ref, *rest,
+    mixed, gq, dkv, hid, gb, back1_ref, back2_ref, *rest,
 ):
-    sums = rest[:-15]
-    q, kv, hid, gb, bias, gm, kcat, acc, dkv, mixed, gq, wkv_ref, wout_ref, gain_ref, sems = rest[-15:]
+    q, kv, bias, gm, kcat, acc, wkv_ref, wout_ref, gain_ref, sems = rest[-10:]
     pairs = [
         (gain_hbm, gain_ref), (wqkv_hbm.at[:, D:], wkv_ref), (wout_hbm, wout_ref),
         (gb_own, gb.at[:4]), (q_own, q.at[:4]), (kv_own, kv.at[:4]), (kv_near, kv.at[4:12]),
@@ -261,11 +262,21 @@
 
     lax.fori_loop(0, 3 * blocks_held, step, 0)
     dkv[...] = acc[...].astype(BF16)
-    own_ref[...] = dkv[:4]
-    gq_ref[...] = gq[:4]
-    mixed_ref[...] = mixed[:4]
-    back1_ref[:2] = dkv[8:10]
-    back2_ref[:2] = dkv[10:12]
+    shares = dot(dkv[8 if pair else 4 : 12 if pair else 16].reshape(-1, 2 * D), wkv_ref[...], 1, 1).astype(BF16)
+    shares = shares.reshape(-1, AREA, D)
+    if pair:
+        back1_ref[...] = shares[:2]
+        back2_ref[...] = shares[2:4]
+    else:
+        rest[0][...] = shares[:4]
+        for ref, at in ((back1_ref, 4), (back2_ref, 6)):
+            ref[:2] = shares[at : at + 2]
+            ref[2:] = shares[at + 4 : at + 6]
+
+
+def sums_kernel(pair, hid, dkv, gq, mixed, gb, keep, send):
+    held = 8 if pair else 4
+    gb_flat = gb[...].reshape(held * AREA, D)
     lev = lax.axis_index("lev")
 
     def columns(rel):
@@ -282,7 +293,6 @@
 
     gq_flat = gq[...].reshape(held * AREA, D)
     if pair:
-        keep, send = sums
         odd, lon = lax.axis_index("lat") % 2, lax.axis_index("lon")
 
         def put(rel, at, value):
@@ -304,10 +314,6 @@
                 put(rel, 0, dot(part, grad_part(0, D), 0, 0))
                 put(rel, D, dot(part, grad_part(D, D), 0, 0))
     else:
-        keep, send, side_ref = sums
-        side_ref[...] = dkv[4:8]
-        back1_ref[2:] = dkv[12:14]
-        back2_ref[2:] = dkv[14:]
         for rel in range(4):
             to = keep if rel % 2 == 0 else send
             to[rel // 2, :, :D] = dot(hid_part(rel, 4), gq_flat, 0, 0).astype(BF16)
@@ -321,32 +327,29 @@
         ref[...] = total.astype(ref.dtype)
 
 
-def input_kernel(
-    pair, own_ref, back1_ref, back2_ref, gq_ref, tok_ref, mixed_ref, *rest,
-):
+def input_kernel(pair, dkv, back1_ref, back2_ref, gq, tok_ref, mixed, *rest):
     refs = rest if pair else rest[1:]
     cot_hbm, x_hbm, mask_hbm, wqkv_hbm, wout_hbm, gain_hbm, out_ref, ing_ref = refs[:8]
-    gkv, cot_ref, x_ref, mask_ref, wqkv_ref, wout_ref, gain_ref, sems = refs[8:]
+    cot_ref, x_ref, mask_ref, wqkv_ref, wout_ref, gain_ref, sems = refs[8:]
     pairs = (
         (x_hbm, x_ref), (mask_hbm, mask_ref), (wout_hbm, wout_ref), (gain_hbm, gain_ref),
         (wqkv_hbm, wqkv_ref), (cot_hbm, cot_ref),
     )
     copies = load(pairs, sems)
     odd = lax.axis_index("lat") % 2 == 1
+    shares = []
     for w in range(4):
         one, two = back1_ref[w % 2].astype(F32), back2_ref[w % 2].astype(F32)
-        lat_part = jnp.where(odd, one, two) if w < 2 else jnp.where(odd, two, one)
-        total = own_ref[w].astype(F32) + lat_part
-        if not pair:
-            total = total + rest[0][w].astype(F32)
-        gkv[w * AREA : (w + 1) * AREA] = total.astype(BF16)
+        share = jnp.where(odd, one, two) if w < 2 else jnp.where(odd, two, one)
+        shares.append(share if pair else share + rest[0][w].astype(F32))
     normed, scaling = norm_rows(tok_ref[...].reshape(4 * AREA, D).astype(F32))
     wait(copies)
     ocean = token_mask(mask_ref[0].astype(F32))
-    added = (dot(mixed_ref[...].reshape(4 * AREA, D), wout_ref[...], 1, 0) * ocean).reshape(4, AREA, D)
+    added = (dot(mixed[:4].reshape(4 * AREA, D), wout_ref[...], 1, 0) * ocean).reshape(4, AREA, D)
     out_ref[0] = (x_ref[0].astype(F32) + grid_of([added[w] for w in range(4)])).astype(BF16)
-    grad_hidden = dot(gq_ref[...].reshape(4 * AREA, D), wqkv_ref[:, :D], 1, 1)
-    grad_hidden = grad_hidden + dot(gkv[...], wqkv_ref[:, D:], 1, 1)
+    grad_hidden = jnp.concatenate(shares, axis=0)
+    grad_hidden = grad_hidden + dot(gq[:4].reshape(4 * AREA, D), wqkv_ref[:, :D], 1, 1)
+    grad_hidden = grad_hidden + dot(dkv[:4].reshape(4 * AREA, 2 * D), wqkv_ref[:, D:], 1, 1)
     scaled = grad_hidden * gain_ref[...]
     correction = (
         scaled
@@ -520,13 +523,12 @@
     from_lat = swap(to_lat, "lat", 1)
     from_lev = swap(to_lev, "lev", 2)
     own = own + from_lev.astype(F32) + from_lat.astype(F32) + from_far.astype(F32)
-    own = own.astype(BF16)
+    return own.astype(BF16)
+
+
+def pair_spread(own):
     for bit in bits("lat")[1:]:
         own = (own.astype(F32) + swap(own, "lat", bit).astype(F32)).astype(BF16)
-    return own
-
-
-def pair_spread(own):
     count = lax.axis_size("lat")
     by_far = lax.ppermute(own, ("lon", "lat"), [(i, i ^ (count + 1)) for i in range(2 * count)])
     return own, swap(own, "lat", 1), swap(own, "lon", 1), by_far
@@ -544,27 +546,26 @@
     grid = vmem(*tokens_in.shape)
     mask = pltpu.VMEM(ocean_mask.shape, jnp.int32)
     weight, gains = vmem(*qkv_weight.shape), vmem32(1, D)
-    tok, tok_first, tok_second, gb = call(
-        "prep", prep_kernel, [four, half, half, four], [], [], [tokens_in, cotangent, ocean_mask],
-        [grid, grid, mask, DMAS((3,))], 8,
+    tok, tok_first, tok_second = call(
+        "prep", prep_kernel, [four, half, half], [], [], [tokens_in, ocean_mask],
+        [grid, mask, DMAS((2,))], 8,
     )
     tok_lon = lon_halo(tok)
     tok_first, tok_second = lat_swaps(tok_first, tok_second)
-    tok, tok_first, tok_second, gb = lax.optimization_barrier((tok, tok_first, tok_second, gb))
-    gb_near = lon_halo(gb) if pair else gb
-    q, kv, hid, bias, info = call(
+    q, kv, hid, gb, bias, info = call(
         "own", own_kernel,
-        [four, wide, shape((4 * AREA, D)), shape((4, 8, AREA), F32), info_shape],
-        [], [tok], [qkv_weight, gain], [weight, gains, DMAS((2,))], 16,
-        flops=2 * 256 * 512 * 1536, out_specs=[VMEM] * 4 + [SMEM],
-    )
-    tok_lon, hid = lax.optimization_barrier((tok_lon, hid))
+        [four, wide, shape((4 * AREA, D)), four, shape((4, 8, AREA), F32), info_shape],
+        [], [tok], [cotangent, ocean_mask, qkv_weight, gain], [grid, mask, weight, gains, DMAS((4,))], 16,
+        flops=2 * 256 * 512 * 1536, out_specs=[VMEM] * 5 + [SMEM],
+    )
+    tok_lon, tok_first, tok_second, gb = lax.optimization_barrier((tok_lon, tok_first, tok_second, gb))
     rows = tok_lon.reshape(2, 2, AREA, D)
     odd = lax.axis_index("lat") % 2
     corner_first, corner_second = lat_swaps(
         lax.dynamic_index_in_dim(rows, 1 - odd, 0, False),
         lax.dynamic_index_in_dim(rows, odd, 0, False),
     )
+    gb_near = lon_halo(gb) if pair else gb
     q_near, kv_near, hid_near, bias_near, info_near = call(
         "near", near_kernel,
         [four, shape((8, AREA, 2 * D)), shape((8 * AREA, D)), shape((8, 8, AREA), F32), info_shape],
@@ -572,42 +573,45 @@
         flops=2 * 512 * 512 * 1280, out_specs=[VMEM] * 4 + [SMEM],
     )
     held = 8 if pair else 4
-    back = shape((2 if pair else 4, AREA, 2 * D))
-    share = shape((2, 2, 64, 2 * D) if pair else (2, 128, 4 * D))
-    mixed, gq, own_kv, back_first, back_second, keep, send, *side = call(
+    back = shape((2 if pair else 4, AREA, D))
+    held_shape, all_shape = shape((held, AREA, D)), shape((16, AREA, 2 * D))
+    mixed, gq, dkv, hid_all, gb_all, back_first, back_second, *side = call(
         "main", lambda *refs: main_kernel(pair, *refs),
-        [four, four, wide, back, back, share, share] + ([] if pair else [wide]),
+        [held_shape, held_shape, all_shape, shape((16 * AREA, D)), held_shape, back, back]
+        + ([] if pair else [four]),
         [info, info_near],
         [q, q_near, kv, kv_near, hid, hid_near, bias, bias_near, gb, gb_near, corner_first, corner_second],
         [qkv_weight, out_weight, gain],
-        [vmem(held, AREA, D), vmem(16, AREA, 2 * D), vmem(16 * AREA, D), vmem(held, AREA, D),
-         vmem32(16, 8, AREA), vmem(held, AREA, D), vmem(KEYS, 2 * D), vmem32(16, AREA, 2 * D),
-         vmem(16, AREA, 2 * D), vmem(held, AREA, D), vmem(held, AREA, D), vmem(D, 2 * D),
-         vmem(D, D), gains, DMAS((13,))],
-        40, flops=3 * 16 * 2 * 512 * 256 * 256 + 2 * 1024 * 512 * 1024,
+        [vmem(held, AREA, D), vmem(16, AREA, 2 * D), vmem32(16, 8, AREA), vmem(held, AREA, D),
+         vmem(KEYS, 2 * D), vmem32(16, AREA, 2 * D), vmem(D, 2 * D), vmem(D, D), gains, DMAS((13,))],
+        36, flops=3 * 16 * 2 * 512 * 256 * 256,
+    )
+    back_first, back_second = lat_swaps(back_first, back_second)
+    share = shape((2, 2, 64, 2 * D) if pair else (2, 128, 4 * D))
+    keep, send = call(
+        "sums", lambda *refs: sums_kernel(pair, *refs), [share, share], [],
+        [hid_all, dkv, gq, mixed, gb_all], [], [], 24, flops=2 * 1024 * 512 * 1024,
     )
     if pair:
         total = pair_sum(keep, send)
-        back_first, back_second = lat_swaps(back_first, back_second)
         total, back_first, back_second = lax.optimization_barrier((total, back_first, back_second))
         sums = pair_spread(total)
-        lon_kv = []
+        lon_share = []
         finish = finish_pair_kernel
     else:
         part = gradient_sum(keep, send)
-        back_first, back_second = lat_swaps(back_first, back_second)
         one, two = back_first[2:].astype(F32), back_second[2:].astype(F32)
         rows = jnp.stack([jnp.where(odd == 1, one, two), jnp.where(odd == 1, two, one)])
-        side_kv = (side[0].reshape(rows.shape).astype(F32) + rows).astype(BF16)
-        lon_kv = [lon_return(side_kv.reshape(wide.shape))]
+        side = (side[0].reshape(rows.shape).astype(F32) + rows).astype(BF16)
+        lon_share = [lon_return(side.reshape(four.shape))]
         sums = plane_sum(part)
         finish = finish_rows_kernel
     layer_out, input_grad = call(
         "input", lambda *refs: input_kernel(pair, *refs),
         [shape(tokens_in.shape), shape(tokens_in.shape)], [],
-        [own_kv, back_first, back_second, gq, tok, mixed] + lon_kv,
+        [dkv, back_first, back_second, gq, tok, mixed] + lon_share,
         [cotangent, tokens_in, ocean_mask, qkv_weight, out_weight, gain],
-        [vmem(4 * AREA, 2 * D), grid, grid, mask, weight, vmem(D, D), gains, DMAS((6,))],
+        [grid, grid, mask, weight, vmem(D, D), gains, DMAS((6,))],
         24, flops=2 * 256 * 512 * 1536,
     )
     qkv_grad, out_grad, gain_grad = call(

time: 75.4 us -> 72.8 us (0.966)
  waiting for transfers between devices: 22.8 us -> 16.9 us
  local copies, waits for them, and re-layouts: 4.74 us -> 8.29 us
    ppermute x6, waiting for transfers between devices: 14.8 us -> 9.53 us  [swap(): lax.ppermute(value, axis, [(i, i ^ bit) for i in range(lax.axis_size(axis...]
    ppermute x6, starting transfers between devices: 7.08 us -> 11.6 us  [swap(): lax.ppermute(value, axis, [(i, i ^ bit) for i in range(lax.axis_size(axis...]
    ppermute x1, starting transfers between devices: 5.45 us -> 1.41 us  [pair_spread(): lax.ppermute(own, ('lon', 'lat'), [(i, i ^ count + 1) for i in range(2 *...]
    ppermute x6, waiting for transfers between devices: 5.28 us -> 1.4 us  [lat_swaps(): swaps.append(lax.ppermute(value, 'lat', pairs + [(b, a) for a, b in pairs]))]
    unnamed x22 -> x36, local copies, waits for them, and re-layouts: 4.71 us -> 8.27 us
    ppermute x1, waiting for transfers between devices: 1.81 us -> 4.29 us  [pair_sum(): lax.ppermute(to_far, ('lat', 'lev'), [(i, i ^ 6) for i in range(4 * count)])]
    ppermute x6, starting transfers between devices: 13.6 us -> 11.4 us  [lat_swaps(): swaps.append(lax.ppermute(value, 'lat', pairs + [(b, a) for a, b in pairs]))]
    ppermute x1, starting transfers between devices: 0.01 us -> 1.39 us  [pair_sum(): lax.ppermute(to_far, ('lat', 'lev'), [(i, i ^ 6) for i in range(4 * count)])]
  transfers between devices with their start and end apart: 16 -> 16, of which waited for: 9 -> 9; matrix products, arithmetic and copies ran while one was open for 0% -> 0% of each run, Pallas kernels for 7% -> 8%
where the time goes in v4:
time: 72.8 us; the launch traced here: 72.2 us
  starting transfers between devices  29.4 us (40%)
  waiting for transfers between devices  16.9 us (23%)
  Pallas kernels  16.7 us (23%)
  local copies, waits for them, and re-layouts  8.29 us (11%)
  between operations  0.82 us (1%)
    pallas_call x8, Pallas kernels, call(): pl.pallas_call(kernel, out_shape=outs, in_specs=[SMEM] * len(scalars) + [...  16.7 us
    ppermute x6, starting transfers between devices, swap(): lax.ppermute(value, axis, [(i, i ^ bit) for i in range(lax.axis_size(axis...  11.6 us
    ppermute x6, starting transfers between devices, lat_swaps(): swaps.append(lax.ppermute(value, 'lat', pairs + [(b, a) for a, b in pairs]))  11.4 us
    ppermute x6, waiting for transfers between devices, swap(): lax.ppermute(value, axis, [(i, i ^ bit) for i in range(lax.axis_size(axis...  9.53 us
    unnamed x36, local copies, waits for them, and re-layouts  8.27 us
    ppermute x1, waiting for transfers between devices, pair_sum(): lax.ppermute(to_far, ('lat', 'lev'), [(i, i ^ 6) for i in range(4 * count)])  4.29 us
    ppermute x2, starting transfers between devices, lon_halo(): return lax.ppermute(own, 'lon', [(0, 1), (1, 0)])  3.54 us
    ppermute x1, waiting for transfers between devices, pair_spread(): lax.ppermute(own, ('lon', 'lat'), [(i, i ^ count + 1) for i in range(2 *...  1.67 us
  transfers between devices with their start and end apart: 16, of which 9 were waited for; matrix products, arithmetic and copies ran while one was open for 0% of the time, Pallas kernels for 8%

profile of v4, /device:TPU:0, one launch (start us, length us, event | category | flops | bytes accessed | tf_op | source)
XLA Modules:
  0.0 72.2 jit_solution(9327145652809115089)
XLA Ops:
  0.6 0.0 copy-start.4
  0.6 0.9 %copy-done.4 = bf16[1,16,16,512]{3,2,1,0:T(8,128)(2,1)S(1)} copy-done((bf16[1,16,16,512]{3,2,1,0:T(8,128)(2,1)S(1)}, bf16[1,16,16,512]{3,2,1,0:T(8,128)(2,1)}, u32[]{:S(2)}) %copy-start.4) | copy-done | bytes 262168
  1.6 0.7 copy-done.7
  2.3 0.4 prep.1
  2.6 3.0 %collective-permute-start = (bf16[4,64,512]{2,1,0:T(8,128)(2,1)S(1)}, bf16[4,64,512]{2,1,0:T(8,128)(2,1)S(1)}, u32[]{:S(2)}, u32[]{:S(2)}) collective-permute-start(bf16[4,64,512]{2,1,0:T(8,128)(2,1)S(1)} %get-tuple-element.44.tok_ref.refs_4_), channel_id=1, source_target_pairs={{0,16},{16,0},{1,17},{17,1},{2,18},{18,2},{3,19},{19,3},{4,20},{20... | collective-permute-start | bytes 786440 | tf_op jit(solution)/shard_map/ppermute | solution.py:444
  5.7 1.6 %collective-permute-start.1 = (bf16[2,64,512]{2,1,0:T(8,128)(2,1)S(1)}, bf16[2,64,512]{2,1,0:T(8,128)(2,1)S(1)}, u32[]{:S(2)}, u32[]{:S(2)}) collective-permute-start(bf16[2,64,512]{2,1,0:T(8,128)(2,1)S(1)} %get-tuple-element.46), channel_id=1, source_target_pairs={{0,4},{8,12},{4,0},{12,8},{1,5},{9,13},{5,1},{13,9},{2,6},{10,14},... | collective-permute-start | bytes 393224 | tf_op jit(solution)/shard_map/ppermute | solution.py:464
  7.2 0.7 collective-permute-start.2
  7.9 0.0 copy-start
  7.9 1.4 %copy-done = bf16[512,1536]{1,0:T(8,128)(2,1)S(1)} copy-done((bf16[512,1536]{1,0:T(8,128)(2,1)S(1)}, bf16[512,1536]{1,0:T(8,128)(2,1)}, u32[]{:S(2)}) %copy-start) | copy-done | bytes 1572888
  9.3 0.9 %copy-done.2 = bf16[1,16,16,512]{3,2,1,0:T(8,128)(2,1)S(1)} copy-done((bf16[1,16,16,512]{3,2,1,0:T(8,128)(2,1)S(1)}, bf16[1,16,16,512]{3,2,1,0:T(8,128)(2,1)}, u32[]{:S(2)}) %copy-start.2) | copy-done | bytes 262168
  10.3 0.7 copy-done.8
  11.0 0.7 copy-done.10
  11.6 1.9 %own.1 = (bf16[4,64,512]{2,1,0:T(8,128)(2,1)S(1)}, bf16[4,64,1024]{2,1,0:T(8,128)(2,1)S(1)}, bf16[256,512]{1,0:T(8,128)(2,1)S(1)}, bf16[4,64,512]{2,1,0:T(8,128)...) custom-call(bf16[4,64,512]{2,1,0:T(8,128)(2,1)S(1)} %get-tuple-element.44.tok_ref.refs_4_, ...), custom_call_target="tpu_custom_call" | custom-call | flops 402653184 | bytes 3419168 | tf_op jit(solution)/shard_map/own/pallas_call | solution.py:419
  13.6 0.0 copy-start.12
  13.6 0.7 copy-done.12
  14.3 0.6 copy-done.16
  14.9 0.0 collective-permute-done.1.first_ref
  14.9 0.0 collective-permute-done.2.second_ref
  14.9 0.7 copy-done.14
  15.5 0.0 collective-permute-done.lon_ref
  15.5 0.5 collective-permute-start.3
  16.1 0.8 %collective-permute-start.5 = (bf16[2,64,512]{2,1,0:T(8,128)(2,1)S(1)}, bf16[2,64,512]{2,1,0:T(8,128)(2,1)S(1)}, u32[]{:S(2)}, u32[]{:S(2)}) collective-permute-start(bf16[2,64,512]{2,1,0:T(8,128)(2,1)S(1)} %get-tuple-element.83), channel_id=1, source_target_pairs={{4,8},{8,4},{5,9},{9,5},{6,10},{10,6},{7,11},{11,7},{20,24},{24,20... | collective-permute-start | bytes 393224 | tf_op jit(solution)/shard_map/ppermute | solution.py:464
  16.9 5.7 %collective-permute-start.4 = (bf16[2,64,512]{2,1,0:T(8,128)(2,1)S(1)}, bf16[2,64,512]{2,1,0:T(8,128)(2,1)S(1)}, u32[]{:S(2)}, u32[]{:S(2)}) collective-permute-start(bf16[2,64,512]{2,1,0:T(8,128)(2,1)S(1)} %get-tuple-element.84), channel_id=1, source_target_pairs={{0,4},{8,12},{4,0},{12,8},{1,5},{9,13},{5,1},{13,9},{2,6},{10,14},... | collective-permute-start | bytes 393224 | tf_op jit(solution)/shard_map/ppermute | solution.py:464
  22.6 0.0 copy-done.11
  22.6 0.0 copy-done.1
  22.6 0.9 %copy-done.15 = bf16[2,64,512]{2,1,0:T(8,128)(2,1)S(1)} copy-done((bf16[2,64,512]{2,1,0:T(8,128)(2,1)S(1)}, bf16[2,64,512]{2,1,0:T(8,128)(2,1)}, u32[]{:S(2)}) %copy-start.15) | copy-done | bytes 131096
  23.5 1.7 %near.1 = (bf16[4,64,512]{2,1,0:T(8,128)(2,1)S(1)}, bf16[8,64,1024]{2,1,0:T(8,128)(2,1)S(1)}, bf16[512,512]{1,0:T(8,128)(2,1)S(1)}, f32[8,8,64]{2,1,0:T(8,128)S(1)}, s32[8]{0:T(128)S(1)}) custom-call(bf16[4,64,512]{2,1,0:T(8,128)(2,1)S(1)} %collective-permute-done.lon_ref, bf16[2,64,512]{2,1,0:T(8,128)(2,1)S(1)} %collective-permute-done.1.first_ref, ...), custom_call_target="tpu_custom_call" | custom-call | flops 671088640 | bytes 3950624 | tf_op jit(solution)/shard_map/near/pallas_call | solution.py:419
  25.2 0.0 collective-permute-done.5.refs_13_
  25.3 0.3 collective-permute-done.4.refs_12_
  25.6 0.0 collective-permute-done.3.refs_11_
  25.6 0.0 copy-done.6
  25.6 0.0 copy-done.13
  25.6 0.0 copy-done.17
  25.6 8.2 %main.1 = (bf16[8,64,512]{2,1,0:T(8,128)(2,1)S(1)}, bf16[8,64,512]{2,1,0:T(8,128)(2,1)S(1)}, bf16[16,64,1024]{2,1,0:T(8,128)(2,1)S(1)}, bf16[1024,512]{1,0:T(8,1...) custom-call(s32[8]{0:T(128)S(1)} %get-tuple-element.45.refs_0_, ...), custom_call_target="tpu_custom_call" | custom-call | flops 3221225472 | bytes 10774528 | tf_op jit(solution)/shard_map/main/pallas_call | solution.py:419
  33.7 0.8 %sums.1 = (bf16[2,2,64,1024]{3,2,1,0:T(8,128)(2,1)S(1)}, bf16[2,2,64,1024]{3,2,1,0:T(8,128)(2,1)S(1)}) custom-call(bf16[1024,512]{1,0:T(8,128)(2,1)S(1)} %get-tuple-element.63.refs_0_, bf16[16,64,1024]{2,1,0:T(8,128)(2,1)S(1)} %get-tuple-element.62.refs_1_.refs_0_, bf16[8,64,512]{2,1,0:T(8,128)(2,1)S(1)} %get-tuple-element.64.refs_2_.refs_3_, ...), custom_call_target="tpu_custom_call" | custom-call | flops 1073741824 | bytes 5767168 | tf_op jit(solution)/shard_map/sums/pallas_call | solution.py:419
  34.6 0.0 copy-start.3
  34.6 0.0 copy-start.5
  34.6 0.0 copy-start.9
  34.6 1.0 %collective-permute-start.6 = (bf16[2,2,64,1024]{3,2,1,0:T(8,128)(2,1)S(1)}, bf16[2,2,64,1024]{3,2,1,0:T(8,128)(2,1)S(1)}, u32[]{:S(2)}, u32[]{:S(2)}) collective-permute-start(bf16[2,2,64,1024]{3,2,1,0:T(8,128)(2,1)S(1)} %get-tuple-element.68), channel_id=1, source_target_pairs={{0,1},{1,0},{2,3},{3,2},{4,5},{5,4},{6,7},{7,6},{8,9},{9,8},{10,11... | collective-permute-start | bytes 1572872 | tf_op jit(solution)/shard_map/ppermute | solution.py:469
  35.6 1.5 %collective-permute-done.6.come_ref = bf16[2,2,64,1024]{3,2,1,0:T(8,128)(2,1)S(1)} collective-permute-done((bf16[2,2,64,1024]{3,2,1,0:T(8,128)(2,1)S(1)}, bf16[2,2,64,1024]{3,2,1,0:T(8,128)(2,1)S(1)}, u32[]{:S(2)}, u32[]{:S(2)}) %collective-permute-start.6) | collective-permute-done | bytes 524320 | tf_op jit(solution)/shard_map/ppermute | solution.py:469
  37.1 0.1 split.1
  37.2 1.1 %collective-permute-start.7 = (bf16[64,1024]{1,0:T(8,128)(2,1)S(1)}, bf16[64,1024]{1,0:T(8,128)(2,1)S(1)}, u32[]{:S(2)}, u32[]{:S(2)}) collective-permute-start(bf16[64,1024]{1,0:T(8,128)(2,1)S(1)} %get-tuple-element.70), channel_id=1, source_target_pairs={{0,2},{1,3},{2,0},{3,1},{4,6},{5,7},{6,4},{7,5},{8,10},{9,11},{10,... | collective-permute-start | bytes 393224 | tf_op jit(solution)/shard_map/ppermute | solution.py:469
  38.3 2.3 %collective-permute-start.8 = (bf16[64,1024]{1,0:T(8,128)(2,1)S(1)}, bf16[64,1024]{1,0:T(8,128)(2,1)S(1)}, u32[]{:S(2)}, u32[]{:S(2)}) collective-permute-start(bf16[64,1024]{1,0:T(8,128)(2,1)S(1)} %get-tuple-element.71), channel_id=1, source_target_pairs={{0,4},{4,0},{8,12},{12,8},{1,5},{5,1},{9,13},{13,9},{2,6},{6,2},{1... | collective-permute-start | bytes 393224 | tf_op jit(solution)/shard_map/ppermute | solution.py:469
  40.6 1.4 %collective-permute-start.9 = (bf16[64,1024]{1,0:T(8,128)(2,1)S(1)}, bf16[64,1024]{1,0:T(8,128)(2,1)S(1)}, u32[]{:S(2)}, u32[]{:S(2)}) collective-permute-start(bf16[64,1024]{1,0:T(8,128)(2,1)S(1)} %get-tuple-element.72), channel_id=1, source_target_pairs={{0,6},{1,7},{2,4},{3,5},{4,2},{5,3},{6,0},{7,1},{8,14},{9,15},{10,... | collective-permute-start | bytes 393224 | tf_op jit(solution)/shard_map/ppermute | solution.py:522
  42.0 2.0 %collective-permute-start.10 = (bf16[2,64,512]{2,1,0:T(8,128)(2,1)S(1)}, bf16[2,64,512]{2,1,0:T(8,128)(2,1)S(1)}, u32[]{:S(2)}, u32[]{:S(2)}) collective-permute-start(bf16[2,64,512]{2,1,0:T(8,128)(2,1)S(1)} %get-tuple-element.73), channel_id=1, source_target_pairs={{0,4},{8,12},{4,0},{12,8},{1,5},{9,13},{5,1},{13,9},{2,6},{10,14},... | collective-permute-start | bytes 393224 | tf_op jit(solution)/shard_map/ppermute | solution.py:464
  44.0 0.7 collective-permute-start.11
  44.7 0.0 collective-permute-done.7
  44.7 0.1 collective-permute-done.8
  44.8 4.3 %collective-permute-done.9 = bf16[64,1024]{1,0:T(8,128)(2,1)S(1)} collective-permute-done((bf16[64,1024]{1,0:T(8,128)(2,1)S(1)}, bf16[64,1024]{1,0:T(8,128)(2,1)S(1)}, u32[]{:S(2)}, u32[]{:S(2)}) %collective-permute-start.9) | collective-permute-done | bytes 131104 | tf_op jit(solution)/shard_map/ppermute | solution.py:522
  49.1 0.1 add_convert_fusion.1
  49.2 1.1 %collective-permute-done.10.refs_1_ = bf16[2,64,512]{2,1,0:T(8,128)(2,1)S(1)} collective-permute-done((bf16[2,64,512]{2,1,0:T(8,128)(2,1)S(1)}, bf16[2,64,512]{2,1,0:T(8,128)(2,1)S(1)}, u32[]{:S(2)}, u32[]{:S(2)}) %collective-permute-start.10) | collective-permute-done | bytes 131104 | tf_op jit(solution)/shard_map/ppermute | solution.py:464
  50.2 0.0 collective-permute-done.11.refs_2_
  50.3 5.1 %collective-permute-start.12 = (bf16[64,1024]{1,0:T(8,128)(2,1)S(1)}, bf16[64,1024]{1,0:T(8,128)(2,1)S(1)}, u32[]{:S(2)}, u32[]{:S(2)}) collective-permute-start(bf16[64,1024]{1,0:T(8,128)(2,1)S(1)} %add_convert_fusion.1), channel_id=1, source_target_pairs={{0,8},{4,12},{8,0},{12,4},{1,9},{5,13},{9,1},{13,5},{2,10},{6,14},... | collective-permute-start | bytes 393224 | tf_op jit(solution)/shard_map/ppermute | solution.py:469
  55.4 5.5 %collective-permute-done.12 = bf16[64,1024]{1,0:T(8,128)(2,1)S(1)} collective-permute-done((bf16[64,1024]{1,0:T(8,128)(2,1)S(1)}, bf16[64,1024]{1,0:T(8,128)(2,1)S(1)}, u32[]{:S(2)}, u32[]{:S(2)}) %collective-permute-start.12) | collective-permute-done | bytes 131104 | tf_op jit(solution)/shard_map/ppermute | solution.py:469
  60.9 1.4 %collective-permute-start.15 = (bf16[64,1024]{1,0:T(8,128)(2,1)S(1)}, bf16[64,1024]{1,0:T(8,128)(2,1)S(1)}, u32[]{:S(2)}, u32[]{:S(2)}) collective-permute-start(bf16[64,1024]{1,0:T(8,128)(2,1)S(1)} %add_convert_fusion.own_ref), channel_id=1, source_target_pairs={{0,20},{4,16},{8,28},{12,24},{16,4},{20,0},{24,12},{28,8},{1,21},{... | collective-permute-start | bytes 393224 | tf_op jit(solution)/shard_map/ppermute | solution.py:533
  62.3 0.8 %collective-permute-start.14 = (bf16[64,1024]{1,0:T(8,128)(2,1)S(1)}, bf16[64,1024]{1,0:T(8,128)(2,1)S(1)}, u32[]{:S(2)}, u32[]{:S(2)}) collective-permute-start(bf16[64,1024]{1,0:T(8,128)(2,1)S(1)} %add_convert_fusion.own_ref), channel_id=1, source_target_pairs={{0,16},{16,0},{1,17},{17,1},{2,18},{18,2},{3,19},{19,3},{4,20},{20... | collective-permute-start | bytes 393224 | tf_op jit(solution)/shard_map/ppermute | solution.py:469
  63.1 1.4 %collective-permute-start.13 = (bf16[64,1024]{1,0:T(8,128)(2,1)S(1)}, bf16[64,1024]{1,0:T(8,128)(2,1)S(1)}, u32[]{:S(2)}, u32[]{:S(2)}) collective-permute-start(bf16[64,1024]{1,0:T(8,128)(2,1)S(1)} %add_convert_fusion.own_ref), channel_id=1, source_target_pairs={{0,4},{4,0},{8,12},{12,8},{1,5},{5,1},{9,13},{13,9},{2,6},{6,2},{1... | collective-permute-start | bytes 393224 | tf_op jit(solution)/shard_map/ppermute | solution.py:469
  64.5 0.0 copy-done.3
  64.5 0.0 copy-done.5
  64.5 2.1 %input.1 = (bf16[1,16,16,512]{3,2,1,0:T(8,128)(2,1)}, bf16[1,16,16,512]{3,2,1,0:T(8,128)(2,1)}) custom-call(bf16[16,64,1024]{2,1,0:T(8,128)(2,1)S(1)} %get-tuple-element.62.refs_1_.refs_0_, bf16[2,64,512]{2,1,0:T(8,128)(2,1)S(1)} %collective-permute-done.10.refs_1_, bf16[2,64,512]{2,1,0:T(8,128)(2,1)S(1)} %collective-permute-done.11.refs_2_, ...), custom_call_target="tpu_custom_call" | custom-call | flops 402653184 | bytes 6818816 | tf_op jit(solution)/shard_map/input/pallas_call | solution.py:419
  66.6 1.7 %collective-permute-done.15.far_ref = bf16[64,1024]{1,0:T(8,128)(2,1)S(1)} collective-permute-done((bf16[64,1024]{1,0:T(8,128)(2,1)S(1)}, bf16[64,1024]{1,0:T(8,128)(2,1)S(1)}, u32[]{:S(2)}, u32[]{:S(2)}) %collective-permute-start.15) | collective-permute-done | bytes 131104 | tf_op jit(solution)/shard_map/ppermute | solution.py:533
  68.2 1.3 %collective-permute-done.14.lon_ref = bf16[64,1024]{1,0:T(8,128)(2,1)S(1)} collective-permute-done((bf16[64,1024]{1,0:T(8,128)(2,1)S(1)}, bf16[64,1024]{1,0:T(8,128)(2,1)S(1)}, u32[]{:S(2)}, u32[]{:S(2)}) %collective-permute-start.14) | collective-permute-done | bytes 131104 | tf_op jit(solution)/shard_map/ppermute | solution.py:469
  69.5 1.1 %collective-permute-done.13.lat_ref = bf16[64,1024]{1,0:T(8,128)(2,1)S(1)} collective-permute-done((bf16[64,1024]{1,0:T(8,128)(2,1)S(1)}, bf16[64,1024]{1,0:T(8,128)(2,1)S(1)}, u32[]{:S(2)}, u32[]{:S(2)}) %collective-permute-start.13) | collective-permute-done | bytes 131104 | tf_op jit(solution)/shard_map/ppermute | solution.py:469
  70.7 1.6 %finish.1 = (f32[128,1536]{1,0:T(8,128)}, f32[128,512]{1,0:T(8,128)}, f32[1,128]{1,0:T(1,128)}) custom-call(bf16[64,1024]{1,0:T(8,128)(2,1)S(1)} %add_convert_fusion.own_ref, bf16[64,1024]{1,0:T(8,128)(2,1)S(1)} %collective-permute-done.13.lat_ref, bf16[64,1024]{1,0:T(8,128)(2,1)S(1)} %collective-permute-done.14.lon_ref, ...), custom_call_target="tpu_custom_call" | custom-call | bytes 3148288 | tf_op jit(solution)/shard_map/finish/pallas_call | solution.py:419
  (15 shorter events, 0.1 us)
Async XLA Ops:
  0.6 1.0 %copy-start.4 = (bf16[1,16,16,512]{3,2,1,0:T(8,128)(2,1)S(1)}, bf16[1,16,16,512]{3,2,1,0:T(8,128)(2,1)}, u32[]{:S(2)}) copy-start(bf16[1,16,16,512]{3,2,1,0:T(8,128)(2,1)} %refs_7_.1) | copy-start | bytes 786436
  1.6 0.7 copy-start.7
  2.3 20.3 %copy-start.11 = (f32[512]{0:T(512)S(1)}, f32[512]{0:T(512)}, u32[]{:S(2)}) copy-start(f32[512]{0:T(512)} %param.10) | copy-start | bytes 6148
  2.6 12.9 %collective-permute-start = (bf16[4,64,512]{2,1,0:T(8,128)(2,1)S(1)}, bf16[4,64,512]{2,1,0:T(8,128)(2,1)S(1)}, u32[]{:S(2)}, u32[]{:S(2)}) collective-permute-start(bf16[4,64,512]{2,1,0:T(8,128)(2,1)S(1)} %get-tuple-element.44.tok_ref.refs_4_), channel_id=1, source_target_pairs={{0,16},{16,0},{1,17},{17,1},{2,18},{18,2},{3,19},{19,3},{4,20},{20... | collective-permute-start | bytes 786440 | tf_op jit(solution)/shard_map/ppermute | solution.py:444
  5.7 9.2 %collective-permute-start.1 = (bf16[2,64,512]{2,1,0:T(8,128)(2,1)S(1)}, bf16[2,64,512]{2,1,0:T(8,128)(2,1)S(1)}, u32[]{:S(2)}, u32[]{:S(2)}) collective-permute-start(bf16[2,64,512]{2,1,0:T(8,128)(2,1)S(1)} %get-tuple-element.46), channel_id=1, source_target_pairs={{0,4},{8,12},{4,0},{12,8},{1,5},{9,13},{5,1},{13,9},{2,6},{10,14},... | collective-permute-start | bytes 393224 | tf_op jit(solution)/shard_map/ppermute | solution.py:464
  7.2 7.6 %collective-permute-start.2 = (bf16[2,64,512]{2,1,0:T(8,128)(2,1)S(1)}, bf16[2,64,512]{2,1,0:T(8,128)(2,1)S(1)}, u32[]{:S(2)}, u32[]{:S(2)}) collective-permute-start(bf16[2,64,512]{2,1,0:T(8,128)(2,1)S(1)} %get-tuple-element.47), channel_id=1, source_target_pairs={{4,8},{8,4},{5,9},{9,5},{6,10},{10,6},{7,11},{11,7},{20,24},{24,20... | collective-permute-start | bytes 393224 | tf_op jit(solution)/shard_map/ppermute | solution.py:464
  7.9 1.4 %copy-start = (bf16[512,1536]{1,0:T(8,128)(2,1)S(1)}, bf16[512,1536]{1,0:T(8,128)(2,1)}, u32[]{:S(2)}) copy-start(bf16[512,1536]{1,0:T(8,128)(2,1)} %wqkv_hbm.5) | copy-start | bytes 4718596
  9.3 0.9 %copy-start.2 = (bf16[1,16,16,512]{3,2,1,0:T(8,128)(2,1)S(1)}, bf16[1,16,16,512]{3,2,1,0:T(8,128)(2,1)}, u32[]{:S(2)}) copy-start(bf16[1,16,16,512]{3,2,1,0:T(8,128)(2,1)} %refs_6_.1) | copy-start | bytes 786436
  10.3 0.7 copy-start.8
  11.0 0.7 copy-start.10
  11.6 11.0 %copy-start.1 = (bf16[512,1536]{1,0:T(8,128)(2,1)S(1)}, bf16[512,1536]{1,0:T(8,128)(2,1)}, u32[]{:S(2)}) copy-start(bf16[512,1536]{1,0:T(8,128)(2,1)} %wqkv_hbm.5) | copy-start | bytes 4718596
  11.6 13.9 %copy-start.6 = (bf16[512,512]{1,0:T(8,128)(2,1)S(1)}, bf16[512,512]{1,0:T(8,128)(2,1)}, u32[]{:S(2)}) copy-start(bf16[512,512]{1,0:T(8,128)(2,1)} %refs_10_.1) | copy-start | bytes 1572868
  13.6 0.7 copy-start.12
  14.3 0.6 copy-start.16
  14.9 0.7 copy-start.14
  15.5 10.0 %collective-permute-start.3 = (bf16[4,64,512]{2,1,0:T(8,128)(2,1)}, bf16[4,64,512]{2,1,0:T(8,128)(2,1)}, u32[]{:S(2)}, u32[]{:S(2)}) collective-permute-start(bf16[4,64,512]{2,1,0:T(8,128)(2,1)} %get-tuple-element.61.refs_10_), channel_id=1, source_target_pairs={{0,16},{16,0},{1,17},{17,1},{2,18},{18,2},{3,19},{19,3},{4,20},{20... | collective-permute-start | bytes 786440 | tf_op jit(solution)/shard_map/ppermute | solution.py:444
  16.1 9.5 %copy-start.13 = (bf16[256,512]{1,0:T(8,128)(2,1)S(1)}, bf16[256,512]{1,0:T(8,128)(2,1)}, u32[]{:S(2)}) copy-start(bf16[256,512]{1,0:T(8,128)(2,1)} %copy-done.12) | copy-start | bytes 786436
  16.1 9.5 %copy-start.17 = (f32[4,8,64]{2,1,0:T(8,128)S(1)}, f32[4,8,64]{2,1,0:T(8,128)}, u32[]{:S(2)}) copy-start(f32[4,8,64]{2,1,0:T(8,128)} %copy-done.16) | copy-start | bytes 24580
  16.1 9.2 %collective-permute-start.5 = (bf16[2,64,512]{2,1,0:T(8,128)(2,1)S(1)}, bf16[2,64,512]{2,1,0:T(8,128)(2,1)S(1)}, u32[]{:S(2)}, u32[]{:S(2)}) collective-permute-start(bf16[2,64,512]{2,1,0:T(8,128)(2,1)S(1)} %get-tuple-element.83), channel_id=1, source_target_pairs={{4,8},{8,4},{5,9},{9,5},{6,10},{10,6},{7,11},{11,7},{20,24},{24,20... | collective-permute-start | bytes 393224 | tf_op jit(solution)/shard_map/ppermute | solution.py:464
  16.9 8.7 %collective-permute-start.4 = (bf16[2,64,512]{2,1,0:T(8,128)(2,1)S(1)}, bf16[2,64,512]{2,1,0:T(8,128)(2,1)S(1)}, u32[]{:S(2)}, u32[]{:S(2)}) collective-permute-start(bf16[2,64,512]{2,1,0:T(8,128)(2,1)S(1)} %get-tuple-element.84), channel_id=1, source_target_pairs={{0,4},{8,12},{4,0},{12,8},{1,5},{9,13},{5,1},{13,9},{2,6},{10,14},... | collective-permute-start | bytes 393224 | tf_op jit(solution)/shard_map/ppermute | solution.py:464
  22.6 0.9 %copy-start.15 = (bf16[2,64,512]{2,1,0:T(8,128)(2,1)S(1)}, bf16[2,64,512]{2,1,0:T(8,128)(2,1)}, u32[]{:S(2)}) copy-start(bf16[2,64,512]{2,1,0:T(8,128)(2,1)} %copy-done.14) | copy-start | bytes 393220
  34.6 29.9 %copy-start.3 = (bf16[1,16,16,512]{3,2,1,0:T(8,128)(2,1)S(1)}, bf16[1,16,16,512]{3,2,1,0:T(8,128)(2,1)}, u32[]{:S(2)}) copy-start(bf16[1,16,16,512]{3,2,1,0:T(8,128)(2,1)} %refs_6_.1) | copy-start | bytes 786436
  34.6 29.9 %copy-start.5 = (bf16[1,16,16,512]{3,2,1,0:T(8,128)(2,1)S(1)}, bf16[1,16,16,512]{3,2,1,0:T(8,128)(2,1)}, u32[]{:S(2)}) copy-start(bf16[1,16,16,512]{3,2,1,0:T(8,128)(2,1)} %refs_7_.1) | copy-start | bytes 786436
  34.6 29.9 %copy-start.9 = (s32[1,16,16]{2,1,0:T(8,128)S(1)}, s32[1,16,16]{2,1,0:T(8,128)}, u32[]{:S(2)}) copy-start(s32[1,16,16]{2,1,0:T(8,128)} %refs_8_.1) | copy-start | bytes 3076
  34.6 2.5 %collective-permute-start.6 = (bf16[2,2,64,1024]{3,2,1,0:T(8,128)(2,1)S(1)}, bf16[2,2,64,1024]{3,2,1,0:T(8,128)(2,1)S(1)}, u32[]{:S(2)}, u32[]{:S(2)}) collective-permute-start(bf16[2,2,64,1024]{3,2,1,0:T(8,128)(2,1)S(1)} %get-tuple-element.68), channel_id=1, source_target_pairs={{0,1},{1,0},{2,3},{3,2},{4,5},{5,4},{6,7},{7,6},{8,9},{9,8},{10,11... | collective-permute-start | bytes 1572872 | tf_op jit(solution)/shard_map/ppermute | solution.py:469
  37.2 7.4 %collective-permute-start.7 = (bf16[64,1024]{1,0:T(8,128)(2,1)S(1)}, bf16[64,1024]{1,0:T(8,128)(2,1)S(1)}, u32[]{:S(2)}, u32[]{:S(2)}) collective-permute-start(bf16[64,1024]{1,0:T(8,128)(2,1)S(1)} %get-tuple-element.70), channel_id=1, source_target_pairs={{0,2},{1,3},{2,0},{3,1},{4,6},{5,7},{6,4},{7,5},{8,10},{9,11},{10,... | collective-permute-start | bytes 393224 | tf_op jit(solution)/shard_map/ppermute | solution.py:469
  38.3 6.5 %collective-permute-start.8 = (bf16[64,1024]{1,0:T(8,128)(2,1)S(1)}, bf16[64,1024]{1,0:T(8,128)(2,1)S(1)}, u32[]{:S(2)}, u32[]{:S(2)}) collective-permute-start(bf16[64,1024]{1,0:T(8,128)(2,1)S(1)} %get-tuple-element.71), channel_id=1, source_target_pairs={{0,4},{4,0},{8,12},{12,8},{1,5},{5,1},{9,13},{13,9},{2,6},{6,2},{1... | collective-permute-start | bytes 393224 | tf_op jit(solution)/shard_map/ppermute | solution.py:469
  40.6 8.5 %collective-permute-start.9 = (bf16[64,1024]{1,0:T(8,128)(2,1)S(1)}, bf16[64,1024]{1,0:T(8,128)(2,1)S(1)}, u32[]{:S(2)}, u32[]{:S(2)}) collective-permute-start(bf16[64,1024]{1,0:T(8,128)(2,1)S(1)} %get-tuple-element.72), channel_id=1, source_target_pairs={{0,6},{1,7},{2,4},{3,5},{4,2},{5,3},{6,0},{7,1},{8,14},{9,15},{10,... | collective-permute-start | bytes 393224 | tf_op jit(solution)/shard_map/ppermute | solution.py:522
  42.0 8.3 %collective-permute-start.10 = (bf16[2,64,512]{2,1,0:T(8,128)(2,1)S(1)}, bf16[2,64,512]{2,1,0:T(8,128)(2,1)S(1)}, u32[]{:S(2)}, u32[]{:S(2)}) collective-permute-start(bf16[2,64,512]{2,1,0:T(8,128)(2,1)S(1)} %get-tuple-element.73), channel_id=1, source_target_pairs={{0,4},{8,12},{4,0},{12,8},{1,5},{9,13},{5,1},{13,9},{2,6},{10,14},... | collective-permute-start | bytes 393224 | tf_op jit(solution)/shard_map/ppermute | solution.py:464
  44.0 6.2 %collective-permute-start.11 = (bf16[2,64,512]{2,1,0:T(8,128)(2,1)S(1)}, bf16[2,64,512]{2,1,0:T(8,128)(2,1)S(1)}, u32[]{:S(2)}, u32[]{:S(2)}) collective-permute-start(bf16[2,64,512]{2,1,0:T(8,128)(2,1)S(1)} %get-tuple-element.74), channel_id=1, source_target_pairs={{4,8},{8,4},{5,9},{9,5},{6,10},{10,6},{7,11},{11,7},{20,24},{24,20... | collective-permute-start | bytes 393224 | tf_op jit(solution)/shard_map/ppermute | solution.py:464
  50.3 10.6 %collective-permute-start.12 = (bf16[64,1024]{1,0:T(8,128)(2,1)S(1)}, bf16[64,1024]{1,0:T(8,128)(2,1)S(1)}, u32[]{:S(2)}, u32[]{:S(2)}) collective-permute-start(bf16[64,1024]{1,0:T(8,128)(2,1)S(1)} %add_convert_fusion.1), channel_id=1, source_target_pairs={{0,8},{4,12},{8,0},{12,4},{1,9},{5,13},{9,1},{13,5},{2,10},{6,14},... | collective-permute-start | bytes 393224 | tf_op jit(solution)/shard_map/ppermute | solution.py:469
  60.9 7.3 %collective-permute-start.15 = (bf16[64,1024]{1,0:T(8,128)(2,1)S(1)}, bf16[64,1024]{1,0:T(8,128)(2,1)S(1)}, u32[]{:S(2)}, u32[]{:S(2)}) collective-permute-start(bf16[64,1024]{1,0:T(8,128)(2,1)S(1)} %add_convert_fusion.own_ref), channel_id=1, source_target_pairs={{0,20},{4,16},{8,28},{12,24},{16,4},{20,0},{24,12},{28,8},{1,21},{... | collective-permute-start | bytes 393224 | tf_op jit(solution)/shard_map/ppermute | solution.py:533
  62.3 7.2 %collective-permute-start.14 = (bf16[64,1024]{1,0:T(8,128)(2,1)S(1)}, bf16[64,1024]{1,0:T(8,128)(2,1)S(1)}, u32[]{:S(2)}, u32[]{:S(2)}) collective-permute-start(bf16[64,1024]{1,0:T(8,128)(2,1)S(1)} %add_convert_fusion.own_ref), channel_id=1, source_target_pairs={{0,16},{16,0},{1,17},{17,1},{2,18},{18,2},{3,19},{19,3},{4,20},{20... | collective-permute-start | bytes 393224 | tf_op jit(solution)/shard_map/ppermute | solution.py:469
  63.1 7.6 %collective-permute-start.13 = (bf16[64,1024]{1,0:T(8,128)(2,1)S(1)}, bf16[64,1024]{1,0:T(8,128)(2,1)S(1)}, u32[]{:S(2)}, u32[]{:S(2)}) collective-permute-start(bf16[64,1024]{1,0:T(8,128)(2,1)S(1)} %add_convert_fusion.own_ref), channel_id=1, source_target_pairs={{0,4},{4,0},{8,12},{12,8},{1,5},{5,1},{9,13},{13,9},{2,6},{6,2},{1... | collective-permute-start | bytes 393224 | tf_op jit(solution)/shard_map/ppermute | solution.py:469

commit v5 on v4

--- a/solution.py
+++ b/solution.py
@@ -147,19 +147,24 @@
 
 
 def own_kernel(
-    tok_ref, cot_hbm, mask_hbm, wqkv_hbm, gain_hbm,
-    q_ref, kv_ref, hid_ref, gb_ref, bias_ref, info_ref, cot_ref, mask_ref, wqkv_ref, gain_ref, sems,
+    tok_ref, cot_hbm, mask_hbm, wqkv_hbm, wout_hbm, gain_hbm,
+    q_ref, kv_ref, hid_ref, gb_ref, bias_ref, wqkv_ref, wout_ref, gain_ref, info_ref,
+    cot_ref, mask_ref, sems,
 ):
-    pairs = ((mask_hbm, mask_ref), (cot_hbm, cot_ref), (gain_hbm, gain_ref), (wqkv_hbm, wqkv_ref))
+    pairs = (
+        (mask_hbm, mask_ref), (cot_hbm, cot_ref), (gain_hbm, gain_ref), (wqkv_hbm, wqkv_ref),
+        (wout_hbm, wout_ref),
+    )
     copies = load(pairs, sems)
     wait(copies[:2])
     ocean = token_mask(mask_ref[0].astype(F32))
     cot = cot_ref[0].astype(F32)
     for w in range(4):
         gb_ref[w] = (window_of(cot, w) * ocean[w * AREA : (w + 1) * AREA]).astype(BF16)
-    wait(copies[2:])
+    wait(copies[2:4])
     tokens = tok_ref[...].reshape(4 * AREA, D)
     write_block(tokens, wqkv_ref, gain_ref, q_ref, kv_ref, hid_ref, bias_ref, info_ref)
+    wait(copies[4:])
 
 
 def lat_block(first_ref, second_ref, wkv_ref, gain_ref, kv_ref, hid_ref, bias_ref, at):
@@ -180,58 +185,59 @@
 
 
 def near_kernel(
-    lon_ref, first_ref, second_ref, wqkv_hbm, gain_hbm,
-    q_ref, kv_ref, hid_ref, bias_ref, info_ref, wqkv_ref, gain_ref, sems,
+    lon_ref, first_ref, second_ref, wqkv_ref, gain_ref, q_ref, kv_ref, hid_ref, bias_ref, info_ref
 ):
-    wait(load(((gain_hbm, gain_ref), (wqkv_hbm, wqkv_ref)), sems))
     tokens = lon_ref[...].reshape(4 * AREA, D)
     write_block(tokens, wqkv_ref, gain_ref, q_ref, kv_ref, hid_ref, bias_ref, info_ref)
     lat_block(first_ref, second_ref, wqkv_ref.at[:, D:], gain_ref, kv_ref, hid_ref, bias_ref, 4)
 
 
-def main_kernel(
-    pair, info_ref, infon_ref, q_own, q_near, kv_own, kv_near, hid_own, hid_near, bias_own,
-    bias_near, gb_own, gb_near, first_ref, second_ref, wqkv_hbm, wout_hbm, gain_hbm,
-    mixed, gq, dkv, hid, gb, back1_ref, back2_ref, *rest,
-):
-    q, kv, bias, gm, kcat, acc, wkv_ref, wout_ref, gain_ref, sems = rest[-10:]
-    pairs = [
-        (gain_hbm, gain_ref), (wqkv_hbm.at[:, D:], wkv_ref), (wout_hbm, wout_ref),
-        (gb_own, gb.at[:4]), (q_own, q.at[:4]), (kv_own, kv.at[:4]), (kv_near, kv.at[4:12]),
-        (hid_own, hid.at[: 4 * AREA]), (hid_near, hid.at[4 * AREA : 12 * AREA]),
-        (bias_own, bias.at[:4]), (bias_near, bias.at[4:12]),
-    ]
-    if pair:
-        pairs += [(q_near, q.at[4:]), (gb_near, gb.at[4:])]
-    copies = load(pairs, sems)
-    acc[...] = jnp.zeros_like(acc)
+def main_kernel(block, last, *refs):
+    refs = list(refs)
+    take = lambda n: [refs.pop(0) for _ in range(n)]
+    info_ref, infon_ref = take(2)
+    wqkv_ref, wout_ref, gain_ref, q, gb = take(5)
+    if block == 0:
+        first_ref, second_ref, kv_own, kv_near, hid_own, hid_near, bias_own, bias_near = take(8)
+    else:
+        kv, bias, _ = take(3)
+    acc, mixed, gq = take(3)
+    if block == 0:
+        hid, kv, bias = take(3)
+    if last:
+        dkv, back1_ref, back2_ref = take(3)
+        side_ref = None if block else take(1)[0]
+    gm, kcat, *sems = refs
+    wkv_ref = wqkv_ref.at[:, D:]
+    if block == 0:
+        pairs = (
+            (kv_own, kv.at[:4]), (kv_near, kv.at[4:12]),
+            (hid_own, hid.at[: 4 * AREA]), (hid_near, hid.at[4 * AREA : 12 * AREA]),
+            (bias_own, bias.at[:4]), (bias_near, bias.at[4:12]),
+        )
+        copies = load(pairs, sems[0])
+        acc[...] = jnp.zeros_like(acc)
+        lat_block(first_ref, second_ref, wkv_ref, gain_ref, kv, hid, bias, 12)
+        wait(copies)
     mixed[...] = jnp.zeros_like(mixed)
     gq[...] = jnp.zeros_like(gq)
     blocks = head_blocks()
-    wait(copies[:2])
-    lat_block(first_ref, second_ref, wkv_ref, gain_ref, kv, hid, bias, 12)
-    wait(copies[2:])
-    blocks_held = 2 if pair else 1
-    held = 4 * blocks_held
-    gb_flat = gb[...].reshape(held * AREA, D)
-    gm[...] = dot(gb_flat, wout_ref[...], 1, 1).astype(BF16).reshape(gm.shape)
-
-    def window_at(b, slot):
-        left_out = jnp.where(b == 0, info_ref[0], infon_ref[0])
-        return slot + (slot >= left_out).astype(jnp.int32)
-
-    def step(n, carry):
-        b = n // 3
-        w = window_at(b, n % 3)
-
-        @pl.when(jnp.where(b == 0, info_ref[1 + w], infon_ref[1 + w]) > 0)
+    gm[...] = dot(gb[...].reshape(4 * AREA, D), wout_ref[...], 1, 1).astype(BF16).reshape(gm.shape)
+    info = infon_ref if block else info_ref
+
+    def window_at(slot):
+        return slot + (slot >= info[0]).astype(jnp.int32)
+
+    def step(slot, carry):
+        at = window_at(slot)
+
+        @pl.when(info[1 + at] > 0)
         def _():
-            r, c = w // 2, w % 2
-            mine, other, side = 4 * b, 4 * (1 - b), 2 * lat_side(r)
-            places = [mine + window_at(b, k) for k in range(3)]
+            r, c = at // 2, at % 2
+            mine, other, side = 4 * block, 4 * (1 - block), 2 * lat_side(r)
+            places = [mine + window_at(k) for k in range(3)]
             places += [other + 1 - c, other + 3 - c]
             places += [8 + mine + side, 9 + mine + side, 8 + other + side + 1 - c]
-            at = mine + w
             for k in range(8):
                 kcat[k * AREA : (k + 1) * AREA] = kv[places[k]]
             bias_row = jnp.concatenate([bias[place][:1] for place in places], axis=1)
@@ -260,38 +266,47 @@
 
         return carry
 
-    lax.fori_loop(0, 3 * blocks_held, step, 0)
+    lax.fori_loop(0, 3, step, 0)
+    if not last:
+        return
     dkv[...] = acc[...].astype(BF16)
-    shares = dot(dkv[8 if pair else 4 : 12 if pair else 16].reshape(-1, 2 * D), wkv_ref[...], 1, 1).astype(BF16)
-    shares = shares.reshape(-1, AREA, D)
-    if pair:
+    near = dkv[8:12] if block else dkv[4:]
+    shares = dot(near.reshape(-1, 2 * D), wkv_ref[...], 1, 1).astype(BF16).reshape(-1, AREA, D)
+    if block:
         back1_ref[...] = shares[:2]
         back2_ref[...] = shares[2:4]
     else:
-        rest[0][...] = shares[:4]
+        side_ref[...] = shares[:4]
         for ref, at in ((back1_ref, 4), (back2_ref, 6)):
             ref[:2] = shares[at : at + 2]
             ref[2:] = shares[at + 4 : at + 6]
 
 
-def sums_kernel(pair, hid, dkv, gq, mixed, gb, keep, send):
-    held = 8 if pair else 4
-    gb_flat = gb[...].reshape(held * AREA, D)
+def sums_kernel(pair, hid, dkv, *refs):
+    held = [refs[k : k + 3] for k in range(0, len(refs) - 2, 3)]
+    keep, send = refs[-2:]
+    flat = lambda ref: ref[...].reshape(4 * AREA, D)
     lev = lax.axis_index("lev")
 
     def columns(rel):
         return pl.ds(pl.multiple_of((lev ^ rel) * 128, 128), 128)
 
-    def hid_part(rel, windows):
-        return hid[: windows * AREA, columns(rel)]
-
-    def mix_part(rel):
-        return mixed[:, :, columns(rel)].reshape(held * AREA, 128)
-
     def grad_part(at, width):
         return dkv[:, :, at : at + width].reshape(16 * AREA, width)
 
-    gq_flat = gq[...].reshape(held * AREA, D)
+    def query_sum(rel):
+        parts = [
+            dot(hid[4 * b * AREA : 4 * (b + 1) * AREA, columns(rel)], flat(gq), 0, 0)
+            for b, (gq, _, _) in enumerate(held)
+        ]
+        return sum(parts[1:], parts[0])
+
+    def out_sum(rel):
+        parts = [
+            dot(mixed[:, :, columns(rel)].reshape(4 * AREA, 128), flat(gb), 0, 0) for _, mixed, gb in held
+        ]
+        return sum(parts[1:], parts[0])
+
     if pair:
         odd, lon = lax.axis_index("lat") % 2, lax.axis_index("lon")
 
@@ -304,21 +319,21 @@
         @pl.when(lon == 0)
         def _():
             for rel in range(4):
-                put(rel, 0, dot(hid_part(rel, 8), gq_flat, 0, 0))
-                put(rel, D, dot(mix_part(rel), gb_flat, 0, 0))
+                put(rel, 0, query_sum(rel))
+                put(rel, D, out_sum(rel))
 
         @pl.when(lon == 1)
         def _():
             for rel in range(4):
-                part = hid_part(rel, 16)
+                part = hid[:, columns(rel)]
                 put(rel, 0, dot(part, grad_part(0, D), 0, 0))
                 put(rel, D, dot(part, grad_part(D, D), 0, 0))
     else:
         for rel in range(4):
             to = keep if rel % 2 == 0 else send
-            to[rel // 2, :, :D] = dot(hid_part(rel, 4), gq_flat, 0, 0).astype(BF16)
-            to[rel // 2, :, D : 2 * D] = dot(mix_part(rel), gb_flat, 0, 0).astype(BF16)
-            to[rel // 2, :, 2 * D :] = dot(hid_part(rel, 16), grad_part(0, 2 * D), 0, 0).astype(BF16)
+            to[rel // 2, :, :D] = query_sum(rel).astype(BF16)
+            to[rel // 2, :, D : 2 * D] = out_sum(rel).astype(BF16)
+            to[rel // 2, :, 2 * D :] = dot(hid[:, columns(rel)], grad_part(0, 2 * D), 0, 0).astype(BF16)
 
 
 def split_kernel(keep_ref, come_ref, own_ref, lev_ref, lat_ref, far_ref):
@@ -329,13 +344,9 @@
 
 def input_kernel(pair, dkv, back1_ref, back2_ref, gq, tok_ref, mixed, *rest):
     refs = rest if pair else rest[1:]
-    cot_hbm, x_hbm, mask_hbm, wqkv_hbm, wout_hbm, gain_hbm, out_ref, ing_ref = refs[:8]
-    cot_ref, x_ref, mask_ref, wqkv_ref, wout_ref, gain_ref, sems = refs[8:]
-    pairs = (
-        (x_hbm, x_ref), (mask_hbm, mask_ref), (wout_hbm, wout_ref), (gain_hbm, gain_ref),
-        (wqkv_hbm, wqkv_ref), (cot_hbm, cot_ref),
-    )
-    copies = load(pairs, sems)
+    wqkv_ref, wout_ref, gain_ref, cot_hbm, x_hbm, mask_hbm, out_ref, ing_ref = refs[:8]
+    cot_ref, x_ref, mask_ref, sems = refs[8:]
+    copies = load(((x_hbm, x_ref), (mask_hbm, mask_ref), (cot_hbm, cot_ref)), sems)
     odd = lax.axis_index("lat") % 2 == 1
     shares = []
     for w in range(4):
@@ -360,21 +371,15 @@
     ing_ref[0] = (cot_ref[0].astype(F32) + grid_of([added[w] for w in range(4)])).astype(BF16)
 
 
-def gain_row(rows_ref, gain_ref, qkv_ref):
+def gain_row(wqkv_ref, gain_ref, qkv_ref):
     at = pl.ds(pl.multiple_of(lax.axis_index("lev") * 128, 128), 128)
-    product = rows_ref[...].astype(F32) * qkv_ref[...]
+    product = wqkv_ref[at, :].astype(F32) * qkv_ref[...]
     return dot(jnp.ones((8, 3 * D), F32), product, 1, 1, EXACT)[:1] / gain_ref[:, at]
 
 
-def load_rows(wqkv_hbm, rows_ref, gain_hbm, gain_ref, sems):
-    at = pl.ds(pl.multiple_of(lax.axis_index("lev") * 128, 128), 128)
-    return load(((wqkv_hbm.at[at, :], rows_ref), (gain_hbm, gain_ref)), sems)
-
-
 def finish_rows_kernel(
-    own_ref, far_ref, wqkv_hbm, gain_hbm, qkv_ref, out_ref, gg_ref, rows_ref, gain_ref, sems
+    own_ref, far_ref, wqkv_ref, gain_ref, qkv_ref, out_ref, gg_ref
 ):
-    copies = load_rows(wqkv_hbm, rows_ref, gain_hbm, gain_ref, sems)
     half = own_ref.shape[0]
     first = lax.axis_index("lon") % 2 == 0
     own, far = own_ref[...], far_ref[...]
@@ -384,15 +389,12 @@
         qkv_ref[rows, :D] = value[:, :D]
         qkv_ref[rows, D:] = value[:, 2 * D :]
         out_ref[rows] = value[:, D : 2 * D]
-    wait(copies)
-    gg_ref[...] = gain_row(rows_ref, gain_ref, qkv_ref)
+    gg_ref[...] = gain_row(wqkv_ref, gain_ref, qkv_ref)
 
 
 def finish_pair_kernel(
-    own_ref, lat_ref, lon_ref, far_ref, wqkv_hbm, gain_hbm, qkv_ref, out_ref, gg_ref,
-    rows_ref, gain_ref, sems,
+    own_ref, lat_ref, lon_ref, far_ref, wqkv_ref, gain_ref, qkv_ref, out_ref, gg_ref
 ):
-    copies = load_rows(wqkv_hbm, rows_ref, gain_hbm, gain_ref, sems)
     odd = lax.axis_index("lat") % 2 == 1
     first = lax.axis_index("lon") == 0
     for k in range(2):
@@ -404,28 +406,32 @@
         qkv_ref[rows, :D] = low[:, :D]
         out_ref[rows] = low[:, D:]
         qkv_ref[rows, D:] = high
-    wait(copies)
-    gg_ref[...] = gain_row(rows_ref, gain_ref, qkv_ref)
+    gg_ref[...] = gain_row(wqkv_ref, gain_ref, qkv_ref)
 
 
 SMEM = pl.BlockSpec(memory_space=pltpu.SMEM)
 VMEM = pl.BlockSpec(memory_space=pltpu.VMEM)
 ANY = pl.BlockSpec(memory_space=pl.ANY)
+HBM = pl.BlockSpec(memory_space=pltpu.HBM)
 DMAS = pltpu.SemaphoreType.DMA
 
 
-def call(name, kernel, outs, scalars, arrays, far, scratch, mebibytes, flops=0, out_specs=None):
-    moved = sum(a.size * a.dtype.itemsize for a in (*arrays, *far, *outs))
+def call(
+    name, kernel, outs, scalars, arrays, loose, far, scratch, mebibytes, flops=0, out_specs=None, aliases=None
+):
+    moved = sum(a.size * a.dtype.itemsize for a in (*arrays, *loose, *far, *outs))
+    specs = [SMEM] * len(scalars) + [VMEM] * len(arrays) + [ANY] * len(loose) + [HBM] * len(far)
     return pl.pallas_call(
         kernel,
         out_shape=outs,
-        in_specs=[SMEM] * len(scalars) + [VMEM] * len(arrays) + [ANY] * len(far),
+        in_specs=specs,
         out_specs=out_specs or [VMEM] * len(outs),
         scratch_shapes=list(scratch),
+        input_output_aliases=aliases or {},
         compiler_params=pltpu.CompilerParams(vmem_limit_bytes=mebibytes * 1024 * 1024),
         cost_estimate=pl.CostEstimate(flops=flops, bytes_accessed=moved, transcendentals=0),
         name=name,
-    )(*scalars, *arrays, *far)
+    )(*scalars, *arrays, *loose, *far)
 
 
 def shape(dims, dtype=BF16):
@@ -456,13 +462,20 @@
     return jnp.stack([from_left, from_right], axis=1).reshape(side.shape)
 
 
+def lat_swap(value, start):
+    pairs = [(i, i + 1) for i in range(start, lax.axis_size("lat") - 1, 2)]
+    return lax.ppermute(value, "lat", pairs + [(b, a) for a, b in pairs])
+
+
 def lat_swaps(first, second):
+    return lat_swap(first, 0), lat_swap(second, 1)
+
+
+def corner_swap(value, start):
     count = lax.axis_size("lat")
-    swaps = []
-    for start, value in ((0, first), (1, second)):
-        pairs = [(i, i + 1) for i in range(start, count - 1, 2)]
-        swaps.append(lax.ppermute(value, "lat", pairs + [(b, a) for a, b in pairs]))
-    return swaps
+    pairs = [(i, i + 1) for i in range(start, count - 1, 2)]
+    pairs = [(a + k * count, b + (1 - k) * count) for a, b in pairs for k in range(2)]
+    return lax.ppermute(value, ("lon", "lat"), pairs + [(b, a) for a, b in pairs])
 
 
 def swap(value, axis, bit):
@@ -517,7 +530,7 @@
     come = swap(send, "lev", 1)
     piece = shape(keep.shape[2:])
     own, to_lev, to_lat, to_far = call(
-        "split", split_kernel, [shape(piece.shape, F32), piece, piece, piece], [], [keep, come], [], [], 8
+        "split", split_kernel, [shape(piece.shape, F32), piece, piece, piece], [], [keep, come], [], [], [], 8
     )
     from_far = lax.ppermute(to_far, ("lat", "lev"), [(i, i ^ 6) for i in range(4 * count)])
     from_lat = swap(to_lat, "lat", 1)
@@ -526,9 +539,13 @@
     return own.astype(BF16)
 
 
-def pair_spread(own):
+def lat_sum(own):
     for bit in bits("lat")[1:]:
         own = (own.astype(F32) + swap(own, "lat", bit).astype(F32)).astype(BF16)
+    return own
+
+
+def pair_spread(own):
     count = lax.axis_size("lat")
     by_far = lax.ppermute(own, ("lon", "lat"), [(i, i ^ (count + 1)) for i in range(2 * count)])
     return own, swap(own, "lat", 1), swap(own, "lon", 1), by_far
@@ -542,64 +559,78 @@
     wide = shape((4, AREA, 2 * D))
     info_shape = shape((8,), jnp.int32)
     vmem = lambda *dims: pltpu.VMEM(dims, BF16)
-    vmem32 = lambda *dims: pltpu.VMEM(dims, F32)
     grid = vmem(*tokens_in.shape)
     mask = pltpu.VMEM(ocean_mask.shape, jnp.int32)
-    weight, gains = vmem(*qkv_weight.shape), vmem32(1, D)
     tok, tok_first, tok_second = call(
-        "prep", prep_kernel, [four, half, half], [], [], [tokens_in, ocean_mask],
-        [grid, mask, DMAS((2,))], 8,
+        "prep", prep_kernel, [four, half, half], [], [], [], [tokens_in, ocean_mask],
+        [grid, mask, DMAS((2,))], 8, flops=10 ** 10,
     )
     tok_lon = lon_halo(tok)
+    odd = lax.axis_index("lat") % 2
+    if pair:
+        corner_first, corner_second = corner_swap(tok_first, 0), corner_swap(tok_second, 1)
     tok_first, tok_second = lat_swaps(tok_first, tok_second)
-    q, kv, hid, gb, bias, info = call(
+    q, kv, hid, gb, bias, wqkv, wout, gain, info = call(
         "own", own_kernel,
-        [four, wide, shape((4 * AREA, D)), four, shape((4, 8, AREA), F32), info_shape],
-        [], [tok], [cotangent, ocean_mask, qkv_weight, gain], [grid, mask, weight, gains, DMAS((4,))], 16,
-        flops=2 * 256 * 512 * 1536, out_specs=[VMEM] * 5 + [SMEM],
-    )
-    tok_lon, tok_first, tok_second, gb = lax.optimization_barrier((tok_lon, tok_first, tok_second, gb))
-    rows = tok_lon.reshape(2, 2, AREA, D)
-    odd = lax.axis_index("lat") % 2
-    corner_first, corner_second = lat_swaps(
-        lax.dynamic_index_in_dim(rows, 1 - odd, 0, False),
-        lax.dynamic_index_in_dim(rows, odd, 0, False),
-    )
-    gb_near = lon_halo(gb) if pair else gb
+        [four, wide, shape((4 * AREA, D)), four, shape((4, 8, AREA), F32), shape(qkv_weight.shape),
+         shape(out_weight.shape), shape(gain.shape, F32), info_shape],
+        [], [tok], [], [cotangent, ocean_mask, qkv_weight, out_weight, gain], [grid, mask, DMAS((5,))], 16,
+        flops=2 * 256 * 512 * 1536, out_specs=[VMEM] * 8 + [SMEM],
+    )
+    if pair:
+        gb_near = lon_halo(gb)
+    else:
+        rows = tok_lon.reshape(2, 2, AREA, D)
+        corner_first, corner_second = lat_swaps(
+            lax.dynamic_index_in_dim(rows, 1 - odd, 0, False),
+            lax.dynamic_index_in_dim(rows, odd, 0, False),
+        )
     q_near, kv_near, hid_near, bias_near, info_near = call(
         "near", near_kernel,
         [four, shape((8, AREA, 2 * D)), shape((8 * AREA, D)), shape((8, 8, AREA), F32), info_shape],
-        [], [tok_lon, tok_first, tok_second], [qkv_weight, gain], [weight, gains, DMAS((2,))], 20,
+        [], [tok_lon, tok_first, tok_second, wqkv, gain], [], [], [], 20,
         flops=2 * 512 * 512 * 1280, out_specs=[VMEM] * 4 + [SMEM],
     )
-    held = 8 if pair else 4
+    all_shape, all32 = shape((16, AREA, 2 * D)), shape((16, AREA, 2 * D), F32)
     back = shape((2 if pair else 4, AREA, D))
-    held_shape, all_shape = shape((held, AREA, D)), shape((16, AREA, 2 * D))
-    mixed, gq, dkv, hid_all, gb_all, back_first, back_second, *side = call(
-        "main", lambda *refs: main_kernel(pair, *refs),
-        [held_shape, held_shape, all_shape, shape((16 * AREA, D)), held_shape, back, back]
-        + ([] if pair else [four]),
-        [info, info_near],
-        [q, q_near, kv, kv_near, hid, hid_near, bias, bias_near, gb, gb_near, corner_first, corner_second],
-        [qkv_weight, out_weight, gain],
-        [vmem(held, AREA, D), vmem(16, AREA, 2 * D), vmem32(16, 8, AREA), vmem(held, AREA, D),
-         vmem(KEYS, 2 * D), vmem32(16, AREA, 2 * D), vmem(D, 2 * D), vmem(D, D), gains, DMAS((13,))],
-        36, flops=3 * 16 * 2 * 512 * 256 * 256,
-    )
-    back_first, back_second = lat_swaps(back_first, back_second)
+    ends = [all_shape, back, back] + ([] if pair else [four])
+    weights = [wqkv, wout, gain]
+    scratch = [vmem(4, AREA, D), vmem(KEYS, 2 * D)]
+    flops = 3 * 12 * 2 * 512 * 256 * 256
+    acc, mixed, gq, hid_all, kv_all, bias_all, *rest = call(
+        "main", lambda *refs: main_kernel(0, not pair, *refs),
+        [all32, four, four, shape((16 * AREA, D)), all_shape, shape((16, 8, AREA), F32)]
+        + ([] if pair else ends),
+        [info, info_near], weights + [q, gb, corner_first, corner_second],
+        [kv, kv_near, hid, hid_near, bias, bias_near], [], scratch + [DMAS((6,))], 28, flops=flops,
+    )
+    parts = [gq, mixed, gb]
+    if pair:
+        _, mixed_near, gq_near, *rest = call(
+            "other", lambda *refs: main_kernel(1, True, *refs), [all32, four, four] + ends,
+            [info, info_near], weights + [q_near, gb_near, kv_all, bias_all, acc], [], [],
+            scratch, 28, flops=flops, aliases={9: 0},
+        )
+        parts += [gq_near, mixed_near, gb_near]
+    dkv, back_first, back_second, *side = rest
     share = shape((2, 2, 64, 2 * D) if pair else (2, 128, 4 * D))
     keep, send = call(
         "sums", lambda *refs: sums_kernel(pair, *refs), [share, share], [],
-        [hid_all, dkv, gq, mixed, gb_all], [], [], 24, flops=2 * 1024 * 512 * 1024,
+        [hid_all, dkv] + parts, [], [], [], 24, flops=2 * 1024 * 512 * 1024,
     )
     if pair:
         total = pair_sum(keep, send)
+        back_second = lat_swap(back_second, 1)
         total, back_first, back_second = lax.optimization_barrier((total, back_first, back_second))
+        back_first = lat_swap(back_first, 0)
+        total = lat_sum(total)
+        total, back_first = lax.optimization_barrier((total, back_first))
         sums = pair_spread(total)
         lon_share = []
         finish = finish_pair_kernel
     else:
         part = gradient_sum(keep, send)
+        back_first, back_second = lat_swaps(back_first, back_second)
         one, two = back_first[2:].astype(F32), back_second[2:].astype(F32)
         rows = jnp.stack([jnp.where(odd == 1, one, two), jnp.where(odd == 1, two, one)])
         side = (side[0].reshape(rows.shape).astype(F32) + rows).astype(BF16)
@@ -609,15 +640,13 @@
     layer_out, input_grad = call(
         "input", lambda *refs: input_kernel(pair, *refs),
         [shape(tokens_in.shape), shape(tokens_in.shape)], [],
-        [dkv, back_first, back_second, gq, tok, mixed] + lon_share,
-        [cotangent, tokens_in, ocean_mask, qkv_weight, out_weight, gain],
-        [grid, grid, mask, weight, vmem(D, D), gains, DMAS((6,))],
-        24, flops=2 * 256 * 512 * 1536,
+        [dkv, back_first, back_second, gq, tok, mixed] + lon_share + weights, [],
+        [cotangent, tokens_in, ocean_mask], [grid, grid, mask, DMAS((3,))], 24, flops=2 * 256 * 512 * 1536,
     )
     qkv_grad, out_grad, gain_grad = call(
         "finish", finish,
         [shape((128, 3 * D), F32), shape((128, D), F32), shape((1, 128), F32)], [],
-        list(sums), [qkv_weight, gain], [vmem(128, 3 * D), gains, DMAS((2,))], 16,
+        [*sums, wqkv, gain], [], [], [], 16,
     )
     return layer_out, input_grad, qkv_grad, out_grad, gain_grad.reshape(128)
 

time: 72.8 us -> 63.5 us (0.87); the launches traced: 72.2 us -> 64 us
  local copies, waits for them, and re-layouts: 8.29 us -> 1.74 us
  starting transfers between devices: 29.4 us -> 25.5 us
  Pallas kernels: 16.7 us -> 20.4 us
  waiting for transfers between devices: 16.9 us -> 15.4 us
    unnamed x36 -> x16, local copies, waits for them, and re-layouts: 8.27 us -> 1.74 us
    ppermute x6, starting transfers between devices: 11.6 us -> 7.48 us  [swap(): lax.ppermute(value, axis, [(i, i ^ bit) for i in range(lax.axis_size(axis...]
    pallas_call x8 -> x9, Pallas kernels: 16.7 us -> 20.4 us  [call(): pl.pallas_call(kernel, out_shape=outs, in_specs=specs, out_specs=out_spec...]
    ppermute x6, starting transfers between devices: 11.4 us -> 7.98 us  [the longest x2 5.09 us: corner_swap(): lax.ppermute(value, ('lon', 'lat'), pairs + [(b, a) for a, b in pairs])]
    ppermute x1, starting transfers between devices: 1.41 us -> 3.67 us  [pair_spread(): lax.ppermute(own, ('lon', 'lat'), [(i, i ^ count + 1) for i in range(2 *...]
    ppermute x6, waiting for transfers between devices: 9.53 us -> 11.2 us  [swap(): lax.ppermute(value, axis, [(i, i ^ bit) for i in range(lax.axis_size(axis...]
    ppermute x1, waiting for transfers between devices: 4.29 us -> 3.11 us  [pair_sum(): lax.ppermute(to_far, ('lat', 'lev'), [(i, i ^ 6) for i in range(4 * count)])]
    ppermute x1, waiting for transfers between devices: 1.67 us -> 0.5 us  [pair_spread(): lax.ppermute(own, ('lon', 'lat'), [(i, i ^ count + 1) for i in range(2 *...]
  transfers between devices with their start and end apart: 16 -> 16, of which waited for: 9 -> 9; matrix products, arithmetic and copies ran while one was open for 0% -> 0% of each run, Pallas kernels for 8% -> 19%
where the time goes in v5:
time: 63.5 us; the launch traced here: 64 us
  starting transfers between devices  25.5 us (40%)
  Pallas kernels  20.4 us (32%)
  waiting for transfers between devices  15.4 us (24%)
  local copies, waits for them, and re-layouts  1.74 us (3%)
  between operations  0.86 us (1%)
    pallas_call x9, Pallas kernels, call(): pl.pallas_call(kernel, out_shape=outs, in_specs=specs, out_specs=out_spec...  20.4 us
    ppermute x6, waiting for transfers between devices, swap(): lax.ppermute(value, axis, [(i, i ^ bit) for i in range(lax.axis_size(axis...  11.2 us
    ppermute x6, starting transfers between devices, swap(): lax.ppermute(value, axis, [(i, i ^ bit) for i in range(lax.axis_size(axis...  7.48 us
    ppermute x2, starting transfers between devices, corner_swap(): lax.ppermute(value, ('lon', 'lat'), pairs + [(b, a) for a, b in pairs])  5.09 us
    ppermute x2, starting transfers between devices, lon_halo(): return lax.ppermute(own, 'lon', [(0, 1), (1, 0)])  4.57 us
    ppermute x1, starting transfers between devices, pair_spread(): lax.ppermute(own, ('lon', 'lat'), [(i, i ^ count + 1) for i in range(2 *...  3.67 us
    ppermute x1, waiting for transfers between devices, pair_sum(): lax.ppermute(to_far, ('lat', 'lev'), [(i, i ^ 6) for i in range(4 * count)])  3.11 us
    ppermute x4, starting transfers between devices, lat_swap(): return lax.ppermute(value, 'lat', pairs + [(b, a) for a, b in pairs])  2.89 us
  transfers between devices with their start and end apart: 16, of which 9 were waited for; matrix products, arithmetic and copies ran while one was open for 0% of the time, Pallas kernels for 19%

profile of v5, /device:TPU:0, one launch (start us, length us, event | category | flops | bytes accessed | tf_op | source)
XLA Modules:
  0.0 64.0 jit_solution(9071220617074421539)
XLA Ops:
  0.6 0.0 copy-start.1
  0.6 0.0 copy-start.2
  0.7 0.0 copy-start.3
  0.7 1.0 %copy-done.3 = bf16[1,16,16,512]{3,2,1,0:T(8,128)(2,1)S(1)} copy-done((bf16[1,16,16,512]{3,2,1,0:T(8,128)(2,1)S(1)}, bf16[1,16,16,512]{3,2,1,0:T(8,128)(2,1)}, u32[]{:S(2)}) %copy-start.3) | copy-done | bytes 262168
  1.7 0.0 copy-start.5
  1.7 0.7 %copy-done.5 = s32[1,16,16]{2,1,0:T(8,128)S(1)} copy-done((s32[1,16,16]{2,1,0:T(8,128)S(1)}, s32[1,16,16]{2,1,0:T(8,128)}, u32[]{:S(2)}) %copy-start.5) | copy-done | bytes 1048
  2.4 0.0 copy-start
  2.4 0.0 copy-start.6
  2.4 0.0 copy-start.7
  2.4 0.4 prep.1
  2.7 3.0 %collective-permute-start = (bf16[4,64,512]{2,1,0:T(8,128)(2,1)S(1)}, bf16[4,64,512]{2,1,0:T(8,128)(2,1)S(1)}, u32[]{:S(2)}, u32[]{:S(2)}) collective-permute-start(bf16[4,64,512]{2,1,0:T(8,128)(2,1)S(1)} %get-tuple-element.49.tok_ref.refs_4_), channel_id=1, source_target_pairs={{0,16},{16,0},{1,17},{17,1},{2,18},{18,2},{3,19},{19,3},{4,20},{20... | collective-permute-start | bytes 786440 | tf_op jit(solution)/shard_map/ppermute | solution.py:450
  5.7 1.6 %collective-permute-start.1 = (bf16[2,64,512]{2,1,0:T(8,128)(2,1)S(1)}, bf16[2,64,512]{2,1,0:T(8,128)(2,1)S(1)}, u32[]{:S(2)}, u32[]{:S(2)}) collective-permute-start(bf16[2,64,512]{2,1,0:T(8,128)(2,1)S(1)} %get-tuple-element.51), channel_id=1, source_target_pairs={{0,4},{8,12},{4,0},{12,8},{1,5},{9,13},{5,1},{13,9},{2,6},{10,14},... | collective-permute-start | bytes 393224 | tf_op jit(solution)/shard_map/ppermute | solution.py:467
  7.3 0.7 %collective-permute-start.2 = (bf16[2,64,512]{2,1,0:T(8,128)(2,1)S(1)}, bf16[2,64,512]{2,1,0:T(8,128)(2,1)S(1)}, u32[]{:S(2)}, u32[]{:S(2)}) collective-permute-start(bf16[2,64,512]{2,1,0:T(8,128)(2,1)S(1)} %get-tuple-element.52), channel_id=1, source_target_pairs={{4,8},{8,4},{5,9},{9,5},{6,10},{10,6},{7,11},{11,7},{20,24},{24,20... | collective-permute-start | bytes 393224 | tf_op jit(solution)/shard_map/ppermute | solution.py:467
  8.0 4.4 %collective-permute-start.4 = (bf16[2,64,512]{2,1,0:T(8,128)(2,1)S(1)}, bf16[2,64,512]{2,1,0:T(8,128)(2,1)S(1)}, u32[]{:S(2)}, u32[]{:S(2)}) collective-permute-start(bf16[2,64,512]{2,1,0:T(8,128)(2,1)S(1)} %get-tuple-element.51), channel_id=1, source_target_pairs={{0,20},{16,4},{8,28},{24,12},{20,0},{4,16},{28,8},{12,24},{1,21},{... | collective-permute-start | bytes 393224 | tf_op jit(solution)/shard_map/ppermute | solution.py:478
  12.4 0.7 %collective-permute-start.5 = (bf16[2,64,512]{2,1,0:T(8,128)(2,1)S(1)}, bf16[2,64,512]{2,1,0:T(8,128)(2,1)S(1)}, u32[]{:S(2)}, u32[]{:S(2)}) collective-permute-start(bf16[2,64,512]{2,1,0:T(8,128)(2,1)S(1)} %get-tuple-element.52), channel_id=1, source_target_pairs={{4,24},{20,8},{24,4},{8,20},{5,25},{21,9},{25,5},{9,21},{6,26},{22... | collective-permute-start | bytes 393224 | tf_op jit(solution)/shard_map/ppermute | solution.py:478
  13.1 0.0 copy-done.1
  13.1 0.0 copy-done.2
  13.1 0.0 copy-done
  13.1 0.0 copy-done.6
  13.1 0.0 copy-done.7
  13.1 2.0 %own.1 = (bf16[4,64,512]{2,1,0:T(8,128)(2,1)S(1)}, bf16[4,64,1024]{2,1,0:T(8,128)(2,1)S(1)}, bf16[256,512]{1,0:T(8,128)(2,1)S(1)}, bf16[4,64,512]{2,1,0:T(8,128)...) custom-call(bf16[4,64,512]{2,1,0:T(8,128)(2,1)S(1)} %get-tuple-eleme, ...), custom_call_target="tpu_custom_call" | custom-call | flops 402653184 | bytes 6042656 | tf_op jit(solution)/shard_map/own/pallas_call | solution.py:424
  15.1 0.0 collective-permute-done.1.first_ref
  15.1 1.6 %collective-permute-start.3 = (bf16[4,64,512]{2,1,0:T(8,128)(2,1)S(1)}, bf16[4,64,512]{2,1,0:T(8,128)(2,1)S(1)}, u32[]{:S(2)}, u32[]{:S(2)}) collective-permute-start(bf16[4,64,512]{2,1,0:T(8,128)(2,1)S(1)} %get-tuple-element.58.refs_6_.refs_4_), channel_id=1, source_target_pairs={{0,16},{16,0},{1,17},{17,1},{2,18},{18,2},{3,19},{19,3},{4,20},{20... | collective-permute-start | bytes 786440 | tf_op jit(solution)/shard_map/ppermute | solution.py:450
  16.7 0.0 collective-permute-done.2.second_ref
  16.7 0.0 collective-permute-done.lon_ref
  16.7 1.6 %near.1 = (bf16[4,64,512]{2,1,0:T(8,128)(2,1)S(1)}, bf16[8,64,1024]{2,1,0:T(8,128)(2,1)S(1)}, bf16[512,512]{1,0:T(8,128)(2,1)S(1)}, f32[8,8,64]{2,1,0:T(8,128)S(1)}, s32[8]{0:T(128)S(1)}) custom-call(bf16[4,64,512]{2,1,0:T(8,128)(2,1)S(1)} %collective-permute-done.lon_ref, bf16[2,64,512]{2,1,0:T(8,128)(2,1)S(1)} %collective-permute-done.1.first_ref, ...), custom_call_target="tpu_custom_call" | custom-call | flops 671088640 | bytes 3950624 | tf_op jit(solution)/shard_map/near/pallas_call | solution.py:424
  18.3 0.0 collective-permute-done.4.refs_7_
  18.3 0.0 collective-permute-done.5.refs_8_
  18.3 6.4 %main.1 = (f32[16,64,1024]{2,1,0:T(8,128)S(1)}, bf16[4,64,512]{2,1,0:T(8,128)(2,1)S(1)}, bf16[4,64,512]{2,1,0:T(8,128)(2,1)S(1)}, bf16[1024,512]{1,0:T(8,128)(2,...) custom-call(s32[8]{0:T(128)S(1)} %get-tuple-element.50.refs_0_, s32[8]{0:T(128)S(1)} %get-tuple-element.55.refs_1_, ...), custom_call_target="tpu_custom_call" | custom-call | flops 2415919104 | bytes 13166592 | tf_op jit(solution)/shard_map/main/pallas_call | solution.py:424
  24.8 0.0 collective-permute-done.3.refs_6_.refs_7_
  24.8 5.8 %other.1 = (f32[16,64,1024]{2,1,0:T(8,128)S(1)}, bf16[4,64,512]{2,1,0:T(8,128)(2,1)S(1)}, bf16[4,64,512]{2,1,0:T(8,128)(2,1)S(1)}, bf16[16,64,1024]{2,1,0:T(8,12...) custom-call(s32[8]{0:T(128)S(1)} %get-tuple-element.50.refs_0_, ...), custom_call_target="tpu_custom_call", output_to_operand_aliasing={{0}: (9, {})} | custom-call | flops 2415919104 | bytes 16025600 | tf_op jit(solution)/shard_map/other/pallas_call | solution.py:424
  30.6 0.8 %sums.1 = (bf16[2,2,64,1024]{3,2,1,0:T(8,128)(2,1)S(1)}, bf16[2,2,64,1024]{3,2,1,0:T(8,128)(2,1)S(1)}) custom-call(bf16[1024,512]{1,0:T(8,128)(2,1)S(1)} %get-tuple-element.70.refs_0_, bf16[16,64,1024]{2,1,0:T(8,128)(2,1)S(1)} %get-tuple-element.69.refs_1_.refs_0_, bf16[4,64,512]{2,1,0:T(8,128)(2,1)S(1)} %get-tuple-element.71.refs_2_.refs_3_, ...), custom_call_target="tpu_custom_call" | custom-call | flops 1073741824 | bytes 5767168 | tf_op jit(solution)/shard_map/sums/pallas_call | solution.py:424
  31.4 0.0 copy-start.4
  31.4 0.1 collective-permute-start.6
  31.5 1.9 %collective-permute-done.6.come_ref = bf16[2,2,64,1024]{3,2,1,0:T(8,128)(2,1)S(1)} collective-permute-done((bf16[2,2,64,1024]{3,2,1,0:T(8,128)(2,1)S(1)}, bf16[2,2,64,1024]{3,2,1,0:T(8,128)(2,1)S(1)}, u32[]{:S(2)}, u32[]{:S(2)}) %collective-permute-start.6) | collective-permute-done | bytes 524320 | tf_op jit(solution)/shard_map/ppermute | solution.py:482
  33.4 0.1 split.1
  33.5 0.1 collective-permute-start.7
  33.6 1.7 %collective-permute-start.8 = (bf16[64,1024]{1,0:T(8,128)(2,1)S(1)}, bf16[64,1024]{1,0:T(8,128)(2,1)S(1)}, u32[]{:S(2)}, u32[]{:S(2)}) collective-permute-start(bf16[64,1024]{1,0:T(8,128)(2,1)S(1)} %get-tuple-element.79), channel_id=1, source_target_pairs={{0,4},{4,0},{8,12},{12,8},{1,5},{5,1},{9,13},{13,9},{2,6},{6,2},{1... | collective-permute-start | bytes 393224 | tf_op jit(solution)/shard_map/ppermute | solution.py:482
  35.2 1.8 %collective-permute-start.9 = (bf16[64,1024]{1,0:T(8,128)(2,1)S(1)}, bf16[64,1024]{1,0:T(8,128)(2,1)S(1)}, u32[]{:S(2)}, u32[]{:S(2)}) collective-permute-start(bf16[64,1024]{1,0:T(8,128)(2,1)S(1)} %get-tuple-element.80), channel_id=1, source_target_pairs={{0,6},{1,7},{2,4},{3,5},{4,2},{5,3},{6,0},{7,1},{8,14},{9,15},{10,... | collective-permute-start | bytes 393224 | tf_op jit(solution)/shard_map/ppermute | solution.py:535
  37.0 0.7 %collective-permute-start.10 = (bf16[2,64,512]{2,1,0:T(8,128)(2,1)S(1)}, bf16[2,64,512]{2,1,0:T(8,128)(2,1)S(1)}, u32[]{:S(2)}, u32[]{:S(2)}) collective-permute-start(bf16[2,64,512]{2,1,0:T(8,128)(2,1)S(1)} %get-tuple-element.82), channel_id=1, source_target_pairs={{4,8},{8,4},{5,9},{9,5},{6,10},{10,6},{7,11},{11,7},{20,24},{24,20... | collective-permute-start | bytes 393224 | tf_op jit(solution)/shard_map/ppermute | solution.py:467
  37.7 1.4 %collective-permute-done.7 = bf16[64,1024]{1,0:T(8,128)(2,1)S(1)} collective-permute-done((bf16[64,1024]{1,0:T(8,128)(2,1)S(1)}, bf16[64,1024]{1,0:T(8,128)(2,1)S(1)}, u32[]{:S(2)}, u32[]{:S(2)}) %collective-permute-start.7) | collective-permute-done | bytes 131104 | tf_op jit(solution)/shard_map/ppermute | solution.py:482
  39.1 0.9 %collective-permute-done.8 = bf16[64,1024]{1,0:T(8,128)(2,1)S(1)} collective-permute-done((bf16[64,1024]{1,0:T(8,128)(2,1)S(1)}, bf16[64,1024]{1,0:T(8,128)(2,1)S(1)}, u32[]{:S(2)}, u32[]{:S(2)}) %collective-permute-start.8) | collective-permute-done | bytes 131104 | tf_op jit(solution)/shard_map/ppermute | solution.py:482
  40.0 3.1 %collective-permute-done.9 = bf16[64,1024]{1,0:T(8,128)(2,1)S(1)} collective-permute-done((bf16[64,1024]{1,0:T(8,128)(2,1)S(1)}, bf16[64,1024]{1,0:T(8,128)(2,1)S(1)}, u32[]{:S(2)}, u32[]{:S(2)}) %collective-permute-start.9) | collective-permute-done | bytes 131104 | tf_op jit(solution)/shard_map/ppermute | solution.py:535
  43.1 0.1 add_convert_fusion.1
  43.2 0.0 collective-permute-done.10.refs_2_
  43.2 4.4 %collective-permute-start.11 = (bf16[64,1024]{1,0:T(8,128)(2,1)S(1)}, bf16[64,1024]{1,0:T(8,128)(2,1)S(1)}, u32[]{:S(2)}, u32[]{:S(2)}) collective-permute-start(bf16[64,1024]{1,0:T(8,128)(2,1)S(1)} %add_convert_fusion.1), channel_id=1, source_target_pairs={{0,8},{4,12},{8,0},{12,4},{1,9},{5,13},{9,1},{13,5},{2,10},{6,14},... | collective-permute-start | bytes 393224 | tf_op jit(solution)/shard_map/ppermute | solution.py:482
  47.5 0.0 collective-permute-start.12
  47.5 5.1 %collective-permute-done.11 = bf16[64,1024]{1,0:T(8,128)(2,1)S(1)} collective-permute-done((bf16[64,1024]{1,0:T(8,128)(2,1)S(1)}, bf16[64,1024]{1,0:T(8,128)(2,1)S(1)}, u32[]{:S(2)}, u32[]{:S(2)}) %collective-permute-start.11) | collective-permute-done | bytes 131104 | tf_op jit(solution)/shard_map/ppermute | solution.py:482
  52.6 0.6 collective-permute-done.12.refs_1_
  53.2 3.7 %collective-permute-start.15 = (bf16[64,1024]{1,0:T(8,128)(2,1)S(1)}, bf16[64,1024]{1,0:T(8,128)(2,1)S(1)}, u32[]{:S(2)}, u32[]{:S(2)}) collective-permute-start(bf16[64,1024]{1,0:T(8,128)(2,1)S(1)} %add_convert_fusion.own_ref), channel_id=1, source_target_pairs={{0,20},{4,16},{8,28},{12,24},{16,4},{20,0},{24,12},{28,8},{1,21},{... | collective-permute-start | bytes 393224 | tf_op jit(solution)/shard_map/ppermute | solution.py:550
  56.9 0.0 collective-permute-start.14
  56.9 1.3 %collective-permute-start.13 = (bf16[64,1024]{1,0:T(8,128)(2,1)S(1)}, bf16[64,1024]{1,0:T(8,128)(2,1)S(1)}, u32[]{:S(2)}, u32[]{:S(2)}) collective-permute-start(bf16[64,1024]{1,0:T(8,128)(2,1)S(1)} %add_convert_fusion.own_ref), channel_id=1, source_target_pairs={{0,4},{4,0},{8,12},{12,8},{1,5},{5,1},{9,13},{13,9},{2,6},{6,2},{1... | collective-permute-start | bytes 393224 | tf_op jit(solution)/shard_map/ppermute | solution.py:482
  58.2 0.0 copy-done.4
  58.2 1.9 %input.1 = (bf16[1,16,16,512]{3,2,1,0:T(8,128)(2,1)}, bf16[1,16,16,512]{3,2,1,0:T(8,128)(2,1)}) custom-call(bf16[16,64,1024]{2,1,0:T(8,128)(2,1)S(1)} %get-tuple-element.69.refs_1_.refs_0_, bf16[2,64,512]{2,1,0:T(8,128)(2,1)S(1)} %collective-permute-done.12.refs_1_, bf16[2,64,512]{2,1,0:T(8,128)(2,1)S(1)} %collective-permute-done.10.refs_2_, ...), custom_call_target="tpu_custom_call" | custom-call | flops 402653184 | bytes 6294528 | tf_op jit(solution)/shard_map/input/pallas_call | solution.py:424
  60.1 0.5 collective-permute-done.15.far_ref
  60.6 1.4 %collective-permute-done.14.lon_ref = bf16[64,1024]{1,0:T(8,128)(2,1)S(1)} collective-permute-done((bf16[64,1024]{1,0:T(8,128)(2,1)S(1)}, bf16[64,1024]{1,0:T(8,128)(2,1)S(1)}, u32[]{:S(2)}, u32[]{:S(2)}) %collective-permute-start.14) | collective-permute-done | bytes 131104 | tf_op jit(solution)/shard_map/ppermute | solution.py:482
  62.0 0.6 collective-permute-done.13.lat_ref
  62.6 1.5 %finish.1 = (f32[128,1536]{1,0:T(8,128)}, f32[128,512]{1,0:T(8,128)}, f32[1,128]{1,0:T(1,128)}) custom-call(bf16[64,1024]{1,0:T(8,128)(2,1)S(1)} %add_convert_fusion.own_ref, bf16[64,1024]{1,0:T(8,128)(2,1)S(1)} %collective-permute-done.13.lat_ref, bf16[64,1024]{1,0:T(8,128)(2,1)S(1)} %collective-permute-done.14.lon_ref, ...), custom_call_target="tpu_custom_call" | custom-call | bytes 3148288 | tf_op jit(solution)/shard_map/finish/pallas_call | solution.py:424
  (1 shorter events, 0.0 us)
Async XLA Ops:
  0.6 12.5 %copy-start.1 = (bf16[1,16,16,512]{3,2,1,0:T(8,128)(2,1)S(1)}, bf16[1,16,16,512]{3,2,1,0:T(8,128)(2,1)}, u32[]{:S(2)}) copy-start(bf16[1,16,16,512]{3,2,1,0:T(8,128)(2,1)} %refs_9_.1) | copy-start | bytes 786436
  0.6 12.5 %copy-start.2 = (bf16[512,512]{1,0:T(8,128)(2,1)S(1)}, bf16[512,512]{1,0:T(8,128)(2,1)}, u32[]{:S(2)}) copy-start(bf16[512,512]{1,0:T(8,128)(2,1)} %wout_hbm.1) | copy-start | bytes 1572868
  0.7 1.0 %copy-start.3 = (bf16[1,16,16,512]{3,2,1,0:T(8,128)(2,1)S(1)}, bf16[1,16,16,512]{3,2,1,0:T(8,128)(2,1)}, u32[]{:S(2)}) copy-start(bf16[1,16,16,512]{3,2,1,0:T(8,128)(2,1)} %refs_10_.1) | copy-start | bytes 786436
  1.7 0.7 %copy-start.5 = (s32[1,16,16]{2,1,0:T(8,128)S(1)}, s32[1,16,16]{2,1,0:T(8,128)}, u32[]{:S(2)}) copy-start(s32[1,16,16]{2,1,0:T(8,128)} %refs_11_.1) | copy-start | bytes 3076
  2.4 10.7 %copy-start = (bf16[512,1536]{1,0:T(8,128)(2,1)S(1)}, bf16[512,1536]{1,0:T(8,128)(2,1)}, u32[]{:S(2)}) copy-start(bf16[512,1536]{1,0:T(8,128)(2,1)} %wqkv_hbm.1) | copy-start | bytes 4718596
  2.4 10.7 %copy-start.6 = (s32[1,16,16]{2,1,0:T(8,128)S(1)}, s32[1,16,16]{2,1,0:T(8,128)}, u32[]{:S(2)}) copy-start(s32[1,16,16]{2,1,0:T(8,128)} %refs_11_.1) | copy-start | bytes 3076
  2.4 10.7 %copy-start.7 = (f32[512]{0:T(512)S(1)}, f32[512]{0:T(512)}, u32[]{:S(2)}) copy-start(f32[512]{0:T(512)} %param.10) | copy-start | bytes 6148
  2.7 14.0 %collective-permute-start = (bf16[4,64,512]{2,1,0:T(8,128)(2,1)S(1)}, bf16[4,64,512]{2,1,0:T(8,128)(2,1)S(1)}, u32[]{:S(2)}, u32[]{:S(2)}) collective-permute-start(bf16[4,64,512]{2,1,0:T(8,128)(2,1)S(1)} %get-tuple-element.49.tok_ref.refs_4_), channel_id=1, source_target_pairs={{0,16},{16,0},{1,17},{17,1},{2,18},{18,2},{3,19},{19,3},{4,20},{20... | collective-permute-start | bytes 786440 | tf_op jit(solution)/shard_map/ppermute | solution.py:450
  5.7 9.4 %collective-permute-start.1 = (bf16[2,64,512]{2,1,0:T(8,128)(2,1)S(1)}, bf16[2,64,512]{2,1,0:T(8,128)(2,1)S(1)}, u32[]{:S(2)}, u32[]{:S(2)}) collective-permute-start(bf16[2,64,512]{2,1,0:T(8,128)(2,1)S(1)} %get-tuple-element.51), channel_id=1, source_target_pairs={{0,4},{8,12},{4,0},{12,8},{1,5},{9,13},{5,1},{13,9},{2,6},{10,14},... | collective-permute-start | bytes 393224 | tf_op jit(solution)/shard_map/ppermute | solution.py:467
  7.3 9.4 %collective-permute-start.2 = (bf16[2,64,512]{2,1,0:T(8,128)(2,1)S(1)}, bf16[2,64,512]{2,1,0:T(8,128)(2,1)S(1)}, u32[]{:S(2)}, u32[]{:S(2)}) collective-permute-start(bf16[2,64,512]{2,1,0:T(8,128)(2,1)S(1)} %get-tuple-element.52), channel_id=1, source_target_pairs={{4,8},{8,4},{5,9},{9,5},{6,10},{10,6},{7,11},{11,7},{20,24},{24,20... | collective-permute-start | bytes 393224 | tf_op jit(solution)/shard_map/ppermute | solution.py:467
  8.0 10.3 %collective-permute-start.4 = (bf16[2,64,512]{2,1,0:T(8,128)(2,1)S(1)}, bf16[2,64,512]{2,1,0:T(8,128)(2,1)S(1)}, u32[]{:S(2)}, u32[]{:S(2)}) collective-permute-start(bf16[2,64,512]{2,1,0:T(8,128)(2,1)S(1)} %get-tuple-element.51), channel_id=1, source_target_pairs={{0,20},{16,4},{8,28},{24,12},{20,0},{4,16},{28,8},{12,24},{1,21},{... | collective-permute-start | bytes 393224 | tf_op jit(solution)/shard_map/ppermute | solution.py:478
  12.4 5.9 %collective-permute-start.5 = (bf16[2,64,512]{2,1,0:T(8,128)(2,1)S(1)}, bf16[2,64,512]{2,1,0:T(8,128)(2,1)S(1)}, u32[]{:S(2)}, u32[]{:S(2)}) collective-permute-start(bf16[2,64,512]{2,1,0:T(8,128)(2,1)S(1)} %get-tuple-element.52), channel_id=1, source_target_pairs={{4,24},{20,8},{24,4},{8,20},{5,25},{21,9},{25,5},{9,21},{6,26},{22... | collective-permute-start | bytes 393224 | tf_op jit(solution)/shard_map/ppermute | solution.py:478
  15.1 9.7 %collective-permute-start.3 = (bf16[4,64,512]{2,1,0:T(8,128)(2,1)S(1)}, bf16[4,64,512]{2,1,0:T(8,128)(2,1)S(1)}, u32[]{:S(2)}, u32[]{:S(2)}) collective-permute-start(bf16[4,64,512]{2,1,0:T(8,128)(2,1)S(1)} %get-tuple-element.58.refs_6_.refs_4_), channel_id=1, source_target_pairs={{0,16},{16,0},{1,17},{17,1},{2,18},{18,2},{3,19},{19,3},{4,20},{20... | collective-permute-start | bytes 786440 | tf_op jit(solution)/shard_map/ppermute | solution.py:450
  31.4 26.8 %copy-start.4 = (bf16[1,16,16,512]{3,2,1,0:T(8,128)(2,1)S(1)}, bf16[1,16,16,512]{3,2,1,0:T(8,128)(2,1)}, u32[]{:S(2)}) copy-start(bf16[1,16,16,512]{3,2,1,0:T(8,128)(2,1)} %refs_10_.1) | copy-start | bytes 786436
  31.4 2.0 %collective-permute-start.6 = (bf16[2,2,64,1024]{3,2,1,0:T(8,128)(2,1)S(1)}, bf16[2,2,64,1024]{3,2,1,0:T(8,128)(2,1)S(1)}, u32[]{:S(2)}, u32[]{:S(2)}) collective-permute-start(bf16[2,2,64,1024]{3,2,1,0:T(8,128)(2,1)S(1)} %get-tuple-element.76), channel_id=1, source_target_pairs={{0,1},{1,0},{2,3},{3,2},{4,5},{5,4},{6,7},{7,6},{8,9},{9,8},{10,11... | collective-permute-start | bytes 1572872 | tf_op jit(solution)/shard_map/ppermute | solution.py:482
  33.5 5.6 %collective-permute-start.7 = (bf16[64,1024]{1,0:T(8,128)(2,1)S(1)}, bf16[64,1024]{1,0:T(8,128)(2,1)S(1)}, u32[]{:S(2)}, u32[]{:S(2)}) collective-permute-start(bf16[64,1024]{1,0:T(8,128)(2,1)S(1)} %get-tuple-element.78), channel_id=1, source_target_pairs={{0,2},{1,3},{2,0},{3,1},{4,6},{5,7},{6,4},{7,5},{8,10},{9,11},{10,... | collective-permute-start | bytes 393224 | tf_op jit(solution)/shard_map/ppermute | solution.py:482
  33.6 6.4 %collective-permute-start.8 = (bf16[64,1024]{1,0:T(8,128)(2,1)S(1)}, bf16[64,1024]{1,0:T(8,128)(2,1)S(1)}, u32[]{:S(2)}, u32[]{:S(2)}) collective-permute-start(bf16[64,1024]{1,0:T(8,128)(2,1)S(1)} %get-tuple-element.79), channel_id=1, source_target_pairs={{0,4},{4,0},{8,12},{12,8},{1,5},{5,1},{9,13},{13,9},{2,6},{6,2},{1... | collective-permute-start | bytes 393224 | tf_op jit(solution)/shard_map/ppermute | solution.py:482
  35.2 7.9 %collective-permute-start.9 = (bf16[64,1024]{1,0:T(8,128)(2,1)S(1)}, bf16[64,1024]{1,0:T(8,128)(2,1)S(1)}, u32[]{:S(2)}, u32[]{:S(2)}) collective-permute-start(bf16[64,1024]{1,0:T(8,128)(2,1)S(1)} %get-tuple-element.80), channel_id=1, source_target_pairs={{0,6},{1,7},{2,4},{3,5},{4,2},{5,3},{6,0},{7,1},{8,14},{9,15},{10,... | collective-permute-start | bytes 393224 | tf_op jit(solution)/shard_map/ppermute | solution.py:535
  37.0 6.1 %collective-permute-start.10 = (bf16[2,64,512]{2,1,0:T(8,128)(2,1)S(1)}, bf16[2,64,512]{2,1,0:T(8,128)(2,1)S(1)}, u32[]{:S(2)}, u32[]{:S(2)}) collective-permute-start(bf16[2,64,512]{2,1,0:T(8,128)(2,1)S(1)} %get-tuple-element.82), channel_id=1, source_target_pairs={{4,8},{8,4},{5,9},{9,5},{6,10},{10,6},{7,11},{11,7},{20,24},{24,20... | collective-permute-start | bytes 393224 | tf_op jit(solution)/shard_map/ppermute | solution.py:467
  43.2 9.4 %collective-permute-start.11 = (bf16[64,1024]{1,0:T(8,128)(2,1)S(1)}, bf16[64,1024]{1,0:T(8,128)(2,1)S(1)}, u32[]{:S(2)}, u32[]{:S(2)}) collective-permute-start(bf16[64,1024]{1,0:T(8,128)(2,1)S(1)} %add_convert_fusion.1), channel_id=1, source_target_pairs={{0,8},{4,12},{8,0},{12,4},{1,9},{5,13},{9,1},{13,5},{2,10},{6,14},... | collective-permute-start | bytes 393224 | tf_op jit(solution)/shard_map/ppermute | solution.py:482
  47.5 5.7 %collective-permute-start.12 = (bf16[2,64,512]{2,1,0:T(8,128)(2,1)S(1)}, bf16[2,64,512]{2,1,0:T(8,128)(2,1)S(1)}, u32[]{:S(2)}, u32[]{:S(2)}) collective-permute-start(bf16[2,64,512]{2,1,0:T(8,128)(2,1)S(1)} %get-tuple-element.84), channel_id=1, source_target_pairs={{0,4},{8,12},{4,0},{12,8},{1,5},{9,13},{5,1},{13,9},{2,6},{10,14},... | collective-permute-start | bytes 393224 | tf_op jit(solution)/shard_map/ppermute | solution.py:467
  53.2 7.4 %collective-permute-start.15 = (bf16[64,1024]{1,0:T(8,128)(2,1)S(1)}, bf16[64,1024]{1,0:T(8,128)(2,1)S(1)}, u32[]{:S(2)}, u32[]{:S(2)}) collective-permute-start(bf16[64,1024]{1,0:T(8,128)(2,1)S(1)} %add_convert_fusion.own_ref), channel_id=1, source_target_pairs={{0,20},{4,16},{8,28},{12,24},{16,4},{20,0},{24,12},{28,8},{1,21},{... | collective-permute-start | bytes 393224 | tf_op jit(solution)/shard_map/ppermute | solution.py:550
  56.9 5.1 %collective-permute-start.14 = (bf16[64,1024]{1,0:T(8,128)(2,1)S(1)}, bf16[64,1024]{1,0:T(8,128)(2,1)S(1)}, u32[]{:S(2)}, u32[]{:S(2)}) collective-permute-start(bf16[64,1024]{1,0:T(8,128)(2,1)S(1)} %add_convert_fusion.own_ref), channel_id=1, source_target_pairs={{0,16},{16,0},{1,17},{17,1},{2,18},{18,2},{3,19},{19,3},{4,20},{20... | collective-permute-start | bytes 393224 | tf_op jit(solution)/shard_map/ppermute | solution.py:482
  56.9 5.7 %collective-permute-start.13 = (bf16[64,1024]{1,0:T(8,128)(2,1)S(1)}, bf16[64,1024]{1,0:T(8,128)(2,1)S(1)}, u32[]{:S(2)}, u32[]{:S(2)}) collective-permute-start(bf16[64,1024]{1,0:T(8,128)(2,1)S(1)} %add_convert_fusion.own_ref), channel_id=1, source_target_pairs={{0,4},{4,0},{8,12},{12,8},{1,5},{5,1},{9,13},{13,9},{2,6},{6,2},{1... | collective-permute-start | bytes 393224 | tf_op jit(solution)/shard_map/ppermute | solution.py:482

commit v6 on v5

--- a/solution.py
+++ b/solution.py
@@ -228,16 +228,18 @@
     def window_at(slot):
         return slot + (slot >= info[0]).astype(jnp.int32)
 
-    def step(slot, carry):
+    def attend(slot, all_keys, all_values, with_out, with_query):
         at = window_at(slot)
 
         @pl.when(info[1 + at] > 0)
         def _():
             r, c = at // 2, at % 2
             mine, other, side = 4 * block, 4 * (1 - block), 2 * lat_side(r)
-            places = [mine + window_at(k) for k in range(3)]
-            places += [other + 1 - c, other + 3 - c]
-            places += [8 + mine + side, 9 + mine + side, 8 + other + side + 1 - c]
+            near = [mine + window_at(k) for k in range(3)] + [8 + mine + side, 9 + mine + side]
+            away = [other + 1 - c, other + 3 - c, 8 + other + side + 1 - c]
+            places = away + near if block else near + away
+            few = 3 if block else 5
+            key_count, value_count = 8 if all_keys else few, 8 if all_values else few
             for k in range(8):
                 kcat[k * AREA : (k + 1) * AREA] = kv[places[k]]
             bias_row = jnp.concatenate([bias[place][:1] for place in places], axis=1)
@@ -248,25 +250,43 @@
             scores = [dot(q_stack[g], kcat[:, lanes(g)], 1, 1) + bias_row for g in both]
             grad_probs = [dot(gm_stack[g], kcat[:, spans[g]], 1, 1) for g in both]
             weights = [jnp.exp(x - jnp.max(x, axis=1, keepdims=True)) for x in scores]
-            probs = [x * (1.0 / jnp.sum(x, axis=1, keepdims=True)) for x in weights]
-            low = [x.astype(BF16) for x in probs]
-            out = [unstack_heads(dot(low[g], kcat[:, spans[g]], 1, 0), blocks).astype(BF16) for g in both]
-            delta = [jnp.sum(probs[g] * grad_probs[g], axis=1, keepdims=True) for g in both]
-            grad_scores = [(probs[g] * (grad_probs[g] - delta[g])).astype(BF16) for g in both]
-            grad = [unstack_heads(dot(grad_scores[g], kcat[:, lanes(g)], 1, 0), blocks) for g in both]
-            grad_keys = [dot(grad_scores[g], q_stack[g], 0, 0) for g in both]
-            grad_values = [dot(low[g], gm_stack[g], 0, 0) for g in both]
+            inverse = [1.0 / jnp.sum(x, axis=1, keepdims=True) for x in weights]
+            low = [(x * y).astype(BF16) for x, y in zip(weights, inverse)]
+            delta = [jnp.sum(weights[g] * grad_probs[g], axis=1, keepdims=True) * inverse[g] for g in both]
+            grad_scores = [
+                (weights[g] * ((grad_probs[g] - delta[g]) * inverse[g])).astype(BF16) for g in both
+            ]
+            if with_out:
+                out = [unstack_heads(dot(low[g], kcat[:, spans[g]], 1, 0), blocks) for g in both]
+            if with_query:
+                grad = [unstack_heads(dot(grad_scores[g], kcat[:, lanes(g)], 1, 0), blocks) for g in both]
+            grad_keys = [dot(grad_scores[g][:, : key_count * AREA], q_stack[g], 0, 0) for g in both]
+            grad_values = [dot(low[g][:, : value_count * AREA], gm_stack[g], 0, 0) for g in both]
             for g in both:
-                mixed[at, :, lanes(g)] = out[g]
-                gq[at, :, lanes(g)] = (grad[g] * HEAD_DIM ** -0.5).astype(BF16)
+                if with_out:
+                    mixed[at, :, lanes(g)] = out[g].astype(BF16)
+                if with_query:
+                    gq[at, :, lanes(g)] = (grad[g] * HEAD_DIM ** -0.5).astype(BF16)
                 for k in range(8):
                     rows = slice(k * AREA, (k + 1) * AREA)
-                    acc[places[k], :, lanes(g)] += grad_keys[g][rows]
-                    acc[places[k], :, spans[g]] += grad_values[g][rows]
-
-        return carry
-
-    lax.fori_loop(0, 3, step, 0)
+                    if k < key_count:
+                        acc[places[k], :, lanes(g)] += grad_keys[g][rows]
+                    if k < value_count:
+                        acc[places[k], :, spans[g]] += grad_values[g][rows]
+
+    def sweep(*wanted):
+        def step(slot, carry):
+            attend(slot, *wanted)
+            return carry
+
+        lax.fori_loop(0, 3, step, 0)
+
+    if block == 0 and last:
+        sweep(True, True, True, True)
+    else:
+        lon = lax.axis_index("lon")
+        pl.when(lon == 0)(lambda: sweep(True, False, block == 0, True))
+        pl.when(lon == 1)(lambda: sweep(False, True, True, block == 0))
     if not last:
         return
     dkv[...] = acc[...].astype(BF16)
@@ -320,14 +340,14 @@
         def _():
             for rel in range(4):
                 put(rel, 0, query_sum(rel))
-                put(rel, D, out_sum(rel))
+                put(rel, D, dot(hid[:, columns(rel)], grad_part(0, D), 0, 0))
 
         @pl.when(lon == 1)
         def _():
             for rel in range(4):
-                part = hid[:, columns(rel)]
-                put(rel, 0, dot(part, grad_part(0, D), 0, 0))
-                put(rel, D, dot(part, grad_part(D, D), 0, 0))
+                put(rel, 0, out_sum(rel))
+                put(rel, D, dot(hid[:, columns(rel)], grad_part(D, D), 0, 0))
+
     else:
         for rel in range(4):
             to = keep if rel % 2 == 0 else send
@@ -336,7 +356,7 @@
             to[rel // 2, :, 2 * D :] = dot(hid[:, columns(rel)], grad_part(0, 2 * D), 0, 0).astype(BF16)
 
 
-def split_kernel(keep_ref, come_ref, own_ref, lev_ref, lat_ref, far_ref):
+def split_kernel(keep_ref, come_ref, far_ref, lat_ref, lev_ref, own_ref):
     for k, ref in enumerate((own_ref, lat_ref, lev_ref, far_ref)):
         total = keep_ref[k // 2, k % 2].astype(F32) + come_ref[k // 2, k % 2].astype(F32)
         ref[...] = total.astype(ref.dtype)
@@ -403,9 +423,9 @@
         near = jnp.where(mine, own_ref[...], lat_ref[...]).astype(F32)
         away = jnp.where(mine, lon_ref[...], far_ref[...]).astype(F32)
         low, high = jnp.where(first, near, away), jnp.where(first, away, near)
-        qkv_ref[rows, :D] = low[:, :D]
-        out_ref[rows] = low[:, D:]
-        qkv_ref[rows, D:] = high
+        qkv_ref[rows, : 2 * D] = low
+        out_ref[rows] = high[:, :D]
+        qkv_ref[rows, 2 * D :] = high[:, D:]
     gg_ref[...] = gain_row(wqkv_ref, gain_ref, qkv_ref)
 
 
@@ -529,8 +549,8 @@
     width = keep.shape[-1]
     come = swap(send, "lev", 1)
     piece = shape(keep.shape[2:])
-    own, to_lev, to_lat, to_far = call(
-        "split", split_kernel, [shape(piece.shape, F32), piece, piece, piece], [], [keep, come], [], [], [], 8
+    to_far, to_lat, to_lev, own = call(
+        "split", split_kernel, [piece, piece, piece, shape(piece.shape, F32)], [], [keep, come], [], [], [], 8
     )
     from_far = lax.ppermute(to_far, ("lat", "lev"), [(i, i ^ 6) for i in range(4 * count)])
     from_lat = swap(to_lat, "lat", 1)

time: 63.5 us -> 61.6 us (0.970); the launches traced: 64 us -> 61.4 us
  Pallas kernels: 20.4 us -> 18.7 us
  starting transfers between devices: 25.5 us -> 24.1 us
    ppermute x1, starting transfers between devices: 1.82 us -> 0.01 us  [pair_sum(): lax.ppermute(to_far, ('lat', 'lev'), [(i, i ^ 6) for i in range(4 * count)])]
    pallas_call x9, Pallas kernels: 20.4 us -> 18.7 us  [call(): pl.pallas_call(kernel, out_shape=outs, in_specs=specs, out_specs=out_spec...]
    ppermute x1, waiting for transfers between devices: 3.11 us -> 1.81 us  [pair_sum(): lax.ppermute(to_far, ('lat', 'lev'), [(i, i ^ 6) for i in range(4 * count)])]
    ppermute x6, waiting for transfers between devices: 11.2 us -> 12.4 us  [swap(): lax.ppermute(value, axis, [(i, i ^ bit) for i in range(lax.axis_size(axis...]
    ppermute x6, starting transfers between devices: 7.48 us -> 8.62 us  [swap(): lax.ppermute(value, axis, [(i, i ^ bit) for i in range(lax.axis_size(axis...]
    ppermute x1, starting transfers between devices: 3.67 us -> 2.77 us  [pair_spread(): lax.ppermute(own, ('lon', 'lat'), [(i, i ^ count + 1) for i in range(2 *...]
  transfers between devices with their start and end apart: 16 -> 16, of which waited for: 9 -> 8; matrix products, arithmetic and copies ran while one was open for 0% -> 0% of each run, Pallas kernels for 19% -> 17%
where the time goes in v6:
time: 61.6 us; the launch traced here: 61.4 us
  starting transfers between devices  24.1 us (39%)
  Pallas kernels  18.7 us (30%)
  waiting for transfers between devices  15.9 us (26%)
  local copies, waits for them, and re-layouts  1.74 us (3%)
  between operations  0.87 us (1%)
    pallas_call x9, Pallas kernels, call(): pl.pallas_call(kernel, out_shape=outs, in_specs=specs, out_specs=out_spec...  18.7 us
    ppermute x6, waiting for transfers between devices, swap(): lax.ppermute(value, axis, [(i, i ^ bit) for i in range(lax.axis_size(axis...  12.4 us
    ppermute x6, starting transfers between devices, swap(): lax.ppermute(value, axis, [(i, i ^ bit) for i in range(lax.axis_size(axis...  8.62 us
    ppermute x2, starting transfers between devices, corner_swap(): lax.ppermute(value, ('lon', 'lat'), pairs + [(b, a) for a, b in pairs])  5.09 us
    ppermute x2, starting transfers between devices, lon_halo(): return lax.ppermute(own, 'lon', [(0, 1), (1, 0)])  4.57 us
    ppermute x4, starting transfers between devices, lat_swap(): return lax.ppermute(value, 'lat', pairs + [(b, a) for a, b in pairs])  3.04 us
    ppermute x1, starting transfers between devices, pair_spread(): lax.ppermute(own, ('lon', 'lat'), [(i, i ^ count + 1) for i in range(2 *...  2.77 us
    ppermute x1, waiting for transfers between devices, pair_sum(): lax.ppermute(to_far, ('lat', 'lev'), [(i, i ^ 6) for i in range(4 * count)])  1.81 us
  transfers between devices with their start and end apart: 16, of which 8 were waited for; matrix products, arithmetic and copies ran while one was open for 0% of the time, Pallas kernels for 17%

profile of v6, /device:TPU:0, one launch (start us, length us, event | category | flops | bytes accessed | tf_op | source)
XLA Modules:
  0.0 61.4 jit_solution(10019044020527989314)
XLA Ops:
  0.6 0.0 copy-start.1
  0.6 0.0 copy-start.2
  0.7 0.0 copy-start.3
  0.7 1.0 %copy-done.3 = bf16[1,16,16,512]{3,2,1,0:T(8,128)(2,1)S(1)} copy-done((bf16[1,16,16,512]{3,2,1,0:T(8,128)(2,1)S(1)}, bf16[1,16,16,512]{3,2,1,0:T(8,128)(2,1)}, u32[]{:S(2)}) %copy-start.3) | copy-done | bytes 262168
  1.7 0.0 copy-start.5
  1.7 0.7 %copy-done.5 = s32[1,16,16]{2,1,0:T(8,128)S(1)} copy-done((s32[1,16,16]{2,1,0:T(8,128)S(1)}, s32[1,16,16]{2,1,0:T(8,128)}, u32[]{:S(2)}) %copy-start.5) | copy-done | bytes 1048
  2.4 0.0 copy-start
  2.4 0.0 copy-start.6
  2.4 0.0 copy-start.7
  2.4 0.4 prep.1
  2.7 3.0 %collective-permute-start = (bf16[4,64,512]{2,1,0:T(8,128)(2,1)S(1)}, bf16[4,64,512]{2,1,0:T(8,128)(2,1)S(1)}, u32[]{:S(2)}, u32[]{:S(2)}) collective-permute-start(bf16[4,64,512]{2,1,0:T(8,128)(2,1)S(1)} %get-tuple-element.49.tok_ref.refs_4_), channel_id=1, source_target_pairs={{0,16},{16,0},{1,17},{17,1},{2,18},{18,2},{3,19},{19,3},{4,20},{20... | collective-permute-start | bytes 786440 | tf_op jit(solution)/shard_map/ppermute | solution.py:470
  5.7 1.6 %collective-permute-start.1 = (bf16[2,64,512]{2,1,0:T(8,128)(2,1)S(1)}, bf16[2,64,512]{2,1,0:T(8,128)(2,1)S(1)}, u32[]{:S(2)}, u32[]{:S(2)}) collective-permute-start(bf16[2,64,512]{2,1,0:T(8,128)(2,1)S(1)} %get-tuple-element.51), channel_id=1, source_target_pairs={{0,4},{8,12},{4,0},{12,8},{1,5},{9,13},{5,1},{13,9},{2,6},{10,14},... | collective-permute-start | bytes 393224 | tf_op jit(solution)/shard_map/ppermute | solution.py:487
  7.3 0.7 %collective-permute-start.2 = (bf16[2,64,512]{2,1,0:T(8,128)(2,1)S(1)}, bf16[2,64,512]{2,1,0:T(8,128)(2,1)S(1)}, u32[]{:S(2)}, u32[]{:S(2)}) collective-permute-start(bf16[2,64,512]{2,1,0:T(8,128)(2,1)S(1)} %get-tuple-element.52), channel_id=1, source_target_pairs={{4,8},{8,4},{5,9},{9,5},{6,10},{10,6},{7,11},{11,7},{20,24},{24,20... | collective-permute-start | bytes 393224 | tf_op jit(solution)/shard_map/ppermute | solution.py:487
  8.0 4.4 %collective-permute-start.4 = (bf16[2,64,512]{2,1,0:T(8,128)(2,1)S(1)}, bf16[2,64,512]{2,1,0:T(8,128)(2,1)S(1)}, u32[]{:S(2)}, u32[]{:S(2)}) collective-permute-start(bf16[2,64,512]{2,1,0:T(8,128)(2,1)S(1)} %get-tuple-element.51), channel_id=1, source_target_pairs={{0,20},{16,4},{8,28},{24,12},{20,0},{4,16},{28,8},{12,24},{1,21},{... | collective-permute-start | bytes 393224 | tf_op jit(solution)/shard_map/ppermute | solution.py:498
  12.4 0.7 %collective-permute-start.5 = (bf16[2,64,512]{2,1,0:T(8,128)(2,1)S(1)}, bf16[2,64,512]{2,1,0:T(8,128)(2,1)S(1)}, u32[]{:S(2)}, u32[]{:S(2)}) collective-permute-start(bf16[2,64,512]{2,1,0:T(8,128)(2,1)S(1)} %get-tuple-element.52), channel_id=1, source_target_pairs={{4,24},{20,8},{24,4},{8,20},{5,25},{21,9},{25,5},{9,21},{6,26},{22... | collective-permute-start | bytes 393224 | tf_op jit(solution)/shard_map/ppermute | solution.py:498
  13.1 0.0 copy-done.1
  13.1 0.0 copy-done.2
  13.1 0.0 copy-done
  13.1 0.0 copy-done.6
  13.1 0.0 copy-done.7
  13.1 2.0 %own.1 = (bf16[4,64,512]{2,1,0:T(8,128)(2,1)S(1)}, bf16[4,64,1024]{2,1,0:T(8,128)(2,1)S(1)}, bf16[256,512]{1,0:T(8,128)(2,1)S(1)}, bf16[4,64,512]{2,1,0:T(8,128)...) custom-call(bf16[4,64,512]{2,1,0:T(8,128)(2,1)S(1)} %get-tuple-eleme, ...), custom_call_target="tpu_custom_call" | custom-call | flops 402653184 | bytes 6042656 | tf_op jit(solution)/shard_map/own/pallas_call | solution.py:444
  15.1 0.0 collective-permute-done.1.first_ref
  15.1 1.6 %collective-permute-start.3 = (bf16[4,64,512]{2,1,0:T(8,128)(2,1)S(1)}, bf16[4,64,512]{2,1,0:T(8,128)(2,1)S(1)}, u32[]{:S(2)}, u32[]{:S(2)}) collective-permute-start(bf16[4,64,512]{2,1,0:T(8,128)(2,1)S(1)} %get-tuple-element.58.refs_6_.refs_4_), channel_id=1, source_target_pairs={{0,16},{16,0},{1,17},{17,1},{2,18},{18,2},{3,19},{19,3},{4,20},{20... | collective-permute-start | bytes 786440 | tf_op jit(solution)/shard_map/ppermute | solution.py:470
  16.7 0.0 collective-permute-done.2.second_ref
  16.7 0.0 collective-permute-done.lon_ref
  16.7 1.6 %near.1 = (bf16[4,64,512]{2,1,0:T(8,128)(2,1)S(1)}, bf16[8,64,1024]{2,1,0:T(8,128)(2,1)S(1)}, bf16[512,512]{1,0:T(8,128)(2,1)S(1)}, f32[8,8,64]{2,1,0:T(8,128)S(1)}, s32[8]{0:T(128)S(1)}) custom-call(bf16[4,64,512]{2,1,0:T(8,128)(2,1)S(1)} %collective-permute-done.lon_ref, bf16[2,64,512]{2,1,0:T(8,128)(2,1)S(1)} %collective-permute-done.1.first_ref, ...), custom_call_target="tpu_custom_call" | custom-call | flops 671088640 | bytes 3950624 | tf_op jit(solution)/shard_map/near/pallas_call | solution.py:444
  18.3 0.0 collective-permute-done.4.refs_7_
  18.3 0.0 collective-permute-done.5.refs_8_
  18.3 5.0 %main.1 = (f32[16,64,1024]{2,1,0:T(8,128)S(1)}, bf16[4,64,512]{2,1,0:T(8,128)(2,1)S(1)}, bf16[4,64,512]{2,1,0:T(8,128)(2,1)S(1)}, bf16[1024,512]{1,0:T(8,128)(2,...) custom-call(s32[8]{0:T(128)S(1)} %get-tuple-element.50.refs_0_, s32[8]{0:T(128)S(1)} %get-tuple-element.55.refs_1_, ...), custom_call_target="tpu_custom_call" | custom-call | flops 2415919104 | bytes 13166592 | tf_op jit(solution)/shard_map/main/pallas_call | solution.py:444
  23.4 0.0 collective-permute-done.3.refs_6_.refs_7_
  23.4 5.3 %other.1 = (f32[16,64,1024]{2,1,0:T(8,128)S(1)}, bf16[4,64,512]{2,1,0:T(8,128)(2,1)S(1)}, bf16[4,64,512]{2,1,0:T(8,128)(2,1)S(1)}, bf16[16,64,1024]{2,1,0:T(8,12...) custom-call(s32[8]{0:T(128)S(1)} %get-tuple-element.50.refs_0_, ...), custom_call_target="tpu_custom_call", output_to_operand_aliasing={{0}: (9, {})} | custom-call | flops 2415919104 | bytes 16025600 | tf_op jit(solution)/shard_map/other/pallas_call | solution.py:444
  28.6 1.1 %sums.1 = (bf16[2,2,64,1024]{3,2,1,0:T(8,128)(2,1)S(1)}, bf16[2,2,64,1024]{3,2,1,0:T(8,128)(2,1)S(1)}) custom-call(bf16[1024,512]{1,0:T(8,128)(2,1)S(1)} %get-tuple-element.70.refs_0_, bf16[16,64,1024]{2,1,0:T(8,128)(2,1)S(1)} %get-tuple-element.69.refs_1_.refs_0_, bf16[4,64,512]{2,1,0:T(8,128)(2,1)S(1)} %get-tuple-element.71.refs_2_.refs_3_, ...), custom_call_target="tpu_custom_call" | custom-call | flops 1073741824 | bytes 5767168 | tf_op jit(solution)/shard_map/sums/pallas_call | solution.py:444
  29.7 0.0 copy-start.4
  29.7 0.1 collective-permute-start.6
  29.8 1.9 %collective-permute-done.6.come_ref = bf16[2,2,64,1024]{3,2,1,0:T(8,128)(2,1)S(1)} collective-permute-done((bf16[2,2,64,1024]{3,2,1,0:T(8,128)(2,1)S(1)}, bf16[2,2,64,1024]{3,2,1,0:T(8,128)(2,1)S(1)}, u32[]{:S(2)}, u32[]{:S(2)}) %collective-permute-start.6) | collective-permute-done | bytes 524320 | tf_op jit(solution)/shard_map/ppermute | solution.py:502
  31.7 0.1 split.1
  31.8 0.1 collective-permute-start.7
  31.9 5.7 %collective-permute-start.8 = (bf16[64,1024]{1,0:T(8,128)(2,1)S(1)}, bf16[64,1024]{1,0:T(8,128)(2,1)S(1)}, u32[]{:S(2)}, u32[]{:S(2)}) collective-permute-start(bf16[64,1024]{1,0:T(8,128)(2,1)S(1)} %get-tuple-element.79), channel_id=1, source_target_pairs={{0,4},{4,0},{8,12},{12,8},{1,5},{5,1},{9,13},{13,9},{2,6},{6,2},{1... | collective-permute-start | bytes 393224 | tf_op jit(solution)/shard_map/ppermute | solution.py:502
  37.6 0.0 collective-permute-start.9
  37.6 0.7 %collective-permute-start.10 = (bf16[2,64,512]{2,1,0:T(8,128)(2,1)S(1)}, bf16[2,64,512]{2,1,0:T(8,128)(2,1)S(1)}, u32[]{:S(2)}, u32[]{:S(2)}) collective-permute-start(bf16[2,64,512]{2,1,0:T(8,128)(2,1)S(1)} %get-tuple-element.82), channel_id=1, source_target_pairs={{4,8},{8,4},{5,9},{9,5},{6,10},{10,6},{7,11},{11,7},{20,24},{24,20... | collective-permute-start | bytes 393224 | tf_op jit(solution)/shard_map/ppermute | solution.py:487
  38.3 0.0 collective-permute-done.7
  38.3 3.6 %collective-permute-done.8 = bf16[64,1024]{1,0:T(8,128)(2,1)S(1)} collective-permute-done((bf16[64,1024]{1,0:T(8,128)(2,1)S(1)}, bf16[64,1024]{1,0:T(8,128)(2,1)S(1)}, u32[]{:S(2)}, u32[]{:S(2)}) %collective-permute-start.8) | collective-permute-done | bytes 131104 | tf_op jit(solution)/shard_map/ppermute | solution.py:502
  41.9 1.8 %collective-permute-done.9 = bf16[64,1024]{1,0:T(8,128)(2,1)S(1)} collective-permute-done((bf16[64,1024]{1,0:T(8,128)(2,1)S(1)}, bf16[64,1024]{1,0:T(8,128)(2,1)S(1)}, u32[]{:S(2)}, u32[]{:S(2)}) %collective-permute-start.9) | collective-permute-done | bytes 131104 | tf_op jit(solution)/shard_map/ppermute | solution.py:555
  43.7 0.1 add_convert_fusion.1
  43.8 0.0 collective-permute-done.10.refs_2_
  43.8 2.1 %collective-permute-start.11 = (bf16[64,1024]{1,0:T(8,128)(2,1)S(1)}, bf16[64,1024]{1,0:T(8,128)(2,1)S(1)}, u32[]{:S(2)}, u32[]{:S(2)}) collective-permute-start(bf16[64,1024]{1,0:T(8,128)(2,1)S(1)} %add_convert_fusion.1), channel_id=1, source_target_pairs={{0,8},{4,12},{8,0},{12,4},{1,9},{5,13},{9,1},{13,5},{2,10},{6,14},... | collective-permute-start | bytes 393224 | tf_op jit(solution)/shard_map/ppermute | solution.py:502
  45.9 0.1 collective-permute-start.12
  46.0 5.3 %collective-permute-done.11 = bf16[64,1024]{1,0:T(8,128)(2,1)S(1)} collective-permute-done((bf16[64,1024]{1,0:T(8,128)(2,1)S(1)}, bf16[64,1024]{1,0:T(8,128)(2,1)S(1)}, u32[]{:S(2)}, u32[]{:S(2)}) %collective-permute-start.11) | collective-permute-done | bytes 131104 | tf_op jit(solution)/shard_map/ppermute | solution.py:502
  51.4 0.7 %collective-permute-done.12.refs_1_ = bf16[2,64,512]{2,1,0:T(8,128)(2,1)S(1)} collective-permute-done((bf16[2,64,512]{2,1,0:T(8,128)(2,1)S(1)}, bf16[2,64,512]{2,1,0:T(8,128)(2,1)S(1)}, u32[]{:S(2)}, u32[]{:S(2)}) %collective-permute-start.12) | collective-permute-done | bytes 131104 | tf_op jit(solution)/shard_map/ppermute | solution.py:487
  52.1 2.8 %collective-permute-start.15 = (bf16[64,1024]{1,0:T(8,128)(2,1)S(1)}, bf16[64,1024]{1,0:T(8,128)(2,1)S(1)}, u32[]{:S(2)}, u32[]{:S(2)}) collective-permute-start(bf16[64,1024]{1,0:T(8,128)(2,1)S(1)} %add_convert_fusion.own_ref), channel_id=1, source_target_pairs={{0,20},{4,16},{8,28},{12,24},{16,4},{20,0},{24,12},{28,8},{1,21},{... | collective-permute-start | bytes 393224 | tf_op jit(solution)/shard_map/ppermute | solution.py:570
  54.9 0.0 collective-permute-start.14
  54.9 0.7 %collective-permute-start.13 = (bf16[64,1024]{1,0:T(8,128)(2,1)S(1)}, bf16[64,1024]{1,0:T(8,128)(2,1)S(1)}, u32[]{:S(2)}, u32[]{:S(2)}) collective-permute-start(bf16[64,1024]{1,0:T(8,128)(2,1)S(1)} %add_convert_fusion.own_ref), channel_id=1, source_target_pairs={{0,4},{4,0},{8,12},{12,8},{1,5},{5,1},{9,13},{13,9},{2,6},{6,2},{1... | collective-permute-start | bytes 393224 | tf_op jit(solution)/shard_map/ppermute | solution.py:502
  55.6 0.0 copy-done.4
  55.6 1.9 %input.1 = (bf16[1,16,16,512]{3,2,1,0:T(8,128)(2,1)}, bf16[1,16,16,512]{3,2,1,0:T(8,128)(2,1)}) custom-call(bf16[16,64,1024]{2,1,0:T(8,128)(2,1)S(1)} %get-tuple-element.69.refs_1_.refs_0_, bf16[2,64,512]{2,1,0:T(8,128)(2,1)S(1)} %collective-permute-done.12.refs_1_, bf16[2,64,512]{2,1,0:T(8,128)(2,1)S(1)} %collective-permute-done.10.refs_2_, ...), custom_call_target="tpu_custom_call" | custom-call | flops 402653184 | bytes 6294528 | tf_op jit(solution)/shard_map/input/pallas_call | solution.py:444
  57.5 1.0 %collective-permute-done.15.far_ref = bf16[64,1024]{1,0:T(8,128)(2,1)S(1)} collective-permute-done((bf16[64,1024]{1,0:T(8,128)(2,1)S(1)}, bf16[64,1024]{1,0:T(8,128)(2,1)S(1)}, u32[]{:S(2)}, u32[]{:S(2)}) %collective-permute-start.15) | collective-permute-done | bytes 131104 | tf_op jit(solution)/shard_map/ppermute | solution.py:570
  58.4 1.4 %collective-permute-done.14.lon_ref = bf16[64,1024]{1,0:T(8,128)(2,1)S(1)} collective-permute-done((bf16[64,1024]{1,0:T(8,128)(2,1)S(1)}, bf16[64,1024]{1,0:T(8,128)(2,1)S(1)}, u32[]{:S(2)}, u32[]{:S(2)}) %collective-permute-start.14) | collective-permute-done | bytes 131104 | tf_op jit(solution)/shard_map/ppermute | solution.py:502
  59.8 0.1 collective-permute-done.13.lat_ref
  59.9 1.4 %finish.1 = (f32[128,1536]{1,0:T(8,128)}, f32[128,512]{1,0:T(8,128)}, f32[1,128]{1,0:T(1,128)}) custom-call(bf16[64,1024]{1,0:T(8,128)(2,1)S(1)} %add_convert_fusion.own_ref, bf16[64,1024]{1,0:T(8,128)(2,1)S(1)} %collective-permute-done.13.lat_ref, bf16[64,1024]{1,0:T(8,128)(2,1)S(1)} %collective-permute-done.14.lon_ref, ...), custom_call_target="tpu_custom_call" | custom-call | bytes 3148288 | tf_op jit(solution)/shard_map/finish/pallas_call | solution.py:444
  (1 shorter events, 0.0 us)
Async XLA Ops:
  0.6 12.5 %copy-start.1 = (bf16[1,16,16,512]{3,2,1,0:T(8,128)(2,1)S(1)}, bf16[1,16,16,512]{3,2,1,0:T(8,128)(2,1)}, u32[]{:S(2)}) copy-start(bf16[1,16,16,512]{3,2,1,0:T(8,128)(2,1)} %refs_9_.1) | copy-start | bytes 786436
  0.6 12.5 %copy-start.2 = (bf16[512,512]{1,0:T(8,128)(2,1)S(1)}, bf16[512,512]{1,0:T(8,128)(2,1)}, u32[]{:S(2)}) copy-start(bf16[512,512]{1,0:T(8,128)(2,1)} %wout_hbm.1) | copy-start | bytes 1572868
  0.7 1.0 %copy-start.3 = (bf16[1,16,16,512]{3,2,1,0:T(8,128)(2,1)S(1)}, bf16[1,16,16,512]{3,2,1,0:T(8,128)(2,1)}, u32[]{:S(2)}) copy-start(bf16[1,16,16,512]{3,2,1,0:T(8,128)(2,1)} %refs_10_.1) | copy-start | bytes 786436
  1.7 0.7 %copy-start.5 = (s32[1,16,16]{2,1,0:T(8,128)S(1)}, s32[1,16,16]{2,1,0:T(8,128)}, u32[]{:S(2)}) copy-start(s32[1,16,16]{2,1,0:T(8,128)} %refs_11_.1) | copy-start | bytes 3076
  2.4 10.7 %copy-start = (bf16[512,1536]{1,0:T(8,128)(2,1)S(1)}, bf16[512,1536]{1,0:T(8,128)(2,1)}, u32[]{:S(2)}) copy-start(bf16[512,1536]{1,0:T(8,128)(2,1)} %wqkv_hbm.1) | copy-start | bytes 4718596
  2.4 10.7 %copy-start.6 = (s32[1,16,16]{2,1,0:T(8,128)S(1)}, s32[1,16,16]{2,1,0:T(8,128)}, u32[]{:S(2)}) copy-start(s32[1,16,16]{2,1,0:T(8,128)} %refs_11_.1) | copy-start | bytes 3076
  2.4 10.7 %copy-start.7 = (f32[512]{0:T(512)S(1)}, f32[512]{0:T(512)}, u32[]{:S(2)}) copy-start(f32[512]{0:T(512)} %param.10) | copy-start | bytes 6148
  2.7 14.0 %collective-permute-start = (bf16[4,64,512]{2,1,0:T(8,128)(2,1)S(1)}, bf16[4,64,512]{2,1,0:T(8,128)(2,1)S(1)}, u32[]{:S(2)}, u32[]{:S(2)}) collective-permute-start(bf16[4,64,512]{2,1,0:T(8,128)(2,1)S(1)} %get-tuple-element.49.tok_ref.refs_4_), channel_id=1, source_target_pairs={{0,16},{16,0},{1,17},{17,1},{2,18},{18,2},{3,19},{19,3},{4,20},{20... | collective-permute-start | bytes 786440 | tf_op jit(solution)/shard_map/ppermute | solution.py:470
  5.7 9.4 %collective-permute-start.1 = (bf16[2,64,512]{2,1,0:T(8,128)(2,1)S(1)}, bf16[2,64,512]{2,1,0:T(8,128)(2,1)S(1)}, u32[]{:S(2)}, u32[]{:S(2)}) collective-permute-start(bf16[2,64,512]{2,1,0:T(8,128)(2,1)S(1)} %get-tuple-element.51), channel_id=1, source_target_pairs={{0,4},{8,12},{4,0},{12,8},{1,5},{9,13},{5,1},{13,9},{2,6},{10,14},... | collective-permute-start | bytes 393224 | tf_op jit(solution)/shard_map/ppermute | solution.py:487
  7.3 9.4 %collective-permute-start.2 = (bf16[2,64,512]{2,1,0:T(8,128)(2,1)S(1)}, bf16[2,64,512]{2,1,0:T(8,128)(2,1)S(1)}, u32[]{:S(2)}, u32[]{:S(2)}) collective-permute-start(bf16[2,64,512]{2,1,0:T(8,128)(2,1)S(1)} %get-tuple-element.52), channel_id=1, source_target_pairs={{4,8},{8,4},{5,9},{9,5},{6,10},{10,6},{7,11},{11,7},{20,24},{24,20... | collective-permute-start | bytes 393224 | tf_op jit(solution)/shard_map/ppermute | solution.py:487
  8.0 10.3 %collective-permute-start.4 = (bf16[2,64,512]{2,1,0:T(8,128)(2,1)S(1)}, bf16[2,64,512]{2,1,0:T(8,128)(2,1)S(1)}, u32[]{:S(2)}, u32[]{:S(2)}) collective-permute-start(bf16[2,64,512]{2,1,0:T(8,128)(2,1)S(1)} %get-tuple-element.51), channel_id=1, source_target_pairs={{0,20},{16,4},{8,28},{24,12},{20,0},{4,16},{28,8},{12,24},{1,21},{... | collective-permute-start | bytes 393224 | tf_op jit(solution)/shard_map/ppermute | solution.py:498
  12.4 5.9 %collective-permute-start.5 = (bf16[2,64,512]{2,1,0:T(8,128)(2,1)S(1)}, bf16[2,64,512]{2,1,0:T(8,128)(2,1)S(1)}, u32[]{:S(2)}, u32[]{:S(2)}) collective-permute-start(bf16[2,64,512]{2,1,0:T(8,128)(2,1)S(1)} %get-tuple-element.52), channel_id=1, source_target_pairs={{4,24},{20,8},{24,4},{8,20},{5,25},{21,9},{25,5},{9,21},{6,26},{22... | collective-permute-start | bytes 393224 | tf_op jit(solution)/shard_map/ppermute | solution.py:498
  15.1 8.2 %collective-permute-start.3 = (bf16[4,64,512]{2,1,0:T(8,128)(2,1)S(1)}, bf16[4,64,512]{2,1,0:T(8,128)(2,1)S(1)}, u32[]{:S(2)}, u32[]{:S(2)}) collective-permute-start(bf16[4,64,512]{2,1,0:T(8,128)(2,1)S(1)} %get-tuple-element.58.refs_6_.refs_4_), channel_id=1, source_target_pairs={{0,16},{16,0},{1,17},{17,1},{2,18},{18,2},{3,19},{19,3},{4,20},{20... | collective-permute-start | bytes 786440 | tf_op jit(solution)/shard_map/ppermute | solution.py:470
  29.7 25.9 %copy-start.4 = (bf16[1,16,16,512]{3,2,1,0:T(8,128)(2,1)S(1)}, bf16[1,16,16,512]{3,2,1,0:T(8,128)(2,1)}, u32[]{:S(2)}) copy-start(bf16[1,16,16,512]{3,2,1,0:T(8,128)(2,1)} %refs_10_.1) | copy-start | bytes 786436
  29.7 2.0 %collective-permute-start.6 = (bf16[2,2,64,1024]{3,2,1,0:T(8,128)(2,1)S(1)}, bf16[2,2,64,1024]{3,2,1,0:T(8,128)(2,1)S(1)}, u32[]{:S(2)}, u32[]{:S(2)}) collective-permute-start(bf16[2,2,64,1024]{3,2,1,0:T(8,128)(2,1)S(1)} %get-tuple-element.76), channel_id=1, source_target_pairs={{0,1},{1,0},{2,3},{3,2},{4,5},{5,4},{6,7},{7,6},{8,9},{9,8},{10,11... | collective-permute-start | bytes 1572872 | tf_op jit(solution)/shard_map/ppermute | solution.py:502
  31.8 6.5 %collective-permute-start.7 = (bf16[64,1024]{1,0:T(8,128)(2,1)S(1)}, bf16[64,1024]{1,0:T(8,128)(2,1)S(1)}, u32[]{:S(2)}, u32[]{:S(2)}) collective-permute-start(bf16[64,1024]{1,0:T(8,128)(2,1)S(1)} %get-tuple-element.78), channel_id=1, source_target_pairs={{0,2},{1,3},{2,0},{3,1},{4,6},{5,7},{6,4},{7,5},{8,10},{9,11},{10,... | collective-permute-start | bytes 393224 | tf_op jit(solution)/shard_map/ppermute | solution.py:502
  31.9 10.0 %collective-permute-start.8 = (bf16[64,1024]{1,0:T(8,128)(2,1)S(1)}, bf16[64,1024]{1,0:T(8,128)(2,1)S(1)}, u32[]{:S(2)}, u32[]{:S(2)}) collective-permute-start(bf16[64,1024]{1,0:T(8,128)(2,1)S(1)} %get-tuple-element.79), channel_id=1, source_target_pairs={{0,4},{4,0},{8,12},{12,8},{1,5},{5,1},{9,13},{13,9},{2,6},{6,2},{1... | collective-permute-start | bytes 393224 | tf_op jit(solution)/shard_map/ppermute | solution.py:502
  37.6 6.1 %collective-permute-start.9 = (bf16[64,1024]{1,0:T(8,128)(2,1)S(1)}, bf16[64,1024]{1,0:T(8,128)(2,1)S(1)}, u32[]{:S(2)}, u32[]{:S(2)}) collective-permute-start(bf16[64,1024]{1,0:T(8,128)(2,1)S(1)} %get-tuple-element.80), channel_id=1, source_target_pairs={{0,6},{1,7},{2,4},{3,5},{4,2},{5,3},{6,0},{7,1},{8,14},{9,15},{10,... | collective-permute-start | bytes 393224 | tf_op jit(solution)/shard_map/ppermute | solution.py:555
  37.6 6.2 %collective-permute-start.10 = (bf16[2,64,512]{2,1,0:T(8,128)(2,1)S(1)}, bf16[2,64,512]{2,1,0:T(8,128)(2,1)S(1)}, u32[]{:S(2)}, u32[]{:S(2)}) collective-permute-start(bf16[2,64,512]{2,1,0:T(8,128)(2,1)S(1)} %get-tuple-element.82), channel_id=1, source_target_pairs={{4,8},{8,4},{5,9},{9,5},{6,10},{10,6},{7,11},{11,7},{20,24},{24,20... | collective-permute-start | bytes 393224 | tf_op jit(solution)/shard_map/ppermute | solution.py:487
  43.8 7.5 %collective-permute-start.11 = (bf16[64,1024]{1,0:T(8,128)(2,1)S(1)}, bf16[64,1024]{1,0:T(8,128)(2,1)S(1)}, u32[]{:S(2)}, u32[]{:S(2)}) collective-permute-start(bf16[64,1024]{1,0:T(8,128)(2,1)S(1)} %add_convert_fusion.1), channel_id=1, source_target_pairs={{0,8},{4,12},{8,0},{12,4},{1,9},{5,13},{9,1},{13,5},{2,10},{6,14},... | collective-permute-start | bytes 393224 | tf_op jit(solution)/shard_map/ppermute | solution.py:502
  45.9 6.2 %collective-permute-start.12 = (bf16[2,64,512]{2,1,0:T(8,128)(2,1)S(1)}, bf16[2,64,512]{2,1,0:T(8,128)(2,1)S(1)}, u32[]{:S(2)}, u32[]{:S(2)}) collective-permute-start(bf16[2,64,512]{2,1,0:T(8,128)(2,1)S(1)} %get-tuple-element.84), channel_id=1, source_target_pairs={{0,4},{8,12},{4,0},{12,8},{1,5},{9,13},{5,1},{13,9},{2,6},{10,14},... | collective-permute-start | bytes 393224 | tf_op jit(solution)/shard_map/ppermute | solution.py:487
  52.1 6.3 %collective-permute-start.15 = (bf16[64,1024]{1,0:T(8,128)(2,1)S(1)}, bf16[64,1024]{1,0:T(8,128)(2,1)S(1)}, u32[]{:S(2)}, u32[]{:S(2)}) collective-permute-start(bf16[64,1024]{1,0:T(8,128)(2,1)S(1)} %add_convert_fusion.own_ref), channel_id=1, source_target_pairs={{0,20},{4,16},{8,28},{12,24},{16,4},{20,0},{24,12},{28,8},{1,21},{... | collective-permute-start | bytes 393224 | tf_op jit(solution)/shard_map/ppermute | solution.py:570
  54.9 5.0 %collective-permute-start.14 = (bf16[64,1024]{1,0:T(8,128)(2,1)S(1)}, bf16[64,1024]{1,0:T(8,128)(2,1)S(1)}, u32[]{:S(2)}, u32[]{:S(2)}) collective-permute-start(bf16[64,1024]{1,0:T(8,128)(2,1)S(1)} %add_convert_fusion.own_ref), channel_id=1, source_target_pairs={{0,16},{16,0},{1,17},{17,1},{2,18},{18,2},{3,19},{19,3},{4,20},{20... | collective-permute-start | bytes 393224 | tf_op jit(solution)/shard_map/ppermute | solution.py:502
  54.9 5.1 %collective-permute-start.13 = (bf16[64,1024]{1,0:T(8,128)(2,1)S(1)}, bf16[64,1024]{1,0:T(8,128)(2,1)S(1)}, u32[]{:S(2)}, u32[]{:S(2)}) collective-permute-start(bf16[64,1024]{1,0:T(8,128)(2,1)S(1)} %add_convert_fusion.own_ref), channel_id=1, source_target_pairs={{0,4},{4,0},{8,12},{12,8},{1,5},{5,1},{9,13},{13,9},{2,6},{6,2},{1... | collective-permute-start | bytes 393224 | tf_op jit(solution)/shard_map/ppermute | solution.py:502

commit v7 on v6

--- a/solution.py
+++ b/solution.py
@@ -147,24 +147,17 @@
 
 
 def own_kernel(
-    tok_ref, cot_hbm, mask_hbm, wqkv_hbm, wout_hbm, gain_hbm,
-    q_ref, kv_ref, hid_ref, gb_ref, bias_ref, wqkv_ref, wout_ref, gain_ref, info_ref,
-    cot_ref, mask_ref, sems,
+    tok_ref, wqkv_ref, gain_ref, cot_hbm, mask_hbm,
+    q_ref, kv_ref, hid_ref, gb_ref, bias_ref, info_ref, cot_ref, mask_ref, sems,
 ):
-    pairs = (
-        (mask_hbm, mask_ref), (cot_hbm, cot_ref), (gain_hbm, gain_ref), (wqkv_hbm, wqkv_ref),
-        (wout_hbm, wout_ref),
-    )
-    copies = load(pairs, sems)
-    wait(copies[:2])
+    copies = load(((mask_hbm, mask_ref), (cot_hbm, cot_ref)), sems)
+    tokens = tok_ref[...].reshape(4 * AREA, D)
+    write_block(tokens, wqkv_ref, gain_ref, q_ref, kv_ref, hid_ref, bias_ref, info_ref)
+    wait(copies)
     ocean = token_mask(mask_ref[0].astype(F32))
     cot = cot_ref[0].astype(F32)
     for w in range(4):
         gb_ref[w] = (window_of(cot, w) * ocean[w * AREA : (w + 1) * AREA]).astype(BF16)
-    wait(copies[2:4])
-    tokens = tok_ref[...].reshape(4 * AREA, D)
-    write_block(tokens, wqkv_ref, gain_ref, q_ref, kv_ref, hid_ref, bias_ref, info_ref)
-    wait(copies[4:])
 
 
 def lat_block(first_ref, second_ref, wkv_ref, gain_ref, kv_ref, hid_ref, bias_ref, at):
@@ -302,9 +295,9 @@
             ref[2:] = shares[at + 4 : at + 6]
 
 
-def sums_kernel(pair, hid, dkv, *refs):
-    held = [refs[k : k + 3] for k in range(0, len(refs) - 2, 3)]
-    keep, send = refs[-2:]
+def sums_kernel(pair, other, hid, dkv, *refs):
+    held = [refs[k : k + 3] for k in range(0, len(refs) - 1, 3)]
+    to = refs[-1]
     flat = lambda ref: ref[...].reshape(4 * AREA, D)
     lev = lax.axis_index("lev")
 
@@ -331,26 +324,24 @@
         odd, lon = lax.axis_index("lat") % 2, lax.axis_index("lon")
 
         def put(rel, at, value):
-            to = keep if rel % 2 == 0 else send
             value = value.astype(BF16)
             for k in range(2):
                 to[rel // 2, k ^ odd, :, at : at + D] = value[k * 64 : (k + 1) * 64]
 
         @pl.when(lon == 0)
         def _():
-            for rel in range(4):
+            for rel in (other, 2 + other):
                 put(rel, 0, query_sum(rel))
                 put(rel, D, dot(hid[:, columns(rel)], grad_part(0, D), 0, 0))
 
         @pl.when(lon == 1)
         def _():
-            for rel in range(4):
+            for rel in (other, 2 + other):
                 put(rel, 0, out_sum(rel))
                 put(rel, D, dot(hid[:, columns(rel)], grad_part(D, D), 0, 0))
 
     else:
-        for rel in range(4):
-            to = keep if rel % 2 == 0 else send
+        for rel in (other, 2 + other):
             to[rel // 2, :, :D] = query_sum(rel).astype(BF16)
             to[rel // 2, :, D : 2 * D] = out_sum(rel).astype(BF16)
             to[rel // 2, :, 2 * D :] = dot(hid[:, columns(rel)], grad_part(0, 2 * D), 0, 0).astype(BF16)
@@ -590,13 +581,13 @@
     if pair:
         corner_first, corner_second = corner_swap(tok_first, 0), corner_swap(tok_second, 1)
     tok_first, tok_second = lat_swaps(tok_first, tok_second)
-    q, kv, hid, gb, bias, wqkv, wout, gain, info = call(
+    q, kv, hid, gb, bias, info = call(
         "own", own_kernel,
-        [four, wide, shape((4 * AREA, D)), four, shape((4, 8, AREA), F32), shape(qkv_weight.shape),
-         shape(out_weight.shape), shape(gain.shape, F32), info_shape],
-        [], [tok], [], [cotangent, ocean_mask, qkv_weight, out_weight, gain], [grid, mask, DMAS((5,))], 16,
-        flops=2 * 256 * 512 * 1536, out_specs=[VMEM] * 8 + [SMEM],
-    )
+        [four, wide, shape((4 * AREA, D)), four, shape((4, 8, AREA), F32), info_shape],
+        [], [tok, qkv_weight, gain], [], [cotangent, ocean_mask], [grid, mask, DMAS((2,))], 16,
+        flops=2 * 256 * 512 * 1536, out_specs=[VMEM] * 5 + [SMEM],
+    )
+    wqkv, wout = qkv_weight, out_weight
     if pair:
         gb_near = lon_halo(gb)
     else:
@@ -634,10 +625,13 @@
         parts += [gq_near, mixed_near, gb_near]
     dkv, back_first, back_second, *side = rest
     share = shape((2, 2, 64, 2 * D) if pair else (2, 128, 4 * D))
-    keep, send = call(
-        "sums", lambda *refs: sums_kernel(pair, *refs), [share, share], [],
-        [hid_all, dkv] + parts, [], [], [], 24, flops=2 * 1024 * 512 * 1024,
-    )
+    send, keep = [
+        call(
+            name, lambda *refs, other=other: sums_kernel(pair, other, *refs), [share], [],
+            [hid_all, dkv] + parts, [], [], [], 24, flops=1024 * 512 * 1024,
+        )[0]
+        for name, other in (("sent", 1), ("kept", 0))
+    ]
     if pair:
         total = pair_sum(keep, send)
         back_second = lat_swap(back_second, 1)

time: 61.6 us -> 60.2 us (0.977); the launches traced: 61.4 us -> 60.9 us
  starting transfers between devices: 24.1 us -> 27.4 us
  Pallas kernels: 18.7 us -> 16.1 us
  waiting for transfers between devices: 15.9 us -> 14.6 us
    pallas_call x9 -> x10, Pallas kernels: 18.7 us -> 16.1 us  [call(): pl.pallas_call(kernel, out_shape=outs, in_specs=specs, out_specs=out_spec...]
    ppermute x6, starting transfers between devices: 8.62 us -> 10.9 us  [swap(): lax.ppermute(value, axis, [(i, i ^ bit) for i in range(lax.axis_size(axis...]
    ppermute x6, waiting for transfers between devices: 12.4 us -> 10.3 us  [swap(): lax.ppermute(value, axis, [(i, i ^ bit) for i in range(lax.axis_size(axis...]
    ppermute x4, starting transfers between devices: 3.04 us -> 3.98 us  [lat_swap(): return lax.ppermute(value, 'lat', pairs + [(b, a) for a, b in pairs])]
    ppermute x1, waiting for transfers between devices: 0.95 us -> 1.88 us  [pair_spread(): lax.ppermute(own, ('lon', 'lat'), [(i, i ^ count + 1) for i in range(2 *...]
    ppermute x4, waiting for transfers between devices: 0.69 us -> 0.01 us  [lat_swap(): return lax.ppermute(value, 'lat', pairs + [(b, a) for a, b in pairs])]
  transfers between devices with their start and end apart: 16 -> 16, of which waited for: 8 -> 7; matrix products, arithmetic and copies ran while one was open for 0% -> 0% of each run, Pallas kernels for 17% -> 16%
where the time goes in v7:
time: 60.2 us; the launch traced here: 60.9 us
  starting transfers between devices  27.4 us (46%)
  Pallas kernels  16.1 us (27%)
  waiting for transfers between devices  14.6 us (24%)
  local copies, waits for them, and re-layouts  1.8 us (3%)
  between operations  0.88 us (1%)
    pallas_call x10, Pallas kernels, call(): pl.pallas_call(kernel, out_shape=outs, in_specs=specs, out_specs=out_spec...  16.1 us
    ppermute x6, starting transfers between devices, swap(): lax.ppermute(value, axis, [(i, i ^ bit) for i in range(lax.axis_size(axis...  10.9 us
    ppermute x6, waiting for transfers between devices, swap(): lax.ppermute(value, axis, [(i, i ^ bit) for i in range(lax.axis_size(axis...  10.3 us
    ppermute x2, starting transfers between devices, corner_swap(): lax.ppermute(value, ('lon', 'lat'), pairs + [(b, a) for a, b in pairs])  5.09 us
    ppermute x2, starting transfers between devices, lon_halo(): return lax.ppermute(own, 'lon', [(0, 1), (1, 0)])  4.56 us
    ppermute x4, starting transfers between devices, lat_swap(): return lax.ppermute(value, 'lat', pairs + [(b, a) for a, b in pairs])  3.98 us
    ppermute x1, starting transfers between devices, pair_spread(): lax.ppermute(own, ('lon', 'lat'), [(i, i ^ count + 1) for i in range(2 *...  2.9 us
    ppermute x1, waiting for transfers between devices, pair_sum(): lax.ppermute(to_far, ('lat', 'lev'), [(i, i ^ 6) for i in range(4 * count)])  2.2 us
  transfers between devices with their start and end apart: 16, of which 7 were waited for; matrix products, arithmetic and copies ran while one was open for 0% of the time, Pallas kernels for 16%

profile of v7, /device:TPU:0, one launch (start us, length us, event | category | flops | bytes accessed | tf_op | source)
XLA Modules:
  0.0 60.9 jit_solution(5598992332433142723)
XLA Ops:
  0.6 0.0 copy-start
  0.6 0.0 copy-start.2
  0.7 0.0 copy-start.3
  0.7 1.1 %copy-done.3 = bf16[1,16,16,512]{3,2,1,0:T(8,128)(2,1)S(1)} copy-done((bf16[1,16,16,512]{3,2,1,0:T(8,128)(2,1)S(1)}, bf16[1,16,16,512]{3,2,1,0:T(8,128)(2,1)}, u32[]{:S(2)}) %copy-start.3) | copy-done | bytes 262168
  1.7 0.0 copy-start.5
  1.7 0.7 %copy-done.5 = s32[1,16,16]{2,1,0:T(8,128)S(1)} copy-done((s32[1,16,16]{2,1,0:T(8,128)S(1)}, s32[1,16,16]{2,1,0:T(8,128)}, u32[]{:S(2)}) %copy-start.5) | copy-done | bytes 1048
  2.4 0.0 copy-start.6
  2.4 0.0 copy-start.7
  2.4 0.4 prep.1
  2.8 3.0 %collective-permute-start = (bf16[4,64,512]{2,1,0:T(8,128)(2,1)S(1)}, bf16[4,64,512]{2,1,0:T(8,128)(2,1)S(1)}, u32[]{:S(2)}, u32[]{:S(2)}) collective-permute-start(bf16[4,64,512]{2,1,0:T(8,128)(2,1)S(1)} %get-tuple-element.44.tok_ref.refs_4_), channel_id=1, source_target_pairs={{0,16},{16,0},{1,17},{17,1},{2,18},{18,2},{3,19},{19,3},{4,20},{20... | collective-permute-start | bytes 786440 | tf_op jit(solution)/shard_map/ppermute | solution.py:461
  5.8 1.6 %collective-permute-start.1 = (bf16[2,64,512]{2,1,0:T(8,128)(2,1)S(1)}, bf16[2,64,512]{2,1,0:T(8,128)(2,1)S(1)}, u32[]{:S(2)}, u32[]{:S(2)}) collective-permute-start(bf16[2,64,512]{2,1,0:T(8,128)(2,1)S(1)} %get-tuple-element.46), channel_id=1, source_target_pairs={{0,4},{8,12},{4,0},{12,8},{1,5},{9,13},{5,1},{13,9},{2,6},{10,14},... | collective-permute-start | bytes 393224 | tf_op jit(solution)/shard_map/ppermute | solution.py:478
  7.4 0.7 %collective-permute-start.2 = (bf16[2,64,512]{2,1,0:T(8,128)(2,1)S(1)}, bf16[2,64,512]{2,1,0:T(8,128)(2,1)S(1)}, u32[]{:S(2)}, u32[]{:S(2)}) collective-permute-start(bf16[2,64,512]{2,1,0:T(8,128)(2,1)S(1)} %get-tuple-element.47), channel_id=1, source_target_pairs={{4,8},{8,4},{5,9},{9,5},{6,10},{10,6},{7,11},{11,7},{20,24},{24,20... | collective-permute-start | bytes 393224 | tf_op jit(solution)/shard_map/ppermute | solution.py:478
  8.0 4.4 %collective-permute-start.4 = (bf16[2,64,512]{2,1,0:T(8,128)(2,1)S(1)}, bf16[2,64,512]{2,1,0:T(8,128)(2,1)S(1)}, u32[]{:S(2)}, u32[]{:S(2)}) collective-permute-start(bf16[2,64,512]{2,1,0:T(8,128)(2,1)S(1)} %get-tuple-element.46), channel_id=1, source_target_pairs={{0,20},{16,4},{8,28},{24,12},{20,0},{4,16},{28,8},{12,24},{1,21},{... | collective-permute-start | bytes 393224 | tf_op jit(solution)/shard_map/ppermute | solution.py:489
  12.5 0.7 %collective-permute-start.5 = (bf16[2,64,512]{2,1,0:T(8,128)(2,1)S(1)}, bf16[2,64,512]{2,1,0:T(8,128)(2,1)S(1)}, u32[]{:S(2)}, u32[]{:S(2)}) collective-permute-start(bf16[2,64,512]{2,1,0:T(8,128)(2,1)S(1)} %get-tuple-element.47), channel_id=1, source_target_pairs={{4,24},{20,8},{24,4},{8,20},{5,25},{21,9},{25,5},{9,21},{6,26},{22... | collective-permute-start | bytes 393224 | tf_op jit(solution)/shard_map/ppermute | solution.py:489
  13.1 0.0 copy-done
  13.2 0.0 copy-done.2
  13.2 0.0 copy-done.6
  13.2 0.0 copy-done.7
  13.2 0.0 copy-start.1
  13.2 1.6 %own.1 = (bf16[4,64,512]{2,1,0:T(8,128)(2,1)S(1)}, bf16[4,64,1024]{2,1,0:T(8,128)(2,1)S(1)}, bf16[256,512]{1,0:T(8,128)(2,1)S(1)}, bf16[4,64,512]{2,1,0:T(8,128)...) custom-call(bf16[4,64,512]{2,1,0:T(8,128)(2,1)S(1)} %get-tuple-element.44.tok_ref.refs_4_, ...), custom_call_target="tpu_custom_call" | custom-call | flops 402653184 | bytes 3419168 | tf_op jit(solution)/shard_map/own/pallas_call | solution.py:435
  14.8 0.0 collective-permute-done.1.first_ref
  14.8 1.6 %collective-permute-start.3 = (bf16[4,64,512]{2,1,0:T(8,128)(2,1)S(1)}, bf16[4,64,512]{2,1,0:T(8,128)(2,1)S(1)}, u32[]{:S(2)}, u32[]{:S(2)}) collective-permute-start(bf16[4,64,512]{2,1,0:T(8,128)(2,1)S(1)} %get-tuple-element.50.refs_6_.refs_4_), channel_id=1, source_target_pairs={{0,16},{16,0},{1,17},{17,1},{2,18},{18,2},{3,19},{19,3},{4,20},{20... | collective-permute-start | bytes 786440 | tf_op jit(solution)/shard_map/ppermute | solution.py:461
  16.3 0.0 collective-permute-done.2.second_ref
  16.3 0.0 collective-permute-done.lon_ref
  16.3 1.6 %near.1 = (bf16[4,64,512]{2,1,0:T(8,128)(2,1)S(1)}, bf16[8,64,1024]{2,1,0:T(8,128)(2,1)S(1)}, bf16[512,512]{1,0:T(8,128)(2,1)S(1)}, f32[8,8,64]{2,1,0:T(8,128)S(1)}, s32[8]{0:T(128)S(1)}) custom-call(bf16[4,64,512]{2,1,0:T(8,128)(2,1)S(1)} %collective-permute-done.lon_ref, bf16[2,64,512]{2,1,0:T(8,128)(2,1)S(1)} %collective-permute-done.1.first_ref, ...), custom_call_target="tpu_custom_call" | custom-call | flops 671088640 | bytes 3950624 | tf_op jit(solution)/shard_map/near/pallas_call | solution.py:435
  18.0 0.0 collective-permute-done.4.refs_7_
  18.0 0.0 collective-permute-done.5.refs_8_
  18.0 0.0 copy-done.1
  18.0 3.6 %main.1 = (f32[16,64,1024]{2,1,0:T(8,128)S(1)}, bf16[4,64,512]{2,1,0:T(8,128)(2,1)S(1)}, bf16[4,64,512]{2,1,0:T(8,128)(2,1)S(1)}, bf16[1024,512]{1,0:T(8,128)(2,...) custom-call(s32[8]{0:T(128)S(1)} %get-tuple-element.45.refs_0_, s32[8]{0:T(128)S(1)} %get-tuple-element.48.refs_1_, ...), custom_call_target="tpu_custom_call" | custom-call | flops 2415919104 | bytes 13166592 | tf_op jit(solution)/shard_map/main/pallas_call | solution.py:435
  21.6 0.2 collective-permute-done.3.refs_6_.refs_7_
  21.8 4.0 %other.1 = (f32[16,64,1024]{2,1,0:T(8,128)S(1)}, bf16[4,64,512]{2,1,0:T(8,128)(2,1)S(1)}, bf16[4,64,512]{2,1,0:T(8,128)(2,1)S(1)}, bf16[16,64,1024]{2,1,0:T(8,12...) custom-call(s32[8]{0:T(128)S(1)} %get-tuple-element.45.refs_0_, ...), custom_call_target="tpu_custom_call", output_to_operand_aliasing={{0}: (9, {})} | custom-call | flops 2415919104 | bytes 16025600 | tf_op jit(solution)/shard_map/other/pallas_call | solution.py:435
  25.8 0.6 %sent.1 = bf16[2,2,64,1024]{3,2,1,0:T(8,128)(2,1)S(1)} custom-call(bf16[1024,512]{1,0:T(8,128)(2,1)S(1)} %get-tuple-element.62.refs_0_, bf16[16,64,1024]{2,1,0:T(8,128)(2,1)S(1)} %get-tuple-element.61.refs_1_.refs_0_, bf16[4,64,512]{2,1,0:T(8,128)(2,1)S(1)} %get-tuple-element.63.refs_2_.refs_3_, bf16[4,64,512]{2,1,0:T(8,128)(2,1)S(1)} %get-tuple-element.64.refs_3_.refs_5_, ...), custom_call_target="tpu_custom_call" | custom-call | flops 536870912 | bytes 5242880 | tf_op jit(solution)/shard_map/sent/pallas_call | solution.py:435
  26.4 0.1 collective-permute-start.6
  26.5 0.8 %kept.1.keep_ref = bf16[2,2,64,1024]{3,2,1,0:T(8,128)(2,1)S(1)} custom-call(bf16[1024,512]{1,0:T(8,128)(2,1)S(1)} %get-tuple-element.62.refs_0_, bf16[16,64,1024]{2,1,0:T(8,128)(2,1)S(1)} %get-tuple-element.61.refs_1_.refs_0_, bf16[4,64,512]{2,1,0:T(8,128)(2,1)S(1)} %get-tuple-element.63.refs_2_.refs_3_, ...), custom_call_target="tpu_custom_call" | custom-call | flops 536870912 | bytes 5242880 | tf_op jit(solution)/shard_map/kept/pallas_call | solution.py:435
  27.4 0.0 copy-start.4
  27.4 1.1 %collective-permute-done.6.come_ref = bf16[2,2,64,1024]{3,2,1,0:T(8,128)(2,1)S(1)} collective-permute-done((bf16[2,2,64,1024]{3,2,1,0:T(8,128)(2,1)S(1)}, bf16[2,2,64,1024]{3,2,1,0:T(8,128)(2,1)S(1)}, u32[]{:S(2)}, u32[]{:S(2)}) %collective-permute-start.6) | collective-permute-done | bytes 524320 | tf_op jit(solution)/shard_map/ppermute | solution.py:493
  28.4 0.1 split.1
  28.5 0.4 collective-permute-start.7
  28.9 7.1 %collective-permute-start.8 = (bf16[64,1024]{1,0:T(8,128)(2,1)S(1)}, bf16[64,1024]{1,0:T(8,128)(2,1)S(1)}, u32[]{:S(2)}, u32[]{:S(2)}) collective-permute-start(bf16[64,1024]{1,0:T(8,128)(2,1)S(1)} %get-tuple-element.69), channel_id=1, source_target_pairs={{0,4},{4,0},{8,12},{12,8},{1,5},{5,1},{9,13},{13,9},{2,6},{6,2},{1... | collective-permute-start | bytes 393224 | tf_op jit(solution)/shard_map/ppermute | solution.py:493
  36.0 0.0 collective-permute-start.9
  36.0 0.7 %collective-permute-start.10 = (bf16[2,64,512]{2,1,0:T(8,128)(2,1)S(1)}, bf16[2,64,512]{2,1,0:T(8,128)(2,1)S(1)}, u32[]{:S(2)}, u32[]{:S(2)}) collective-permute-start(bf16[2,64,512]{2,1,0:T(8,128)(2,1)S(1)} %get-tuple-element.72), channel_id=1, source_target_pairs={{4,8},{8,4},{5,9},{9,5},{6,10},{10,6},{7,11},{11,7},{20,24},{24,20... | collective-permute-start | bytes 393224 | tf_op jit(solution)/shard_map/ppermute | solution.py:478
  36.6 0.0 collective-permute-done.7
  36.7 3.6 %collective-permute-done.8 = bf16[64,1024]{1,0:T(8,128)(2,1)S(1)} collective-permute-done((bf16[64,1024]{1,0:T(8,128)(2,1)S(1)}, bf16[64,1024]{1,0:T(8,128)(2,1)S(1)}, u32[]{:S(2)}, u32[]{:S(2)}) %collective-permute-start.8) | collective-permute-done | bytes 131104 | tf_op jit(solution)/shard_map/ppermute | solution.py:493
  40.3 2.2 %collective-permute-done.9 = bf16[64,1024]{1,0:T(8,128)(2,1)S(1)} collective-permute-done((bf16[64,1024]{1,0:T(8,128)(2,1)S(1)}, bf16[64,1024]{1,0:T(8,128)(2,1)S(1)}, u32[]{:S(2)}, u32[]{:S(2)}) %collective-permute-start.9) | collective-permute-done | bytes 131104 | tf_op jit(solution)/shard_map/ppermute | solution.py:546
  42.5 0.1 add_convert_fusion.1
  42.5 0.0 collective-permute-done.10.refs_2_
  42.5 2.7 %collective-permute-start.11 = (bf16[64,1024]{1,0:T(8,128)(2,1)S(1)}, bf16[64,1024]{1,0:T(8,128)(2,1)S(1)}, u32[]{:S(2)}, u32[]{:S(2)}) collective-permute-start(bf16[64,1024]{1,0:T(8,128)(2,1)S(1)} %add_convert_fusion.1), channel_id=1, source_target_pairs={{0,8},{4,12},{8,0},{12,4},{1,9},{5,13},{9,1},{13,5},{2,10},{6,14},... | collective-permute-start | bytes 393224 | tf_op jit(solution)/shard_map/ppermute | solution.py:493
  45.3 1.1 %collective-permute-start.12 = (bf16[2,64,512]{2,1,0:T(8,128)(2,1)S(1)}, bf16[2,64,512]{2,1,0:T(8,128)(2,1)S(1)}, u32[]{:S(2)}, u32[]{:S(2)}) collective-permute-start(bf16[2,64,512]{2,1,0:T(8,128)(2,1)S(1)} %get-tuple-element.74), channel_id=1, source_target_pairs={{0,4},{8,12},{4,0},{12,8},{1,5},{9,13},{5,1},{13,9},{2,6},{10,14},... | collective-permute-start | bytes 393224 | tf_op jit(solution)/shard_map/ppermute | solution.py:478
  46.3 4.7 %collective-permute-done.11 = bf16[64,1024]{1,0:T(8,128)(2,1)S(1)} collective-permute-done((bf16[64,1024]{1,0:T(8,128)(2,1)S(1)}, bf16[64,1024]{1,0:T(8,128)(2,1)S(1)}, u32[]{:S(2)}, u32[]{:S(2)}) %collective-permute-start.11) | collective-permute-done | bytes 131104 | tf_op jit(solution)/shard_map/ppermute | solution.py:493
  51.1 0.0 collective-permute-done.12.refs_1_
  51.1 2.9 %collective-permute-start.15 = (bf16[64,1024]{1,0:T(8,128)(2,1)S(1)}, bf16[64,1024]{1,0:T(8,128)(2,1)S(1)}, u32[]{:S(2)}, u32[]{:S(2)}) collective-permute-start(bf16[64,1024]{1,0:T(8,128)(2,1)S(1)} %add_convert_fusion.own_ref), channel_id=1, source_target_pairs={{0,20},{4,16},{8,28},{12,24},{16,4},{20,0},{24,12},{28,8},{1,21},{... | collective-permute-start | bytes 393224 | tf_op jit(solution)/shard_map/ppermute | solution.py:561
  54.0 0.0 collective-permute-start.14
  54.0 0.6 %collective-permute-start.13 = (bf16[64,1024]{1,0:T(8,128)(2,1)S(1)}, bf16[64,1024]{1,0:T(8,128)(2,1)S(1)}, u32[]{:S(2)}, u32[]{:S(2)}) collective-permute-start(bf16[64,1024]{1,0:T(8,128)(2,1)S(1)} %add_convert_fusion.own_ref), channel_id=1, source_target_pairs={{0,4},{4,0},{8,12},{12,8},{1,5},{5,1},{9,13},{13,9},{2,6},{6,2},{1... | collective-permute-start | bytes 393224 | tf_op jit(solution)/shard_map/ppermute | solution.py:493
  54.7 0.0 copy-done.4
  54.7 1.9 %input.1 = (bf16[1,16,16,512]{3,2,1,0:T(8,128)(2,1)}, bf16[1,16,16,512]{3,2,1,0:T(8,128)(2,1)}) custom-call(bf16[16,64,1024]{2,1,0:T(8,128)(2,1)S(1)} %get-tuple-element.61.refs_1_.refs_0_, bf16[2,64,512]{2,1,0:T(8,128)(2,1)S(1)} %collective-permute-done.12.refs_1_, bf16[2,64,512]{2,1,0:T(8,128)(2,1)S(1)} %collective-permute-done.10.refs_2_, ...), custom_call_target="tpu_custom_call" | custom-call | flops 402653184 | bytes 6294528 | tf_op jit(solution)/shard_map/input/pallas_call | solution.py:435
  56.6 1.9 %collective-permute-done.15.far_ref = bf16[64,1024]{1,0:T(8,128)(2,1)S(1)} collective-permute-done((bf16[64,1024]{1,0:T(8,128)(2,1)S(1)}, bf16[64,1024]{1,0:T(8,128)(2,1)S(1)}, u32[]{:S(2)}, u32[]{:S(2)}) %collective-permute-start.15) | collective-permute-done | bytes 131104 | tf_op jit(solution)/shard_map/ppermute | solution.py:561
  58.5 1.0 %collective-permute-done.14.lon_ref = bf16[64,1024]{1,0:T(8,128)(2,1)S(1)} collective-permute-done((bf16[64,1024]{1,0:T(8,128)(2,1)S(1)}, bf16[64,1024]{1,0:T(8,128)(2,1)S(1)}, u32[]{:S(2)}, u32[]{:S(2)}) %collective-permute-start.14) | collective-permute-done | bytes 131104 | tf_op jit(solution)/shard_map/ppermute | solution.py:493
  59.4 0.0 collective-permute-done.13.lat_ref
  59.4 1.5 %finish.1 = (f32[128,1536]{1,0:T(8,128)}, f32[128,512]{1,0:T(8,128)}, f32[1,128]{1,0:T(1,128)}) custom-call(bf16[64,1024]{1,0:T(8,128)(2,1)S(1)} %add_convert_fusion.own_ref, bf16[64,1024]{1,0:T(8,128)(2,1)S(1)} %collective-permute-done.13.lat_ref, bf16[64,1024]{1,0:T(8,128)(2,1)S(1)} %collective-permute-done.14.lon_ref, ...), custom_call_target="tpu_custom_call" | custom-call | bytes 3148288 | tf_op jit(solution)/shard_map/finish/pallas_call | solution.py:435
  (1 shorter events, 0.0 us)
Async XLA Ops:
  0.6 12.5 %copy-start = (bf16[512,1536]{1,0:T(8,128)(2,1)S(1)}, bf16[512,1536]{1,0:T(8,128)(2,1)}, u32[]{:S(2)}) copy-start(bf16[512,1536]{1,0:T(8,128)(2,1)} %wqkv_ref.5) | copy-start | bytes 4718596
  0.6 12.5 %copy-start.2 = (bf16[1,16,16,512]{3,2,1,0:T(8,128)(2,1)S(1)}, bf16[1,16,16,512]{3,2,1,0:T(8,128)(2,1)}, u32[]{:S(2)}) copy-start(bf16[1,16,16,512]{3,2,1,0:T(8,128)(2,1)} %refs_9_.1) | copy-start | bytes 786436
  0.7 1.1 %copy-start.3 = (bf16[1,16,16,512]{3,2,1,0:T(8,128)(2,1)S(1)}, bf16[1,16,16,512]{3,2,1,0:T(8,128)(2,1)}, u32[]{:S(2)}) copy-start(bf16[1,16,16,512]{3,2,1,0:T(8,128)(2,1)} %refs_10_.1) | copy-start | bytes 786436
  1.7 0.7 %copy-start.5 = (s32[1,16,16]{2,1,0:T(8,128)S(1)}, s32[1,16,16]{2,1,0:T(8,128)}, u32[]{:S(2)}) copy-start(s32[1,16,16]{2,1,0:T(8,128)} %refs_11_.1) | copy-start | bytes 3076
  2.4 10.7 %copy-start.6 = (s32[1,16,16]{2,1,0:T(8,128)S(1)}, s32[1,16,16]{2,1,0:T(8,128)}, u32[]{:S(2)}) copy-start(s32[1,16,16]{2,1,0:T(8,128)} %refs_11_.1) | copy-start | bytes 3076
  2.4 10.7 %copy-start.7 = (f32[512]{0:T(512)S(1)}, f32[512]{0:T(512)}, u32[]{:S(2)}) copy-start(f32[512]{0:T(512)} %param.10) | copy-start | bytes 6148
  2.8 13.5 %collective-permute-start = (bf16[4,64,512]{2,1,0:T(8,128)(2,1)S(1)}, bf16[4,64,512]{2,1,0:T(8,128)(2,1)S(1)}, u32[]{:S(2)}, u32[]{:S(2)}) collective-permute-start(bf16[4,64,512]{2,1,0:T(8,128)(2,1)S(1)} %get-tuple-element.44.tok_ref.refs_4_), channel_id=1, source_target_pairs={{0,16},{16,0},{1,17},{17,1},{2,18},{18,2},{3,19},{19,3},{4,20},{20... | collective-permute-start | bytes 786440 | tf_op jit(solution)/shard_map/ppermute | solution.py:461
  5.8 9.0 %collective-permute-start.1 = (bf16[2,64,512]{2,1,0:T(8,128)(2,1)S(1)}, bf16[2,64,512]{2,1,0:T(8,128)(2,1)S(1)}, u32[]{:S(2)}, u32[]{:S(2)}) collective-permute-start(bf16[2,64,512]{2,1,0:T(8,128)(2,1)S(1)} %get-tuple-element.46), channel_id=1, source_target_pairs={{0,4},{8,12},{4,0},{12,8},{1,5},{9,13},{5,1},{13,9},{2,6},{10,14},... | collective-permute-start | bytes 393224 | tf_op jit(solution)/shard_map/ppermute | solution.py:478
  7.4 8.9 %collective-permute-start.2 = (bf16[2,64,512]{2,1,0:T(8,128)(2,1)S(1)}, bf16[2,64,512]{2,1,0:T(8,128)(2,1)S(1)}, u32[]{:S(2)}, u32[]{:S(2)}) collective-permute-start(bf16[2,64,512]{2,1,0:T(8,128)(2,1)S(1)} %get-tuple-element.47), channel_id=1, source_target_pairs={{4,8},{8,4},{5,9},{9,5},{6,10},{10,6},{7,11},{11,7},{20,24},{24,20... | collective-permute-start | bytes 393224 | tf_op jit(solution)/shard_map/ppermute | solution.py:478
  8.0 9.9 %collective-permute-start.4 = (bf16[2,64,512]{2,1,0:T(8,128)(2,1)S(1)}, bf16[2,64,512]{2,1,0:T(8,128)(2,1)S(1)}, u32[]{:S(2)}, u32[]{:S(2)}) collective-permute-start(bf16[2,64,512]{2,1,0:T(8,128)(2,1)S(1)} %get-tuple-element.46), channel_id=1, source_target_pairs={{0,20},{16,4},{8,28},{24,12},{20,0},{4,16},{28,8},{12,24},{1,21},{... | collective-permute-start | bytes 393224 | tf_op jit(solution)/shard_map/ppermute | solution.py:489
  12.5 5.5 %collective-permute-start.5 = (bf16[2,64,512]{2,1,0:T(8,128)(2,1)S(1)}, bf16[2,64,512]{2,1,0:T(8,128)(2,1)S(1)}, u32[]{:S(2)}, u32[]{:S(2)}) collective-permute-start(bf16[2,64,512]{2,1,0:T(8,128)(2,1)S(1)} %get-tuple-element.47), channel_id=1, source_target_pairs={{4,24},{20,8},{24,4},{8,20},{5,25},{21,9},{25,5},{9,21},{6,26},{22... | collective-permute-start | bytes 393224 | tf_op jit(solution)/shard_map/ppermute | solution.py:489
  13.2 4.8 %copy-start.1 = (bf16[512,512]{1,0:T(8,128)(2,1)S(1)}, bf16[512,512]{1,0:T(8,128)(2,1)}, u32[]{:S(2)}) copy-start(bf16[512,512]{1,0:T(8,128)(2,1)} %refs_7_.1) | copy-start | bytes 1572868
  14.8 7.0 %collective-permute-start.3 = (bf16[4,64,512]{2,1,0:T(8,128)(2,1)S(1)}, bf16[4,64,512]{2,1,0:T(8,128)(2,1)S(1)}, u32[]{:S(2)}, u32[]{:S(2)}) collective-permute-start(bf16[4,64,512]{2,1,0:T(8,128)(2,1)S(1)} %get-tuple-element.50.refs_6_.refs_4_), channel_id=1, source_target_pairs={{0,16},{16,0},{1,17},{17,1},{2,18},{18,2},{3,19},{19,3},{4,20},{20... | collective-permute-start | bytes 786440 | tf_op jit(solution)/shard_map/ppermute | solution.py:461
  26.4 2.0 %collective-permute-start.6 = (bf16[2,2,64,1024]{3,2,1,0:T(8,128)(2,1)S(1)}, bf16[2,2,64,1024]{3,2,1,0:T(8,128)(2,1)S(1)}, u32[]{:S(2)}, u32[]{:S(2)}) collective-permute-start(bf16[2,2,64,1024]{3,2,1,0:T(8,128)(2,1)S(1)} %sent.1), channel_id=1, source_target_pairs={{0,1},{1,0},{2,3},{3,2},{4,5},{5,4},{6,7},{7,6},{8,9},{9,8},{10,11... | collective-permute-start | bytes 1572872 | tf_op jit(solution)/shard_map/ppermute | solution.py:493
  27.4 27.3 %copy-start.4 = (bf16[1,16,16,512]{3,2,1,0:T(8,128)(2,1)S(1)}, bf16[1,16,16,512]{3,2,1,0:T(8,128)(2,1)}, u32[]{:S(2)}) copy-start(bf16[1,16,16,512]{3,2,1,0:T(8,128)(2,1)} %refs_10_.1) | copy-start | bytes 786436
  28.5 8.1 %collective-permute-start.7 = (bf16[64,1024]{1,0:T(8,128)(2,1)S(1)}, bf16[64,1024]{1,0:T(8,128)(2,1)S(1)}, u32[]{:S(2)}, u32[]{:S(2)}) collective-permute-start(bf16[64,1024]{1,0:T(8,128)(2,1)S(1)} %get-tuple-element.68), channel_id=1, source_target_pairs={{0,2},{1,3},{2,0},{3,1},{4,6},{5,7},{6,4},{7,5},{8,10},{9,11},{10,... | collective-permute-start | bytes 393224 | tf_op jit(solution)/shard_map/ppermute | solution.py:493
  28.9 11.4 %collective-permute-start.8 = (bf16[64,1024]{1,0:T(8,128)(2,1)S(1)}, bf16[64,1024]{1,0:T(8,128)(2,1)S(1)}, u32[]{:S(2)}, u32[]{:S(2)}) collective-permute-start(bf16[64,1024]{1,0:T(8,128)(2,1)S(1)} %get-tuple-element.69), channel_id=1, source_target_pairs={{0,4},{4,0},{8,12},{12,8},{1,5},{5,1},{9,13},{13,9},{2,6},{6,2},{1... | collective-permute-start | bytes 393224 | tf_op jit(solution)/shard_map/ppermute | solution.py:493
  36.0 6.5 %collective-permute-start.9 = (bf16[64,1024]{1,0:T(8,128)(2,1)S(1)}, bf16[64,1024]{1,0:T(8,128)(2,1)S(1)}, u32[]{:S(2)}, u32[]{:S(2)}) collective-permute-start(bf16[64,1024]{1,0:T(8,128)(2,1)S(1)} %get-tuple-element.70), channel_id=1, source_target_pairs={{0,6},{1,7},{2,4},{3,5},{4,2},{5,3},{6,0},{7,1},{8,14},{9,15},{10,... | collective-permute-start | bytes 393224 | tf_op jit(solution)/shard_map/ppermute | solution.py:546
  36.0 6.6 %collective-permute-start.10 = (bf16[2,64,512]{2,1,0:T(8,128)(2,1)S(1)}, bf16[2,64,512]{2,1,0:T(8,128)(2,1)S(1)}, u32[]{:S(2)}, u32[]{:S(2)}) collective-permute-start(bf16[2,64,512]{2,1,0:T(8,128)(2,1)S(1)} %get-tuple-element.72), channel_id=1, source_target_pairs={{4,8},{8,4},{5,9},{9,5},{6,10},{10,6},{7,11},{11,7},{20,24},{24,20... | collective-permute-start | bytes 393224 | tf_op jit(solution)/shard_map/ppermute | solution.py:478
  42.5 8.5 %collective-permute-start.11 = (bf16[64,1024]{1,0:T(8,128)(2,1)S(1)}, bf16[64,1024]{1,0:T(8,128)(2,1)S(1)}, u32[]{:S(2)}, u32[]{:S(2)}) collective-permute-start(bf16[64,1024]{1,0:T(8,128)(2,1)S(1)} %add_convert_fusion.1), channel_id=1, source_target_pairs={{0,8},{4,12},{8,0},{12,4},{1,9},{5,13},{9,1},{13,5},{2,10},{6,14},... | collective-permute-start | bytes 393224 | tf_op jit(solution)/shard_map/ppermute | solution.py:493
  45.3 5.8 %collective-permute-start.12 = (bf16[2,64,512]{2,1,0:T(8,128)(2,1)S(1)}, bf16[2,64,512]{2,1,0:T(8,128)(2,1)S(1)}, u32[]{:S(2)}, u32[]{:S(2)}) collective-permute-start(bf16[2,64,512]{2,1,0:T(8,128)(2,1)S(1)} %get-tuple-element.74), channel_id=1, source_target_pairs={{0,4},{8,12},{4,0},{12,8},{1,5},{9,13},{5,1},{13,9},{2,6},{10,14},... | collective-permute-start | bytes 393224 | tf_op jit(solution)/shard_map/ppermute | solution.py:478
  51.1 7.3 %collective-permute-start.15 = (bf16[64,1024]{1,0:T(8,128)(2,1)S(1)}, bf16[64,1024]{1,0:T(8,128)(2,1)S(1)}, u32[]{:S(2)}, u32[]{:S(2)}) collective-permute-start(bf16[64,1024]{1,0:T(8,128)(2,1)S(1)} %add_convert_fusion.own_ref), channel_id=1, source_target_pairs={{0,20},{4,16},{8,28},{12,24},{16,4},{20,0},{24,12},{28,8},{1,21},{... | collective-permute-start | bytes 393224 | tf_op jit(solution)/shard_map/ppermute | solution.py:561
  54.0 5.4 %collective-permute-start.14 = (bf16[64,1024]{1,0:T(8,128)(2,1)S(1)}, bf16[64,1024]{1,0:T(8,128)(2,1)S(1)}, u32[]{:S(2)}, u32[]{:S(2)}) collective-permute-start(bf16[64,1024]{1,0:T(8,128)(2,1)S(1)} %add_convert_fusion.own_ref), channel_id=1, source_target_pairs={{0,16},{16,0},{1,17},{17,1},{2,18},{18,2},{3,19},{19,3},{4,20},{20... | collective-permute-start | bytes 393224 | tf_op jit(solution)/shard_map/ppermute | solution.py:493
  54.0 5.4 %collective-permute-start.13 = (bf16[64,1024]{1,0:T(8,128)(2,1)S(1)}, bf16[64,1024]{1,0:T(8,128)(2,1)S(1)}, u32[]{:S(2)}, u32[]{:S(2)}) collective-permute-start(bf16[64,1024]{1,0:T(8,128)(2,1)S(1)} %add_convert_fusion.own_ref), channel_id=1, source_target_pairs={{0,4},{4,0},{8,12},{12,8},{1,5},{5,1},{9,13},{13,9},{2,6},{6,2},{1... | collective-permute-start | bytes 393224 | tf_op jit(solution)/shard_map/ppermute | solution.py:493

commit v8 on v7

--- a/solution.py
+++ b/solution.py
@@ -578,8 +578,7 @@
     )
     tok_lon = lon_halo(tok)
     odd = lax.axis_index("lat") % 2
-    if pair:
-        corner_first, corner_second = corner_swap(tok_first, 0), corner_swap(tok_second, 1)
+    sides = tok_first, tok_second
     tok_first, tok_second = lat_swaps(tok_first, tok_second)
     q, kv, hid, gb, bias, info = call(
         "own", own_kernel,
@@ -589,6 +588,8 @@
     )
     wqkv, wout = qkv_weight, out_weight
     if pair:
+        sides, gb = lax.optimization_barrier((sides, gb))
+        corner_first, corner_second = corner_swap(sides[0], 0), corner_swap(sides[1], 1)
         gb_near = lon_halo(gb)
     else:
         rows = tok_lon.reshape(2, 2, AREA, D)

time: 60.2 us -> 61.6 us (1.023); the launches traced: 60.9 us -> 60.9 us
  Pallas kernels: 16.1 us -> 18.9 us
  starting transfers between devices: 27.4 us -> 25 us
    pallas_call x10, Pallas kernels: 16.1 us -> 18.9 us  [call(): pl.pallas_call(kernel, out_shape=outs, in_specs=specs, out_specs=out_spec...]
    ppermute x1, starting transfers between devices: 2.9 us -> 0.5 us  [pair_spread(): lax.ppermute(own, ('lon', 'lat'), [(i, i ^ count + 1) for i in range(2 *...]
    ppermute x1, waiting for transfers between devices: 1.88 us -> 0.57 us  [pair_spread(): lax.ppermute(own, ('lon', 'lat'), [(i, i ^ count + 1) for i in range(2 *...]
    ppermute x4, starting transfers between devices: 3.98 us -> 3.05 us  [lat_swap(): return lax.ppermute(value, 'lat', pairs + [(b, a) for a, b in pairs])]
    ppermute x1, starting transfers between devices: 0.01 us -> 0.74 us  [pair_sum(): lax.ppermute(to_far, ('lat', 'lev'), [(i, i ^ 6) for i in range(4 * count)])]
  transfers between devices with their start and end apart: 16 -> 16, of which waited for: 7 -> 7; matrix products, arithmetic and copies ran while one was open for 0% -> 0% of each run, Pallas kernels for 16% -> 20%
where the time goes in v8:
time: 61.6 us; the launch traced here: 60.9 us
  starting transfers between devices  25 us (41%)
  Pallas kernels  18.9 us (31%)
  waiting for transfers between devices  14.2 us (23%)
  local copies, waits for them, and re-layouts  1.8 us (3%)
  between operations  0.89 us (1%)
    pallas_call x10, Pallas kernels, call(): pl.pallas_call(kernel, out_shape=outs, in_specs=specs, out_specs=out_spec...  18.9 us
    ppermute x6, starting transfers between devices, swap(): lax.ppermute(value, axis, [(i, i ^ bit) for i in range(lax.axis_size(axis...  11.1 us
    ppermute x6, waiting for transfers between devices, swap(): lax.ppermute(value, axis, [(i, i ^ bit) for i in range(lax.axis_size(axis...  10.9 us
    ppermute x2, starting transfers between devices, corner_swap(): lax.ppermute(value, ('lon', 'lat'), pairs + [(b, a) for a, b in pairs])  5.09 us
    ppermute x2, starting transfers between devices, lon_halo(): return lax.ppermute(own, 'lon', [(0, 1), (1, 0)])  4.56 us
    ppermute x4, starting transfers between devices, lat_swap(): return lax.ppermute(value, 'lat', pairs + [(b, a) for a, b in pairs])  3.05 us
    ppermute x1, waiting for transfers between devices, pair_sum(): lax.ppermute(to_far, ('lat', 'lev'), [(i, i ^ 6) for i in range(4 * count)])  2.77 us
    unnamed x16, local copies, waits for them, and re-layouts  1.8 us
  transfers between devices with their start and end apart: 16, of which 7 were waited for; matrix products, arithmetic and copies ran while one was open for 0% of the time, Pallas kernels for 20%

profile of v8, /device:TPU:0, one launch (start us, length us, event | category | flops | bytes accessed | tf_op | source)
XLA Modules:
  0.0 60.9 jit_solution(12610998468820624810)
XLA Ops:
  0.6 0.0 copy-start
  0.6 0.0 copy-start.2
  0.7 0.0 copy-start.3
  0.7 1.1 %copy-done.3 = bf16[1,16,16,512]{3,2,1,0:T(8,128)(2,1)S(1)} copy-done((bf16[1,16,16,512]{3,2,1,0:T(8,128)(2,1)S(1)}, bf16[1,16,16,512]{3,2,1,0:T(8,128)(2,1)}, u32[]{:S(2)}) %copy-start.3) | copy-done | bytes 262168
  1.7 0.0 copy-start.5
  1.7 0.7 %copy-done.5 = s32[1,16,16]{2,1,0:T(8,128)S(1)} copy-done((s32[1,16,16]{2,1,0:T(8,128)S(1)}, s32[1,16,16]{2,1,0:T(8,128)}, u32[]{:S(2)}) %copy-start.5) | copy-done | bytes 1048
  2.4 0.0 copy-start.6
  2.4 0.0 copy-start.7
  2.4 0.4 prep.1
  2.8 3.0 %collective-permute-start = (bf16[4,64,512]{2,1,0:T(8,128)(2,1)S(1)}, bf16[4,64,512]{2,1,0:T(8,128)(2,1)S(1)}, u32[]{:S(2)}, u32[]{:S(2)}) collective-permute-start(bf16[4,64,512]{2,1,0:T(8,128)(2,1)S(1)} %get-tuple-element.47.tok_ref.refs_4_), channel_id=1, source_target_pairs={{0,16},{16,0},{1,17},{17,1},{2,18},{18,2},{3,19},{19,3},{4,20},{20... | collective-permute-start | bytes 786440 | tf_op jit(solution)/shard_map/ppermute | solution.py:461
  5.8 1.6 %collective-permute-start.1 = (bf16[2,64,512]{2,1,0:T(8,128)(2,1)S(1)}, bf16[2,64,512]{2,1,0:T(8,128)(2,1)S(1)}, u32[]{:S(2)}, u32[]{:S(2)}) collective-permute-start(bf16[2,64,512]{2,1,0:T(8,128)(2,1)S(1)} %get-tuple-element.56), channel_id=1, source_target_pairs={{0,4},{8,12},{4,0},{12,8},{1,5},{9,13},{5,1},{13,9},{2,6},{10,14},... | collective-permute-start | bytes 393224 | tf_op jit(solution)/shard_map/ppermute | solution.py:478
  7.4 0.7 %collective-permute-start.2 = (bf16[2,64,512]{2,1,0:T(8,128)(2,1)S(1)}, bf16[2,64,512]{2,1,0:T(8,128)(2,1)S(1)}, u32[]{:S(2)}, u32[]{:S(2)}) collective-permute-start(bf16[2,64,512]{2,1,0:T(8,128)(2,1)S(1)} %get-tuple-element.57), channel_id=1, source_target_pairs={{4,8},{8,4},{5,9},{9,5},{6,10},{10,6},{7,11},{11,7},{20,24},{24,20... | collective-permute-start | bytes 393224 | tf_op jit(solution)/shard_map/ppermute | solution.py:478
  8.0 0.0 copy-done
  8.1 0.0 copy-done.2
  8.1 0.0 copy-done.6
  8.1 0.0 copy-done.7
  8.1 0.0 copy-start.1
  8.1 1.6 %own.1 = (bf16[4,64,512]{2,1,0:T(8,128)(2,1)S(1)}, bf16[4,64,1024]{2,1,0:T(8,128)(2,1)S(1)}, bf16[256,512]{1,0:T(8,128)(2,1)S(1)}, bf16[4,64,512]{2,1,0:T(8,128)...) custom-call(bf16[4,64,512]{2,1,0:T(8,128)(2,1)S(1)} %get-tuple-element.47.tok_ref.refs_4_, ...), custom_call_target="tpu_custom_call" | custom-call | flops 402653184 | bytes 3419168 | tf_op jit(solution)/shard_map/own/pallas_call | solution.py:435
  9.7 4.4 %collective-permute-start.4 = (bf16[2,64,512]{2,1,0:T(8,128)(2,1)S(1)}, bf16[2,64,512]{2,1,0:T(8,128)(2,1)S(1)}, u32[]{:S(2)}, u32[]{:S(2)}) collective-permute-start(bf16[2,64,512]{2,1,0:T(8,128)(2,1)S(1)} %get-tuple-element.56), channel_id=1, source_target_pairs={{0,20},{16,4},{8,28},{24,12},{20,0},{4,16},{28,8},{12,24},{1,21},{... | collective-permute-start | bytes 393224 | tf_op jit(solution)/shard_map/ppermute | solution.py:489
  14.1 0.7 %collective-permute-start.5 = (bf16[2,64,512]{2,1,0:T(8,128)(2,1)S(1)}, bf16[2,64,512]{2,1,0:T(8,128)(2,1)S(1)}, u32[]{:S(2)}, u32[]{:S(2)}) collective-permute-start(bf16[2,64,512]{2,1,0:T(8,128)(2,1)S(1)} %get-tuple-element.57), channel_id=1, source_target_pairs={{4,24},{20,8},{24,4},{8,20},{5,25},{21,9},{25,5},{9,21},{6,26},{22... | collective-permute-start | bytes 393224 | tf_op jit(solution)/shard_map/ppermute | solution.py:489
  14.8 0.0 collective-permute-done.1.first_ref
  14.8 1.6 %collective-permute-start.3 = (bf16[4,64,512]{2,1,0:T(8,128)(2,1)S(1)}, bf16[4,64,512]{2,1,0:T(8,128)(2,1)S(1)}, u32[]{:S(2)}, u32[]{:S(2)}) collective-permute-start(bf16[4,64,512]{2,1,0:T(8,128)(2,1)S(1)} %get-tuple-element.54.refs_6_.refs_4_), channel_id=1, source_target_pairs={{0,16},{16,0},{1,17},{17,1},{2,18},{18,2},{3,19},{19,3},{4,20},{20... | collective-permute-start | bytes 786440 | tf_op jit(solution)/shard_map/ppermute | solution.py:461
  16.3 0.0 collective-permute-done.2.second_ref
  16.3 0.0 collective-permute-done.lon_ref
  16.3 1.6 %near.1 = (bf16[4,64,512]{2,1,0:T(8,128)(2,1)S(1)}, bf16[8,64,1024]{2,1,0:T(8,128)(2,1)S(1)}, bf16[512,512]{1,0:T(8,128)(2,1)S(1)}, f32[8,8,64]{2,1,0:T(8,128)S(1)}, s32[8]{0:T(128)S(1)}) custom-call(bf16[4,64,512]{2,1,0:T(8,128)(2,1)S(1)} %collective-permute-done.lon_ref, bf16[2,64,512]{2,1,0:T(8,128)(2,1)S(1)} %collective-permute-done.1.first_ref, ...), custom_call_target="tpu_custom_call" | custom-call | flops 671088640 | bytes 3950624 | tf_op jit(solution)/shard_map/near/pallas_call | solution.py:435
  18.0 0.0 collective-permute-done.4.refs_7_
  18.0 0.0 collective-permute-done.5.refs_8_
  18.0 0.0 copy-done.1
  18.0 6.4 %main.1 = (f32[16,64,1024]{2,1,0:T(8,128)S(1)}, bf16[4,64,512]{2,1,0:T(8,128)(2,1)S(1)}, bf16[4,64,512]{2,1,0:T(8,128)(2,1)S(1)}, bf16[1024,512]{1,0:T(8,128)(2,...) custom-call(s32[8]{0:T(128)S(1)} %get-tuple-element.48.refs_0_, s32[8]{0:T(128)S(1)} %get-tuple-element.51.refs_1_, ...), custom_call_target="tpu_custom_call" | custom-call | flops 2415919104 | bytes 13166592 | tf_op jit(solution)/shard_map/main/pallas_call | solution.py:435
  24.4 0.0 collective-permute-done.3.refs_6_.refs_7_
  24.4 4.0 %other.1 = (f32[16,64,1024]{2,1,0:T(8,128)S(1)}, bf16[4,64,512]{2,1,0:T(8,128)(2,1)S(1)}, bf16[4,64,512]{2,1,0:T(8,128)(2,1)S(1)}, bf16[16,64,1024]{2,1,0:T(8,12...) custom-call(s32[8]{0:T(128)S(1)} %get-tuple-element.48.refs_0_, ...), custom_call_target="tpu_custom_call", output_to_operand_aliasing={{0}: (9, {})} | custom-call | flops 2415919104 | bytes 16025600 | tf_op jit(solution)/shard_map/other/pallas_call | solution.py:435
  28.5 0.6 %sent.1 = bf16[2,2,64,1024]{3,2,1,0:T(8,128)(2,1)S(1)} custom-call(bf16[1024,512]{1,0:T(8,128)(2,1)S(1)} %get-tuple-element.68.refs_0_, bf16[16,64,1024]{2,1,0:T(8,128)(2,1)S(1)} %get-tuple-element.67.refs_1_.refs_0_, bf16[4,64,512]{2,1,0:T(8,128)(2,1)S(1)} %get-tuple-element.69.refs_2_.refs_3_, bf16[4,64,512]{2,1,0:T(8,128)(2,1)S(1)} %get-tuple-element.70.refs_3_.refs_5_, ...), custom_call_target="tpu_custom_call" | custom-call | flops 536870912 | bytes 5242880 | tf_op jit(solution)/shard_map/sent/pallas_call | solution.py:435
  29.1 0.1 collective-permute-start.6
  29.2 0.8 %kept.1.keep_ref = bf16[2,2,64,1024]{3,2,1,0:T(8,128)(2,1)S(1)} custom-call(bf16[1024,512]{1,0:T(8,128)(2,1)S(1)} %get-tuple-element.68.refs_0_, bf16[16,64,1024]{2,1,0:T(8,128)(2,1)S(1)} %get-tuple-element.67.refs_1_.refs_0_, bf16[4,64,512]{2,1,0:T(8,128)(2,1)S(1)} %get-tuple-element.69.refs_2_.refs_3_, ...), custom_call_target="tpu_custom_call" | custom-call | flops 536870912 | bytes 5242880 | tf_op jit(solution)/shard_map/kept/pallas_call | solution.py:435
  30.0 0.0 copy-start.4
  30.0 1.1 %collective-permute-done.6.come_ref = bf16[2,2,64,1024]{3,2,1,0:T(8,128)(2,1)S(1)} collective-permute-done((bf16[2,2,64,1024]{3,2,1,0:T(8,128)(2,1)S(1)}, bf16[2,2,64,1024]{3,2,1,0:T(8,128)(2,1)S(1)}, u32[]{:S(2)}, u32[]{:S(2)}) %collective-permute-start.6) | collective-permute-done | bytes 524320 | tf_op jit(solution)/shard_map/ppermute | solution.py:493
  31.1 0.1 split.1
  31.2 1.0 %collective-permute-start.7 = (bf16[64,1024]{1,0:T(8,128)(2,1)S(1)}, bf16[64,1024]{1,0:T(8,128)(2,1)S(1)}, u32[]{:S(2)}, u32[]{:S(2)}) collective-permute-start(bf16[64,1024]{1,0:T(8,128)(2,1)S(1)} %get-tuple-element.74), channel_id=1, source_target_pairs={{0,2},{1,3},{2,0},{3,1},{4,6},{5,7},{6,4},{7,5},{8,10},{9,11},{10,... | collective-permute-start | bytes 393224 | tf_op jit(solution)/shard_map/ppermute | solution.py:493
  32.3 4.6 %collective-permute-start.8 = (bf16[64,1024]{1,0:T(8,128)(2,1)S(1)}, bf16[64,1024]{1,0:T(8,128)(2,1)S(1)}, u32[]{:S(2)}, u32[]{:S(2)}) collective-permute-start(bf16[64,1024]{1,0:T(8,128)(2,1)S(1)} %get-tuple-element.75), channel_id=1, source_target_pairs={{0,4},{4,0},{8,12},{12,8},{1,5},{5,1},{9,13},{13,9},{2,6},{6,2},{1... | collective-permute-start | bytes 393224 | tf_op jit(solution)/shard_map/ppermute | solution.py:493
  36.8 0.7 %collective-permute-start.9 = (bf16[64,1024]{1,0:T(8,128)(2,1)S(1)}, bf16[64,1024]{1,0:T(8,128)(2,1)S(1)}, u32[]{:S(2)}, u32[]{:S(2)}) collective-permute-start(bf16[64,1024]{1,0:T(8,128)(2,1)S(1)} %get-tuple-element.76), channel_id=1, source_target_pairs={{0,6},{1,7},{2,4},{3,5},{4,2},{5,3},{6,0},{7,1},{8,14},{9,15},{10,... | collective-permute-start | bytes 393224 | tf_op jit(solution)/shard_map/ppermute | solution.py:546
  37.6 0.7 %collective-permute-start.10 = (bf16[2,64,512]{2,1,0:T(8,128)(2,1)S(1)}, bf16[2,64,512]{2,1,0:T(8,128)(2,1)S(1)}, u32[]{:S(2)}, u32[]{:S(2)}) collective-permute-start(bf16[2,64,512]{2,1,0:T(8,128)(2,1)S(1)} %get-tuple-element.78), channel_id=1, source_target_pairs={{4,8},{8,4},{5,9},{9,5},{6,10},{10,6},{7,11},{11,7},{20,24},{24,20... | collective-permute-start | bytes 393224 | tf_op jit(solution)/shard_map/ppermute | solution.py:478
  38.2 0.0 collective-permute-done.7
  38.3 2.9 %collective-permute-done.8 = bf16[64,1024]{1,0:T(8,128)(2,1)S(1)} collective-permute-done((bf16[64,1024]{1,0:T(8,128)(2,1)S(1)}, bf16[64,1024]{1,0:T(8,128)(2,1)S(1)}, u32[]{:S(2)}, u32[]{:S(2)}) %collective-permute-start.8) | collective-permute-done | bytes 131104 | tf_op jit(solution)/shard_map/ppermute | solution.py:493
  41.1 2.8 %collective-permute-done.9 = bf16[64,1024]{1,0:T(8,128)(2,1)S(1)} collective-permute-done((bf16[64,1024]{1,0:T(8,128)(2,1)S(1)}, bf16[64,1024]{1,0:T(8,128)(2,1)S(1)}, u32[]{:S(2)}, u32[]{:S(2)}) %collective-permute-start.9) | collective-permute-done | bytes 131104 | tf_op jit(solution)/shard_map/ppermute | solution.py:546
  43.9 0.1 add_convert_fusion.1
  44.0 0.0 collective-permute-done.10.refs_2_
  44.0 2.3 %collective-permute-start.11 = (bf16[64,1024]{1,0:T(8,128)(2,1)S(1)}, bf16[64,1024]{1,0:T(8,128)(2,1)S(1)}, u32[]{:S(2)}, u32[]{:S(2)}) collective-permute-start(bf16[64,1024]{1,0:T(8,128)(2,1)S(1)} %add_convert_fusion.1), channel_id=1, source_target_pairs={{0,8},{4,12},{8,0},{12,4},{1,9},{5,13},{9,1},{13,5},{2,10},{6,14},... | collective-permute-start | bytes 393224 | tf_op jit(solution)/shard_map/ppermute | solution.py:493
  46.3 0.2 collective-permute-start.12
  46.5 6.0 %collective-permute-done.11 = bf16[64,1024]{1,0:T(8,128)(2,1)S(1)} collective-permute-done((bf16[64,1024]{1,0:T(8,128)(2,1)S(1)}, bf16[64,1024]{1,0:T(8,128)(2,1)S(1)}, u32[]{:S(2)}, u32[]{:S(2)}) %collective-permute-start.11) | collective-permute-done | bytes 131104 | tf_op jit(solution)/shard_map/ppermute | solution.py:493
  52.5 0.0 collective-permute-done.12.refs_1_
  52.5 0.5 collective-permute-start.15
  53.0 1.5 %collective-permute-start.14 = (bf16[64,1024]{1,0:T(8,128)(2,1)S(1)}, bf16[64,1024]{1,0:T(8,128)(2,1)S(1)}, u32[]{:S(2)}, u32[]{:S(2)}) collective-permute-start(bf16[64,1024]{1,0:T(8,128)(2,1)S(1)} %add_convert_fusion.own_ref), channel_id=1, source_target_pairs={{0,16},{16,0},{1,17},{17,1},{2,18},{18,2},{3,19},{19,3},{4,20},{20... | collective-permute-start | bytes 393224 | tf_op jit(solution)/shard_map/ppermute | solution.py:493
  54.5 1.6 %collective-permute-start.13 = (bf16[64,1024]{1,0:T(8,128)(2,1)S(1)}, bf16[64,1024]{1,0:T(8,128)(2,1)S(1)}, u32[]{:S(2)}, u32[]{:S(2)}) collective-permute-start(bf16[64,1024]{1,0:T(8,128)(2,1)S(1)} %add_convert_fusion.own_ref), channel_id=1, source_target_pairs={{0,4},{4,0},{8,12},{12,8},{1,5},{5,1},{9,13},{13,9},{2,6},{6,2},{1... | collective-permute-start | bytes 393224 | tf_op jit(solution)/shard_map/ppermute | solution.py:493
  56.1 0.0 copy-done.4
  56.1 1.9 %input.1 = (bf16[1,16,16,512]{3,2,1,0:T(8,128)(2,1)}, bf16[1,16,16,512]{3,2,1,0:T(8,128)(2,1)}) custom-call(bf16[16,64,1024]{2,1,0:T(8,128)(2,1)S(1)} %get-tuple-element.67.refs_1_.refs_0_, bf16[2,64,512]{2,1,0:T(8,128)(2,1)S(1)} %collective-permute-done.12.refs_1_, bf16[2,64,512]{2,1,0:T(8,128)(2,1)S(1)} %collective-permute-done.10.refs_2_, ...), custom_call_target="tpu_custom_call" | custom-call | flops 402653184 | bytes 6294528 | tf_op jit(solution)/shard_map/input/pallas_call | solution.py:435
  58.0 0.6 collective-permute-done.15.far_ref
  58.6 0.8 %collective-permute-done.14.lon_ref = bf16[64,1024]{1,0:T(8,128)(2,1)S(1)} collective-permute-done((bf16[64,1024]{1,0:T(8,128)(2,1)S(1)}, bf16[64,1024]{1,0:T(8,128)(2,1)S(1)}, u32[]{:S(2)}, u32[]{:S(2)}) %collective-permute-start.14) | collective-permute-done | bytes 131104 | tf_op jit(solution)/shard_map/ppermute | solution.py:493
  59.4 0.1 collective-permute-done.13.lat_ref
  59.5 1.4 %finish.1 = (f32[128,1536]{1,0:T(8,128)}, f32[128,512]{1,0:T(8,128)}, f32[1,128]{1,0:T(1,128)}) custom-call(bf16[64,1024]{1,0:T(8,128)(2,1)S(1)} %add_convert_fusion.own_ref, bf16[64,1024]{1,0:T(8,128)(2,1)S(1)} %collective-permute-done.13.lat_ref, bf16[64,1024]{1,0:T(8,128)(2,1)S(1)} %collective-permute-done.14.lon_ref, ...), custom_call_target="tpu_custom_call" | custom-call | bytes 3148288 | tf_op jit(solution)/shard_map/finish/pallas_call | solution.py:435
  (1 shorter events, 0.0 us)
Async XLA Ops:
  0.6 7.4 %copy-start = (bf16[512,1536]{1,0:T(8,128)(2,1)S(1)}, bf16[512,1536]{1,0:T(8,128)(2,1)}, u32[]{:S(2)}) copy-start(bf16[512,1536]{1,0:T(8,128)(2,1)} %wqkv_ref.5) | copy-start | bytes 4718596
  0.6 7.4 %copy-start.2 = (bf16[1,16,16,512]{3,2,1,0:T(8,128)(2,1)S(1)}, bf16[1,16,16,512]{3,2,1,0:T(8,128)(2,1)}, u32[]{:S(2)}) copy-start(bf16[1,16,16,512]{3,2,1,0:T(8,128)(2,1)} %refs_9_.1) | copy-start | bytes 786436
  0.7 1.1 %copy-start.3 = (bf16[1,16,16,512]{3,2,1,0:T(8,128)(2,1)S(1)}, bf16[1,16,16,512]{3,2,1,0:T(8,128)(2,1)}, u32[]{:S(2)}) copy-start(bf16[1,16,16,512]{3,2,1,0:T(8,128)(2,1)} %refs_10_.1) | copy-start | bytes 786436
  1.7 0.7 %copy-start.5 = (s32[1,16,16]{2,1,0:T(8,128)S(1)}, s32[1,16,16]{2,1,0:T(8,128)}, u32[]{:S(2)}) copy-start(s32[1,16,16]{2,1,0:T(8,128)} %refs_11_.1) | copy-start | bytes 3076
  2.4 5.6 %copy-start.6 = (s32[1,16,16]{2,1,0:T(8,128)S(1)}, s32[1,16,16]{2,1,0:T(8,128)}, u32[]{:S(2)}) copy-start(s32[1,16,16]{2,1,0:T(8,128)} %refs_11_.1) | copy-start | bytes 3076
  2.4 5.6 %copy-start.7 = (f32[512]{0:T(512)S(1)}, f32[512]{0:T(512)}, u32[]{:S(2)}) copy-start(f32[512]{0:T(512)} %param.10) | copy-start | bytes 6148
  2.8 13.5 %collective-permute-start = (bf16[4,64,512]{2,1,0:T(8,128)(2,1)S(1)}, bf16[4,64,512]{2,1,0:T(8,128)(2,1)S(1)}, u32[]{:S(2)}, u32[]{:S(2)}) collective-permute-start(bf16[4,64,512]{2,1,0:T(8,128)(2,1)S(1)} %get-tuple-element.47.tok_ref.refs_4_), channel_id=1, source_target_pairs={{0,16},{16,0},{1,17},{17,1},{2,18},{18,2},{3,19},{19,3},{4,20},{20... | collective-permute-start | bytes 786440 | tf_op jit(solution)/shard_map/ppermute | solution.py:461
  5.8 9.0 %collective-permute-start.1 = (bf16[2,64,512]{2,1,0:T(8,128)(2,1)S(1)}, bf16[2,64,512]{2,1,0:T(8,128)(2,1)S(1)}, u32[]{:S(2)}, u32[]{:S(2)}) collective-permute-start(bf16[2,64,512]{2,1,0:T(8,128)(2,1)S(1)} %get-tuple-element.56), channel_id=1, source_target_pairs={{0,4},{8,12},{4,0},{12,8},{1,5},{9,13},{5,1},{13,9},{2,6},{10,14},... | collective-permute-start | bytes 393224 | tf_op jit(solution)/shard_map/ppermute | solution.py:478
  7.4 8.9 %collective-permute-start.2 = (bf16[2,64,512]{2,1,0:T(8,128)(2,1)S(1)}, bf16[2,64,512]{2,1,0:T(8,128)(2,1)S(1)}, u32[]{:S(2)}, u32[]{:S(2)}) collective-permute-start(bf16[2,64,512]{2,1,0:T(8,128)(2,1)S(1)} %get-tuple-element.57), channel_id=1, source_target_pairs={{4,8},{8,4},{5,9},{9,5},{6,10},{10,6},{7,11},{11,7},{20,24},{24,20... | collective-permute-start | bytes 393224 | tf_op jit(solution)/shard_map/ppermute | solution.py:478
  8.1 9.9 %copy-start.1 = (bf16[512,512]{1,0:T(8,128)(2,1)S(1)}, bf16[512,512]{1,0:T(8,128)(2,1)}, u32[]{:S(2)}) copy-start(bf16[512,512]{1,0:T(8,128)(2,1)} %refs_7_.1) | copy-start | bytes 1572868
  9.7 8.3 %collective-permute-start.4 = (bf16[2,64,512]{2,1,0:T(8,128)(2,1)S(1)}, bf16[2,64,512]{2,1,0:T(8,128)(2,1)S(1)}, u32[]{:S(2)}, u32[]{:S(2)}) collective-permute-start(bf16[2,64,512]{2,1,0:T(8,128)(2,1)S(1)} %get-tuple-element.56), channel_id=1, source_target_pairs={{0,20},{16,4},{8,28},{24,12},{20,0},{4,16},{28,8},{12,24},{1,21},{... | collective-permute-start | bytes 393224 | tf_op jit(solution)/shard_map/ppermute | solution.py:489
  14.1 3.9 %collective-permute-start.5 = (bf16[2,64,512]{2,1,0:T(8,128)(2,1)S(1)}, bf16[2,64,512]{2,1,0:T(8,128)(2,1)S(1)}, u32[]{:S(2)}, u32[]{:S(2)}) collective-permute-start(bf16[2,64,512]{2,1,0:T(8,128)(2,1)S(1)} %get-tuple-element.57), channel_id=1, source_target_pairs={{4,24},{20,8},{24,4},{8,20},{5,25},{21,9},{25,5},{9,21},{6,26},{22... | collective-permute-start | bytes 393224 | tf_op jit(solution)/shard_map/ppermute | solution.py:489
  14.8 9.6 %collective-permute-start.3 = (bf16[4,64,512]{2,1,0:T(8,128)(2,1)S(1)}, bf16[4,64,512]{2,1,0:T(8,128)(2,1)S(1)}, u32[]{:S(2)}, u32[]{:S(2)}) collective-permute-start(bf16[4,64,512]{2,1,0:T(8,128)(2,1)S(1)} %get-tuple-element.54.refs_6_.refs_4_), channel_id=1, source_target_pairs={{0,16},{16,0},{1,17},{17,1},{2,18},{18,2},{3,19},{19,3},{4,20},{20... | collective-permute-start | bytes 786440 | tf_op jit(solution)/shard_map/ppermute | solution.py:461
  29.1 2.0 %collective-permute-start.6 = (bf16[2,2,64,1024]{3,2,1,0:T(8,128)(2,1)S(1)}, bf16[2,2,64,1024]{3,2,1,0:T(8,128)(2,1)S(1)}, u32[]{:S(2)}, u32[]{:S(2)}) collective-permute-start(bf16[2,2,64,1024]{3,2,1,0:T(8,128)(2,1)S(1)} %sent.1), channel_id=1, source_target_pairs={{0,1},{1,0},{2,3},{3,2},{4,5},{5,4},{6,7},{7,6},{8,9},{9,8},{10,11... | collective-permute-start | bytes 1572872 | tf_op jit(solution)/shard_map/ppermute | solution.py:493
  30.0 26.0 %copy-start.4 = (bf16[1,16,16,512]{3,2,1,0:T(8,128)(2,1)S(1)}, bf16[1,16,16,512]{3,2,1,0:T(8,128)(2,1)}, u32[]{:S(2)}) copy-start(bf16[1,16,16,512]{3,2,1,0:T(8,128)(2,1)} %refs_10_.1) | copy-start | bytes 786436
  31.2 7.0 %collective-permute-start.7 = (bf16[64,1024]{1,0:T(8,128)(2,1)S(1)}, bf16[64,1024]{1,0:T(8,128)(2,1)S(1)}, u32[]{:S(2)}, u32[]{:S(2)}) collective-permute-start(bf16[64,1024]{1,0:T(8,128)(2,1)S(1)} %get-tuple-element.74), channel_id=1, source_target_pairs={{0,2},{1,3},{2,0},{3,1},{4,6},{5,7},{6,4},{7,5},{8,10},{9,11},{10,... | collective-permute-start | bytes 393224 | tf_op jit(solution)/shard_map/ppermute | solution.py:493
  32.3 8.9 %collective-permute-start.8 = (bf16[64,1024]{1,0:T(8,128)(2,1)S(1)}, bf16[64,1024]{1,0:T(8,128)(2,1)S(1)}, u32[]{:S(2)}, u32[]{:S(2)}) collective-permute-start(bf16[64,1024]{1,0:T(8,128)(2,1)S(1)} %get-tuple-element.75), channel_id=1, source_target_pairs={{0,4},{4,0},{8,12},{12,8},{1,5},{5,1},{9,13},{13,9},{2,6},{6,2},{1... | collective-permute-start | bytes 393224 | tf_op jit(solution)/shard_map/ppermute | solution.py:493
  36.8 7.1 %collective-permute-start.9 = (bf16[64,1024]{1,0:T(8,128)(2,1)S(1)}, bf16[64,1024]{1,0:T(8,128)(2,1)S(1)}, u32[]{:S(2)}, u32[]{:S(2)}) collective-permute-start(bf16[64,1024]{1,0:T(8,128)(2,1)S(1)} %get-tuple-element.76), channel_id=1, source_target_pairs={{0,6},{1,7},{2,4},{3,5},{4,2},{5,3},{6,0},{7,1},{8,14},{9,15},{10,... | collective-permute-start | bytes 393224 | tf_op jit(solution)/shard_map/ppermute | solution.py:546
  37.6 6.4 %collective-permute-start.10 = (bf16[2,64,512]{2,1,0:T(8,128)(2,1)S(1)}, bf16[2,64,512]{2,1,0:T(8,128)(2,1)S(1)}, u32[]{:S(2)}, u32[]{:S(2)}) collective-permute-start(bf16[2,64,512]{2,1,0:T(8,128)(2,1)S(1)} %get-tuple-element.78), channel_id=1, source_target_pairs={{4,8},{8,4},{5,9},{9,5},{6,10},{10,6},{7,11},{11,7},{20,24},{24,20... | collective-permute-start | bytes 393224 | tf_op jit(solution)/shard_map/ppermute | solution.py:478
  44.0 8.5 %collective-permute-start.11 = (bf16[64,1024]{1,0:T(8,128)(2,1)S(1)}, bf16[64,1024]{1,0:T(8,128)(2,1)S(1)}, u32[]{:S(2)}, u32[]{:S(2)}) collective-permute-start(bf16[64,1024]{1,0:T(8,128)(2,1)S(1)} %add_convert_fusion.1), channel_id=1, source_target_pairs={{0,8},{4,12},{8,0},{12,4},{1,9},{5,13},{9,1},{13,5},{2,10},{6,14},... | collective-permute-start | bytes 393224 | tf_op jit(solution)/shard_map/ppermute | solution.py:493
  46.3 6.2 %collective-permute-start.12 = (bf16[2,64,512]{2,1,0:T(8,128)(2,1)S(1)}, bf16[2,64,512]{2,1,0:T(8,128)(2,1)S(1)}, u32[]{:S(2)}, u32[]{:S(2)}) collective-permute-start(bf16[2,64,512]{2,1,0:T(8,128)(2,1)S(1)} %get-tuple-element.80), channel_id=1, source_target_pairs={{0,4},{8,12},{4,0},{12,8},{1,5},{9,13},{5,1},{13,9},{2,6},{10,14},... | collective-permute-start | bytes 393224 | tf_op jit(solution)/shard_map/ppermute | solution.py:478
  52.5 6.0 %collective-permute-start.15 = (bf16[64,1024]{1,0:T(8,128)(2,1)S(1)}, bf16[64,1024]{1,0:T(8,128)(2,1)S(1)}, u32[]{:S(2)}, u32[]{:S(2)}) collective-permute-start(bf16[64,1024]{1,0:T(8,128)(2,1)S(1)} %add_convert_fusion.own_ref), channel_id=1, source_target_pairs={{0,20},{4,16},{8,28},{12,24},{16,4},{20,0},{24,12},{28,8},{1,21},{... | collective-permute-start | bytes 393224 | tf_op jit(solution)/shard_map/ppermute | solution.py:561
  53.0 6.4 %collective-permute-start.14 = (bf16[64,1024]{1,0:T(8,128)(2,1)S(1)}, bf16[64,1024]{1,0:T(8,128)(2,1)S(1)}, u32[]{:S(2)}, u32[]{:S(2)}) collective-permute-start(bf16[64,1024]{1,0:T(8,128)(2,1)S(1)} %add_convert_fusion.own_ref), channel_id=1, source_target_pairs={{0,16},{16,0},{1,17},{17,1},{2,18},{18,2},{3,19},{19,3},{4,20},{20... | collective-permute-start | bytes 393224 | tf_op jit(solution)/shard_map/ppermute | solution.py:493
  54.5 5.0 %collective-permute-start.13 = (bf16[64,1024]{1,0:T(8,128)(2,1)S(1)}, bf16[64,1024]{1,0:T(8,128)(2,1)S(1)}, u32[]{:S(2)}, u32[]{:S(2)}) collective-permute-start(bf16[64,1024]{1,0:T(8,128)(2,1)S(1)} %add_convert_fusion.own_ref), channel_id=1, source_target_pairs={{0,4},{4,0},{8,12},{12,8},{1,5},{5,1},{9,13},{13,9},{2,6},{6,2},{1... | collective-permute-start | bytes 393224 | tf_op jit(solution)/shard_map/ppermute | solution.py:493

commit v9 on v8

--- a/solution.py
+++ b/solution.py
@@ -385,7 +385,8 @@
 def gain_row(wqkv_ref, gain_ref, qkv_ref):
     at = pl.ds(pl.multiple_of(lax.axis_index("lev") * 128, 128), 128)
     product = wqkv_ref[at, :].astype(F32) * qkv_ref[...]
-    return dot(jnp.ones((8, 3 * D), F32), product, 1, 1, EXACT)[:1] / gain_ref[:, at]
+    product = sum(product[:, k : k + 128] for k in range(0, 3 * D, 128))
+    return dot(jnp.ones((8, 128), F32), product, 1, 1, EXACT)[:1] / gain_ref[:, at]
 
 
 def finish_rows_kernel(

time: 61.6 us -> 61.3 us (level)
  Pallas kernels: 18.9 us -> 16.9 us
  waiting for transfers between devices: 14.2 us -> 15.4 us
    pallas_call x10, Pallas kernels: 18.9 us -> 16.9 us  [call(): pl.pallas_call(kernel, out_shape=outs, in_specs=specs, out_specs=out_spec...]
    ppermute x2, waiting for transfers between devices: 0.01 us -> 1.04 us  [lon_halo(): return lax.ppermute(own, 'lon', [(0, 1), (1, 0)])]
    ppermute x1, waiting for transfers between devices: 2.77 us -> 3.43 us  [pair_sum(): lax.ppermute(to_far, ('lat', 'lev'), [(i, i ^ 6) for i in range(4 * count)])]
  transfers between devices with their start and end apart: 16 -> 16, of which waited for: 7 -> 7; matrix products, arithmetic and copies ran while one was open for 0% -> 0% of each run, Pallas kernels for 20% -> 15%
where the time goes in v9:
time: 61.3 us; the launch traced here: 60.4 us
  starting transfers between devices  25.4 us (41%)
  Pallas kernels  16.9 us (28%)
  waiting for transfers between devices  15.4 us (25%)
  local copies, waits for them, and re-layouts  1.8 us (3%)
  between operations  0.88 us (1%)
    pallas_call x10, Pallas kernels, call(): pl.pallas_call(kernel, out_shape=outs, in_specs=specs, out_specs=out_spec...  16.9 us
    ppermute x6, starting transfers between devices, swap(): lax.ppermute(value, axis, [(i, i ^ bit) for i in range(lax.axis_size(axis...  11 us
    ppermute x6, waiting for transfers between devices, swap(): lax.ppermute(value, axis, [(i, i ^ bit) for i in range(lax.axis_size(axis...  10.4 us
    ppermute x2, starting transfers between devices, corner_swap(): lax.ppermute(value, ('lon', 'lat'), pairs + [(b, a) for a, b in pairs])  5.09 us
    ppermute x2, starting transfers between devices, lon_halo(): return lax.ppermute(own, 'lon', [(0, 1), (1, 0)])  4.56 us
    ppermute x1, waiting for transfers between devices, pair_sum(): lax.ppermute(to_far, ('lat', 'lev'), [(i, i ^ 6) for i in range(4 * count)])  3.43 us
    ppermute x4, starting transfers between devices, lat_swap(): return lax.ppermute(value, 'lat', pairs + [(b, a) for a, b in pairs])  3.19 us
    unnamed x16, local copies, waits for them, and re-layouts  1.8 us
  transfers between devices with their start and end apart: 16, of which 7 were waited for; matrix products, arithmetic and copies ran while one was open for 0% of the time, Pallas kernels for 15%

profile of v9, /device:TPU:0, one launch (start us, length us, event | category | flops | bytes accessed | tf_op | source)
XLA Modules:
  0.0 60.4 jit_solution(12331053280686413956)
XLA Ops:
  0.6 0.0 copy-start
  0.6 0.0 copy-start.2
  0.7 0.0 copy-start.3
  0.7 1.1 %copy-done.3 = bf16[1,16,16,512]{3,2,1,0:T(8,128)(2,1)S(1)} copy-done((bf16[1,16,16,512]{3,2,1,0:T(8,128)(2,1)S(1)}, bf16[1,16,16,512]{3,2,1,0:T(8,128)(2,1)}, u32[]{:S(2)}) %copy-start.3) | copy-done | bytes 262168
  1.7 0.0 copy-start.5
  1.7 0.7 %copy-done.5 = s32[1,16,16]{2,1,0:T(8,128)S(1)} copy-done((s32[1,16,16]{2,1,0:T(8,128)S(1)}, s32[1,16,16]{2,1,0:T(8,128)}, u32[]{:S(2)}) %copy-start.5) | copy-done | bytes 1048
  2.4 0.0 copy-start.6
  2.4 0.0 copy-start.7
  2.4 0.4 prep.1
  2.8 3.0 %collective-permute-start = (bf16[4,64,512]{2,1,0:T(8,128)(2,1)S(1)}, bf16[4,64,512]{2,1,0:T(8,128)(2,1)S(1)}, u32[]{:S(2)}, u32[]{:S(2)}) collective-permute-start(bf16[4,64,512]{2,1,0:T(8,128)(2,1)S(1)} %get-tuple-element.47.tok_ref.refs_4_), channel_id=1, source_target_pairs={{0,16},{16,0},{1,17},{17,1},{2,18},{18,2},{3,19},{19,3},{4,20},{20... | collective-permute-start | bytes 786440 | tf_op jit(solution)/shard_map/ppermute | solution.py:462
  5.8 1.6 %collective-permute-start.1 = (bf16[2,64,512]{2,1,0:T(8,128)(2,1)S(1)}, bf16[2,64,512]{2,1,0:T(8,128)(2,1)S(1)}, u32[]{:S(2)}, u32[]{:S(2)}) collective-permute-start(bf16[2,64,512]{2,1,0:T(8,128)(2,1)S(1)} %get-tuple-element.56), channel_id=1, source_target_pairs={{0,4},{8,12},{4,0},{12,8},{1,5},{9,13},{5,1},{13,9},{2,6},{10,14},... | collective-permute-start | bytes 393224 | tf_op jit(solution)/shard_map/ppermute | solution.py:479
  7.4 0.7 %collective-permute-start.2 = (bf16[2,64,512]{2,1,0:T(8,128)(2,1)S(1)}, bf16[2,64,512]{2,1,0:T(8,128)(2,1)S(1)}, u32[]{:S(2)}, u32[]{:S(2)}) collective-permute-start(bf16[2,64,512]{2,1,0:T(8,128)(2,1)S(1)} %get-tuple-element.57), channel_id=1, source_target_pairs={{4,8},{8,4},{5,9},{9,5},{6,10},{10,6},{7,11},{11,7},{20,24},{24,20... | collective-permute-start | bytes 393224 | tf_op jit(solution)/shard_map/ppermute | solution.py:479
  8.0 0.0 copy-done
  8.1 0.0 copy-done.2
  8.1 0.0 copy-done.6
  8.1 0.0 copy-done.7
  8.1 0.0 copy-start.1
  8.1 1.6 %own.1 = (bf16[4,64,512]{2,1,0:T(8,128)(2,1)S(1)}, bf16[4,64,1024]{2,1,0:T(8,128)(2,1)S(1)}, bf16[256,512]{1,0:T(8,128)(2,1)S(1)}, bf16[4,64,512]{2,1,0:T(8,128)...) custom-call(bf16[4,64,512]{2,1,0:T(8,128)(2,1)S(1)} %get-tuple-element.47.tok_ref.refs_4_, ...), custom_call_target="tpu_custom_call" | custom-call | flops 402653184 | bytes 3419168 | tf_op jit(solution)/shard_map/own/pallas_call | solution.py:436
  9.7 4.4 %collective-permute-start.4 = (bf16[2,64,512]{2,1,0:T(8,128)(2,1)S(1)}, bf16[2,64,512]{2,1,0:T(8,128)(2,1)S(1)}, u32[]{:S(2)}, u32[]{:S(2)}) collective-permute-start(bf16[2,64,512]{2,1,0:T(8,128)(2,1)S(1)} %get-tuple-element.56), channel_id=1, source_target_pairs={{0,20},{16,4},{8,28},{24,12},{20,0},{4,16},{28,8},{12,24},{1,21},{... | collective-permute-start | bytes 393224 | tf_op jit(solution)/shard_map/ppermute | solution.py:490
  14.1 0.7 %collective-permute-start.5 = (bf16[2,64,512]{2,1,0:T(8,128)(2,1)S(1)}, bf16[2,64,512]{2,1,0:T(8,128)(2,1)S(1)}, u32[]{:S(2)}, u32[]{:S(2)}) collective-permute-start(bf16[2,64,512]{2,1,0:T(8,128)(2,1)S(1)} %get-tuple-element.57), channel_id=1, source_target_pairs={{4,24},{20,8},{24,4},{8,20},{5,25},{21,9},{25,5},{9,21},{6,26},{22... | collective-permute-start | bytes 393224 | tf_op jit(solution)/shard_map/ppermute | solution.py:490
  14.8 0.0 collective-permute-done.1.first_ref
  14.8 1.6 %collective-permute-start.3 = (bf16[4,64,512]{2,1,0:T(8,128)(2,1)S(1)}, bf16[4,64,512]{2,1,0:T(8,128)(2,1)S(1)}, u32[]{:S(2)}, u32[]{:S(2)}) collective-permute-start(bf16[4,64,512]{2,1,0:T(8,128)(2,1)S(1)} %get-tuple-element.54.refs_6_.refs_4_), channel_id=1, source_target_pairs={{0,16},{16,0},{1,17},{17,1},{2,18},{18,2},{3,19},{19,3},{4,20},{20... | collective-permute-start | bytes 786440 | tf_op jit(solution)/shard_map/ppermute | solution.py:462
  16.3 0.0 collective-permute-done.2.second_ref
  16.3 0.0 collective-permute-done.lon_ref
  16.3 1.6 %near.1 = (bf16[4,64,512]{2,1,0:T(8,128)(2,1)S(1)}, bf16[8,64,1024]{2,1,0:T(8,128)(2,1)S(1)}, bf16[512,512]{1,0:T(8,128)(2,1)S(1)}, f32[8,8,64]{2,1,0:T(8,128)S(1)}, s32[8]{0:T(128)S(1)}) custom-call(bf16[4,64,512]{2,1,0:T(8,128)(2,1)S(1)} %collective-permute-done.lon_ref, bf16[2,64,512]{2,1,0:T(8,128)(2,1)S(1)} %collective-permute-done.1.first_ref, ...), custom_call_target="tpu_custom_call" | custom-call | flops 671088640 | bytes 3950624 | tf_op jit(solution)/shard_map/near/pallas_call | solution.py:436
  18.0 0.0 collective-permute-done.4.refs_7_
  18.0 0.0 collective-permute-done.5.refs_8_
  18.0 0.0 copy-done.1
  18.0 3.6 %main.1 = (f32[16,64,1024]{2,1,0:T(8,128)S(1)}, bf16[4,64,512]{2,1,0:T(8,128)(2,1)S(1)}, bf16[4,64,512]{2,1,0:T(8,128)(2,1)S(1)}, bf16[1024,512]{1,0:T(8,128)(2,...) custom-call(s32[8]{0:T(128)S(1)} %get-tuple-element.48.refs_0_, s32[8]{0:T(128)S(1)} %get-tuple-element.51.refs_1_, ...), custom_call_target="tpu_custom_call" | custom-call | flops 2415919104 | bytes 13166592 | tf_op jit(solution)/shard_map/main/pallas_call | solution.py:436
  21.6 1.0 %collective-permute-done.3.refs_6_.refs_7_ = bf16[4,64,512]{2,1,0:T(8,128)(2,1)S(1)} collective-permute-done((bf16[4,64,512]{2,1,0:T(8,128)(2,1)S(1)}, bf16[4,64,512]{2,1,0:T(8,128)(2,1)S(1)}, u32[]{:S(2)}, u32[]{:S(2)}) %collective-permute-start.3) | collective-permute-done | bytes 262176 | tf_op jit(solution)/shard_map/ppermute | solution.py:462
  22.7 5.3 %other.1 = (f32[16,64,1024]{2,1,0:T(8,128)S(1)}, bf16[4,64,512]{2,1,0:T(8,128)(2,1)S(1)}, bf16[4,64,512]{2,1,0:T(8,128)(2,1)S(1)}, bf16[16,64,1024]{2,1,0:T(8,12...) custom-call(s32[8]{0:T(128)S(1)} %get-tuple-element.48.refs_0_, ...), custom_call_target="tpu_custom_call", output_to_operand_aliasing={{0}: (9, {})} | custom-call | flops 2415919104 | bytes 16025600 | tf_op jit(solution)/shard_map/other/pallas_call | solution.py:436
  27.9 0.7 %sent.1 = bf16[2,2,64,1024]{3,2,1,0:T(8,128)(2,1)S(1)} custom-call(bf16[1024,512]{1,0:T(8,128)(2,1)S(1)} %get-tuple-element.68.refs_0_, bf16[16,64,1024]{2,1,0:T(8,128)(2,1)S(1)} %get-tuple-element.67.refs_1_.refs_0_, bf16[4,64,512]{2,1,0:T(8,128)(2,1)S(1)} %get-tuple-element.69.refs_2_.refs_3_, bf16[4,64,512]{2,1,0:T(8,128)(2,1)S(1)} %get-tuple-element.70.refs_3_.refs_5_, ...), custom_call_target="tpu_custom_call" | custom-call | flops 536870912 | bytes 5242880 | tf_op jit(solution)/shard_map/sent/pallas_call | solution.py:436
  28.6 0.1 collective-permute-start.6
  28.7 0.6 %kept.1.keep_ref = bf16[2,2,64,1024]{3,2,1,0:T(8,128)(2,1)S(1)} custom-call(bf16[1024,512]{1,0:T(8,128)(2,1)S(1)} %get-tuple-element.68.refs_0_, bf16[16,64,1024]{2,1,0:T(8,128)(2,1)S(1)} %get-tuple-element.67.refs_1_.refs_0_, bf16[4,64,512]{2,1,0:T(8,128)(2,1)S(1)} %get-tuple-element.69.refs_2_.refs_3_, ...), custom_call_target="tpu_custom_call" | custom-call | flops 536870912 | bytes 5242880 | tf_op jit(solution)/shard_map/kept/pallas_call | solution.py:436
  29.3 0.0 copy-start.4
  29.3 1.2 %collective-permute-done.6.come_ref = bf16[2,2,64,1024]{3,2,1,0:T(8,128)(2,1)S(1)} collective-permute-done((bf16[2,2,64,1024]{3,2,1,0:T(8,128)(2,1)S(1)}, bf16[2,2,64,1024]{3,2,1,0:T(8,128)(2,1)S(1)}, u32[]{:S(2)}, u32[]{:S(2)}) %collective-permute-start.6) | collective-permute-done | bytes 524320 | tf_op jit(solution)/shard_map/ppermute | solution.py:494
  30.6 0.1 split.1
  30.7 1.4 %collective-permute-start.7 = (bf16[64,1024]{1,0:T(8,128)(2,1)S(1)}, bf16[64,1024]{1,0:T(8,128)(2,1)S(1)}, u32[]{:S(2)}, u32[]{:S(2)}) collective-permute-start(bf16[64,1024]{1,0:T(8,128)(2,1)S(1)} %get-tuple-element.74), channel_id=1, source_target_pairs={{0,2},{1,3},{2,0},{3,1},{4,6},{5,7},{6,4},{7,5},{8,10},{9,11},{10,... | collective-permute-start | bytes 393224 | tf_op jit(solution)/shard_map/ppermute | solution.py:494
  32.1 4.3 %collective-permute-start.8 = (bf16[64,1024]{1,0:T(8,128)(2,1)S(1)}, bf16[64,1024]{1,0:T(8,128)(2,1)S(1)}, u32[]{:S(2)}, u32[]{:S(2)}) collective-permute-start(bf16[64,1024]{1,0:T(8,128)(2,1)S(1)} %get-tuple-element.75), channel_id=1, source_target_pairs={{0,4},{4,0},{8,12},{12,8},{1,5},{5,1},{9,13},{13,9},{2,6},{6,2},{1... | collective-permute-start | bytes 393224 | tf_op jit(solution)/shard_map/ppermute | solution.py:494
  36.4 1.0 %collective-permute-start.9 = (bf16[64,1024]{1,0:T(8,128)(2,1)S(1)}, bf16[64,1024]{1,0:T(8,128)(2,1)S(1)}, u32[]{:S(2)}, u32[]{:S(2)}) collective-permute-start(bf16[64,1024]{1,0:T(8,128)(2,1)S(1)} %get-tuple-element.76), channel_id=1, source_target_pairs={{0,6},{1,7},{2,4},{3,5},{4,2},{5,3},{6,0},{7,1},{8,14},{9,15},{10,... | collective-permute-start | bytes 393224 | tf_op jit(solution)/shard_map/ppermute | solution.py:547
  37.4 0.7 %collective-permute-start.10 = (bf16[2,64,512]{2,1,0:T(8,128)(2,1)S(1)}, bf16[2,64,512]{2,1,0:T(8,128)(2,1)S(1)}, u32[]{:S(2)}, u32[]{:S(2)}) collective-permute-start(bf16[2,64,512]{2,1,0:T(8,128)(2,1)S(1)} %get-tuple-element.78), channel_id=1, source_target_pairs={{4,8},{8,4},{5,9},{9,5},{6,10},{10,6},{7,11},{11,7},{20,24},{24,20... | collective-permute-start | bytes 393224 | tf_op jit(solution)/shard_map/ppermute | solution.py:479
  38.1 0.0 collective-permute-done.7
  38.1 2.2 %collective-permute-done.8 = bf16[64,1024]{1,0:T(8,128)(2,1)S(1)} collective-permute-done((bf16[64,1024]{1,0:T(8,128)(2,1)S(1)}, bf16[64,1024]{1,0:T(8,128)(2,1)S(1)}, u32[]{:S(2)}, u32[]{:S(2)}) %collective-permute-start.8) | collective-permute-done | bytes 131104 | tf_op jit(solution)/shard_map/ppermute | solution.py:494
  40.3 3.4 %collective-permute-done.9 = bf16[64,1024]{1,0:T(8,128)(2,1)S(1)} collective-permute-done((bf16[64,1024]{1,0:T(8,128)(2,1)S(1)}, bf16[64,1024]{1,0:T(8,128)(2,1)S(1)}, u32[]{:S(2)}, u32[]{:S(2)}) %collective-permute-start.9) | collective-permute-done | bytes 131104 | tf_op jit(solution)/shard_map/ppermute | solution.py:547
  43.7 0.1 add_convert_fusion.1
  43.8 0.0 collective-permute-done.10.refs_2_
  43.8 2.2 %collective-permute-start.11 = (bf16[64,1024]{1,0:T(8,128)(2,1)S(1)}, bf16[64,1024]{1,0:T(8,128)(2,1)S(1)}, u32[]{:S(2)}, u32[]{:S(2)}) collective-permute-start(bf16[64,1024]{1,0:T(8,128)(2,1)S(1)} %add_convert_fusion.1), channel_id=1, source_target_pairs={{0,8},{4,12},{8,0},{12,4},{1,9},{5,13},{9,1},{13,5},{2,10},{6,14},... | collective-permute-start | bytes 393224 | tf_op jit(solution)/shard_map/ppermute | solution.py:494
  46.0 0.3 collective-permute-start.12
  46.3 6.0 %collective-permute-done.11 = bf16[64,1024]{1,0:T(8,128)(2,1)S(1)} collective-permute-done((bf16[64,1024]{1,0:T(8,128)(2,1)S(1)}, bf16[64,1024]{1,0:T(8,128)(2,1)S(1)}, u32[]{:S(2)}, u32[]{:S(2)}) %collective-permute-start.11) | collective-permute-done | bytes 131104 | tf_op jit(solution)/shard_map/ppermute | solution.py:494
  52.4 0.0 collective-permute-done.12.refs_1_
  52.4 0.5 collective-permute-start.15
  52.9 1.3 %collective-permute-start.14 = (bf16[64,1024]{1,0:T(8,128)(2,1)S(1)}, bf16[64,1024]{1,0:T(8,128)(2,1)S(1)}, u32[]{:S(2)}, u32[]{:S(2)}) collective-permute-start(bf16[64,1024]{1,0:T(8,128)(2,1)S(1)} %add_convert_fusion.own_ref), channel_id=1, source_target_pairs={{0,16},{16,0},{1,17},{17,1},{2,18},{18,2},{3,19},{19,3},{4,20},{20... | collective-permute-start | bytes 393224 | tf_op jit(solution)/shard_map/ppermute | solution.py:494
  54.2 1.7 %collective-permute-start.13 = (bf16[64,1024]{1,0:T(8,128)(2,1)S(1)}, bf16[64,1024]{1,0:T(8,128)(2,1)S(1)}, u32[]{:S(2)}, u32[]{:S(2)}) collective-permute-start(bf16[64,1024]{1,0:T(8,128)(2,1)S(1)} %add_convert_fusion.own_ref), channel_id=1, source_target_pairs={{0,4},{4,0},{8,12},{12,8},{1,5},{5,1},{9,13},{13,9},{2,6},{6,2},{1... | collective-permute-start | bytes 393224 | tf_op jit(solution)/shard_map/ppermute | solution.py:494
  55.9 0.0 copy-done.4
  55.9 1.9 %input.1 = (bf16[1,16,16,512]{3,2,1,0:T(8,128)(2,1)}, bf16[1,16,16,512]{3,2,1,0:T(8,128)(2,1)}) custom-call(bf16[16,64,1024]{2,1,0:T(8,128)(2,1)S(1)} %get-tuple-element.67.refs_1_.refs_0_, bf16[2,64,512]{2,1,0:T(8,128)(2,1)S(1)} %collective-permute-done.12.refs_1_, bf16[2,64,512]{2,1,0:T(8,128)(2,1)S(1)} %collective-permute-done.10.refs_2_, ...), custom_call_target="tpu_custom_call" | custom-call | flops 402653184 | bytes 6294528 | tf_op jit(solution)/shard_map/input/pallas_call | solution.py:436
  57.8 0.6 collective-permute-done.15.far_ref
  58.4 0.9 %collective-permute-done.14.lon_ref = bf16[64,1024]{1,0:T(8,128)(2,1)S(1)} collective-permute-done((bf16[64,1024]{1,0:T(8,128)(2,1)S(1)}, bf16[64,1024]{1,0:T(8,128)(2,1)S(1)}, u32[]{:S(2)}, u32[]{:S(2)}) %collective-permute-start.14) | collective-permute-done | bytes 131104 | tf_op jit(solution)/shard_map/ppermute | solution.py:494
  59.3 0.0 collective-permute-done.13.lat_ref
  59.3 1.2 %finish.1 = (f32[128,1536]{1,0:T(8,128)}, f32[128,512]{1,0:T(8,128)}, f32[1,128]{1,0:T(1,128)}) custom-call(bf16[64,1024]{1,0:T(8,128)(2,1)S(1)} %add_convert_fusion.own_ref, bf16[64,1024]{1,0:T(8,128)(2,1)S(1)} %collective-permute-done.13.lat_ref, bf16[64,1024]{1,0:T(8,128)(2,1)S(1)} %collective-permute-done.14.lon_ref, ...), custom_call_target="tpu_custom_call" | custom-call | bytes 3148288 | tf_op jit(solution)/shard_map/finish/pallas_call | solution.py:436
  (1 shorter events, 0.0 us)
Async XLA Ops:
  0.6 7.4 %copy-start = (bf16[512,1536]{1,0:T(8,128)(2,1)S(1)}, bf16[512,1536]{1,0:T(8,128)(2,1)}, u32[]{:S(2)}) copy-start(bf16[512,1536]{1,0:T(8,128)(2,1)} %wqkv_ref.5) | copy-start | bytes 4718596
  0.6 7.4 %copy-start.2 = (bf16[1,16,16,512]{3,2,1,0:T(8,128)(2,1)S(1)}, bf16[1,16,16,512]{3,2,1,0:T(8,128)(2,1)}, u32[]{:S(2)}) copy-start(bf16[1,16,16,512]{3,2,1,0:T(8,128)(2,1)} %refs_9_.1) | copy-start | bytes 786436
  0.7 1.1 %copy-start.3 = (bf16[1,16,16,512]{3,2,1,0:T(8,128)(2,1)S(1)}, bf16[1,16,16,512]{3,2,1,0:T(8,128)(2,1)}, u32[]{:S(2)}) copy-start(bf16[1,16,16,512]{3,2,1,0:T(8,128)(2,1)} %refs_10_.1) | copy-start | bytes 786436
  1.7 0.7 %copy-start.5 = (s32[1,16,16]{2,1,0:T(8,128)S(1)}, s32[1,16,16]{2,1,0:T(8,128)}, u32[]{:S(2)}) copy-start(s32[1,16,16]{2,1,0:T(8,128)} %refs_11_.1) | copy-start | bytes 3076
  2.4 5.6 %copy-start.6 = (s32[1,16,16]{2,1,0:T(8,128)S(1)}, s32[1,16,16]{2,1,0:T(8,128)}, u32[]{:S(2)}) copy-start(s32[1,16,16]{2,1,0:T(8,128)} %refs_11_.1) | copy-start | bytes 3076
  2.4 5.6 %copy-start.7 = (f32[512]{0:T(512)S(1)}, f32[512]{0:T(512)}, u32[]{:S(2)}) copy-start(f32[512]{0:T(512)} %param.10) | copy-start | bytes 6148
  2.8 13.5 %collective-permute-start = (bf16[4,64,512]{2,1,0:T(8,128)(2,1)S(1)}, bf16[4,64,512]{2,1,0:T(8,128)(2,1)S(1)}, u32[]{:S(2)}, u32[]{:S(2)}) collective-permute-start(bf16[4,64,512]{2,1,0:T(8,128)(2,1)S(1)} %get-tuple-element.47.tok_ref.refs_4_), channel_id=1, source_target_pairs={{0,16},{16,0},{1,17},{17,1},{2,18},{18,2},{3,19},{19,3},{4,20},{20... | collective-permute-start | bytes 786440 | tf_op jit(solution)/shard_map/ppermute | solution.py:462
  5.8 9.0 %collective-permute-start.1 = (bf16[2,64,512]{2,1,0:T(8,128)(2,1)S(1)}, bf16[2,64,512]{2,1,0:T(8,128)(2,1)S(1)}, u32[]{:S(2)}, u32[]{:S(2)}) collective-permute-start(bf16[2,64,512]{2,1,0:T(8,128)(2,1)S(1)} %get-tuple-element.56), channel_id=1, source_target_pairs={{0,4},{8,12},{4,0},{12,8},{1,5},{9,13},{5,1},{13,9},{2,6},{10,14},... | collective-permute-start | bytes 393224 | tf_op jit(solution)/shard_map/ppermute | solution.py:479
  7.4 8.9 %collective-permute-start.2 = (bf16[2,64,512]{2,1,0:T(8,128)(2,1)S(1)}, bf16[2,64,512]{2,1,0:T(8,128)(2,1)S(1)}, u32[]{:S(2)}, u32[]{:S(2)}) collective-permute-start(bf16[2,64,512]{2,1,0:T(8,128)(2,1)S(1)} %get-tuple-element.57), channel_id=1, source_target_pairs={{4,8},{8,4},{5,9},{9,5},{6,10},{10,6},{7,11},{11,7},{20,24},{24,20... | collective-permute-start | bytes 393224 | tf_op jit(solution)/shard_map/ppermute | solution.py:479
  8.1 9.9 %copy-start.1 = (bf16[512,512]{1,0:T(8,128)(2,1)S(1)}, bf16[512,512]{1,0:T(8,128)(2,1)}, u32[]{:S(2)}) copy-start(bf16[512,512]{1,0:T(8,128)(2,1)} %refs_7_.1) | copy-start | bytes 1572868
  9.7 8.3 %collective-permute-start.4 = (bf16[2,64,512]{2,1,0:T(8,128)(2,1)S(1)}, bf16[2,64,512]{2,1,0:T(8,128)(2,1)S(1)}, u32[]{:S(2)}, u32[]{:S(2)}) collective-permute-start(bf16[2,64,512]{2,1,0:T(8,128)(2,1)S(1)} %get-tuple-element.56), channel_id=1, source_target_pairs={{0,20},{16,4},{8,28},{24,12},{20,0},{4,16},{28,8},{12,24},{1,21},{... | collective-permute-start | bytes 393224 | tf_op jit(solution)/shard_map/ppermute | solution.py:490
  14.1 3.9 %collective-permute-start.5 = (bf16[2,64,512]{2,1,0:T(8,128)(2,1)S(1)}, bf16[2,64,512]{2,1,0:T(8,128)(2,1)S(1)}, u32[]{:S(2)}, u32[]{:S(2)}) collective-permute-start(bf16[2,64,512]{2,1,0:T(8,128)(2,1)S(1)} %get-tuple-element.57), channel_id=1, source_target_pairs={{4,24},{20,8},{24,4},{8,20},{5,25},{21,9},{25,5},{9,21},{6,26},{22... | collective-permute-start | bytes 393224 | tf_op jit(solution)/shard_map/ppermute | solution.py:490
  14.8 7.9 %collective-permute-start.3 = (bf16[4,64,512]{2,1,0:T(8,128)(2,1)S(1)}, bf16[4,64,512]{2,1,0:T(8,128)(2,1)S(1)}, u32[]{:S(2)}, u32[]{:S(2)}) collective-permute-start(bf16[4,64,512]{2,1,0:T(8,128)(2,1)S(1)} %get-tuple-element.54.refs_6_.refs_4_), channel_id=1, source_target_pairs={{0,16},{16,0},{1,17},{17,1},{2,18},{18,2},{3,19},{19,3},{4,20},{20... | collective-permute-start | bytes 786440 | tf_op jit(solution)/shard_map/ppermute | solution.py:462
  28.6 2.0 %collective-permute-start.6 = (bf16[2,2,64,1024]{3,2,1,0:T(8,128)(2,1)S(1)}, bf16[2,2,64,1024]{3,2,1,0:T(8,128)(2,1)S(1)}, u32[]{:S(2)}, u32[]{:S(2)}) collective-permute-start(bf16[2,2,64,1024]{3,2,1,0:T(8,128)(2,1)S(1)} %sent.1), channel_id=1, source_target_pairs={{0,1},{1,0},{2,3},{3,2},{4,5},{5,4},{6,7},{7,6},{8,9},{9,8},{10,11... | collective-permute-start | bytes 1572872 | tf_op jit(solution)/shard_map/ppermute | solution.py:494
  29.3 26.6 %copy-start.4 = (bf16[1,16,16,512]{3,2,1,0:T(8,128)(2,1)S(1)}, bf16[1,16,16,512]{3,2,1,0:T(8,128)(2,1)}, u32[]{:S(2)}) copy-start(bf16[1,16,16,512]{3,2,1,0:T(8,128)(2,1)} %refs_10_.1) | copy-start | bytes 786436
  30.7 7.4 %collective-permute-start.7 = (bf16[64,1024]{1,0:T(8,128)(2,1)S(1)}, bf16[64,1024]{1,0:T(8,128)(2,1)S(1)}, u32[]{:S(2)}, u32[]{:S(2)}) collective-permute-start(bf16[64,1024]{1,0:T(8,128)(2,1)S(1)} %get-tuple-element.74), channel_id=1, source_target_pairs={{0,2},{1,3},{2,0},{3,1},{4,6},{5,7},{6,4},{7,5},{8,10},{9,11},{10,... | collective-permute-start | bytes 393224 | tf_op jit(solution)/shard_map/ppermute | solution.py:494
  32.1 8.2 %collective-permute-start.8 = (bf16[64,1024]{1,0:T(8,128)(2,1)S(1)}, bf16[64,1024]{1,0:T(8,128)(2,1)S(1)}, u32[]{:S(2)}, u32[]{:S(2)}) collective-permute-start(bf16[64,1024]{1,0:T(8,128)(2,1)S(1)} %get-tuple-element.75), channel_id=1, source_target_pairs={{0,4},{4,0},{8,12},{12,8},{1,5},{5,1},{9,13},{13,9},{2,6},{6,2},{1... | collective-permute-start | bytes 393224 | tf_op jit(solution)/shard_map/ppermute | solution.py:494
  36.4 7.3 %collective-permute-start.9 = (bf16[64,1024]{1,0:T(8,128)(2,1)S(1)}, bf16[64,1024]{1,0:T(8,128)(2,1)S(1)}, u32[]{:S(2)}, u32[]{:S(2)}) collective-permute-start(bf16[64,1024]{1,0:T(8,128)(2,1)S(1)} %get-tuple-element.76), channel_id=1, source_target_pairs={{0,6},{1,7},{2,4},{3,5},{4,2},{5,3},{6,0},{7,1},{8,14},{9,15},{10,... | collective-permute-start | bytes 393224 | tf_op jit(solution)/shard_map/ppermute | solution.py:547
  37.4 6.4 %collective-permute-start.10 = (bf16[2,64,512]{2,1,0:T(8,128)(2,1)S(1)}, bf16[2,64,512]{2,1,0:T(8,128)(2,1)S(1)}, u32[]{:S(2)}, u32[]{:S(2)}) collective-permute-start(bf16[2,64,512]{2,1,0:T(8,128)(2,1)S(1)} %get-tuple-element.78), channel_id=1, source_target_pairs={{4,8},{8,4},{5,9},{9,5},{6,10},{10,6},{7,11},{11,7},{20,24},{24,20... | collective-permute-start | bytes 393224 | tf_op jit(solution)/shard_map/ppermute | solution.py:479
  43.8 8.5 %collective-permute-start.11 = (bf16[64,1024]{1,0:T(8,128)(2,1)S(1)}, bf16[64,1024]{1,0:T(8,128)(2,1)S(1)}, u32[]{:S(2)}, u32[]{:S(2)}) collective-permute-start(bf16[64,1024]{1,0:T(8,128)(2,1)S(1)} %add_convert_fusion.1), channel_id=1, source_target_pairs={{0,8},{4,12},{8,0},{12,4},{1,9},{5,13},{9,1},{13,5},{2,10},{6,14},... | collective-permute-start | bytes 393224 | tf_op jit(solution)/shard_map/ppermute | solution.py:494
  46.0 6.4 %collective-permute-start.12 = (bf16[2,64,512]{2,1,0:T(8,128)(2,1)S(1)}, bf16[2,64,512]{2,1,0:T(8,128)(2,1)S(1)}, u32[]{:S(2)}, u32[]{:S(2)}) collective-permute-start(bf16[2,64,512]{2,1,0:T(8,128)(2,1)S(1)} %get-tuple-element.80), channel_id=1, source_target_pairs={{0,4},{8,12},{4,0},{12,8},{1,5},{9,13},{5,1},{13,9},{2,6},{10,14},... | collective-permute-start | bytes 393224 | tf_op jit(solution)/shard_map/ppermute | solution.py:479
  52.4 6.0 %collective-permute-start.15 = (bf16[64,1024]{1,0:T(8,128)(2,1)S(1)}, bf16[64,1024]{1,0:T(8,128)(2,1)S(1)}, u32[]{:S(2)}, u32[]{:S(2)}) collective-permute-start(bf16[64,1024]{1,0:T(8,128)(2,1)S(1)} %add_convert_fusion.own_ref), channel_id=1, source_target_pairs={{0,20},{4,16},{8,28},{12,24},{16,4},{20,0},{24,12},{28,8},{1,21},{... | collective-permute-start | bytes 393224 | tf_op jit(solution)/shard_map/ppermute | solution.py:562
  52.9 6.4 %collective-permute-start.14 = (bf16[64,1024]{1,0:T(8,128)(2,1)S(1)}, bf16[64,1024]{1,0:T(8,128)(2,1)S(1)}, u32[]{:S(2)}, u32[]{:S(2)}) collective-permute-start(bf16[64,1024]{1,0:T(8,128)(2,1)S(1)} %add_convert_fusion.own_ref), channel_id=1, source_target_pairs={{0,16},{16,0},{1,17},{17,1},{2,18},{18,2},{3,19},{19,3},{4,20},{20... | collective-permute-start | bytes 393224 | tf_op jit(solution)/shard_map/ppermute | solution.py:494
  54.2 5.1 %collective-permute-start.13 = (bf16[64,1024]{1,0:T(8,128)(2,1)S(1)}, bf16[64,1024]{1,0:T(8,128)(2,1)S(1)}, u32[]{:S(2)}, u32[]{:S(2)}) collective-permute-start(bf16[64,1024]{1,0:T(8,128)(2,1)S(1)} %add_convert_fusion.own_ref), channel_id=1, source_target_pairs={{0,4},{4,0},{8,12},{12,8},{1,5},{5,1},{9,13},{13,9},{2,6},{6,2},{1... | collective-permute-start | bytes 393224 | tf_op jit(solution)/shard_map/ppermute | solution.py:494

commit v10 on v8

--- a/solution.py
+++ b/solution.py
@@ -590,7 +590,6 @@
     if pair:
         sides, gb = lax.optimization_barrier((sides, gb))
         corner_first, corner_second = corner_swap(sides[0], 0), corner_swap(sides[1], 1)
-        gb_near = lon_halo(gb)
     else:
         rows = tok_lon.reshape(2, 2, AREA, D)
         corner_first, corner_second = lat_swaps(
@@ -603,6 +602,9 @@
         [], [tok_lon, tok_first, tok_second, wqkv, gain], [], [], [], 20,
         flops=2 * 512 * 512 * 1280, out_specs=[VMEM] * 4 + [SMEM],
     )
+    if pair:
+        kv_near, gb = lax.optimization_barrier((kv_near, gb))
+        gb_near = lon_halo(gb)
     all_shape, all32 = shape((16, AREA, 2 * D)), shape((16, AREA, 2 * D), F32)
     back = shape((2 if pair else 4, AREA, D))
     ends = [all_shape, back, back] + ([] if pair else [four])

time: 61.6 us -> 61.3 us (level)
    ppermute x6, starting transfers between devices: 11.1 us -> 11.9 us  [swap(): lax.ppermute(value, axis, [(i, i ^ bit) for i in range(lax.axis_size(axis...]
  transfers between devices with their start and end apart: 16 -> 16, of which waited for: 7 -> 8; matrix products, arithmetic and copies ran while one was open for 0% -> 0% of each run, Pallas kernels for 20% -> 20%
where the time goes in v10:
time: 61.3 us; the launch traced here: 61.2 us
  starting transfers between devices  25.2 us (41%)
  Pallas kernels  18.9 us (31%)
  waiting for transfers between devices  14.2 us (23%)
  local copies, waits for them, and re-layouts  1.8 us (3%)
  between operations  0.87 us (1%)
    pallas_call x10, Pallas kernels, call(): pl.pallas_call(kernel, out_shape=outs, in_specs=specs, out_specs=out_spec...  18.9 us
    ppermute x6, starting transfers between devices, swap(): lax.ppermute(value, axis, [(i, i ^ bit) for i in range(lax.axis_size(axis...  11.9 us
    ppermute x6, waiting for transfers between devices, swap(): lax.ppermute(value, axis, [(i, i ^ bit) for i in range(lax.axis_size(axis...  11.1 us
    ppermute x2, starting transfers between devices, corner_swap(): lax.ppermute(value, ('lon', 'lat'), pairs + [(b, a) for a, b in pairs])  5.09 us
    ppermute x2, starting transfers between devices, lon_halo(): return lax.ppermute(own, 'lon', [(0, 1), (1, 0)])  4.56 us
    ppermute x4, starting transfers between devices, lat_swap(): return lax.ppermute(value, 'lat', pairs + [(b, a) for a, b in pairs])  3.36 us
    ppermute x1, waiting for transfers between devices, pair_sum(): lax.ppermute(to_far, ('lat', 'lev'), [(i, i ^ 6) for i in range(4 * count)])  2.32 us
    unnamed x16, local copies, waits for them, and re-layouts  1.8 us
  transfers between devices with their start and end apart: 16, of which 8 were waited for; matrix products, arithmetic and copies ran while one was open for 0% of the time, Pallas kernels for 20%

profile of v10, /device:TPU:0, one launch (start us, length us, event | category | flops | bytes accessed | tf_op | source)
XLA Modules:
  0.0 61.2 jit_solution(14815978696398624199)
XLA Ops:
  0.6 0.0 copy-start
  0.6 0.0 copy-start.2
  0.7 0.0 copy-start.3
  0.7 1.1 %copy-done.3 = bf16[1,16,16,512]{3,2,1,0:T(8,128)(2,1)S(1)} copy-done((bf16[1,16,16,512]{3,2,1,0:T(8,128)(2,1)S(1)}, bf16[1,16,16,512]{3,2,1,0:T(8,128)(2,1)}, u32[]{:S(2)}) %copy-start.3) | copy-done | bytes 262168
  1.7 0.0 copy-start.5
  1.7 0.7 %copy-done.5 = s32[1,16,16]{2,1,0:T(8,128)S(1)} copy-done((s32[1,16,16]{2,1,0:T(8,128)S(1)}, s32[1,16,16]{2,1,0:T(8,128)}, u32[]{:S(2)}) %copy-start.5) | copy-done | bytes 1048
  2.4 0.0 copy-start.6
  2.4 0.0 copy-start.7
  2.4 0.4 prep.1
  2.8 3.0 %collective-permute-start = (bf16[4,64,512]{2,1,0:T(8,128)(2,1)S(1)}, bf16[4,64,512]{2,1,0:T(8,128)(2,1)S(1)}, u32[]{:S(2)}, u32[]{:S(2)}) collective-permute-start(bf16[4,64,512]{2,1,0:T(8,128)(2,1)S(1)} %get-tuple-element.49.tok_ref.refs_4_), channel_id=1, source_target_pairs={{0,16},{16,0},{1,17},{17,1},{2,18},{18,2},{3,19},{19,3},{4,20},{20... | collective-permute-start | bytes 786440 | tf_op jit(solution)/shard_map/ppermute | solution.py:461
  5.8 1.6 %collective-permute-start.1 = (bf16[2,64,512]{2,1,0:T(8,128)(2,1)S(1)}, bf16[2,64,512]{2,1,0:T(8,128)(2,1)S(1)}, u32[]{:S(2)}, u32[]{:S(2)}) collective-permute-start(bf16[2,64,512]{2,1,0:T(8,128)(2,1)S(1)} %get-tuple-element.60), channel_id=1, source_target_pairs={{0,4},{8,12},{4,0},{12,8},{1,5},{9,13},{5,1},{13,9},{2,6},{10,14},... | collective-permute-start | bytes 393224 | tf_op jit(solution)/shard_map/ppermute | solution.py:478
  7.4 0.7 %collective-permute-start.2 = (bf16[2,64,512]{2,1,0:T(8,128)(2,1)S(1)}, bf16[2,64,512]{2,1,0:T(8,128)(2,1)S(1)}, u32[]{:S(2)}, u32[]{:S(2)}) collective-permute-start(bf16[2,64,512]{2,1,0:T(8,128)(2,1)S(1)} %get-tuple-element.61), channel_id=1, source_target_pairs={{4,8},{8,4},{5,9},{9,5},{6,10},{10,6},{7,11},{11,7},{20,24},{24,20... | collective-permute-start | bytes 393224 | tf_op jit(solution)/shard_map/ppermute | solution.py:478
  8.0 0.0 copy-done
  8.1 0.0 copy-done.2
  8.1 0.0 copy-done.6
  8.1 0.0 copy-done.7
  8.1 0.0 copy-start.1
  8.1 1.6 %own.1 = (bf16[4,64,512]{2,1,0:T(8,128)(2,1)S(1)}, bf16[4,64,1024]{2,1,0:T(8,128)(2,1)S(1)}, bf16[256,512]{1,0:T(8,128)(2,1)S(1)}, bf16[4,64,512]{2,1,0:T(8,128)...) custom-call(bf16[4,64,512]{2,1,0:T(8,128)(2,1)S(1)} %get-tuple-element.49.tok_ref.refs_4_, ...), custom_call_target="tpu_custom_call" | custom-call | flops 402653184 | bytes 3419168 | tf_op jit(solution)/shard_map/own/pallas_call | solution.py:435
  9.7 4.4 %collective-permute-start.4 = (bf16[2,64,512]{2,1,0:T(8,128)(2,1)S(1)}, bf16[2,64,512]{2,1,0:T(8,128)(2,1)S(1)}, u32[]{:S(2)}, u32[]{:S(2)}) collective-permute-start(bf16[2,64,512]{2,1,0:T(8,128)(2,1)S(1)} %get-tuple-element.60), channel_id=1, source_target_pairs={{0,20},{16,4},{8,28},{24,12},{20,0},{4,16},{28,8},{12,24},{1,21},{... | collective-permute-start | bytes 393224 | tf_op jit(solution)/shard_map/ppermute | solution.py:489
  14.1 0.7 %collective-permute-start.5 = (bf16[2,64,512]{2,1,0:T(8,128)(2,1)S(1)}, bf16[2,64,512]{2,1,0:T(8,128)(2,1)S(1)}, u32[]{:S(2)}, u32[]{:S(2)}) collective-permute-start(bf16[2,64,512]{2,1,0:T(8,128)(2,1)S(1)} %get-tuple-element.61), channel_id=1, source_target_pairs={{4,24},{20,8},{24,4},{8,20},{5,25},{21,9},{25,5},{9,21},{6,26},{22... | collective-permute-start | bytes 393224 | tf_op jit(solution)/shard_map/ppermute | solution.py:489
  14.8 0.0 collective-permute-done.1.first_ref
  14.8 0.0 collective-permute-done.2.second_ref
  14.8 0.0 collective-permute-done.lon_ref
  14.8 1.6 %near.1 = (bf16[4,64,512]{2,1,0:T(8,128)(2,1)S(1)}, bf16[8,64,1024]{2,1,0:T(8,128)(2,1)S(1)}, bf16[512,512]{1,0:T(8,128)(2,1)S(1)}, f32[8,8,64]{2,1,0:T(8,128)S(1)}, s32[8]{0:T(128)S(1)}) custom-call(bf16[4,64,512]{2,1,0:T(8,128)(2,1)S(1)} %collective-permute-done.lon_ref, bf16[2,64,512]{2,1,0:T(8,128)(2,1)S(1)} %collective-permute-done.1.first_ref, ...), custom_call_target="tpu_custom_call" | custom-call | flops 671088640 | bytes 3950624 | tf_op jit(solution)/shard_map/near/pallas_call | solution.py:435
  16.4 1.6 %collective-permute-start.3 = (bf16[4,64,512]{2,1,0:T(8,128)(2,1)S(1)}, bf16[4,64,512]{2,1,0:T(8,128)(2,1)S(1)}, u32[]{:S(2)}, u32[]{:S(2)}) collective-permute-start(bf16[4,64,512]{2,1,0:T(8,128)(2,1)S(1)} %get-tuple-element.58.refs_6_.refs_4_), channel_id=1, source_target_pairs={{0,16},{16,0},{1,17},{17,1},{2,18},{18,2},{3,19},{19,3},{4,20},{20... | collective-permute-start | bytes 786440 | tf_op jit(solution)/shard_map/ppermute | solution.py:461
  18.0 0.0 collective-permute-done.4.refs_7_
  18.0 0.0 collective-permute-done.5.refs_8_
  18.0 0.0 copy-done.1
  18.0 6.4 %main.1 = (f32[16,64,1024]{2,1,0:T(8,128)S(1)}, bf16[4,64,512]{2,1,0:T(8,128)(2,1)S(1)}, bf16[4,64,512]{2,1,0:T(8,128)(2,1)S(1)}, bf16[1024,512]{1,0:T(8,128)(2,...) custom-call(s32[8]{0:T(128)S(1)} %get-tuple-element.50.refs_0_, s32[8]{0:T(128)S(1)} %get-tuple-element.53.refs_1_, ...), custom_call_target="tpu_custom_call" | custom-call | flops 2415919104 | bytes 13166592 | tf_op jit(solution)/shard_map/main/pallas_call | solution.py:435
  24.4 0.0 collective-permute-done.3.refs_6_.refs_7_
  24.4 4.0 %other.1 = (f32[16,64,1024]{2,1,0:T(8,128)S(1)}, bf16[4,64,512]{2,1,0:T(8,128)(2,1)S(1)}, bf16[4,64,512]{2,1,0:T(8,128)(2,1)S(1)}, bf16[16,64,1024]{2,1,0:T(8,12...) custom-call(s32[8]{0:T(128)S(1)} %get-tuple-element.50.refs_0_, ...), custom_call_target="tpu_custom_call", output_to_operand_aliasing={{0}: (9, {})} | custom-call | flops 2415919104 | bytes 16025600 | tf_op jit(solution)/shard_map/other/pallas_call | solution.py:435
  28.5 0.6 %sent.1 = bf16[2,2,64,1024]{3,2,1,0:T(8,128)(2,1)S(1)} custom-call(bf16[1024,512]{1,0:T(8,128)(2,1)S(1)} %get-tuple-element.72.refs_0_, bf16[16,64,1024]{2,1,0:T(8,128)(2,1)S(1)} %get-tuple-element.71.refs_1_.refs_0_, bf16[4,64,512]{2,1,0:T(8,128)(2,1)S(1)} %get-tuple-element.73.refs_2_.refs_3_, bf16[4,64,512]{2,1,0:T(8,128)(2,1)S(1)} %get-tuple-element.74.refs_3_.refs_5_, ...), custom_call_target="tpu_custom_call" | custom-call | flops 536870912 | bytes 5242880 | tf_op jit(solution)/shard_map/sent/pallas_call | solution.py:435
  29.1 0.1 collective-permute-start.6
  29.2 0.8 %kept.1.keep_ref = bf16[2,2,64,1024]{3,2,1,0:T(8,128)(2,1)S(1)} custom-call(bf16[1024,512]{1,0:T(8,128)(2,1)S(1)} %get-tuple-element.72.refs_0_, bf16[16,64,1024]{2,1,0:T(8,128)(2,1)S(1)} %get-tuple-element.71.refs_1_.refs_0_, bf16[4,64,512]{2,1,0:T(8,128)(2,1)S(1)} %get-tuple-element.73.refs_2_.refs_3_, ...), custom_call_target="tpu_custom_call" | custom-call | flops 536870912 | bytes 5242880 | tf_op jit(solution)/shard_map/kept/pallas_call | solution.py:435
  30.0 0.0 copy-start.4
  30.0 1.1 %collective-permute-done.6.come_ref = bf16[2,2,64,1024]{3,2,1,0:T(8,128)(2,1)S(1)} collective-permute-done((bf16[2,2,64,1024]{3,2,1,0:T(8,128)(2,1)S(1)}, bf16[2,2,64,1024]{3,2,1,0:T(8,128)(2,1)S(1)}, u32[]{:S(2)}, u32[]{:S(2)}) %collective-permute-start.6) | collective-permute-done | bytes 524320 | tf_op jit(solution)/shard_map/ppermute | solution.py:493
  31.1 0.1 split.1
  31.2 0.6 collective-permute-start.7
  31.8 5.8 %collective-permute-start.8 = (bf16[64,1024]{1,0:T(8,128)(2,1)S(1)}, bf16[64,1024]{1,0:T(8,128)(2,1)S(1)}, u32[]{:S(2)}, u32[]{:S(2)}) collective-permute-start(bf16[64,1024]{1,0:T(8,128)(2,1)S(1)} %get-tuple-element.79), channel_id=1, source_target_pairs={{0,4},{4,0},{8,12},{12,8},{1,5},{5,1},{9,13},{13,9},{2,6},{6,2},{1... | collective-permute-start | bytes 393224 | tf_op jit(solution)/shard_map/ppermute | solution.py:493
  37.6 0.3 collective-permute-start.9
  37.9 0.7 %collective-permute-start.10 = (bf16[2,64,512]{2,1,0:T(8,128)(2,1)S(1)}, bf16[2,64,512]{2,1,0:T(8,128)(2,1)S(1)}, u32[]{:S(2)}, u32[]{:S(2)}) collective-permute-start(bf16[2,64,512]{2,1,0:T(8,128)(2,1)S(1)} %get-tuple-element.82), channel_id=1, source_target_pairs={{4,8},{8,4},{5,9},{9,5},{6,10},{10,6},{7,11},{11,7},{20,24},{24,20... | collective-permute-start | bytes 393224 | tf_op jit(solution)/shard_map/ppermute | solution.py:478
  38.6 0.0 collective-permute-done.7
  38.6 3.3 %collective-permute-done.8 = bf16[64,1024]{1,0:T(8,128)(2,1)S(1)} collective-permute-done((bf16[64,1024]{1,0:T(8,128)(2,1)S(1)}, bf16[64,1024]{1,0:T(8,128)(2,1)S(1)}, u32[]{:S(2)}, u32[]{:S(2)}) %collective-permute-start.8) | collective-permute-done | bytes 131104 | tf_op jit(solution)/shard_map/ppermute | solution.py:493
  41.9 2.3 %collective-permute-done.9 = bf16[64,1024]{1,0:T(8,128)(2,1)S(1)} collective-permute-done((bf16[64,1024]{1,0:T(8,128)(2,1)S(1)}, bf16[64,1024]{1,0:T(8,128)(2,1)S(1)}, u32[]{:S(2)}, u32[]{:S(2)}) %collective-permute-start.9) | collective-permute-done | bytes 131104 | tf_op jit(solution)/shard_map/ppermute | solution.py:546
  44.2 0.1 add_convert_fusion.1
  44.3 0.0 collective-permute-done.10.refs_2_
  44.3 2.0 %collective-permute-start.11 = (bf16[64,1024]{1,0:T(8,128)(2,1)S(1)}, bf16[64,1024]{1,0:T(8,128)(2,1)S(1)}, u32[]{:S(2)}, u32[]{:S(2)}) collective-permute-start(bf16[64,1024]{1,0:T(8,128)(2,1)S(1)} %add_convert_fusion.1), channel_id=1, source_target_pairs={{0,8},{4,12},{8,0},{12,4},{1,9},{5,13},{9,1},{13,5},{2,10},{6,14},... | collective-permute-start | bytes 393224 | tf_op jit(solution)/shard_map/ppermute | solution.py:493
  46.3 0.5 collective-permute-start.12
  46.8 6.2 %collective-permute-done.11 = bf16[64,1024]{1,0:T(8,128)(2,1)S(1)} collective-permute-done((bf16[64,1024]{1,0:T(8,128)(2,1)S(1)}, bf16[64,1024]{1,0:T(8,128)(2,1)S(1)}, u32[]{:S(2)}, u32[]{:S(2)}) %collective-permute-start.11) | collective-permute-done | bytes 131104 | tf_op jit(solution)/shard_map/ppermute | solution.py:493
  53.0 0.3 collective-permute-done.12.refs_1_
  53.3 0.0 collective-permute-start.15
  53.3 1.4 %collective-permute-start.14 = (bf16[64,1024]{1,0:T(8,128)(2,1)S(1)}, bf16[64,1024]{1,0:T(8,128)(2,1)S(1)}, u32[]{:S(2)}, u32[]{:S(2)}) collective-permute-start(bf16[64,1024]{1,0:T(8,128)(2,1)S(1)} %add_convert_fusion.own_ref), channel_id=1, source_target_pairs={{0,16},{16,0},{1,17},{17,1},{2,18},{18,2},{3,19},{19,3},{4,20},{20... | collective-permute-start | bytes 393224 | tf_op jit(solution)/shard_map/ppermute | solution.py:493
  54.7 2.1 %collective-permute-start.13 = (bf16[64,1024]{1,0:T(8,128)(2,1)S(1)}, bf16[64,1024]{1,0:T(8,128)(2,1)S(1)}, u32[]{:S(2)}, u32[]{:S(2)}) collective-permute-start(bf16[64,1024]{1,0:T(8,128)(2,1)S(1)} %add_convert_fusion.own_ref), channel_id=1, source_target_pairs={{0,4},{4,0},{8,12},{12,8},{1,5},{5,1},{9,13},{13,9},{2,6},{6,2},{1... | collective-permute-start | bytes 393224 | tf_op jit(solution)/shard_map/ppermute | solution.py:493
  56.8 0.0 copy-done.4
  56.8 1.9 %input.1 = (bf16[1,16,16,512]{3,2,1,0:T(8,128)(2,1)}, bf16[1,16,16,512]{3,2,1,0:T(8,128)(2,1)}) custom-call(bf16[16,64,1024]{2,1,0:T(8,128)(2,1)S(1)} %get-tuple-element.71.refs_1_.refs_0_, bf16[2,64,512]{2,1,0:T(8,128)(2,1)S(1)} %collective-permute-done.12.refs_1_, bf16[2,64,512]{2,1,0:T(8,128)(2,1)S(1)} %collective-permute-done.10.refs_2_, ...), custom_call_target="tpu_custom_call" | custom-call | flops 402653184 | bytes 6294528 | tf_op jit(solution)/shard_map/input/pallas_call | solution.py:435
  58.7 0.6 collective-permute-done.15.far_ref
  59.3 0.4 collective-permute-done.14.lon_ref
  59.7 0.1 collective-permute-done.13.lat_ref
  59.7 1.4 %finish.1 = (f32[128,1536]{1,0:T(8,128)}, f32[128,512]{1,0:T(8,128)}, f32[1,128]{1,0:T(1,128)}) custom-call(bf16[64,1024]{1,0:T(8,128)(2,1)S(1)} %add_convert_fusion.own_ref, bf16[64,1024]{1,0:T(8,128)(2,1)S(1)} %collective-permute-done.13.lat_ref, bf16[64,1024]{1,0:T(8,128)(2,1)S(1)} %collective-permute-done.14.lon_ref, ...), custom_call_target="tpu_custom_call" | custom-call | bytes 3148288 | tf_op jit(solution)/shard_map/finish/pallas_call | solution.py:435
  (1 shorter events, 0.0 us)
Async XLA Ops:
  0.6 7.4 %copy-start = (bf16[512,1536]{1,0:T(8,128)(2,1)S(1)}, bf16[512,1536]{1,0:T(8,128)(2,1)}, u32[]{:S(2)}) copy-start(bf16[512,1536]{1,0:T(8,128)(2,1)} %wqkv_ref.5) | copy-start | bytes 4718596
  0.6 7.4 %copy-start.2 = (bf16[1,16,16,512]{3,2,1,0:T(8,128)(2,1)S(1)}, bf16[1,16,16,512]{3,2,1,0:T(8,128)(2,1)}, u32[]{:S(2)}) copy-start(bf16[1,16,16,512]{3,2,1,0:T(8,128)(2,1)} %refs_9_.1) | copy-start | bytes 786436
  0.7 1.1 %copy-start.3 = (bf16[1,16,16,512]{3,2,1,0:T(8,128)(2,1)S(1)}, bf16[1,16,16,512]{3,2,1,0:T(8,128)(2,1)}, u32[]{:S(2)}) copy-start(bf16[1,16,16,512]{3,2,1,0:T(8,128)(2,1)} %refs_10_.1) | copy-start | bytes 786436
  1.7 0.7 %copy-start.5 = (s32[1,16,16]{2,1,0:T(8,128)S(1)}, s32[1,16,16]{2,1,0:T(8,128)}, u32[]{:S(2)}) copy-start(s32[1,16,16]{2,1,0:T(8,128)} %refs_11_.1) | copy-start | bytes 3076
  2.4 5.6 %copy-start.6 = (s32[1,16,16]{2,1,0:T(8,128)S(1)}, s32[1,16,16]{2,1,0:T(8,128)}, u32[]{:S(2)}) copy-start(s32[1,16,16]{2,1,0:T(8,128)} %refs_11_.1) | copy-start | bytes 3076
  2.4 5.6 %copy-start.7 = (f32[512]{0:T(512)S(1)}, f32[512]{0:T(512)}, u32[]{:S(2)}) copy-start(f32[512]{0:T(512)} %param.10) | copy-start | bytes 6148
  2.8 12.0 %collective-permute-start = (bf16[4,64,512]{2,1,0:T(8,128)(2,1)S(1)}, bf16[4,64,512]{2,1,0:T(8,128)(2,1)S(1)}, u32[]{:S(2)}, u32[]{:S(2)}) collective-permute-start(bf16[4,64,512]{2,1,0:T(8,128)(2,1)S(1)} %get-tuple-element.49.tok_ref.refs_4_), channel_id=1, source_target_pairs={{0,16},{16,0},{1,17},{17,1},{2,18},{18,2},{3,19},{19,3},{4,20},{20... | collective-permute-start | bytes 786440 | tf_op jit(solution)/shard_map/ppermute | solution.py:461
  5.8 9.0 %collective-permute-start.1 = (bf16[2,64,512]{2,1,0:T(8,128)(2,1)S(1)}, bf16[2,64,512]{2,1,0:T(8,128)(2,1)S(1)}, u32[]{:S(2)}, u32[]{:S(2)}) collective-permute-start(bf16[2,64,512]{2,1,0:T(8,128)(2,1)S(1)} %get-tuple-element.60), channel_id=1, source_target_pairs={{0,4},{8,12},{4,0},{12,8},{1,5},{9,13},{5,1},{13,9},{2,6},{10,14},... | collective-permute-start | bytes 393224 | tf_op jit(solution)/shard_map/ppermute | solution.py:478
  7.4 7.4 %collective-permute-start.2 = (bf16[2,64,512]{2,1,0:T(8,128)(2,1)S(1)}, bf16[2,64,512]{2,1,0:T(8,128)(2,1)S(1)}, u32[]{:S(2)}, u32[]{:S(2)}) collective-permute-start(bf16[2,64,512]{2,1,0:T(8,128)(2,1)S(1)} %get-tuple-element.61), channel_id=1, source_target_pairs={{4,8},{8,4},{5,9},{9,5},{6,10},{10,6},{7,11},{11,7},{20,24},{24,20... | collective-permute-start | bytes 393224 | tf_op jit(solution)/shard_map/ppermute | solution.py:478
  8.1 9.9 %copy-start.1 = (bf16[512,512]{1,0:T(8,128)(2,1)S(1)}, bf16[512,512]{1,0:T(8,128)(2,1)}, u32[]{:S(2)}) copy-start(bf16[512,512]{1,0:T(8,128)(2,1)} %refs_7_.1) | copy-start | bytes 1572868
  9.7 8.3 %collective-permute-start.4 = (bf16[2,64,512]{2,1,0:T(8,128)(2,1)S(1)}, bf16[2,64,512]{2,1,0:T(8,128)(2,1)S(1)}, u32[]{:S(2)}, u32[]{:S(2)}) collective-permute-start(bf16[2,64,512]{2,1,0:T(8,128)(2,1)S(1)} %get-tuple-element.60), channel_id=1, source_target_pairs={{0,20},{16,4},{8,28},{24,12},{20,0},{4,16},{28,8},{12,24},{1,21},{... | collective-permute-start | bytes 393224 | tf_op jit(solution)/shard_map/ppermute | solution.py:489
  14.1 3.9 %collective-permute-start.5 = (bf16[2,64,512]{2,1,0:T(8,128)(2,1)S(1)}, bf16[2,64,512]{2,1,0:T(8,128)(2,1)S(1)}, u32[]{:S(2)}, u32[]{:S(2)}) collective-permute-start(bf16[2,64,512]{2,1,0:T(8,128)(2,1)S(1)} %get-tuple-element.61), channel_id=1, source_target_pairs={{4,24},{20,8},{24,4},{8,20},{5,25},{21,9},{25,5},{9,21},{6,26},{22... | collective-permute-start | bytes 393224 | tf_op jit(solution)/shard_map/ppermute | solution.py:489
  16.4 8.0 %collective-permute-start.3 = (bf16[4,64,512]{2,1,0:T(8,128)(2,1)S(1)}, bf16[4,64,512]{2,1,0:T(8,128)(2,1)S(1)}, u32[]{:S(2)}, u32[]{:S(2)}) collective-permute-start(bf16[4,64,512]{2,1,0:T(8,128)(2,1)S(1)} %get-tuple-element.58.refs_6_.refs_4_), channel_id=1, source_target_pairs={{0,16},{16,0},{1,17},{17,1},{2,18},{18,2},{3,19},{19,3},{4,20},{20... | collective-permute-start | bytes 786440 | tf_op jit(solution)/shard_map/ppermute | solution.py:461
  29.1 2.0 %collective-permute-start.6 = (bf16[2,2,64,1024]{3,2,1,0:T(8,128)(2,1)S(1)}, bf16[2,2,64,1024]{3,2,1,0:T(8,128)(2,1)S(1)}, u32[]{:S(2)}, u32[]{:S(2)}) collective-permute-start(bf16[2,2,64,1024]{3,2,1,0:T(8,128)(2,1)S(1)} %sent.1), channel_id=1, source_target_pairs={{0,1},{1,0},{2,3},{3,2},{4,5},{5,4},{6,7},{7,6},{8,9},{9,8},{10,11... | collective-permute-start | bytes 1572872 | tf_op jit(solution)/shard_map/ppermute | solution.py:493
  30.0 26.8 %copy-start.4 = (bf16[1,16,16,512]{3,2,1,0:T(8,128)(2,1)S(1)}, bf16[1,16,16,512]{3,2,1,0:T(8,128)(2,1)}, u32[]{:S(2)}) copy-start(bf16[1,16,16,512]{3,2,1,0:T(8,128)(2,1)} %refs_10_.1) | copy-start | bytes 786436
  31.2 7.3 %collective-permute-start.7 = (bf16[64,1024]{1,0:T(8,128)(2,1)S(1)}, bf16[64,1024]{1,0:T(8,128)(2,1)S(1)}, u32[]{:S(2)}, u32[]{:S(2)}) collective-permute-start(bf16[64,1024]{1,0:T(8,128)(2,1)S(1)} %get-tuple-element.78), channel_id=1, source_target_pairs={{0,2},{1,3},{2,0},{3,1},{4,6},{5,7},{6,4},{7,5},{8,10},{9,11},{10,... | collective-permute-start | bytes 393224 | tf_op jit(solution)/shard_map/ppermute | solution.py:493
  31.8 10.1 %collective-permute-start.8 = (bf16[64,1024]{1,0:T(8,128)(2,1)S(1)}, bf16[64,1024]{1,0:T(8,128)(2,1)S(1)}, u32[]{:S(2)}, u32[]{:S(2)}) collective-permute-start(bf16[64,1024]{1,0:T(8,128)(2,1)S(1)} %get-tuple-element.79), channel_id=1, source_target_pairs={{0,4},{4,0},{8,12},{12,8},{1,5},{5,1},{9,13},{13,9},{2,6},{6,2},{1... | collective-permute-start | bytes 393224 | tf_op jit(solution)/shard_map/ppermute | solution.py:493
  37.6 6.6 %collective-permute-start.9 = (bf16[64,1024]{1,0:T(8,128)(2,1)S(1)}, bf16[64,1024]{1,0:T(8,128)(2,1)S(1)}, u32[]{:S(2)}, u32[]{:S(2)}) collective-permute-start(bf16[64,1024]{1,0:T(8,128)(2,1)S(1)} %get-tuple-element.80), channel_id=1, source_target_pairs={{0,6},{1,7},{2,4},{3,5},{4,2},{5,3},{6,0},{7,1},{8,14},{9,15},{10,... | collective-permute-start | bytes 393224 | tf_op jit(solution)/shard_map/ppermute | solution.py:546
  37.9 6.4 %collective-permute-start.10 = (bf16[2,64,512]{2,1,0:T(8,128)(2,1)S(1)}, bf16[2,64,512]{2,1,0:T(8,128)(2,1)S(1)}, u32[]{:S(2)}, u32[]{:S(2)}) collective-permute-start(bf16[2,64,512]{2,1,0:T(8,128)(2,1)S(1)} %get-tuple-element.82), channel_id=1, source_target_pairs={{4,8},{8,4},{5,9},{9,5},{6,10},{10,6},{7,11},{11,7},{20,24},{24,20... | collective-permute-start | bytes 393224 | tf_op jit(solution)/shard_map/ppermute | solution.py:478
  44.3 8.7 %collective-permute-start.11 = (bf16[64,1024]{1,0:T(8,128)(2,1)S(1)}, bf16[64,1024]{1,0:T(8,128)(2,1)S(1)}, u32[]{:S(2)}, u32[]{:S(2)}) collective-permute-start(bf16[64,1024]{1,0:T(8,128)(2,1)S(1)} %add_convert_fusion.1), channel_id=1, source_target_pairs={{0,8},{4,12},{8,0},{12,4},{1,9},{5,13},{9,1},{13,5},{2,10},{6,14},... | collective-permute-start | bytes 393224 | tf_op jit(solution)/shard_map/ppermute | solution.py:493
  46.3 7.0 %collective-permute-start.12 = (bf16[2,64,512]{2,1,0:T(8,128)(2,1)S(1)}, bf16[2,64,512]{2,1,0:T(8,128)(2,1)S(1)}, u32[]{:S(2)}, u32[]{:S(2)}) collective-permute-start(bf16[2,64,512]{2,1,0:T(8,128)(2,1)S(1)} %get-tuple-element.84), channel_id=1, source_target_pairs={{0,4},{8,12},{4,0},{12,8},{1,5},{9,13},{5,1},{13,9},{2,6},{10,14},... | collective-permute-start | bytes 393224 | tf_op jit(solution)/shard_map/ppermute | solution.py:478
  53.3 6.0 %collective-permute-start.15 = (bf16[64,1024]{1,0:T(8,128)(2,1)S(1)}, bf16[64,1024]{1,0:T(8,128)(2,1)S(1)}, u32[]{:S(2)}, u32[]{:S(2)}) collective-permute-start(bf16[64,1024]{1,0:T(8,128)(2,1)S(1)} %add_convert_fusion.own_ref), channel_id=1, source_target_pairs={{0,20},{4,16},{8,28},{12,24},{16,4},{20,0},{24,12},{28,8},{1,21},{... | collective-permute-start | bytes 393224 | tf_op jit(solution)/shard_map/ppermute | solution.py:561
  53.3 6.4 %collective-permute-start.14 = (bf16[64,1024]{1,0:T(8,128)(2,1)S(1)}, bf16[64,1024]{1,0:T(8,128)(2,1)S(1)}, u32[]{:S(2)}, u32[]{:S(2)}) collective-permute-start(bf16[64,1024]{1,0:T(8,128)(2,1)S(1)} %add_convert_fusion.own_ref), channel_id=1, source_target_pairs={{0,16},{16,0},{1,17},{17,1},{2,18},{18,2},{3,19},{19,3},{4,20},{20... | collective-permute-start | bytes 393224 | tf_op jit(solution)/shard_map/ppermute | solution.py:493
  54.7 5.1 %collective-permute-start.13 = (bf16[64,1024]{1,0:T(8,128)(2,1)S(1)}, bf16[64,1024]{1,0:T(8,128)(2,1)S(1)}, u32[]{:S(2)}, u32[]{:S(2)}) collective-permute-start(bf16[64,1024]{1,0:T(8,128)(2,1)S(1)} %add_convert_fusion.own_ref), channel_id=1, source_target_pairs={{0,4},{4,0},{8,12},{12,8},{1,5},{5,1},{9,13},{13,9},{2,6},{6,2},{1... | collective-permute-start | bytes 393224 | tf_op jit(solution)/shard_map/ppermute | solution.py:493
